TPU v7x, 32 devices: a whole 2x2x4 slice. The times are simulated.
32 devices in a mesh: dp: 8 (over z, core), ctx: 4 (over y, x).
Axes of the slice: x: 2, y: 2, z: 4, core: 2. Of those that a mesh axis runs over, the one named last changes fastest.
Arguments:
- tokens: bfloat16 [8, 1024, 1024], P('dp', 'ctx'), may hold values from -6 to 6
- cotangent: bfloat16 [8, 1024, 1024], P('dp', 'ctx'), may hold values from -6 to 6
- routes: int32 [8, 1024, 1], P('dp', 'ctx'), may hold values from 0 to 1; in each aligned block of 256 rows (0 to 255, 256 to 511, ..., all dimensions but the last counted through in order) at most 160 rows name the same one
- ln1_gain: bfloat16 [1024], P(('dp', 'ctx')), may hold values from 0.5 to 1.5
- ln1_bias: bfloat16 [1024], P(('dp', 'ctx')), may hold values from -4 to 4
- qkv_weight: bfloat16 [1024, 3072], P(('dp', 'ctx')), may hold values from -0.1875 to 0.1875
- qv_bias: bfloat16 [2048], P(('dp', 'ctx')), may hold values from -4 to 4
- out_weight: bfloat16 [1024, 1024], P(('dp', 'ctx')), may hold values from -3 to 3
- out_bias: bfloat16 [1024], P(('dp', 'ctx')), may hold values from -4 to 4
- ln2_gain: bfloat16 [1024], P(('dp', 'ctx')), may hold values from 0.5 to 1.5
- ln2_bias: bfloat16 [1024], P(('dp', 'ctx')), may hold values from -4 to 4
- up_weight: bfloat16 [1024, 4096], P(('dp', 'ctx')), may hold values from -0.1875 to 0.1875
- up_bias: bfloat16 [4096], P(('dp', 'ctx')), may hold values from -4 to 4
- down_weight: bfloat16 [4096, 1024], P(('dp', 'ctx')), may hold values from -0.25 to 0.25
- down_bias: bfloat16 [1024], P(('dp', 'ctx')), may hold values from -4 to 4
- router_weight: bfloat16 [1024, 2], P(('dp', 'ctx')), may hold values from -0.375 to 0.375
- mix_weight: bfloat16 [1024, 2], P(('dp', 'ctx')), may hold values from -0.4375 to 0.4375
- expert_up: bfloat16 [2, 1024, 4096], P(None, ('dp', 'ctx')), may hold values from -0.1875 to 0.1875
- expert_up_bias: bfloat16 [2, 4096], P(None, ('dp', 'ctx')), may hold values from -4 to 4
- expert_down: bfloat16 [2, 4096, 1024], P(None, ('dp', 'ctx')), may hold values from -0.375 to 0.375
- expert_down_bias: bfloat16 [2, 1024], P(None, ('dp', 'ctx')), may hold values from -4 to 4
Outputs:
- result: float32 [8, 1024, 1024], P('dp', 'ctx')
- tokens_grad: float32 [8, 1024, 1024], P('dp', 'ctx')
- ln1_gain_grad: float32 [1024], P(('dp', 'ctx'))
- ln1_bias_grad: float32 [1024], P(('dp', 'ctx'))
- qkv_weight_grad: float32 [1024, 3072], P(('dp', 'ctx'))
- qv_bias_grad: float32 [2048], P(('dp', 'ctx'))
- out_weight_grad: float32 [1024, 1024], P(('dp', 'ctx'))
- out_bias_grad: float32 [1024], P(('dp', 'ctx'))
- ln2_gain_grad: float32 [1024], P(('dp', 'ctx'))
- ln2_bias_grad: float32 [1024], P(('dp', 'ctx'))
- up_weight_grad: float32 [1024, 4096], P(('dp', 'ctx'))
- up_bias_grad: float32 [4096], P(('dp', 'ctx'))
- down_weight_grad: float32 [4096, 1024], P(('dp', 'ctx'))
- down_bias_grad: float32 [1024], P(('dp', 'ctx'))
- router_weight_grad: float32 [1024, 2], P(('dp', 'ctx'))
- mix_weight_grad: float32 [1024, 2], P(('dp', 'ctx'))
- expert_up_grad: float32 [2, 1024, 4096], P(None, ('dp', 'ctx'))
- expert_up_bias_grad: float32 [2, 4096], P(None, ('dp', 'ctx'))
- expert_down_grad: float32 [2, 4096, 1024], P(None, ('dp', 'ctx'))
- expert_down_bias_grad: float32 [2, 1024], P(None, ('dp', 'ctx'))
Inputs may be any that keep to these rules, and one draw needn't show every extreme that they name: `routes`: in each aligned block of 256 tokens (one sequence's tokens on one device) each expert is named by at most 160 tokens, and in some blocks exactly 160.
All inputs are finite; a program needn't handle non-finite values.
Results may differ from a plain program's by a relative error of at most 0.01.
The roundings to bfloat16 on the way count: a program that leaves them out, or rounds other values in their place, can miss the bound.
Values may be sent and summed in bfloat16 or wider, within the bound.
No kernel may reach another device: no remote copies, remote signals or barrier semaphores. Data moves between devices by JAX's collectives and lax.ppermute only.
A program may use at most 320 MiB of HBM per device.

v0:
```python
import jax
import jax.numpy as jnp
from jax import lax
from jax.sharding import PartitionSpec as P

HEAD_DIM = 64


highest = lax.Precision.HIGHEST
group_heads = 2
epsilon = 1e-05


def product(left_op, right_op):
    return jnp.dot(left_op, right_op, preferred_element_type=jnp.float32)


def left_product(left_op, right_op):
    return lax.dot_general(
        left_op, right_op, (((0,), (0,)), ((), ())), preferred_element_type=jnp.float32
    )


def right_product(left_op, right_op):
    return lax.dot_general(
        left_op, right_op, (((1,), (1,)), ((), ())), preferred_element_type=jnp.float32
    )


def layer_stats(values):
    row_mean = jnp.mean(values, -1, keepdims=True)
    centred = values - row_mean
    inverse = lax.rsqrt(jnp.mean(centred * centred, -1, keepdims=True) + epsilon)
    return (centred * inverse, inverse)


def norm_back(grad_norm, normed, inverse, gain):
    scaled = grad_norm * gain
    return inverse * (
        scaled
        - jnp.mean(scaled, -1, keepdims=True)
        - normed * jnp.mean(scaled * normed, -1, keepdims=True)
    )


def gelu_grad(pre_act, grad_act):
    return jax.vjp(lambda inner_val: jax.nn.gelu(inner_val, approximate=True), pre_act)[1](
        grad_act
    )[0]


def fetch_expert(up_shards, up_bias_shards, down_shards, down_bias_shards, expert):
    return (
        lax.all_gather(up_shards[expert], ("dp", "ctx"), axis=0, tiled=True),
        lax.all_gather(up_bias_shards[expert], ("dp", "ctx"), axis=0, tiled=True),
        lax.all_gather(down_shards[expert], ("dp", "ctx"), axis=0, tiled=True),
        lax.all_gather(down_bias_shards[expert], ("dp", "ctx"), axis=0, tiled=True),
    )


def refetch_expert(up_shards, up_bias_shards, down_shards, down_bias_shards, expert):
    return (
        lax.all_gather(up_shards[expert], ("dp", "ctx"), axis=0, tiled=True),
        lax.all_gather(up_bias_shards[expert], ("dp", "ctx"), axis=0, tiled=True),
        lax.all_gather(down_shards[expert], ("dp", "ctx"), axis=0, tiled=True),
        lax.all_gather(down_bias_shards[expert], ("dp", "ctx"), axis=0, tiled=True),
    )


def send_expert_grads(up_grad, up_bias_grad, down_grad, down_bias_grad):
    return (
        lax.psum_scatter(up_grad, ("dp", "ctx"), scatter_dimension=0, tiled=True),
        lax.psum_scatter(up_bias_grad, ("dp", "ctx"), scatter_dimension=0, tiled=True),
        lax.psum_scatter(down_grad, ("dp", "ctx"), scatter_dimension=0, tiled=True),
        lax.psum_scatter(down_bias_grad, ("dp", "ctx"), scatter_dimension=0, tiled=True),
    )


def shards(
    tokens,
    cotangent,
    routes,
    ln1_gain,
    ln1_bias,
    qkv_weight,
    qv_bias,
    out_weight,
    out_bias,
    ln2_gain,
    ln2_bias,
    up_weight,
    up_bias,
    down_weight,
    down_bias,
    router_weight,
    mix_weight,
    expert_up,
    expert_up_bias,
    expert_down,
    expert_down_bias,
):
    f32 = jnp.float32
    bf16 = jnp.bfloat16
    seq_count, row_count, model_width = tokens.shape
    token_count = seq_count * row_count
    experts = expert_up.shape[0]
    capacity = row_count * 5 // 8
    head_dim = HEAD_DIM
    head_count = model_width // head_dim
    score_scale = HEAD_DIM ** (-0.5)
    group_width = group_heads * head_dim
    head_steps = model_width // group_width
    gathered = (
        lax.all_gather(ln1_gain, ("dp", "ctx"), axis=0, tiled=True),
        lax.all_gather(ln1_bias, ("dp", "ctx"), axis=0, tiled=True),
        lax.all_gather(qkv_weight, ("dp", "ctx"), axis=0, tiled=True),
        lax.all_gather(qv_bias, ("dp", "ctx"), axis=0, tiled=True),
        lax.all_gather(out_weight, ("dp", "ctx"), axis=0, tiled=True),
        lax.all_gather(out_bias, ("dp", "ctx"), axis=0, tiled=True),
        lax.all_gather(ln2_gain, ("dp", "ctx"), axis=0, tiled=True),
        lax.all_gather(ln2_bias, ("dp", "ctx"), axis=0, tiled=True),
        lax.all_gather(up_weight, ("dp", "ctx"), axis=0, tiled=True),
        lax.all_gather(up_bias, ("dp", "ctx"), axis=0, tiled=True),
        lax.all_gather(down_weight, ("dp", "ctx"), axis=0, tiled=True),
        lax.all_gather(down_bias, ("dp", "ctx"), axis=0, tiled=True),
        lax.all_gather(router_weight, ("dp", "ctx"), axis=0, tiled=True),
        lax.all_gather(mix_weight, ("dp", "ctx"), axis=0, tiled=True),
    )
    (
        gain_one,
        shift_one,
        full_qkv,
        full_qv,
        full_out,
        full_outb,
        gain_two,
        shift_two,
        full_up,
        full_upb,
        full_down,
        full_downb,
        full_router,
        full_mix,
    ) = gathered
    inputs = tokens.astype(f32).reshape(token_count, model_width)
    normed_one, inverse_one = layer_stats(inputs)
    attn_in = (normed_one * gain_one.astype(f32) + shift_one.astype(f32)).astype(bf16)
    qkv_out = product(attn_in, full_qkv)
    bias_qv = full_qv.astype(f32)
    queries = (
        (qkv_out[:, :model_width] + bias_qv[:model_width])
        .astype(bf16)
        .reshape(seq_count, row_count, model_width)
    )
    keys_local = (
        qkv_out[:, model_width : 2 * model_width]
        .astype(bf16)
        .reshape(seq_count, row_count, model_width)
    )
    values_local = (
        (qkv_out[:, 2 * model_width :] + bias_qv[model_width:])
        .astype(bf16)
        .reshape(seq_count, row_count, model_width)
    )
    key_all, value_all = (
        lax.all_gather(keys_local, "ctx", axis=1, tiled=True),
        lax.all_gather(values_local, "ctx", axis=1, tiled=True),
    )
    length = key_all.shape[1]
    offset = lax.axis_index("ctx") * row_count
    query_pos = offset + jnp.arange(row_count)
    allowed = jnp.arange(length)[None, :] <= query_pos[:, None]

    def split_heads(array, column):
        part = lax.dynamic_slice_in_dim(array, column, group_width, 2)
        return part.reshape(part.shape[0], part.shape[1], group_heads, head_dim)

    def scores_of(query_part, key_part, mask):
        raw_scores = (
            jnp.einsum("sqhd,skhd->shqk", query_part, key_part, preferred_element_type=f32)
            * score_scale
        )
        return jnp.where(mask[None, None], raw_scores, -1e30)

    def softmax_parts(masked):
        row_max = jnp.max(masked, -1, keepdims=True)
        exp_terms = jnp.exp(masked - row_max)
        row_sum = jnp.sum(exp_terms, -1, keepdims=True)
        return (exp_terms / row_sum, row_max, row_sum)

    def forward_step(head_step, outputs):
        column = head_step * group_width
        attn_probs, row_max, row_sum = softmax_parts(
            scores_of(split_heads(queries, column), split_heads(key_all, column), allowed)
        )
        mixed_out = jnp.einsum(
            "shqk,skhd->sqhd",
            attn_probs.astype(bf16),
            split_heads(value_all, column),
            preferred_element_type=f32,
        )
        return lax.dynamic_update_slice_in_dim(
            outputs, mixed_out.reshape(seq_count, row_count, group_width), column, 2
        )

    attended = lax.fori_loop(
        0, head_steps, forward_step, jnp.zeros((seq_count, row_count, model_width), f32)
    )
    attended = attended.astype(bf16).reshape(token_count, model_width)
    hidden_state = inputs + (product(attended, full_out) + full_outb.astype(f32))
    normed_two, inverse_two = layer_stats(hidden_state)
    ffn_in = (normed_two * gain_two.astype(f32) + shift_two.astype(f32)).astype(bf16)
    route_probs = jax.nn.softmax(product(ffn_in, full_router), axis=-1)
    route_hot = (routes.reshape(token_count, 1) == jnp.arange(experts)[None, :]).astype(f32)
    gate_value = jnp.sum(route_probs * route_hot, -1)
    mix_coef = jax.nn.softmax(product(ffn_in, full_mix), axis=-1)
    up_dense = product(ffn_in, full_up) + full_upb.astype(f32)
    act_dense = jax.nn.gelu(up_dense, approximate=True).astype(bf16)
    out_dense = product(act_dense, full_down) + full_downb.astype(f32)
    hot_rows = route_hot.reshape(seq_count, row_count, experts)
    ranks = jnp.cumsum(hot_rows, axis=1) - 1.0
    hot_turned = jnp.transpose(hot_rows, (0, 2, 1))
    rank_turned = jnp.transpose(ranks, (0, 2, 1))
    slot_ids = jnp.arange(capacity).astype(f32)
    selector = hot_turned[:, :, None, :] * (
        rank_turned[:, :, None, :] == slot_ids[None, None, :, None]
    ).astype(f32)
    selector_low = selector.astype(bf16)
    ffn_rows = ffn_in.reshape(seq_count, row_count, model_width)
    moe_out = jnp.zeros((seq_count, row_count, model_width), f32)
    fetched = []
    expert_cache = []
    for expert in range(experts):
        expert_set = fetch_expert(expert_up, expert_up_bias, expert_down, expert_down_bias, expert)
        fetched.append(expert_set)
        slot_in = (
            jnp.einsum(
                "scr,srd->scd", selector_low[:, expert], ffn_rows, preferred_element_type=f32
            )
            .astype(bf16)
            .reshape(seq_count * capacity, model_width)
        )
        slot_up = product(slot_in, expert_set[0]) + expert_set[1].astype(f32)
        slot_act = jax.nn.gelu(slot_up, approximate=True).astype(bf16)
        slot_out = product(slot_act, expert_set[2]) + expert_set[3].astype(f32)
        moe_out = moe_out + jnp.einsum(
            "scr,scd->srd",
            selector[:, expert],
            slot_out.reshape(seq_count, capacity, model_width),
            precision=highest,
        )
        expert_cache.append((slot_in, slot_up, slot_act))
    moe_flat = moe_out.reshape(token_count, model_width)
    branch_coef = mix_coef[:, 1] * gate_value
    result = hidden_state + mix_coef[:, 0:1] * out_dense + branch_coef[:, None] * moe_flat
    gathered = (
        lax.all_gather(ln1_gain, ("dp", "ctx"), axis=0, tiled=True),
        lax.all_gather(ln1_bias, ("dp", "ctx"), axis=0, tiled=True),
        lax.all_gather(qkv_weight, ("dp", "ctx"), axis=0, tiled=True),
        lax.all_gather(qv_bias, ("dp", "ctx"), axis=0, tiled=True),
        lax.all_gather(out_weight, ("dp", "ctx"), axis=0, tiled=True),
        lax.all_gather(out_bias, ("dp", "ctx"), axis=0, tiled=True),
        lax.all_gather(ln2_gain, ("dp", "ctx"), axis=0, tiled=True),
        lax.all_gather(ln2_bias, ("dp", "ctx"), axis=0, tiled=True),
        lax.all_gather(up_weight, ("dp", "ctx"), axis=0, tiled=True),
        lax.all_gather(up_bias, ("dp", "ctx"), axis=0, tiled=True),
        lax.all_gather(down_weight, ("dp", "ctx"), axis=0, tiled=True),
        lax.all_gather(down_bias, ("dp", "ctx"), axis=0, tiled=True),
        lax.all_gather(router_weight, ("dp", "ctx"), axis=0, tiled=True),
        lax.all_gather(mix_weight, ("dp", "ctx"), axis=0, tiled=True),
    )
    (
        gain_one,
        shift_one,
        full_qkv,
        full_qv,
        full_out,
        full_outb,
        gain_two,
        shift_two,
        full_up,
        full_upb,
        full_down,
        full_downb,
        full_router,
        full_mix,
    ) = gathered
    back_experts = [
        refetch_expert(expert_up, expert_up_bias, expert_down, expert_down_bias, expert)
        for expert in range(experts)
    ]
    grad_out = cotangent.astype(f32).reshape(token_count, model_width)
    grad_dense_out = (grad_out * mix_coef[:, 0:1]).astype(bf16)
    grad_moe = (grad_out * branch_coef[:, None]).reshape(seq_count, row_count, model_width)
    moe_dot = jnp.sum(grad_out * moe_flat, -1)
    grad_mixc = jnp.stack([jnp.sum(grad_out * out_dense, -1), moe_dot * gate_value], -1)
    grad_gate = moe_dot * mix_coef[:, 1]
    grad_mix_logits = mix_coef * (grad_mixc - jnp.sum(mix_coef * grad_mixc, -1, keepdims=True))
    grad_probs = route_hot * grad_gate[:, None]
    grad_router_logits = route_probs * (
        grad_probs - jnp.sum(route_probs * grad_probs, -1, keepdims=True)
    )
    grad_w_down = left_product(act_dense, grad_dense_out)
    grad_b_down = jnp.sum(grad_dense_out.astype(f32), 0)
    grad_act = right_product(grad_dense_out, full_down)
    grad_up_dense = gelu_grad(up_dense, grad_act).astype(bf16)
    grad_w_up = left_product(ffn_in, grad_up_dense)
    grad_b_up = jnp.sum(grad_up_dense.astype(f32), 0)
    grad_ffn = right_product(grad_up_dense, full_up)
    grad_small = jnp.concatenate([grad_router_logits, grad_mix_logits], -1)
    small_weights = jnp.concatenate([full_router, full_mix], 1).astype(f32)
    grad_small_w = jnp.einsum(
        "nd,ne->de", ffn_in, grad_small, precision=highest, preferred_element_type=f32
    )
    grad_ffn = grad_ffn + jnp.einsum("ne,de->nd", grad_small, small_weights, precision=highest)
    expert_grad_sets = []
    for expert in range(experts):
        slot_in, slot_up, slot_act = expert_cache[expert]
        expert_set = back_experts[expert]
        grad_slot = (
            jnp.einsum("scr,srd->scd", selector[:, expert], grad_moe, precision=highest)
            .astype(bf16)
            .reshape(seq_count * capacity, model_width)
        )
        grad_down_e = left_product(slot_act, grad_slot)
        grad_downb_e = jnp.sum(grad_slot.astype(f32), 0)
        grad_slot_act = right_product(grad_slot, expert_set[2])
        grad_slot_up = gelu_grad(slot_up, grad_slot_act).astype(bf16)
        grad_up_e = left_product(slot_in, grad_slot_up)
        grad_upb_e = jnp.sum(grad_slot_up.astype(f32), 0)
        grad_slot_in = right_product(grad_slot_up, expert_set[0]).reshape(
            seq_count, capacity, model_width
        )
        grad_ffn = grad_ffn + jnp.einsum(
            "scr,scd->srd", selector[:, expert], grad_slot_in, precision=highest
        ).reshape(token_count, model_width)
        expert_grad_sets.append(send_expert_grads(grad_up_e, grad_upb_e, grad_down_e, grad_downb_e))
    grad_gain_two = jnp.sum(grad_ffn * normed_two, 0)
    grad_shift_two = jnp.sum(grad_ffn, 0)
    grad_hidden = grad_out + norm_back(grad_ffn, normed_two, inverse_two, gain_two.astype(f32))
    grad_proj = grad_hidden.astype(bf16)
    grad_w_out = left_product(attended, grad_proj)
    grad_b_out = jnp.sum(grad_proj.astype(f32), 0)
    grad_attended = (
        right_product(grad_proj, full_out).astype(bf16).reshape(seq_count, row_count, model_width)
    )
    key_width = 1

    def query_step(head_step, state_in):
        grad_q, grad_k, grad_v, maxima, totals, deltas = state_in
        column = head_step * group_width
        first_head = head_step * group_heads
        q_part = split_heads(queries, column)
        k_part = split_heads(key_all, column)
        v_part = split_heads(value_all, column)
        o_grad = split_heads(grad_attended, column)
        attn_probs, row_max, row_sum = softmax_parts(scores_of(q_part, k_part, allowed))
        prob_grad = jnp.einsum("sqhd,skhd->shqk", o_grad, v_part, preferred_element_type=f32)
        delta_val = jnp.sum(attn_probs * prob_grad, -1, keepdims=True)
        score_grad = (attn_probs * (prob_grad - delta_val)).astype(bf16)
        q_grad = (
            jnp.einsum("shqk,skhd->sqhd", score_grad, k_part, preferred_element_type=f32)
            * score_scale
        )
        grad_q = lax.dynamic_update_slice_in_dim(
            grad_q, q_grad.reshape(seq_count, row_count, group_width), column, 2
        )
        maxima = lax.dynamic_update_slice_in_dim(maxima, row_max[..., 0], first_head, 1)
        totals = lax.dynamic_update_slice_in_dim(totals, row_sum[..., 0], first_head, 1)
        deltas = lax.dynamic_update_slice_in_dim(deltas, delta_val[..., 0], first_head, 1)
        return (grad_q, grad_k, grad_v, maxima, totals, deltas)

    stat_zeros = jnp.zeros((seq_count, head_count, row_count), f32)
    start_state = (
        jnp.zeros((seq_count, row_count, model_width), f32),
        jnp.zeros((seq_count, key_width, model_width), f32),
        jnp.zeros((seq_count, key_width, model_width), f32),
        stat_zeros,
        stat_zeros,
        stat_zeros,
    )
    grad_q, grad_k, grad_v, maxima, totals, deltas = lax.fori_loop(
        0, head_steps, query_step, start_state
    )
    query_all, grad_att_all = (
        lax.all_gather(queries, "ctx", axis=1, tiled=True),
        lax.all_gather(grad_attended, "ctx", axis=1, tiled=True),
    )
    max_all, sum_all, delta_all = (
        lax.all_gather(maxima, "ctx", axis=2, tiled=True),
        lax.all_gather(totals, "ctx", axis=2, tiled=True),
        lax.all_gather(deltas, "ctx", axis=2, tiled=True),
    )
    key_mask = query_pos[None, :] <= jnp.arange(length)[:, None]

    def key_step(head_step, state_in):
        grad_keys_acc, grad_values_acc = state_in
        column = head_step * group_width
        first_head = head_step * group_heads
        q_part = split_heads(query_all, column)
        k_part = split_heads(keys_local, column)
        v_part = split_heads(values_local, column)
        o_grad = split_heads(grad_att_all, column)
        masked = scores_of(q_part, k_part, key_mask)
        part_max = lax.dynamic_slice_in_dim(max_all, first_head, group_heads, 1)[..., None]
        part_sum = lax.dynamic_slice_in_dim(sum_all, first_head, group_heads, 1)[..., None]
        part_delta = lax.dynamic_slice_in_dim(delta_all, first_head, group_heads, 1)[..., None]
        attn_probs = jnp.exp(masked - part_max) / part_sum
        prob_grad = jnp.einsum("sqhd,skhd->shqk", o_grad, v_part, preferred_element_type=f32)
        score_grad = (attn_probs * (prob_grad - part_delta)).astype(bf16)
        value_grad = jnp.einsum(
            "shqk,sqhd->skhd", attn_probs.astype(bf16), o_grad, preferred_element_type=f32
        )
        key_grad = (
            jnp.einsum("shqk,sqhd->skhd", score_grad, q_part, preferred_element_type=f32)
            * score_scale
        )
        grad_keys_acc = lax.dynamic_update_slice_in_dim(
            grad_keys_acc, key_grad.reshape(seq_count, row_count, group_width), column, 2
        )
        grad_values_acc = lax.dynamic_update_slice_in_dim(
            grad_values_acc, value_grad.reshape(seq_count, row_count, group_width), column, 2
        )
        return (grad_keys_acc, grad_values_acc)

    local_zeros = jnp.zeros((seq_count, row_count, model_width), f32)
    key_grad_local, value_grad_local = lax.fori_loop(
        0, head_steps, key_step, (local_zeros, local_zeros)
    )
    grad_q_low = grad_q.astype(bf16).reshape(token_count, model_width)
    grad_k_low = key_grad_local.astype(bf16).reshape(token_count, model_width)
    grad_v_low = value_grad_local.astype(bf16).reshape(token_count, model_width)
    grad_qkv = jnp.concatenate([grad_q_low, grad_k_low, grad_v_low], -1)
    grad_w_qkv = left_product(attn_in, grad_qkv)
    grad_b_qv = jnp.concatenate(
        [jnp.sum(grad_q_low.astype(f32), 0), jnp.sum(grad_v_low.astype(f32), 0)], 0
    )
    grad_attn_in = right_product(grad_qkv, full_qkv)
    grad_gain_one = jnp.sum(grad_attn_in * normed_one, 0)
    grad_shift_one = jnp.sum(grad_attn_in, 0)
    grad_inputs = grad_hidden + norm_back(
        grad_attn_in, normed_one, inverse_one, gain_one.astype(f32)
    )
    reduced = (
        lax.psum_scatter(grad_gain_one, ("dp", "ctx"), scatter_dimension=0, tiled=True),
        lax.psum_scatter(grad_shift_one, ("dp", "ctx"), scatter_dimension=0, tiled=True),
        lax.psum_scatter(grad_w_qkv, ("dp", "ctx"), scatter_dimension=0, tiled=True),
        lax.psum_scatter(grad_b_qv, ("dp", "ctx"), scatter_dimension=0, tiled=True),
        lax.psum_scatter(grad_w_out, ("dp", "ctx"), scatter_dimension=0, tiled=True),
        lax.psum_scatter(grad_b_out, ("dp", "ctx"), scatter_dimension=0, tiled=True),
        lax.psum_scatter(grad_gain_two, ("dp", "ctx"), scatter_dimension=0, tiled=True),
        lax.psum_scatter(grad_shift_two, ("dp", "ctx"), scatter_dimension=0, tiled=True),
        lax.psum_scatter(grad_w_up, ("dp", "ctx"), scatter_dimension=0, tiled=True),
        lax.psum_scatter(grad_b_up, ("dp", "ctx"), scatter_dimension=0, tiled=True),
        lax.psum_scatter(grad_w_down, ("dp", "ctx"), scatter_dimension=0, tiled=True),
        lax.psum_scatter(grad_b_down, ("dp", "ctx"), scatter_dimension=0, tiled=True),
        lax.psum_scatter(grad_small_w[:, :experts], ("dp", "ctx"), scatter_dimension=0, tiled=True),
        lax.psum_scatter(grad_small_w[:, experts:], ("dp", "ctx"), scatter_dimension=0, tiled=True),
    )
    expert_up_grad = jnp.stack([grad_set[0] for grad_set in expert_grad_sets], 0)
    expert_up_bias_grad = jnp.stack([grad_set[1] for grad_set in expert_grad_sets], 0)
    expert_down_grad = jnp.stack([grad_set[2] for grad_set in expert_grad_sets], 0)
    expert_down_bias_grad = jnp.stack([grad_set[3] for grad_set in expert_grad_sets], 0)
    return (
        result.reshape(seq_count, row_count, model_width),
        grad_inputs.reshape(seq_count, row_count, model_width),
        reduced[0],
        reduced[1],
        reduced[2],
        reduced[3],
        reduced[4],
        reduced[5],
        reduced[6],
        reduced[7],
        reduced[8],
        reduced[9],
        reduced[10],
        reduced[11],
        reduced[12],
        reduced[13],
        expert_up_grad,
        expert_up_bias_grad,
        expert_down_grad,
        expert_down_bias_grad,
    )


def solution(mesh):
    return jax.shard_map(
        shards,
        mesh=mesh,
        in_specs=(
            P("dp", "ctx", None),
            P("dp", "ctx", None),
            P("dp", "ctx", None),
            P(("dp", "ctx")),
            P(("dp", "ctx")),
            P(("dp", "ctx"), None),
            P(("dp", "ctx")),
            P(("dp", "ctx"), None),
            P(("dp", "ctx")),
            P(("dp", "ctx")),
            P(("dp", "ctx")),
            P(("dp", "ctx"), None),
            P(("dp", "ctx")),
            P(("dp", "ctx"), None),
            P(("dp", "ctx")),
            P(("dp", "ctx"), None),
            P(("dp", "ctx"), None),
            P(None, ("dp", "ctx"), None),
            P(None, ("dp", "ctx")),
            P(None, ("dp", "ctx"), None),
            P(None, ("dp", "ctx")),
        ),
        out_specs=(
            P("dp", "ctx", None),
            P("dp", "ctx", None),
            P(("dp", "ctx")),
            P(("dp", "ctx")),
            P(("dp", "ctx"), None),
            P(("dp", "ctx")),
            P(("dp", "ctx"), None),
            P(("dp", "ctx")),
            P(("dp", "ctx")),
            P(("dp", "ctx")),
            P(("dp", "ctx"), None),
            P(("dp", "ctx")),
            P(("dp", "ctx"), None),
            P(("dp", "ctx")),
            P(("dp", "ctx"), None),
            P(("dp", "ctx"), None),
            P(None, ("dp", "ctx"), None),
            P(None, ("dp", "ctx")),
            P(None, ("dp", "ctx"), None),
            P(None, ("dp", "ctx")),
        ),
        check_vma=False,
    )
```

profile of v0, /device:TPU:0, one launch (start us, length us, event | category | flops | bytes accessed | tf_op | source)
XLA Modules:
  0.0 3718.9 jit_solution(11571604929768126411)
XLA Ops:
  15.0 42.6 %all-reduce.22 = (bf16[1024]{0:T(1024)(128)(2,1)S(1)}, bf16[1024]{0:T(1024)(128)(2,1)S(1)}, bf16[1024]{0:T(1024)(128)(2,1)S(1)}, bf16[1024]{0:T(1024)(128)(2,1)S...) all-reduce(bf16[1024]{0:T(1024)(128)(2,1)S(1)} %dynamic-update-slic, ...), channel_id=7, replica_groups=mesh['dp'=8,'ctx'=4] {'dp','ctx'}, use_global_device_ids=true, to_apply=%add.7 | all-reduce | flops 10240 | bytes 40960
  60.4 23.0 all-gather.28.cloned.1.call-done
  83.3 4.9 fusion.153
  99.8 65.5 %all-gather.13 = bf16[32,1,128]{2,1,0:T(2,128)(2,1)S(1)} all-gather(bf16[1,1,128]{2,1,0:T(2,128)(2,1)S(1)} %bitcast.438), channel_id=1, replica_groups=mesh['dp'=8,'ctx'=4] {'dp','ctx'}, dimensions={0}, use_global_device_ids=true | all-gather | bytes 8448 | tf_op jit(solution)/shard_map/all_gather | solution.py:123
  166.0 63.0 %all-gather.12 = bf16[32,32,2]{1,2,0:T(2,128)(2,1)S(1)} all-gather(bf16[1,32,2]{1,2,0:T(2,128)(2,1)S(1)} %bitcast.439), channel_id=1, replica_groups=mesh['dp'=8,'ctx'=4] {'dp','ctx'}, dimensions={0}, use_global_device_ids=true | all-gather | bytes 4224 | tf_op jit(solution)/shard_map/all_gather | solution.py:127
  229.1 65.7 %all-gather.14 = bf16[32,32,2]{1,2,0:T(2,128)(2,1)S(1)} all-gather(bf16[1,32,2]{1,2,0:T(2,128)(2,1)S(1)} %bitcast.440), channel_id=1, replica_groups=mesh['dp'=8,'ctx'=4] {'dp','ctx'}, dimensions={0}, use_global_device_ids=true | all-gather | bytes 4224 | tf_op jit(solution)/shard_map/all_gather | solution.py:126
  296.2 63.1 %all-gather.3 = bf16[1,4096]{1,0:T(2,128)(2,1)S(1)} all-gather(bf16[1,128]{1,0:T(2,128)(2,1)S(1)} %get-tuple-element.758), channel_id=5, replica_groups=mesh['dp'=8,'ctx'=4] {'dp','ctx'}, dimensions={1}, use_global_device_ids=true | all-gather | bytes 8448 | tf_op jit(solution)/shard_map/all_gather | solution.py:55
  360.5 65.3 %all-gather.7 = bf16[1,4096]{1,0:T(2,128)(2,1)S(1)} all-gather(bf16[1,128]{1,0:T(2,128)(2,1)S(1)} %get-tuple-element.757), channel_id=9, replica_groups=mesh['dp'=8,'ctx'=4] {'dp','ctx'}, dimensions={1}, use_global_device_ids=true | all-gather | bytes 8448 | tf_op jit(solution)/shard_map/all_gather | solution.py:55
  435.4 4.0 copy.66
  440.2 49.1 %while.50 = (s32[]{:T(128)}, bf16[1,256,1024]{1,2,0:T(8,128)(2,1)}, bf16[1,1024,1024]{1,2,0:T(8,128)(2,1)S(1)}, bf16[1,256,1024]{1,2,0:T(8,128)(2,1)}, bf16[1,10...) while((s32[]{:T(128)}, bf16[1,256,1024]{1,2,0:T(8,128)(2,1)}, ...), condition=%wide.region_5.6_spmd.clone, body=%wide.region_2.5_spmd.clone.sunk | while | flops 206309888 | bytes 3085479 | solution.py:206
  495.5 6.5 fusion.49
  502.0 6.0 fusion.92
  510.1 8.1 convolution_add_fusion
  518.2 21.5 all-gather.34.cloned.1.call-done
  539.7 8.4 convolution_add_fusion.6
  548.1 70.7 %all-gather.44.cloned.1.call-done = bf16[1,1024,4096]{2,1,0:T(8,128)(2,1)} async-done(((bf16[1,32,4096]{2,1,0:T(8,128)(2,1)}), bf16[1,1024,4096]{2,1,0:T(8,128)(2,1)}) %all-gather.44.cloned.1.call-update) | async-done | bytes 8388624 | tf_op jit(solution)/shard_map/all_gather | solution.py:54
  618.8 6.4 fusion.52
  625.2 73.0 %all-gather.46.cloned.1.call-done = bf16[1,4096,1024]{2,1,0:T(8,128)(2,1)} async-done(((bf16[1,128,1024]{2,1,0:T(8,128)(2,1)}), bf16[1,4096,1024]{2,1,0:T(8,128)(2,1)}) %all-gather.46.cloned.1.call-update) | async-done | bytes 8388624 | tf_op jit(solution)/shard_map/all_gather | solution.py:56
  698.2 18.7 fusion.95
  720.6 7.8 convert_reduce_fusion
  728.4 6.8 fusion.169
  735.9 8.2 convert_reduce_fusion.2
  744.1 2.9 fusion.45
  749.6 8.6 convert_reduce_fusion.1
  758.3 2.9 fusion.37
  768.0 63.4 %while.51 = (s32[]{:T(128)}, bf16[1,256,1024]{1,2,0:T(8,128)(2,1)}, f32[1,16,256]{2,1,0:T(8,128)S(1)}, f32[1,16,256]{2,1,0:T(8,128)S(1)}, f32[1,16,256]{2,1,0:T(...) while((s32[]{:T(128)}, bf16[1,256,1024]{1,2,0:T(8,128)(2,1)}, ...), condition=%wide.region_25.26_spmd.clone, body=%wide.region_21.0_spmd.clone.sunk | while | flops 212138496 | bytes 16481557 | solution.py:382
  832.8 8.8 all_gather.124
  842.9 8.3 all_gather.125
  852.3 8.5 all_gather.127
  862.6 64.1 %while.52 = (s32[]{:T(128)}, bf16[1,256,1024]{1,2,0:T(8,128)(2,1)}, bf16[1,256,1024]{1,2,0:T(8,128)(2,1)}, bf16[1,1024,1024]{2,1,0:T(8,128)(2,1)}, bf16[1,256,10...) while((s32[]{:T(128)}, bf16[1,256,1024]{1,2,0:T(8,128)(2,1)}, ...), condition=%wide.region_27.28_spmd.clone, body=%wide.region_26.27_spmd.clone.sunk | while | flops 272957440 | bytes 11085081 | solution.py:427
  928.0 7.0 fusion.105
  935.7 8.2 fusion.156
  945.6 8.2 fusion.155
  955.2 8.1 fusion.172
  964.7 8.1 fusion.171
  978.2 7.6 fusion.115
  985.8 9.8 fusion.170
  996.7 10.9 fusion.146
  1009.1 99.2 %reduce-scatter.33.cloned.1.call-done = f32[32,2]{1,0:T(8,128)} async-done(((f32[1024,2]{1,0:T(8,128)}), f32[32,2]{1,0:T(8,128)}) %reduce-scatter.33.cloned.1.call-update) | async-done | bytes 272
  1111.0 127.8 %all-reduce.25.cloned.1.call-done = (f32[1024]{0:T(1024)}, f32[1024]{0:T(1024)}, f32[2048]{0:T(1024)}, f32[1024]{0:T(1024)}, f32[1024]{0:T(1024)}, /*index=5*/f3...) async-done(((f32[1024]{0:T(1024)}, f32[1024]{0:T(1024)}, f32[2048]{0:T(1024)}, ...) | async-done | bytes 90128
  1253.0 346.7 %reduce-scatter.29.cloned.1.call-done = f32[128,1024]{1,0:T(8,128)} async-done(((f32[4096,1024]{1,0:T(8,128)}), f32[128,1024]{1,0:T(8,128)}) %reduce-scatter.29.cloned.1.call-update) | async-done | bytes 524304 | tf_op jit(solution)/shard_map/reduce_scatter | solution.py:74
  1599.7 361.5 %reduce-scatter.27.cloned.1.call-done = f32[128,1024]{1,0:T(8,128)} async-done(((f32[4096,1024]{1,0:T(8,128)}), f32[128,1024]{1,0:T(8,128)}) %reduce-scatter.27.cloned.1.call-update) | async-done | bytes 524304 | tf_op jit(solution)/shard_map/reduce_scatter | solution.py:74
  1963.4 359.0 %reduce-scatter.25.cloned.1.call-done = f32[32,4096]{1,0:T(8,128)} async-done(((f32[1024,4096]{1,0:T(8,128)}), f32[32,4096]{1,0:T(8,128)}) %reduce-scatter.25.cloned.1.call-update) | async-done | bytes 524304 | tf_op jit(solution)/shard_map/reduce_scatter | solution.py:72
  2322.5 361.5 %reduce-scatter.23.cloned.1.call-done = f32[32,4096]{1,0:T(8,128)} async-done(((f32[1024,4096]{1,0:T(8,128)}), f32[32,4096]{1,0:T(8,128)}) %reduce-scatter.23.cloned.1.call-update) | async-done | bytes 524304 | tf_op jit(solution)/shard_map/reduce_scatter | solution.py:72
  2686.2 143.8 %reduce-scatter.17.cloned.1.call-done = f32[32,1024]{1,0:T(8,128)} async-done(((f32[1024,1024]{1,0:T(8,128)}), f32[32,1024]{1,0:T(8,128)}) %reduce-scatter.17.cloned.1.call-update) | async-done | bytes 131088 | tf_op jit(solution)/shard_map/reduce_scatter | solution.py:449
  2830.0 160.6 %reduce-scatter.15.cloned.1.call-done = f32[32,3072]{1,0:T(8,128)} async-done(((f32[1024,3072]{1,0:T(8,128)}), f32[32,3072]{1,0:T(8,128)}) %reduce-scatter.15.cloned.1.call-update) | async-done | bytes 393232 | tf_op jit(solution)/shard_map/reduce_scatter | solution.py:447
  2990.6 359.6 %reduce-scatter.19.cloned.1.call-done = f32[32,4096]{1,0:T(8,128)} async-done(((f32[1024,4096]{1,0:T(8,128)}), f32[32,4096]{1,0:T(8,128)}) %reduce-scatter.19.cloned.1.call-update) | async-done | bytes 524304 | tf_op jit(solution)/shard_map/reduce_scatter | solution.py:453
  3350.2 362.0 %reduce-scatter.21.cloned.1.call-done = f32[128,1024]{1,0:T(8,128)} async-done(((f32[4096,1024]{1,0:T(8,128)}), f32[128,1024]{1,0:T(8,128)}) %reduce-scatter.21.cloned.1.call-update) | async-done | bytes 524304 | tf_op jit(solution)/shard_map/reduce_scatter | solution.py:455
  (573 shorter events, 273.7 us)
Async XLA Ops:
  7.2 76.2 %all-gather.28.cloned.1.call-start = ((), (), s32[]{:S(2)}) async-start(), calls=%async_computation.10 | async-start | bytes 6488064 | tf_op jit(solution)/shard_map/all_gather | solution.py:116
  7.9 424.6 %all-gather.36.cloned.1.call-start = ((), (), s32[]{:S(2)}) async-start(), calls=%async_computation.22 | async-start | bytes 2621440 | tf_op jit(solution)/shard_map/all_gather | solution.py:167
  57.6 30.6 copy-start.40
  57.6 30.6 copy-start.38
  58.8 29.4 copy-start.44
  60.3 27.9 copy-start.46
  91.0 338.0 %copy-start.19 = (bf16[256,1024]{1,0:T(8,128)(2,1)}, bf16[256,1024]{1,0:T(8,128)(2,1)S(1)}, u32[]{:S(2)}) copy-start(bf16[256,1024]{1,0:T(8,128)(2,1)S(1)} %get-tuple-element.742) | copy-start | bytes 1572868
  91.0 8.8 copy-start.57
  91.0 75.0 %copy-start.58 = (bf16[32,2]{0,1:T(2,128)(2,1)S(1)}, bf16[32,2]{0,1:T(2,128)(2,1)}, u32[]{:S(2)}) copy-start(bf16[32,2]{0,1:T(2,128)(2,1)} %param.43) | copy-start | bytes 388
  91.0 138.1 %copy-start.59 = (bf16[32,2]{0,1:T(2,128)(2,1)S(1)}, bf16[32,2]{0,1:T(2,128)(2,1)}, u32[]{:S(2)}) copy-start(bf16[32,2]{0,1:T(2,128)(2,1)} %param.42) | copy-start | bytes 388
  91.1 205.1 %copy-start.50 = (s32[1,256,1]{1,2,0:T(1,128)S(1)}, s32[1,256,1]{1,2,0:T(1,128)}, u32[]{:S(2)}) copy-start(s32[1,256,1]{1,2,0:T(1,128)} %param.29) | copy-start | bytes 3076
  91.1 205.1 %copy-start.56 = (bf16[2,128]{1,0:T(2,128)(2,1)S(1)}, bf16[2,128]{1,0:T(2,128)(2,1)}, u32[]{:S(2)}) copy-start(bf16[2,128]{1,0:T(2,128)(2,1)} %param.45) | copy-start | bytes 1540
  91.1 344.3 %all-gather.38.cloned.1.call-start = ((), (), s32[]{:S(2)}) async-start(), calls=%async_computation.23 | async-start | bytes 2621440 | tf_op jit(solution)/shard_map/all_gather | solution.py:166
  93.4 396.0 %all-gather.30.cloned.1.call-start = ((), (), s32[]{:S(2)}) async-start(), calls=%async_computation.11 | async-start | bytes 2162688 | tf_op jit(solution)/shard_map/all_gather | solution.py:118
  94.0 401.6 %all-gather.40.cloned.1.call-start = ((), (), s32[]{:S(2)}) async-start(), calls=%async_computation.24 | async-start | bytes 8650752 | tf_op jit(solution)/shard_map/all_gather | solution.py:54
  94.9 407.1 %all-gather.42.cloned.1.call-start = ((), (), s32[]{:S(2)}) async-start(), calls=%async_computation.25 | async-start | bytes 8650752 | tf_op jit(solution)/shard_map/all_gather | solution.py:56
  95.8 414.3 %all-gather.32.cloned.1.call-start = ((), (), s32[]{:S(2)}) async-start(), calls=%async_computation.12 | async-start | bytes 8650752 | tf_op jit(solution)/shard_map/all_gather | solution.py:122
  96.5 443.1 %all-gather.34.cloned.1.call-start = ((), (), s32[]{:S(2)}) async-start(), calls=%async_computation.13 | async-start | bytes 8650752 | tf_op jit(solution)/shard_map/all_gather | solution.py:124
  97.3 521.5 %all-gather.44.cloned.1.call-start = ((), (), s32[]{:S(2)}) async-start(), calls=%async_computation.26 | async-start | bytes 8650752 | tf_op jit(solution)/shard_map/all_gather | solution.py:54
  98.0 600.2 %all-gather.46.cloned.1.call-start = ((), (), s32[]{:S(2)}) async-start(), calls=%async_computation.27 | async-start | bytes 8650752 | tf_op jit(solution)/shard_map/all_gather | solution.py:56
  98.6 762.2 %all-gather.48.cloned.1.call-start = ((), (), s32[]{:S(2)}) async-start(), calls=%async_computation.28 | async-start | bytes 2621440 | tf_op jit(solution)/shard_map/all_gather | solution.py:386
  432.4 428.4 %all-gather.50.cloned.1.call-start = ((), (), s32[]{:S(2)}) async-start(), calls=%async_computation.29 | async-start | bytes 2621440 | tf_op jit(solution)/shard_map/all_gather | solution.py:387
  440.2 50.5 %copy-start.2 = (bf16[1,256,1024]{2,1,0:T(8,128)(2,1)S(1)}, bf16[1,256,1024]{2,1,0:T(8,128)(2,1)}, u32[]{:S(2)}) copy-start(bf16[1,256,1024]{2,1,0:T(8,128)(2,1)} %param.27) | copy-start | bytes 1572868
  494.3 124.4 %copy-start.23 = (bf16[160,1024]{1,0:T(8,128)(2,1)}, bf16[160,1024]{1,0:T(8,128)(2,1)S(1)}, u32[]{:S(2)}) copy-start(bf16[160,1024]{1,0:T(8,128)(2,1)S(1)} %convolution_convert_fusion.3) | copy-start | bytes 983044
  510.1 29.6 copy-start.52
  518.2 100.5 %copy-start.42 = (f32[1,4096]{1,0:T(1,128)S(1)}, f32[1,4096]{1,0:T(1,128)}, u32[]{:S(2)}) copy-start(f32[1,4096]{1,0:T(1,128)} %convert_element_type.247) | copy-start | bytes 49156
  618.8 79.5 %copy-start.53 = (f32[1024]{0:T(1024)S(1)}, f32[1024]{0:T(1024)}, u32[]{:S(2)}) copy-start(f32[1024]{0:T(1024)} %convert_element_type.251) | copy-start | bytes 12292
  625.2 91.8 %copy-start.4 = (bf16[1,256,1024]{2,1,0:T(8,128)(2,1)S(1)}, bf16[1,256,1024]{2,1,0:T(8,128)(2,1)}, u32[]{:S(2)}) copy-start(bf16[1,256,1024]{2,1,0:T(8,128)(2,1)} %param.28) | copy-start | bytes 1572868
  625.2 91.8 %copy-start.25 = (f32[256,1024]{1,0:T(8,128)S(1)}, f32[256,1024]{1,0:T(8,128)}, u32[]{:S(2)}) copy-start(f32[256,1024]{1,0:T(8,128)} %fusion.124) | copy-start | bytes 3145732
  698.2 18.7 copy-start.26
  720.5 15.4 copy-start.30
  728.4 15.7 slice-start
  747.1 11.2 slice-start.2
  767.1 240.5 %reduce-scatter.31.cloned.1.call-start = ((), (), s32[]{:S(2)}) async-start(), calls=%async_computation.30 | async-start | bytes 540672
  842.9 265.4 %reduce-scatter.33.cloned.1.call-start = ((), (), s32[]{:S(2)}) async-start(), calls=%async_computation.31 | async-start | bytes 540672
  860.8 378.0 %all-reduce.25.cloned.1.call-start = ((), (), s32[]{:S(2)}) async-start(), calls=%async_computation.32 | async-start | bytes 180224
  862.6 65.4 %copy-start.39 = (f32[1024]{0:T(1024)S(1)}, f32[1024]{0:T(1024)}, u32[]{:S(2)}) copy-start(f32[1024]{0:T(1024)} %copy-done.38) | copy-start | bytes 12292
  862.6 65.4 %copy-start.45 = (f32[256]{0:T(256)S(1)}, f32[256]{0:T(256)}, u32[]{:S(2)}) copy-start(f32[256]{0:T(256)} %copy-done.44) | copy-start | bytes 3076
  862.6 65.4 %copy-start.47 = (f32[256]{0:T(256)S(1)}, f32[256]{0:T(256)}, u32[]{:S(2)}) copy-start(f32[256]{0:T(256)} %copy-done.46) | copy-start | bytes 3076
  935.6 664.0 %reduce-scatter.29.cloned.1.call-start = ((), (), s32[]{:S(2)}) async-start(), calls=%async_computation.21 | async-start | bytes 17301504 | tf_op jit(solution)/shard_map/reduce_scatter | solution.py:74
  943.9 1017.3 %reduce-scatter.27.cloned.1.call-start = ((), (), s32[]{:S(2)}) async-start(), calls=%async_computation.20 | async-start | bytes 17301504 | tf_op jit(solution)/shard_map/reduce_scatter | solution.py:74
  953.8 1368.6 %reduce-scatter.25.cloned.1.call-start = ((), (), s32[]{:S(2)}) async-start(), calls=%async_computation.19 | async-start | bytes 17301504 | tf_op jit(solution)/shard_map/reduce_scatter | solution.py:72
  963.3 1720.6 %reduce-scatter.23.cloned.1.call-start = ((), (), s32[]{:S(2)}) async-start(), calls=%async_computation.18 | async-start | bytes 17301504 | tf_op jit(solution)/shard_map/reduce_scatter | solution.py:72
  972.8 1857.2 %reduce-scatter.17.cloned.1.call-start = ((), (), s32[]{:S(2)}) async-start(), calls=%async_computation.15 | async-start | bytes 4325376 | tf_op jit(solution)/shard_map/reduce_scatter | solution.py:449
  976.9 2013.7 %reduce-scatter.15.cloned.1.call-start = ((), (), s32[]{:S(2)}) async-start(), calls=%async_computation.14 | async-start | bytes 12976128 | tf_op jit(solution)/shard_map/reduce_scatter | solution.py:447
  985.8 2364.4 %reduce-scatter.19.cloned.1.call-start = ((), (), s32[]{:S(2)}) async-start(), calls=%async_computation.16 | async-start | bytes 17301504 | tf_op jit(solution)/shard_map/reduce_scatter | solution.py:453
  995.7 2716.5 %reduce-scatter.21.cloned.1.call-start = ((), (), s32[]{:S(2)}) async-start(), calls=%async_computation.17 | async-start | bytes 17301504 | tf_op jit(solution)/shard_map/reduce_scatter | solution.py:455
  1007.6 102.1 %copy-start.34 = (f32[256,1024]{1,0:T(8,128)S(1)}, f32[256,1024]{1,0:T(8,128)}, u32[]{:S(2)}) copy-start(f32[256,1024]{1,0:T(8,128)} %get-tuple-element.769) | copy-start | bytes 3145732
  (39 other events, 145.4 us)
Sparse Core Ops, SparseCore 0:
  10.9 72.3 all-gather.27
  91.1 33.8 all-gather.35
  127.5 35.3 all-gather.37
  165.6 56.4 all-gather.29
  225.4 76.5 all-gather.39
  305.3 76.2 all-gather.41
  384.5 76.2 all-gather.31
  463.6 76.0 all-gather.33
  542.6 76.1 all-gather.43
  622.0 76.1 all-gather.45
  700.1 33.8 all-gather.47
  767.2 34.2 all-gather.49
  843.0 133.0 reduce-scatter.30
  978.3 129.9 reduce-scatter.32
  1114.6 124.1 all-reduce.24
  1241.1 358.5 reduce-scatter.28
  1601.9 359.1 reduce-scatter.26
  1963.4 359.0 reduce-scatter.24
  2324.9 359.0 reduce-scatter.22
  2686.8 143.1 reduce-scatter.16
  2837.6 152.9 reduce-scatter.14
  2993.5 356.6 reduce-scatter.18
  3353.1 359.0 reduce-scatter.20
where the time goes:
time: 3730 us; the launch traced here: 3720 us
  waiting for transfers between devices  2870 us (77%)
  blocking collectives  391 us (10%)
  matrix products  251 us (7%)
  local copies, waits for them, and re-layouts  151 us (4%)
    reduce_scatter x2, waiting for transfers between devices, send_expert_grads(): lax.psum_scatter(up_grad, ('dp', 'ctx'), scatter_dimension=0, tiled=True)  721 us
    reduce_scatter x2, waiting for transfers between devices, send_expert_grads(): lax.psum_scatter(down_grad, ('dp', 'ctx'), scatter_dimension=0, tiled=True)  708 us
    reduce_scatter x1, waiting for transfers between devices, shards(): lax.psum_scatter(grad_w_down, ('dp', 'ctx'), scatter_dimension=0, tiled=T...  362 us
    reduce_scatter x1, waiting for transfers between devices, shards(): lax.psum_scatter(grad_w_up, ('dp', 'ctx'), scatter_dimension=0, tiled=True)  360 us
    unnamed x26, waiting for transfers between devices  231 us
    reduce_scatter x1, waiting for transfers between devices, shards(): lax.psum_scatter(grad_w_qkv, ('dp', 'ctx'), scatter_dimension=0, tiled=True)  161 us
    reduce_scatter x1, waiting for transfers between devices, shards(): lax.psum_scatter(grad_w_out, ('dp', 'ctx'), scatter_dimension=0, tiled=True)  144 us
    all_gather x2, blocking collectives, fetch_expert(): lax.all_gather(up_bias_shards[expert], ('dp', 'ctx'), axis=0, tiled=True)  128 us
  transfers between devices with their start and end apart: 23, of which 14 were waited for; matrix products, arithmetic and copies ran while one was open for 11% of the time, Pallas kernels for 0%

commit v1 on v0

v1 whole, which is shorter than its diff:
```python
import functools

import jax
import jax.numpy as jnp
from jax import lax
from jax.experimental import pallas as pl
from jax.experimental.pallas import tpu as pltpu
from jax.sharding import PartitionSpec as P

HEAD_DIM = 64
EPSILON = 1e-05
f32 = jnp.float32
bf16 = jnp.bfloat16
highest = lax.Precision.HIGHEST


def product(left_op, right_op):
    return jnp.dot(left_op, right_op, preferred_element_type=f32)


def left_product(left_op, right_op):
    return lax.dot_general(left_op, right_op, (((0,), (0,)), ((), ())), preferred_element_type=f32)


def right_product(left_op, right_op):
    return lax.dot_general(left_op, right_op, (((1,), (1,)), ((), ())), preferred_element_type=f32)


def layer_stats(values):
    row_mean = jnp.mean(values, -1, keepdims=True)
    centred = values - row_mean
    inverse = lax.rsqrt(jnp.mean(centred * centred, -1, keepdims=True) + EPSILON)
    return (centred * inverse, inverse)


def norm_back(grad_norm, normed, inverse, gain):
    scaled = grad_norm * gain
    return inverse * (
        scaled
        - jnp.mean(scaled, -1, keepdims=True)
        - normed * jnp.mean(scaled * normed, -1, keepdims=True)
    )


def gelu(pre_act):
    return jax.nn.gelu(pre_act, approximate=True)


def gelu_grad(pre_act, grad_act):
    return jax.vjp(gelu, pre_act)[1](grad_act)[0]


def score_parts(q_part, k_ref, column, step, block):
    scale = HEAD_DIM ** (-0.5)
    parts = []
    if step:
        parts.append(right_product(q_part, k_ref[0 : step * block, column]) * scale)
    diagonal = right_product(q_part, k_ref[step * block : (step + 1) * block, column]) * scale
    rows = lax.broadcasted_iota(jnp.int32, (block, block), 0)
    keys = lax.broadcasted_iota(jnp.int32, (block, block), 1)
    parts.append(jnp.where(keys <= rows, diagonal, -1e30))
    return parts


def softmax_of(parts):
    row_max = functools.reduce(jnp.maximum, [jnp.max(part, -1, keepdims=True) for part in parts])
    terms = [jnp.exp(part - row_max) for part in parts]
    total = functools.reduce(jnp.add, [jnp.sum(term, -1, keepdims=True) for term in terms])
    inverse = 1.0 / total
    return [term * inverse for term in terms]


def key_spans(step, block):
    spans = [slice(0, step * block)] if step else []
    return spans + [slice(step * block, (step + 1) * block)]


def attention_forward_kernel(heads, block, q_ref, k_ref, v_ref, out_ref):
    for head in range(heads):
        column = slice(head * HEAD_DIM, (head + 1) * HEAD_DIM)
        for step in range(q_ref.shape[0] // block):
            rows = slice(step * block, (step + 1) * block)
            probs = softmax_of(score_parts(q_ref[rows, column], k_ref, column, step, block))
            mixed = functools.reduce(
                jnp.add,
                [
                    product(prob.astype(bf16), v_ref[span, column])
                    for prob, span in zip(probs, key_spans(step, block))
                ],
            )
            out_ref[rows, column] = mixed.astype(bf16)


def attention_backward_kernel(
    heads, block, q_ref, k_ref, v_ref, o_ref, dq_ref, dk_ref, dv_ref, k_acc, v_acc
):
    scale = HEAD_DIM ** (-0.5)
    for head in range(heads):
        column = slice(head * HEAD_DIM, (head + 1) * HEAD_DIM)
        for step in reversed(range(q_ref.shape[0] // block)):
            rows = slice(step * block, (step + 1) * block)
            spans = key_spans(step, block)
            q_part, o_part = q_ref[rows, column], o_ref[rows, column]
            probs = softmax_of(score_parts(q_part, k_ref, column, step, block))
            prob_grads = [right_product(o_part, v_ref[span, column]) for span in spans]
            delta = functools.reduce(
                jnp.add,
                [jnp.sum(p * g, -1, keepdims=True) for p, g in zip(probs, prob_grads)],
            )
            score_grads = [(p * (g - delta)).astype(bf16) for p, g in zip(probs, prob_grads)]
            q_grad = functools.reduce(
                jnp.add,
                [product(s, k_ref[span, column]) for s, span in zip(score_grads, spans)],
            )
            dq_ref[rows, column] = (q_grad * scale).astype(bf16)
            first = step == q_ref.shape[0] // block - 1
            for span, score_grad, prob in zip(spans, score_grads, probs):
                key_grad = left_product(score_grad, q_part)
                value_grad = left_product(prob.astype(bf16), o_part)
                k_acc[span, column] = key_grad if first else k_acc[span, column] + key_grad
                v_acc[span, column] = value_grad if first else v_acc[span, column] + value_grad
    dk_ref[...] = (k_acc[...] * scale).astype(bf16)
    dv_ref[...] = v_acc[...].astype(bf16)


def attention_plan(qkv, width):
    length = qkv.shape[0]
    heads = min(2, width // HEAD_DIM)
    block = min(256, length)
    lanes = heads * HEAD_DIM
    steps = width // lanes

    whole = lanes % 128 == 0
    joined = [qkv] * 3 if whole else [qkv[:, i * width : (i + 1) * width] for i in range(3)]

    def spec(part):
        first = part * steps if whole else 0
        return pl.BlockSpec((length, lanes), lambda step: (0, first + step))

    params = pltpu.CompilerParams(
        dimension_semantics=("arbitrary",), vmem_limit_bytes=48 * 1024 * 1024
    )
    return length, heads, block, lanes, steps, spec, params, joined


def attention_forward(qkv, width):
    length, heads, block, lanes, steps, spec, params, joined = attention_plan(qkv, width)
    return pl.pallas_call(
        functools.partial(attention_forward_kernel, heads, block),
        grid=(steps,),
        in_specs=[spec(0), spec(1), spec(2)],
        out_specs=spec(0),
        out_shape=jax.ShapeDtypeStruct((length, width), bf16),
        compiler_params=params,
        cost_estimate=pl.CostEstimate(
            flops=2 * length * length * width,
            bytes_accessed=8 * length * width,
            transcendentals=length * length * width // HEAD_DIM // 2,
        ),
        name="attention_forward",
    )(*joined)


def attention_backward(qkv, grad_attended, width):
    length, heads, block, lanes, steps, spec, params, joined = attention_plan(qkv, width)
    shape = jax.ShapeDtypeStruct((length, width), bf16)
    return pl.pallas_call(
        functools.partial(attention_backward_kernel, heads, block),
        grid=(steps,),
        in_specs=[spec(0), spec(1), spec(2), spec(0)],
        out_specs=[spec(0), spec(0), spec(0)],
        out_shape=[shape, shape, shape],
        scratch_shapes=[pltpu.VMEM((length, lanes), f32), pltpu.VMEM((length, lanes), f32)],
        compiler_params=params,
        cost_estimate=pl.CostEstimate(
            flops=5 * length * length * width,
            bytes_accessed=14 * length * width,
            transcendentals=length * length * width // HEAD_DIM // 2,
        ),
        name="attention_backward",
    )(*joined, grad_attended)


def layer(
    dp,
    ctx,
    tokens,
    cotangent,
    routes,
    ln1_gain,
    ln1_bias,
    qkv_weight,
    qv_bias,
    out_weight,
    out_bias,
    ln2_gain,
    ln2_bias,
    up_weight,
    up_bias,
    down_weight,
    down_bias,
    router_weight,
    mix_weight,
    expert_up,
    expert_up_bias,
    expert_down,
    expert_down_bias,
):
    rows, width = tokens.shape[0] * tokens.shape[1], tokens.shape[2]
    experts, share, hidden = expert_up.shape
    own_hidden = hidden // ctx
    own_width = width // ctx
    length = rows * ctx
    capacity = rows * 5 // 8
    me = lax.axis_index("ctx")
    shifts = range(1, ctx)

    def swap(array, shift):
        return lax.ppermute(array, "ctx", [(i, i ^ shift) for i in range(ctx)])

    def gather_ctx(array):
        return [array] + [swap(array, s) for s in shifts]

    def exchange(pieces):
        own = [lax.dynamic_index_in_dim(pieces, me ^ s, 0, keepdims=False) for s in range(ctx)]
        return [own[0]] + [swap(own[s], s) for s in shifts]

    def natural(pieces, axis=0):
        size = pieces[0].shape[axis]
        shape = list(pieces[0].shape)
        shape[axis] = size * ctx
        whole = jnp.zeros(shape, pieces[0].dtype)
        for s, piece in enumerate(pieces):
            whole = lax.dynamic_update_slice_in_dim(whole, piece, (me ^ s) * size, axis)
        return whole

    def gather_dp(array, axis=0):
        return lax.all_gather(array, "dp", axis=axis, tiled=True)

    def scatter_dp(array, axis=0):
        return lax.psum_scatter(
            array.astype(bf16), "dp", scatter_dimension=axis, tiled=True
        )

    def total(pieces):
        return functools.reduce(jnp.add, [piece.astype(f32) for piece in pieces])

    tokens = tokens.reshape(rows, width)
    cotangent = cotangent.reshape(rows, width)
    routes = routes.reshape(rows)
    first_hot = routes == 0
    first_count = jnp.sum(first_hot.astype(f32))
    smalls = [
        ln1_gain,
        ln1_bias,
        qv_bias,
        out_bias,
        ln2_gain,
        ln2_bias,
        down_bias,
        router_weight,
        mix_weight,
        expert_down_bias,
        up_bias,
        expert_up_bias,
        first_count[None].astype(bf16),
    ]
    sizes = [small.size for small in smalls]
    packed = jnp.concatenate([small.reshape(-1) for small in smalls])
    plane_small = lax.all_gather(packed, "ctx", axis=0)
    all_small = lax.all_gather(plane_small, "dp", axis=0)
    unpacked, at = [], 0
    for size in sizes:
        unpacked.append(all_small[:, :, at : at + size])
        at += size
    (gain_one, shift_one, full_qv, full_outb, gain_two, shift_two, full_downb) = [
        part.reshape(-1).astype(f32) for part in unpacked[:7]
    ]
    full_router = unpacked[7].reshape(width, -1)
    full_mix = unpacked[8].reshape(width, -1)
    full_expert_downb = (
        unpacked[9].reshape(dp, ctx, experts, -1).transpose(2, 0, 1, 3).reshape(experts, width)
    ).astype(f32)
    own_upb = lax.dynamic_index_in_dim(unpacked[10], me, 1, keepdims=False).reshape(-1).astype(f32)
    own_expert_upb = (
        lax.dynamic_index_in_dim(unpacked[11], me, 1, keepdims=False)
        .reshape(dp, experts, -1)
        .transpose(1, 0, 2)
        .reshape(experts, own_hidden)
        .astype(f32)
    )
    counts = plane_small[:, -1].astype(f32)

    token_all = natural(gather_ctx(tokens))
    qkv_cut = qkv_weight.reshape(share, 3, ctx, own_width).transpose(2, 0, 1, 3)
    own_qkv = gather_dp(natural(exchange(qkv_cut.reshape(ctx, share, 3 * own_width))))
    out_parts = gather_dp(out_weight)
    full_out = natural(
        [part.reshape(dp, share, width) for part in gather_ctx(out_parts)], 1
    ).reshape(width, width)

    unit = hidden // (dp * ctx)
    ups = jnp.concatenate([up_weight[None], expert_up], 0)
    ups_cut = ups.reshape(experts + 1, share, dp, ctx, unit).transpose(3, 0, 1, 2, 4)
    ups_cut = ups_cut.reshape(ctx, experts + 1, share, own_hidden)
    ups_rows = natural(exchange(ups_cut), 1)
    own_up = gather_dp(ups_rows[0])
    own_down = gather_dp(down_weight)
    own_expert_up = [gather_dp(ups_rows[e + 1]) for e in range(experts)]
    own_expert_down = [gather_dp(expert_down[e]) for e in range(experts)]

    normed_all, _ = layer_stats(token_all.astype(f32))
    attn_in = (normed_all * gain_one + shift_one).astype(bf16)
    own_q_bias = lax.dynamic_slice_in_dim(full_qv, me * own_width, own_width)
    own_v_bias = lax.dynamic_slice_in_dim(full_qv, width + me * own_width, own_width)
    own_bias = jnp.concatenate([own_q_bias, jnp.zeros_like(own_q_bias), own_v_bias])
    qkv = (product(attn_in, own_qkv) + own_bias).astype(bf16)
    attended_heads = attention_forward(qkv, own_width)
    attended = natural(exchange(attended_heads.reshape(ctx, rows, own_width)), 1)

    inputs = tokens.astype(f32)
    hidden_state = inputs + (product(attended, full_out) + full_outb)
    normed_two, inverse_two = layer_stats(hidden_state)
    ffn_in = (normed_two * gain_two + shift_two).astype(bf16)

    order = jnp.arange(rows).astype(f32)
    counted = jnp.cumsum(first_hot.astype(f32))
    place = jnp.where(first_hot, counted - 1.0, first_count + order - counted)
    sort_t = (place[:, None] == order[None, :]).astype(bf16)
    sort = (place[None, :] == order[:, None]).astype(bf16)
    grad_rows = jnp.concatenate(gather_ctx(product(sort, cotangent).astype(bf16)))
    ffn_rows = jnp.concatenate(gather_ctx(product(sort, ffn_in).astype(bf16)))
    row_counts = jnp.stack([counts[me ^ s] for s in range(ctx)])
    first_mask = order[None, :] < row_counts[:, None]

    def router(values):
        return (
            jax.nn.softmax(product(values, full_router), axis=-1),
            jax.nn.softmax(product(values, full_mix), axis=-1),
        )

    route_rows, mix_rows = router(ffn_rows)
    gate_rows = jnp.where(first_mask.reshape(-1), route_rows[:, 0], route_rows[:, 1])
    mix_zero = mix_rows[:, 0:1]
    branch = (mix_rows[:, 1] * gate_rows)[:, None]

    up_dense = product(ffn_rows, own_up) + own_upb
    act_dense = gelu(up_dense).astype(bf16)
    out_dense = product(act_dense, own_down)
    ffn_blocks = ffn_rows.reshape(ctx, rows, width)
    spans = (slice(0, capacity), slice(rows - capacity, rows))
    masks = (first_mask, ~first_mask)
    caches = []
    for e in range(experts):
        slot_in = ffn_blocks[:, spans[e]].reshape(ctx * capacity, width)
        slot_up = product(slot_in, own_expert_up[e]) + own_expert_upb[e]
        slot_act = gelu(slot_up).astype(bf16)
        slot_out = product(slot_act, own_expert_down[e]).reshape(ctx, capacity, width)
        caches.append((slot_in, slot_up, slot_act, slot_out))
    edge = rows - capacity
    overlap = capacity - edge
    moe = jnp.concatenate(
        [
            caches[0][3][:, :edge],
            jnp.where(
                first_mask[:, edge:capacity, None],
                caches[0][3][:, edge:],
                caches[1][3][:, :overlap],
            ),
            caches[1][3][:, overlap:],
        ],
        1,
    ).reshape(length, width)
    grad_f = grad_rows.astype(f32)
    dots = jnp.stack([jnp.sum(grad_f * out_dense, -1), jnp.sum(grad_f * moe, -1)], -1)
    mixed_out = (mix_zero * out_dense + branch * moe).astype(bf16)

    def scatter_ctx(array):
        blocks = array.reshape(ctx, rows, array.shape[-1])
        return [blocks[0]] + [swap(blocks[s], s) for s in shifts]

    sort_t_all = jnp.concatenate([sort_t] * ctx, 1)

    def back_in_order(pieces):
        return product(sort_t_all, jnp.concatenate(pieces, 0))

    grad_dense_out = (grad_f * mix_zero).astype(bf16)
    grad_moe = (grad_f * branch).astype(bf16).reshape(ctx, rows, width)
    grad_w_down = left_product(act_dense, grad_dense_out)
    grad_act = right_product(grad_dense_out, own_down)
    grad_up_dense = gelu_grad(up_dense, grad_act).astype(bf16)
    grad_w_up = left_product(ffn_rows, grad_up_dense)
    grad_b_up = jnp.sum(grad_up_dense.astype(f32), 0)
    grad_ffn_rows = right_product(grad_up_dense, own_up).reshape(ctx, rows, width)
    down_grad = scatter_dp(grad_w_down).astype(f32)
    up_part = scatter_dp(grad_w_up)
    expert_down_grads, expert_up_parts, expert_upb_grads, slot_grads = [], [], [], []
    for e in range(experts):
        slot_in, slot_up, slot_act, _ = caches[e]
        grad_slot = jnp.where(masks[e][:, spans[e], None], grad_moe[:, spans[e]], 0)
        grad_slot = grad_slot.reshape(ctx * capacity, width)
        expert_down_grads.append(scatter_dp(left_product(slot_act, grad_slot)).astype(f32))
        grad_slot_act = right_product(grad_slot, own_expert_down[e])
        grad_slot_up = gelu_grad(slot_up, grad_slot_act).astype(bf16)
        expert_up_parts.append(scatter_dp(left_product(slot_in, grad_slot_up)))
        expert_upb_grads.append(jnp.sum(grad_slot_up.astype(f32), 0))
        grad_slot_in = right_product(grad_slot_up, own_expert_up[e])
        slot_grads.append(grad_slot_in.reshape(ctx, capacity, width))
    grad_ffn_rows = jnp.concatenate(
        [
            grad_ffn_rows[:, :edge] + slot_grads[0][:, :edge],
            grad_ffn_rows[:, edge:capacity]
            + (slot_grads[0][:, edge:] + slot_grads[1][:, :overlap]),
            grad_ffn_rows[:, capacity:] + slot_grads[1][:, overlap:],
        ],
        1,
    ).reshape(length, width)
    grad_ffn = back_in_order(scatter_ctx(grad_ffn_rows.astype(bf16)))
    own_dots = jnp.dot(sort_t.astype(f32), total(scatter_ctx(dots)), precision=highest)
    mlp_out = back_in_order(scatter_ctx(mixed_out))

    route_probs, mix_coef = router(ffn_in)
    hot = jnp.stack([first_hot, ~first_hot], -1).astype(f32)
    gate_value = jnp.sum(route_probs * hot, -1)
    branch_coef = mix_coef[:, 1] * gate_value
    bias_moe = jnp.where(first_hot[:, None], full_expert_downb[0], full_expert_downb[1])
    result = (
        hidden_state
        + mlp_out
        + mix_coef[:, 0:1] * full_downb
        + branch_coef[:, None] * bias_moe
    )
    grad_out = cotangent.astype(f32)
    dense_dot = own_dots[:, 0] + jnp.sum(grad_out * full_downb, -1)
    moe_dot = own_dots[:, 1] + jnp.sum(grad_out * bias_moe, -1)
    grad_mixc = jnp.stack([dense_dot, moe_dot * gate_value], -1)
    grad_gate = moe_dot * mix_coef[:, 1]
    grad_mix_logits = mix_coef * (grad_mixc - jnp.sum(mix_coef * grad_mixc, -1, keepdims=True))
    grad_probs = hot * grad_gate[:, None]
    grad_router_logits = route_probs * (
        grad_probs - jnp.sum(route_probs * grad_probs, -1, keepdims=True)
    )
    grad_small = jnp.concatenate([grad_router_logits, grad_mix_logits], -1)
    small_weights = jnp.concatenate([full_router, full_mix], 1).astype(f32)
    grad_small_w = jnp.einsum("nd,ne->de", ffn_in.astype(f32), grad_small, precision=highest)
    grad_ffn = grad_ffn + jnp.einsum("ne,de->nd", grad_small, small_weights, precision=highest)
    own_grad_dense = (grad_out * mix_coef[:, 0:1]).astype(bf16).astype(f32)
    own_grad_moe = (grad_out * branch_coef[:, None]).astype(bf16).astype(f32)
    grad_b_down = jnp.sum(own_grad_dense, 0)
    grad_b_expert_down = jnp.stack(
        [jnp.sum(own_grad_moe * hot[:, e : e + 1], 0) for e in range(experts)]
    )
    grad_gain_two = jnp.sum(grad_ffn * normed_two, 0)
    grad_shift_two = jnp.sum(grad_ffn, 0)
    grad_hidden = grad_out + norm_back(grad_ffn, normed_two, inverse_two, gain_two)
    grad_proj = grad_hidden.astype(bf16)
    grad_b_out = jnp.sum(grad_proj.astype(f32), 0)
    grad_attended = right_product(grad_proj, full_out).astype(bf16)
    grad_cut = grad_attended.reshape(rows, ctx, own_width).transpose(1, 0, 2)
    grad_heads = natural(exchange(grad_cut))
    grad_w_out = left_product(attended, grad_proj).astype(bf16)
    grad_w_out = grad_w_out.reshape(dp, ctx, share, width).transpose(1, 0, 2, 3)
    out_part = total(exchange(grad_w_out.reshape(ctx, dp * share, width)))
    out_grad = scatter_dp(out_part).astype(f32)

    grad_qkv = jnp.concatenate(attention_backward(qkv, grad_heads, own_width), 1)
    qkv_part = scatter_dp(left_product(attn_in, grad_qkv))
    grad_b_qkv = jnp.sum(grad_qkv.astype(f32), 0)
    grad_attn_rows = right_product(grad_qkv, own_qkv).astype(bf16)
    grad_attn_in = total(exchange(grad_attn_rows.reshape(ctx, rows, width)))
    normed_one, inverse_one = layer_stats(inputs)
    grad_gain_one = jnp.sum(grad_attn_in * normed_one, 0)
    grad_shift_one = jnp.sum(grad_attn_in, 0)
    grad_inputs = grad_hidden + norm_back(grad_attn_in, normed_one, inverse_one, gain_one)

    up_parts = jnp.stack([up_part] + expert_up_parts)
    up_cut = up_parts.reshape(experts + 1, ctx, share, own_hidden).transpose(1, 0, 2, 3)
    up_grads = natural(
        [p.reshape(experts + 1, share, dp, 1, unit) for p in exchange(up_cut)], 3
    )
    up_grads = up_grads.reshape(experts + 1, share, hidden).astype(f32)
    qkv_cut = qkv_part.reshape(ctx, share, 3 * own_width)
    qkv_grad = natural([p.reshape(share, 3, own_width) for p in exchange(qkv_cut)], 2)
    qkv_grad = qkv_grad.reshape(share, 3 * width).astype(f32)

    zero_qv = jnp.zeros((2, width), f32)
    grad_qv = lax.dynamic_update_slice(
        zero_qv,
        jnp.stack([grad_b_qkv[:own_width], grad_b_qkv[2 * own_width :]]),
        (0, me * own_width),
    )

    def own_columns(array):
        whole = jnp.zeros((dp, ctx, array.shape[-1]), f32)
        return lax.dynamic_update_slice_in_dim(whole, array[:, None], me, 1)

    expert_upb = jnp.stack(expert_upb_grads).reshape(experts, dp, unit).transpose(1, 0, 2)
    small_grads = [
        grad_gain_one,
        grad_shift_one,
        grad_qv,
        grad_b_out,
        grad_gain_two,
        grad_shift_two,
        grad_b_down,
        grad_small_w[:, :experts],
        grad_small_w[:, experts:],
        grad_b_expert_down.reshape(experts, dp, ctx, share).transpose(1, 2, 0, 3),
        own_columns(grad_b_up.reshape(dp, unit)),
        own_columns(expert_upb.reshape(dp, experts * unit)),
    ]
    small_sum = jnp.concatenate([g.reshape(dp, ctx, -1) for g in small_grads], -1)
    small_sum = total(exchange(small_sum.transpose(1, 0, 2)))
    place_dp = lax.axis_index("dp")
    own = [
        lax.dynamic_index_in_dim(small_sum, place_dp ^ s, 0, keepdims=False) for s in range(dp)
    ]
    small_sum = total(
        [own[0]]
        + [lax.ppermute(own[s], "dp", [(i, i ^ s) for i in range(dp)]) for s in range(1, dp)]
    )
    outs, at = [], 0
    for size in sizes[:-1]:
        outs.append(small_sum[at : at + size])
        at += size
    return (
        result[None],
        grad_inputs[None],
        outs[0],
        outs[1],
        qkv_grad,
        outs[2],
        out_grad,
        outs[3],
        outs[4],
        outs[5],
        up_grads[0],
        outs[10],
        down_grad,
        outs[6],
        outs[7].reshape(router_weight.shape),
        outs[8].reshape(mix_weight.shape),
        up_grads[1:],
        outs[11].reshape(expert_up_bias.shape),
        jnp.stack(expert_down_grads),
        outs[9].reshape(expert_down_bias.shape),
    )


def solution(mesh):
    both = ("dp", "ctx")
    data = P("dp", "ctx", None)
    vector = P(both)
    matrix = P(both, None)
    expert_matrix = P(None, both, None)
    expert_vector = P(None, both)
    weights = (
        vector,
        vector,
        matrix,
        vector,
        matrix,
        vector,
        vector,
        vector,
        matrix,
        vector,
        matrix,
        vector,
        matrix,
        matrix,
        expert_matrix,
        expert_vector,
        expert_matrix,
        expert_vector,
    )
    return jax.shard_map(
        functools.partial(layer, mesh.shape["dp"], mesh.shape["ctx"]),
        mesh=mesh,
        in_specs=(data, data, data) + weights,
        out_specs=(data, data) + weights,
        check_vma=False,
    )
```

time: 3730 us -> 670 us (0.18)
  waiting for transfers between devices: 2870 us -> 266 us
  blocking collectives: 391 us -> 42.7 us
  matrix products: 251 us -> 114 us
  starting transfers between devices: 1.15 us -> 67.5 us
  local copies, waits for them, and re-layouts: 151 us -> 97.9 us
    reduce_scatter x8, waiting for transfers between devices: 2450 us -> 137 us  [scatter_dp(): lax.psum_scatter(array.astype(bf16), 'dp', scatter_dimension=axis, tiled=...]
    all_gather x8 -> x2, blocking collectives: 348 us -> 30.5 us  [the longest x1 16.3 us: gather_dp(): return lax.all_gather(array, 'dp', axis=axis, tiled=True)]
    unnamed x26 -> x15, waiting for transfers between devices: 231 us -> 1.78 us
    all_gather x12 -> x7, waiting for transfers between devices: 188 us -> 0.03 us  [gather_dp(): return lax.all_gather(array, 'dp', axis=axis, tiled=True)]
    ppermute x0 -> x55, waiting for transfers between devices: none -> 128 us  [the longest x48 125 us: swap(): return lax.ppermute(array, 'ctx', [(i, i ^ shift) for i in range(ctx)])]
    dot_general x76 -> x19, matrix products: 129 us -> 41.8 us  [the longest x16 40.6 us: product(): return jnp.dot(left_op, right_op, preferred_element_type=f32)]
    ppermute x0 -> x55, starting transfers between devices: none -> 66.7 us  [the longest x48 58.6 us: swap(): return lax.ppermute(array, 'ctx', [(i, i ^ shift) for i in range(ctx)])]
    dynamic_slice x104 -> x3, local copies, waits for them, and re-layouts: 64.6 us -> 0.7 us  [the longest x1 0.53 us: layer(): row_counts = jnp.stack([counts[me ^ s] for s in range(ctx)])]
  transfers between devices with their start and end apart: 23 -> 70, of which waited for: 14 -> 34; matrix products, arithmetic and copies ran while one was open for 11% -> 28% of each run, Pallas kernels for 0% -> 4%
where the time goes in v1:
time: 670 us; the launch traced here: 665 us
  waiting for transfers between devices  266 us (40%)
  matrix products  114 us (17%)
  local copies, waits for them, and re-layouts  97.9 us (15%)
  starting transfers between devices  67.5 us (10%)
  blocking collectives  42.7 us (6%)
  other arithmetic  32.6 us (5%)
  Pallas kernels  25.8 us (4%)
  between operations  18 us (3%)
    reduce_scatter x8, waiting for transfers between devices, scatter_dp(): lax.psum_scatter(array.astype(bf16), 'dp', scatter_dimension=axis, tiled=...  137 us
    ppermute x48, waiting for transfers between devices, swap(): return lax.ppermute(array, 'ctx', [(i, i ^ shift) for i in range(ctx)])  125 us
    ppermute x48, starting transfers between devices, swap(): return lax.ppermute(array, 'ctx', [(i, i ^ shift) for i in range(ctx)])  58.6 us
    dot_general x16, matrix products, product(): return jnp.dot(left_op, right_op, preferred_element_type=f32)  40.6 us
    dynamic_update_slice x32, local copies, waits for them, and re-layouts, natural(): whole = lax.dynamic_update_slice_in_dim(whole, piece, (me ^ s) * size, axis)  39.2 us
    dot_general x8, matrix products, left_product(): lax.dot_general(left_op, right_op, (((0,), (0,)), ((), ())), preferred_el...  37 us
    dot_general x8, matrix products, right_product(): lax.dot_general(left_op, right_op, (((1,), (1,)), ((), ())), preferred_el...  35.2 us
    unnamed x270, local copies, waits for them, and re-layouts  23.5 us
  transfers between devices with their start and end apart: 70, of which 34 were waited for; matrix products, arithmetic and copies ran while one was open for 28% of the time, Pallas kernels for 4%

profile of v1, /device:TPU:0, one launch (start us, length us, event | category | flops | bytes accessed | tf_op | source)
XLA Modules:
  0.0 664.5 jit_solution(5232791641914687434)
XLA Ops:
  8.8 3.0 collective-permute-start.3
  23.9 3.4 collective-permute-done.15
  37.4 16.3 %all_gather.41 = bf16[256,1024]{1,0:T(8,128)(2,1)} all-gather(bf16[32,1024]{1,0:T(8,128)(2,1)S(1)} %copy-done.47), channel_id=1, replica_groups=mesh['dp'=8,'ctx'=4] {'dp'}, dimensions={0}, use_global_device_ids=true | all-gather | bytes 589824 | tf_op jit(solution)/shard_map/all_gather | solution.py:238
  60.4 12.2 %all-reduce = bf16[3332]{0:T(1024)(128)(2,1)S(1)} all-reduce(bf16[3332]{0:T(1024)(128)(2,1)S(1)} %dynamic-update-slice), channel_id=2, replica_groups=mesh['dp'=8,'ctx'=4] {'ctx'}, use_global_device_ids=true, to_apply=%add | all-reduce | flops 3332 | bytes 13328
  72.6 14.2 %all-gather.7 = bf16[8,4,833]{2,1,0:T(4,128)(2,1)S(1)} all-gather(bf16[1,4,833]{2,1,0:T(4,128)(2,1)S(1)} %reshape.679), channel_id=3, replica_groups=mesh['dp'=8,'ctx'=4] {'dp'}, dimensions={0}, use_global_device_ids=true | all-gather | bytes 59976 | tf_op jit(solution)/shard_map/all_gather | solution.py:271
  117.2 15.0 %collective-permute-done.21 = bf16[256,1024]{1,0:T(8,128)(2,1)S(1)} collective-permute-done((bf16[256,1024]{1,0:T(8,128)(2,1)S(1)}, bf16[256,1024]{1,0:T(8,128)(2,1)S(1)}, u32[]{:S(2)}, u32[]{:S(2)}) %collective-permute-start.21) | collective-permute-done | bytes 524320 | tf_op jit(solution)/shard_map/ppermute | solution.py:219
  132.2 10.5 %collective-permute-done.23 = bf16[256,1024]{1,0:T(8,128)(2,1)S(1)} collective-permute-done((bf16[256,1024]{1,0:T(8,128)(2,1)S(1)}, bf16[256,1024]{1,0:T(8,128)(2,1)S(1)}, u32[]{:S(2)}, u32[]{:S(2)}) %collective-permute-start.23) | collective-permute-done | bytes 524320 | tf_op jit(solution)/shard_map/ppermute | solution.py:219
  146.1 4.1 add_convert_fusion.q_ref.k_ref.v_ref
  150.2 9.3 %attention_forward.1 = bf16[1024,256]{1,0:T(8,128)(2,1)S(1)} custom-call(bf16[1024,768]{1,0:T(8,128)(2,1)S(1)} %add_convert_fusion.q_ref.k_ref.v_ref, bf16[1024,768]{1,0:T(8,128)(2,1)S(1)} %add_convert_fusion.q_ref.k_ref.v_ref, bf16[1024,768]{1,0:T(8,128)(2,1)S(1)} %add_convert_fusion.q_ref.k_ref.v_ref), custom_call_target="tpu_custom_call" | custom-call | flops 536870912 | bytes 2097152 | tf_op jit(solution)/shard_map/attention_forward/pallas_call | solution.py:148
  164.9 4.1 collective-permute-done.7
  177.7 8.9 %collective-permute-done.12 = bf16[256,1024]{1,0:T(8,128)(2,1)S(1)} collective-permute-done((bf16[256,1024]{1,0:T(8,128)(2,1)S(1)}, bf16[256,1024]{1,0:T(8,128)(2,1)S(1)}, u32[]{:S(2)}, u32[]{:S(2)}) %collective-permute-start.12) | collective-permute-done | bytes 524320 | tf_op jit(solution)/shard_map/ppermute | solution.py:219
  186.6 9.3 %collective-permute-done.13 = bf16[256,1024]{1,0:T(8,128)(2,1)S(1)} collective-permute-done((bf16[256,1024]{1,0:T(8,128)(2,1)S(1)}, bf16[256,1024]{1,0:T(8,128)(2,1)S(1)}, u32[]{:S(2)}, u32[]{:S(2)}) %collective-permute-start.13) | collective-permute-done | bytes 524320 | tf_op jit(solution)/shard_map/ppermute | solution.py:219
  199.9 3.3 fusion.181
  205.7 5.0 fusion.52
  210.7 6.7 %convert_reduce_fusion.3 = (f32[1024]{0:T(1024)}, bf16[640,1024]{1,0:T(8,128)(2,1)S(1)}) fusion(f32[640,1024]{1,0:T(8,128)} %fusion.52, f32[1024]{0:T(1024)S(1)} %bitcast.370, bf16[640,1024]{1,0:T(8,128)(2,1)} %bitcast.326, bf16[1,1024,1024]{2,1,0:T(8,128)(2,1)} %all-gather.28.cloned.1.call-done), kind=kOutput, calls=%fused_computation.48 | convolution fusion | flops 1357249536 | bytes 7348224 | tf_op jit(solution)/shard_map/dot_general | solution.py:26
  218.5 3.0 fusion.50
  221.5 4.6 fusion.60
  226.1 6.9 %fusion.64 = f32[1024,1024]{1,0:T(8,128)} fusion(bf16[1024,1024]{1,0:T(8,128)(2,1)} %copy-done, bf16[1,1024,1024]{2,1,0:T(8,128)(2,1)} %all-gather.20.cloned.1.call-done), kind=kOutput, calls=%fused_computation.89 | convolution fusion | flops 2147483648 | bytes 8388608 | tf_op jit(solution)/shard_map/dot_general | solution.py:18
  233.1 9.9 %convert_reduce_fusion.1 = (f32[1024]{0:T(1024)}, bf16[1024,1024]{1,0:T(8,128)(2,1)S(1)}) fusion(f32[1024,1024]{1,0:T(8,128)} %fusion.64, f32[1024]{0:T(1024)S(1)} %bitcast.366, bf16[1024,1024]{1,0:T(8,128)(2,1)} %all-gather.18.cloned.1.call-done, f32[1024]{0:T(1024)S(1)} %bitcast.380, bf16[256,1024]{1,0:T(8,128)(2,1)} %copy-done.41, ...), kind=kOutput, calls=%fused_computation.23 | convolution fusion | flops 2182085632 | bytes 10498048 | tf_op jit(solution)/shard_map/dot_general | solution.py:26
  244.3 4.4 fusion.62
  248.7 6.2 convert_reduce_fusion.4
  270.7 7.6 %multiply_reduce_fusion = (f32[1024]{0:T(1024)S(1)}, f32[1024]{0:T(1024)S(1)}, bf16[1024,1024]{1,0:T(8,128)(2,1)}) fusion(bf16[256,1024]{1,0:T(8,128)(2,1)S(1)} %copy-done.42, bf16[256,1024]{1,0:T(8,128)(2,1)S(1)} %copy-done.39, bf16[256,1024]{1,0:T(8,128)(2,1)S(1)} %copy-done.35, bf16[256,1024]{1,0:T(8,128)(2,1)S(1)} %copy-done.25, ...), kind=kOutput, calls=%fused_computation.24 | convolution fusion | flops 2174744576 | bytes 14700544 | tf_op jit(solution)/shard_map/dot_general | solution.py:18
  287.0 9.8 %collective-permute-done.24 = bf16[256,1024]{1,0:T(8,128)(2,1)S(1)} collective-permute-done((bf16[256,1024]{1,0:T(8,128)(2,1)S(1)}, bf16[256,1024]{1,0:T(8,128)(2,1)S(1)}, u32[]{:S(2)}, u32[]{:S(2)}) %collective-permute-start.24) | collective-permute-done | bytes 524320 | tf_op jit(solution)/shard_map/ppermute | solution.py:219
  296.7 5.7 collective-permute-done.25
  319.9 15.8 %collective-permute-done.30 = bf16[256,256]{1,0:T(8,128)(2,1)S(1)} collective-permute-done((bf16[256,256]{1,0:T(8,128)(2,1)S(1)}, bf16[256,256]{1,0:T(8,128)(2,1)S(1)}, u32[]{:S(2)}, u32[]{:S(2)}) %collective-permute-start.30) | collective-permute-done | bytes 131104 | tf_op jit(solution)/shard_map/ppermute | solution.py:219
  336.7 4.8 collective-permute-done.32
  344.3 16.4 %attention_backward.1 = (bf16[1024,256]{1,0:T(8,128)(2,1)S(1)}, bf16[1024,256]{1,0:T(8,128)(2,1)S(1)}, bf16[1024,256]{1,0:T(8,128)(2,1)S(1)}) custom-call(bf16[1024,768]{1,0:T(8,128)(2,1)S(1)} %add_convert_fusion.q_ref.k_ref.v_ref, bf16[1024,768]{1,0:T(8,128)(2,1)S(1)} %add_convert_fusion.q_ref.k_ref.v_ref, ...), custom_call_target="tpu_custom_call" | custom-call | flops 1342177280 | bytes 3670016 | tf_op jit(solution)/shard_map/attention_backward/pallas_call | solution.py:167
  363.0 3.4 convolution_convert_fusion.8
  366.5 5.0 convolution_convert_fusion.5
  371.8 5.4 convolution_convert_fusion.1
  377.3 5.0 convolution_convert_fusion.6
  382.4 6.9 %convolution_convert_fusion = bf16[1024,1024]{1,0:T(8,128)(2,1)} fusion(f32[1024]{0:T(1024)S(1)} %bitcast.382, f32[1024,1024]{1,0:T(8,128)} %fusion.64, f32[1024]{0:T(1024)S(1)} %bitcast.368, bf16[256,1024]{1,0:T(8,128)(2,1)S(1)} %copy-done.43, bf16[256,1024]{1,0:T(8,128)(2,1)S(1)} %copy-done.40, bf16[256,1024]{1,0:T(8,128)(2,1)S(1)} %copy-done.36, ...), kind=kOutput, calls=%fused_computation.96 | convolution fusion | flops 2169503744 | bytes 8396800 | tf_op jit(solution)/shard_map/dot_general | solution.py:22
  389.5 5.6 convolution_convert_fusion.4
  396.0 3.0 fusion.180
  402.7 4.9 convolution_convert_fusion.3
  411.7 6.9 %collective-permute-done.19 = bf16[256,1024]{1,0:T(8,128)(2,1)} collective-permute-done((bf16[256,1024]{1,0:T(8,128)(2,1)}, bf16[256,1024]{1,0:T(8,128)(2,1)}, u32[]{:S(2)}, u32[]{:S(2)}) %collective-permute-start.19) | collective-permute-done | bytes 524320 | tf_op jit(solution)/shard_map/ppermute | solution.py:219
  418.6 3.4 fusion.84
  428.0 6.7 %collective-permute-done.33 = bf16[256,1024]{1,0:T(8,128)(2,1)} collective-permute-done((bf16[256,1024]{1,0:T(8,128)(2,1)S(1)}, bf16[256,1024]{1,0:T(8,128)(2,1)}, u32[]{:S(2)}, u32[]{:S(2)}) %collective-permute-start.33) | collective-permute-done | bytes 524320 | tf_op jit(solution)/shard_map/ppermute | solution.py:219
  437.5 3.9 collective-permute-done.35
  477.1 5.4 reduce-scatter.13.cloned.1.call-done
  482.6 36.7 %reduce-scatter.15.cloned.1.call-done = bf16[128,1024]{1,0:T(8,128)(2,1)} async-done(((bf16[1024,1024]{1,0:T(8,128)(2,1)}), bf16[128,1024]{1,0:T(8,128)(2,1)}) %reduce-scatter.15.cloned.1.call-update) | async-done | bytes 262160 | tf_op jit(solution)/shard_map/reduce_scatter | solution.py:241
  525.4 7.7 %dynamic_update_slice.136 = bf16[3,32,8,4,128]{4,3,2,1,0:T(4,128)(2,1)S(1)} dynamic-update-slice(bf16[3,32,8,4,128]{4,3,2,1,0:T(4,128)(2,1)S(1)} %broadcast_in_dim.151, bf16[3,32,8,1,128]{4,3,2,1,0:T(2,128)(2,1)S(1)} %reshape.686, s32[]{:T(128)} %constant.187.clone.1, s32[]{:T(128)} %constant.187.clone.1, s32[]{:T(128)} %constant.187.clone.1, s32[]{:T(128)S(6)} %select_n.175, s32[]{:T(128)} %constant.187.clone.1) | dynamic-update-slice | bytes 393220 | tf_op jit(solution)/shard_map/dynamic_update_slice | solution.py:234
  533.1 23.1 %reduce-scatter.19.cloned.1.call-done = bf16[128,1024]{1,0:T(8,128)(2,1)} async-done(((bf16[1024,1024]{1,0:T(8,128)(2,1)}), bf16[128,1024]{1,0:T(8,128)(2,1)}) %reduce-scatter.19.cloned.1.call-update) | async-done | bytes 262160 | tf_op jit(solution)/shard_map/reduce_scatter | solution.py:241
  558.0 34.7 %reduce-scatter.21.cloned.1.call-done = bf16[128,1024]{1,0:T(8,128)(2,1)} async-done(((bf16[1024,1024]{1,0:T(8,128)(2,1)}), bf16[128,1024]{1,0:T(8,128)(2,1)}) %reduce-scatter.21.cloned.1.call-update) | async-done | bytes 262160 | tf_op jit(solution)/shard_map/reduce_scatter | solution.py:241
  592.7 36.8 %reduce-scatter.23.cloned.1.call-done = bf16[128,1024]{1,0:T(8,128)(2,1)} async-done(((bf16[1024,1024]{1,0:T(8,128)(2,1)}), bf16[128,1024]{1,0:T(8,128)(2,1)}) %reduce-scatter.23.cloned.1.call-update) | async-done | bytes 262160 | tf_op jit(solution)/shard_map/reduce_scatter | solution.py:241
  631.7 7.7 %dynamic_update_slice.137 = bf16[3,32,8,4,128]{4,3,2,1,0:T(4,128)(2,1)S(1)} dynamic-update-slice(bf16[3,32,8,4,128]{4,3,2,1,0:T(4,128)(2,1)S(1)} %dynamic_update_slice.136, bf16[3,32,8,1,128]{4,3,2,1,0:T(2,128)(2,1)S(1)} %reshape.687, s32[]{:T(128)} %constant.187.clone.1, s32[]{:T(128)} %constant.187.clone.1, s32[]{:T(128)} %constant.187.clone.1, s32[]{:T(128)S(6)} %select_n.177, s32[]{:T(128)} %constant.187.clone.1) | dynamic-update-slice | bytes 393220 | tf_op jit(solution)/shard_map/dynamic_update_slice | solution.py:234
  639.6 7.7 %dynamic_update_slice.138 = bf16[3,32,8,4,128]{4,3,2,1,0:T(4,128)(2,1)S(1)} dynamic-update-slice(bf16[3,32,8,4,128]{4,3,2,1,0:T(4,128)(2,1)S(1)} %dynamic_update_slice.137, bf16[3,32,8,1,128]{4,3,2,1,0:T(2,128)(2,1)S(1)} %reshape.688, s32[]{:T(128)} %constant.187.clone.1, s32[]{:T(128)} %constant.187.clone.1, s32[]{:T(128)} %constant.187.clone.1, s32[]{:T(128)S(6)} %select_n.179, s32[]{:T(128)} %constant.187.clone.1) | dynamic-update-slice | bytes 393220 | tf_op jit(solution)/shard_map/dynamic_update_slice | solution.py:234
  647.4 7.7 %dynamic_update_slice.139 = bf16[3,32,8,4,128]{4,3,2,1,0:T(4,128)(2,1)S(1)} dynamic-update-slice(bf16[3,32,8,4,128]{4,3,2,1,0:T(4,128)(2,1)S(1)} %dynamic_update_slice.138, bf16[3,32,8,1,128]{4,3,2,1,0:T(2,128)(2,1)S(1)} %reshape.689, s32[]{:T(128)} %constant.187.clone.1, s32[]{:T(128)} %constant.187.clone.1, s32[]{:T(128)} %constant.187.clone.1, s32[]{:T(128)S(6)} %select_n.181, s32[]{:T(128)} %constant.187.clone.1) | dynamic-update-slice | bytes 393220 | tf_op jit(solution)/shard_map/dynamic_update_slice | solution.py:234
  (634 shorter events, 198.5 us)
Async XLA Ops:
  7.2 138.8 %all-gather.16.cloned.1.call-start = ((), (), s32[]{:S(2)}) async-start(), calls=%async_computation.8 | async-start | bytes 1769472 | tf_op jit(solution)/shard_map/all_gather | solution.py:238
  19.0 186.7 %all-gather.26.cloned.1.call-start = ((), (), s32[]{:S(2)}) async-start(), calls=%async_computation.21 | async-start | bytes 2359296 | tf_op jit(solution)/shard_map/all_gather | solution.py:238
  20.8 9.1 %collective-permute-start.16 = (bf16[3,32,1024]{2,1,0:T(8,128)(2,1)S(1)}, bf16[3,32,1024]{2,1,0:T(8,128)(2,1)S(1)}, u32[]{:S(2)}, u32[]{:S(2)}) collective-permute-start(bf16[3,32,1024]{2,1,0:T(8,128)(2,1)S(1)} %get-tuple-element.169), channel_id=1, source_target_pairs={{0,2},{1,3},{2,0},{3,1},{4,6},{5,7},{6,4},{7,5},{8,10},{9,11},{10,... | collective-permute-start | bytes 589832 | tf_op jit(solution)/shard_map/ppermute | solution.py:219
  20.9 9.2 %collective-permute-start.17 = (bf16[3,32,1024]{2,1,0:T(8,128)(2,1)S(1)}, bf16[3,32,1024]{2,1,0:T(8,128)(2,1)S(1)}, u32[]{:S(2)}, u32[]{:S(2)}) collective-permute-start(bf16[3,32,1024]{2,1,0:T(8,128)(2,1)S(1)} %get-tuple-element.168), channel_id=1, source_target_pairs={{0,3},{1,2},{2,1},{3,0},{4,7},{5,6},{6,5},{7,4},{8,11},{9,10},{10,... | collective-permute-start | bytes 589832 | tf_op jit(solution)/shard_map/ppermute | solution.py:219
  31.1 179.6 %all-gather.28.cloned.1.call-start = ((), (), s32[]{:S(2)}) async-start(), calls=%async_computation.22 | async-start | bytes 2359296 | tf_op jit(solution)/shard_map/all_gather | solution.py:238
  32.0 189.5 %all-gather.22.cloned.1.call-start = ((), (), s32[]{:S(2)}) async-start(), calls=%async_computation.19 | async-start | bytes 2359296 | tf_op jit(solution)/shard_map/all_gather | solution.py:238
  32.6 193.5 %all-gather.20.cloned.1.call-start = ((), (), s32[]{:S(2)}) async-start(), calls=%async_computation.18 | async-start | bytes 2359296 | tf_op jit(solution)/shard_map/all_gather | solution.py:238
  33.2 199.8 %all-gather.18.cloned.1.call-start = ((), (), s32[]{:S(2)}) async-start(), calls=%async_computation.9 | async-start | bytes 2359296 | tf_op jit(solution)/shard_map/all_gather | solution.py:238
  33.8 214.9 %all-gather.24.cloned.1.call-start = ((), (), s32[]{:S(2)}) async-start(), calls=%async_computation.20 | async-start | bytes 2359296 | tf_op jit(solution)/shard_map/all_gather | solution.py:238
  33.8 72.7 %collective-permute-start = (bf16[256,1024]{1,0:T(8,128)(2,1)S(1)}, bf16[256,1024]{1,0:T(8,128)(2,1)}, u32[]{:S(2)}, u32[]{:S(2)}) collective-permute-start(bf16[256,1024]{1,0:T(8,128)(2,1)S(1)} %bitcast.302), channel_id=1, source_target_pairs={{0,1},{1,0},{2,3},{3,2},{4,5},{5,4},{6,7},{7,6},{8,9},{9,8},{10,11... | collective-permute-start | bytes 1572872 | tf_op jit(solution)/shard_map/ppermute | solution.py:219
  35.2 75.0 %collective-permute-start.1 = (bf16[256,1024]{1,0:T(8,128)(2,1)S(1)}, bf16[256,1024]{1,0:T(8,128)(2,1)}, u32[]{:S(2)}, u32[]{:S(2)}) collective-permute-start(bf16[256,1024]{1,0:T(8,128)(2,1)S(1)} %bitcast.303), channel_id=1, source_target_pairs={{0,2},{1,3},{2,0},{3,1},{4,6},{5,7},{6,4},{7,5},{8,10},{9,11},{10,... | collective-permute-start | bytes 1572872 | tf_op jit(solution)/shard_map/ppermute | solution.py:219
  36.0 75.8 %collective-permute-start.2 = (bf16[256,1024]{1,0:T(8,128)(2,1)S(1)}, bf16[256,1024]{1,0:T(8,128)(2,1)}, u32[]{:S(2)}, u32[]{:S(2)}) collective-permute-start(bf16[256,1024]{1,0:T(8,128)(2,1)S(1)} %bitcast.304), channel_id=1, source_target_pairs={{0,3},{1,2},{2,1},{3,0},{4,7},{5,6},{6,5},{7,4},{8,11},{9,10},{10,... | collective-permute-start | bytes 1572872 | tf_op jit(solution)/shard_map/ppermute | solution.py:219
  53.7 51.2 %collective-permute-start.9 = (bf16[256,1024]{1,0:T(8,128)(2,1)}, bf16[256,1024]{1,0:T(8,128)(2,1)}, u32[]{:S(2)}, u32[]{:S(2)}) collective-permute-start(bf16[256,1024]{1,0:T(8,128)(2,1)} %all_gather.41), channel_id=1, source_target_pairs={{0,1},{1,0},{2,3},{3,2},{4,5},{5,4},{6,7},{7,6},{8,9},{9,8},{10,11... | collective-permute-start | bytes 1572872 | tf_op jit(solution)/shard_map/ppermute | solution.py:219
  55.2 59.1 %collective-permute-start.10 = (bf16[256,1024]{1,0:T(8,128)(2,1)}, bf16[256,1024]{1,0:T(8,128)(2,1)}, u32[]{:S(2)}, u32[]{:S(2)}) collective-permute-start(bf16[256,1024]{1,0:T(8,128)(2,1)} %all_gather.41), channel_id=1, source_target_pairs={{0,2},{1,3},{2,0},{3,1},{4,6},{5,7},{6,4},{7,5},{8,10},{9,11},{10,... | collective-permute-start | bytes 1572872 | tf_op jit(solution)/shard_map/ppermute | solution.py:219
  56.8 410.6 %reduce-scatter.11.cloned.1.call-start = ((), (), s32[]{:S(2)}) async-start(), calls=%async_computation.11 | async-start | bytes 589824 | tf_op jit(solution)/shard_map/reduce_scatter | solution.py:241
  104.9 55.2 %collective-permute-start.11 = (bf16[256,1024]{1,0:T(8,128)(2,1)}, bf16[256,1024]{1,0:T(8,128)(2,1)}, u32[]{:S(2)}, u32[]{:S(2)}) collective-permute-start(bf16[256,1024]{1,0:T(8,128)(2,1)} %all_gather.41), channel_id=1, source_target_pairs={{0,3},{1,2},{2,1},{3,0},{4,7},{5,6},{6,5},{7,4},{8,11},{9,10},{10,... | collective-permute-start | bytes 1572872 | tf_op jit(solution)/shard_map/ppermute | solution.py:219
  106.5 25.6 %collective-permute-start.21 = (bf16[256,1024]{1,0:T(8,128)(2,1)S(1)}, bf16[256,1024]{1,0:T(8,128)(2,1)S(1)}, u32[]{:S(2)}, u32[]{:S(2)}) collective-permute-start(bf16[256,1024]{1,0:T(8,128)(2,1)S(1)} %copy-done.24), channel_id=1, source_target_pairs={{0,1},{1,0},{2,3},{3,2},{4,5},{5,4},{6,7},{7,6},{8,9},{9,8},{10,11... | collective-permute-start | bytes 1572872 | tf_op jit(solution)/shard_map/ppermute | solution.py:219
  110.2 22.0 %collective-permute-start.22 = (bf16[256,1024]{1,0:T(8,128)(2,1)S(1)}, bf16[256,1024]{1,0:T(8,128)(2,1)S(1)}, u32[]{:S(2)}, u32[]{:S(2)}) collective-permute-start(bf16[256,1024]{1,0:T(8,128)(2,1)S(1)} %copy-done.24), channel_id=1, source_target_pairs={{0,2},{1,3},{2,0},{3,1},{4,6},{5,7},{6,4},{7,5},{8,10},{9,11},{10,... | collective-permute-start | bytes 1572872 | tf_op jit(solution)/shard_map/ppermute | solution.py:219
  111.9 30.9 %collective-permute-start.23 = (bf16[256,1024]{1,0:T(8,128)(2,1)S(1)}, bf16[256,1024]{1,0:T(8,128)(2,1)S(1)}, u32[]{:S(2)}, u32[]{:S(2)}) collective-permute-start(bf16[256,1024]{1,0:T(8,128)(2,1)S(1)} %copy-done.24), channel_id=1, source_target_pairs={{0,3},{1,2},{2,1},{3,0},{4,7},{5,6},{6,5},{7,4},{8,11},{9,10},{10,... | collective-permute-start | bytes 1572872 | tf_op jit(solution)/shard_map/ppermute | solution.py:219
  161.2 7.8 %collective-permute-start.7 = (bf16[256,256]{1,0:T(8,128)(2,1)S(1)}, bf16[256,256]{1,0:T(8,128)(2,1)S(1)}, u32[]{:S(2)}, u32[]{:S(2)}) collective-permute-start(bf16[256,256]{1,0:T(8,128)(2,1)S(1)} %get-tuple-element.178), channel_id=1, source_target_pairs={{0,2},{1,3},{2,0},{3,1},{4,6},{5,7},{6,4},{7,5},{8,10},{9,11},{10,... | collective-permute-start | bytes 393224 | tf_op jit(solution)/shard_map/ppermute | solution.py:219
  171.7 14.9 %collective-permute-start.12 = (bf16[256,1024]{1,0:T(8,128)(2,1)S(1)}, bf16[256,1024]{1,0:T(8,128)(2,1)S(1)}, u32[]{:S(2)}, u32[]{:S(2)}) collective-permute-start(bf16[256,1024]{1,0:T(8,128)(2,1)S(1)} %convolution_convert_fusion.11), channel_id=1, source_target_pairs={{0,1},{1,0},{2,3},{3,2},{4,5},{5,4},{6,7},{7,6},{8,9},{9,8},{10,11... | collective-permute-start | bytes 1572872 | tf_op jit(solution)/shard_map/ppermute | solution.py:219
  173.4 22.5 %collective-permute-start.13 = (bf16[256,1024]{1,0:T(8,128)(2,1)S(1)}, bf16[256,1024]{1,0:T(8,128)(2,1)S(1)}, u32[]{:S(2)}, u32[]{:S(2)}) collective-permute-start(bf16[256,1024]{1,0:T(8,128)(2,1)S(1)} %convolution_convert_fusion.11), channel_id=1, source_target_pairs={{0,2},{1,3},{2,0},{3,1},{4,6},{5,7},{6,4},{7,5},{8,10},{9,11},{10,... | collective-permute-start | bytes 1572872 | tf_op jit(solution)/shard_map/ppermute | solution.py:219
  174.6 21.2 %collective-permute-start.14 = (bf16[256,1024]{1,0:T(8,128)(2,1)S(1)}, bf16[256,1024]{1,0:T(8,128)(2,1)S(1)}, u32[]{:S(2)}, u32[]{:S(2)}) collective-permute-start(bf16[256,1024]{1,0:T(8,128)(2,1)S(1)} %convolution_convert_fusion.11), channel_id=1, source_target_pairs={{0,3},{1,2},{2,1},{3,0},{4,7},{5,6},{6,5},{7,4},{8,11},{9,10},{10,... | collective-permute-start | bytes 1572872 | tf_op jit(solution)/shard_map/ppermute | solution.py:219
  282.3 14.5 %collective-permute-start.24 = (bf16[256,1024]{1,0:T(8,128)(2,1)S(1)}, bf16[256,1024]{1,0:T(8,128)(2,1)S(1)}, u32[]{:S(2)}, u32[]{:S(2)}) collective-permute-start(bf16[256,1024]{1,0:T(8,128)(2,1)S(1)} %get-tuple-element.152), channel_id=1, source_target_pairs={{0,1},{1,0},{2,3},{3,2},{4,5},{5,4},{6,7},{7,6},{8,9},{9,8},{10,11... | collective-permute-start | bytes 1572872 | tf_op jit(solution)/shard_map/ppermute | solution.py:219
  283.0 19.4 %collective-permute-start.25 = (bf16[256,1024]{1,0:T(8,128)(2,1)S(1)}, bf16[256,1024]{1,0:T(8,128)(2,1)S(1)}, u32[]{:S(2)}, u32[]{:S(2)}) collective-permute-start(bf16[256,1024]{1,0:T(8,128)(2,1)S(1)} %get-tuple-element.151), channel_id=1, source_target_pairs={{0,2},{1,3},{2,0},{3,1},{4,6},{5,7},{6,4},{7,5},{8,10},{9,11},{10,... | collective-permute-start | bytes 1572872 | tf_op jit(solution)/shard_map/ppermute | solution.py:219
  284.3 19.3 %collective-permute-start.26 = (bf16[256,1024]{1,0:T(8,128)(2,1)S(1)}, bf16[256,1024]{1,0:T(8,128)(2,1)S(1)}, u32[]{:S(2)}, u32[]{:S(2)}) collective-permute-start(bf16[256,1024]{1,0:T(8,128)(2,1)S(1)} %get-tuple-element.150), channel_id=1, source_target_pairs={{0,3},{1,2},{2,1},{3,0},{4,7},{5,6},{6,5},{7,4},{8,11},{9,10},{10,... | collective-permute-start | bytes 1572872 | tf_op jit(solution)/shard_map/ppermute | solution.py:219
  311.3 30.3 %collective-permute-start.49 = (bf16[256,1024]{1,0:T(8,128)(2,1)}, bf16[256,1024]{1,0:T(8,128)(2,1)}, u32[]{:S(2)}, u32[]{:S(2)}) collective-permute-start(bf16[256,1024]{1,0:T(8,128)(2,1)} %get-tuple-element.143), channel_id=1, source_target_pairs={{0,1},{1,0},{2,3},{3,2},{4,5},{5,4},{6,7},{7,6},{8,9},{9,8},{10,11... | collective-permute-start | bytes 1572872 | tf_op jit(solution)/shard_map/ppermute | solution.py:219
  312.5 29.0 %collective-permute-start.50 = (bf16[256,1024]{1,0:T(8,128)(2,1)}, bf16[256,1024]{1,0:T(8,128)(2,1)}, u32[]{:S(2)}, u32[]{:S(2)}) collective-permute-start(bf16[256,1024]{1,0:T(8,128)(2,1)} %get-tuple-element.145), channel_id=1, source_target_pairs={{0,2},{1,3},{2,0},{3,1},{4,6},{5,7},{6,4},{7,5},{8,10},{9,11},{10,... | collective-permute-start | bytes 1572872 | tf_op jit(solution)/shard_map/ppermute | solution.py:219
  313.6 28.0 %collective-permute-start.51 = (bf16[256,1024]{1,0:T(8,128)(2,1)}, bf16[256,1024]{1,0:T(8,128)(2,1)}, u32[]{:S(2)}, u32[]{:S(2)}) collective-permute-start(bf16[256,1024]{1,0:T(8,128)(2,1)} %get-tuple-element.144), channel_id=1, source_target_pairs={{0,3},{1,2},{2,1},{3,0},{4,7},{5,6},{6,5},{7,4},{8,11},{9,10},{10,... | collective-permute-start | bytes 1572872 | tf_op jit(solution)/shard_map/ppermute | solution.py:219
  317.3 18.3 %collective-permute-start.30 = (bf16[256,256]{1,0:T(8,128)(2,1)S(1)}, bf16[256,256]{1,0:T(8,128)(2,1)S(1)}, u32[]{:S(2)}, u32[]{:S(2)}) collective-permute-start(bf16[256,256]{1,0:T(8,128)(2,1)S(1)} %bitcast.341), channel_id=1, source_target_pairs={{0,1},{1,0},{2,3},{3,2},{4,5},{5,4},{6,7},{7,6},{8,9},{9,8},{10,11... | collective-permute-start | bytes 393224 | tf_op jit(solution)/shard_map/ppermute | solution.py:219
  318.7 18.0 %collective-permute-start.31 = (bf16[256,256]{1,0:T(8,128)(2,1)S(1)}, bf16[256,256]{1,0:T(8,128)(2,1)S(1)}, u32[]{:S(2)}, u32[]{:S(2)}) collective-permute-start(bf16[256,256]{1,0:T(8,128)(2,1)S(1)} %bitcast.339), channel_id=1, source_target_pairs={{0,2},{1,3},{2,0},{3,1},{4,6},{5,7},{6,4},{7,5},{8,10},{9,11},{10,... | collective-permute-start | bytes 393224 | tf_op jit(solution)/shard_map/ppermute | solution.py:219
  344.3 124.6 %reduce-scatter.9.cloned.1.call-start = ((), (), s32[]{:S(2)}) async-start(), calls=%async_computation.10 | async-start | bytes 1769472 | tf_op jit(solution)/shard_map/reduce_scatter | solution.py:241
  366.4 110.7 %reduce-scatter.17.cloned.1.call-start = ((), (), s32[]{:S(2)}) async-start(), calls=%async_computation.14 | async-start | bytes 2359296 | tf_op jit(solution)/shard_map/reduce_scatter | solution.py:241
  371.5 111.0 %reduce-scatter.13.cloned.1.call-start = ((), (), s32[]{:S(2)}) async-start(), calls=%async_computation.12 | async-start | bytes 2359296 | tf_op jit(solution)/shard_map/reduce_scatter | solution.py:241
  377.2 142.0 %reduce-scatter.15.cloned.1.call-start = ((), (), s32[]{:S(2)}) async-start(), calls=%async_computation.13 | async-start | bytes 2359296 | tf_op jit(solution)/shard_map/reduce_scatter | solution.py:241
  382.3 173.8 %reduce-scatter.19.cloned.1.call-start = ((), (), s32[]{:S(2)}) async-start(), calls=%async_computation.15 | async-start | bytes 2359296 | tf_op jit(solution)/shard_map/reduce_scatter | solution.py:241
  389.4 203.3 %reduce-scatter.21.cloned.1.call-start = ((), (), s32[]{:S(2)}) async-start(), calls=%async_computation.16 | async-start | bytes 2359296 | tf_op jit(solution)/shard_map/reduce_scatter | solution.py:241
  395.1 234.4 %reduce-scatter.23.cloned.1.call-start = ((), (), s32[]{:S(2)}) async-start(), calls=%async_computation.17 | async-start | bytes 2359296 | tf_op jit(solution)/shard_map/reduce_scatter | solution.py:241
  399.1 12.6 %collective-permute-start.18 = (bf16[256,1024]{1,0:T(8,128)(2,1)}, bf16[256,1024]{1,0:T(8,128)(2,1)}, u32[]{:S(2)}, u32[]{:S(2)}) collective-permute-start(bf16[256,1024]{1,0:T(8,128)(2,1)} %get-tuple-element.158), channel_id=1, source_target_pairs={{0,1},{1,0},{2,3},{3,2},{4,5},{5,4},{6,7},{7,6},{8,9},{9,8},{10,11... | collective-permute-start | bytes 1572872 | tf_op jit(solution)/shard_map/ppermute | solution.py:219
  400.4 18.2 %collective-permute-start.19 = (bf16[256,1024]{1,0:T(8,128)(2,1)}, bf16[256,1024]{1,0:T(8,128)(2,1)}, u32[]{:S(2)}, u32[]{:S(2)}) collective-permute-start(bf16[256,1024]{1,0:T(8,128)(2,1)} %get-tuple-element.157), channel_id=1, source_target_pairs={{0,2},{1,3},{2,0},{3,1},{4,6},{5,7},{6,4},{7,5},{8,10},{9,11},{10,... | collective-permute-start | bytes 1572872 | tf_op jit(solution)/shard_map/ppermute | solution.py:219
  400.7 17.9 %collective-permute-start.20 = (bf16[256,1024]{1,0:T(8,128)(2,1)}, bf16[256,1024]{1,0:T(8,128)(2,1)}, u32[]{:S(2)}, u32[]{:S(2)}) collective-permute-start(bf16[256,1024]{1,0:T(8,128)(2,1)} %get-tuple-element.156), channel_id=1, source_target_pairs={{0,3},{1,2},{2,1},{3,0},{4,7},{5,6},{6,5},{7,4},{8,11},{9,10},{10,... | collective-permute-start | bytes 1572872 | tf_op jit(solution)/shard_map/ppermute | solution.py:219
  424.1 10.7 %collective-permute-start.33 = (bf16[256,1024]{1,0:T(8,128)(2,1)S(1)}, bf16[256,1024]{1,0:T(8,128)(2,1)}, u32[]{:S(2)}, u32[]{:S(2)}) collective-permute-start(bf16[256,1024]{1,0:T(8,128)(2,1)S(1)} %get-tuple-element.146), channel_id=1, source_target_pairs={{0,1},{1,0},{2,3},{3,2},{4,5},{5,4},{6,7},{7,6},{8,9},{9,8},{10,11... | collective-permute-start | bytes 1572872 | tf_op jit(solution)/shard_map/ppermute | solution.py:219
  424.6 12.9 %collective-permute-start.34 = (bf16[256,1024]{1,0:T(8,128)(2,1)S(1)}, bf16[256,1024]{1,0:T(8,128)(2,1)}, u32[]{:S(2)}, u32[]{:S(2)}) collective-permute-start(bf16[256,1024]{1,0:T(8,128)(2,1)S(1)} %get-tuple-element.148), channel_id=1, source_target_pairs={{0,2},{1,3},{2,0},{3,1},{4,6},{5,7},{6,4},{7,5},{8,10},{9,11},{10,... | collective-permute-start | bytes 1572872 | tf_op jit(solution)/shard_map/ppermute | solution.py:219
  425.9 15.4 %collective-permute-start.35 = (bf16[256,1024]{1,0:T(8,128)(2,1)S(1)}, bf16[256,1024]{1,0:T(8,128)(2,1)}, u32[]{:S(2)}, u32[]{:S(2)}) collective-permute-start(bf16[256,1024]{1,0:T(8,128)(2,1)S(1)} %get-tuple-element.147), channel_id=1, source_target_pairs={{0,3},{1,2},{2,1},{3,0},{4,7},{5,6},{6,5},{7,4},{8,11},{9,10},{10,... | collective-permute-start | bytes 1572872 | tf_op jit(solution)/shard_map/ppermute | solution.py:219
  451.2 9.3 %collective-permute-start.41 = (f32[832]{0:T(1024)S(1)}, f32[832]{0:T(1024)S(1)}, u32[]{:S(2)}, u32[]{:S(2)}) collective-permute-start(f32[832]{0:T(1024)S(1)} %get-tuple-element.128), channel_id=1, source_target_pairs={{0,12},{4,8},{8,4},{12,0},{16,28},{20,24},{24,20},{28,16},{1,13},{... | collective-permute-start | bytes 9992 | tf_op jit(solution)/shard_map/ppermute | solution.py:520
  520.6 111.0 %collective-permute-start.52 = (bf16[3,32,1024]{2,1,0:T(8,128)(2,1)S(1)}, bf16[3,32,1024]{2,1,0:T(8,128)(2,1)S(1)}, u32[]{:S(2)}, u32[]{:S(2)}) collective-permute-start(bf16[3,32,1024]{2,1,0:T(8,128)(2,1)S(1)} %get-tuple-element.163), channel_id=1, source_target_pairs={{0,1},{1,0},{2,3},{3,2},{4,5},{5,4},{6,7},{7,6},{8,9},{9,8},{10,11... | collective-permute-start | bytes 589832 | tf_op jit(solution)/shard_map/ppermute | solution.py:219
  522.1 117.3 %collective-permute-start.53 = (bf16[3,32,1024]{2,1,0:T(8,128)(2,1)S(1)}, bf16[3,32,1024]{2,1,0:T(8,128)(2,1)S(1)}, u32[]{:S(2)}, u32[]{:S(2)}) collective-permute-start(bf16[3,32,1024]{2,1,0:T(8,128)(2,1)S(1)} %get-tuple-element.162), channel_id=1, source_target_pairs={{0,2},{1,3},{2,0},{3,1},{4,6},{5,7},{6,4},{7,5},{8,10},{9,11},{10,... | collective-permute-start | bytes 589832 | tf_op jit(solution)/shard_map/ppermute | solution.py:219
  523.6 123.6 %collective-permute-start.54 = (bf16[3,32,1024]{2,1,0:T(8,128)(2,1)S(1)}, bf16[3,32,1024]{2,1,0:T(8,128)(2,1)S(1)}, u32[]{:S(2)}, u32[]{:S(2)}) collective-permute-start(bf16[3,32,1024]{2,1,0:T(8,128)(2,1)S(1)} %get-tuple-element.161), channel_id=1, source_target_pairs={{0,3},{1,2},{2,1},{3,0},{4,7},{5,6},{6,5},{7,4},{8,11},{9,10},{10,... | collective-permute-start | bytes 589832 | tf_op jit(solution)/shard_map/ppermute | solution.py:219
  (148 other events, 1424.5 us)
Sparse Core Ops, SparseCore 0:
  19.1 24.9 all-gather.15
  45.7 28.8 all-gather.25
  76.2 28.5 all-gather.27
  106.3 28.5 all-gather.21
  136.4 28.5 all-gather.19
  166.5 28.5 all-gather.17
  197.3 28.5 all-gather.23
  344.4 29.9 reduce-scatter.10
  376.8 32.5 reduce-scatter.8
  411.6 33.6 reduce-scatter.16
  447.7 34.8 reduce-scatter.12
  484.8 34.4 reduce-scatter.14
  521.7 34.4 reduce-scatter.18
  558.4 34.2 reduce-scatter.20
  594.9 34.4 reduce-scatter.22

commit v2 on v1

v2 whole, which is shorter than its diff:
```python
import functools

import jax
import jax.numpy as jnp
from jax import lax
from jax.experimental import pallas as pl
from jax.experimental.pallas import tpu as pltpu
from jax.sharding import PartitionSpec as P

HEAD_DIM = 64
EPSILON = 1e-05
ROOT = 0.7978845608028654
CUBE = 0.044715
LANES = 128
f32 = jnp.float32
bf16 = jnp.bfloat16

ROUTER, MIX, GAIN_ONE, SHIFT_ONE, QV, OUT_BIAS, GAIN_TWO, SHIFT_TWO, DOWN_BIAS, EXPERT_DOWN, COUNT = (
    0,
    2,
    4,
    5,
    6,
    8,
    9,
    10,
    11,
    12,
    14,
)
UP_BIAS = 15
SMALL_ROWS = 24

anywhere = pl.BlockSpec(memory_space=pl.ANY)
inside = pl.BlockSpec(memory_space=pltpu.VMEM)
scalar = pl.BlockSpec(memory_space=pltpu.SMEM)


def product(left_op, right_op):
    return jnp.dot(left_op, right_op, preferred_element_type=f32)


def left_product(left_op, right_op):
    return lax.dot_general(left_op, right_op, (((0,), (0,)), ((), ())), preferred_element_type=f32)


def right_product(left_op, right_op):
    return lax.dot_general(left_op, right_op, (((1,), (1,)), ((), ())), preferred_element_type=f32)


def layer_stats(values):
    row_mean = jnp.mean(values, -1, keepdims=True)
    centred = values - row_mean
    inverse = lax.rsqrt(jnp.mean(centred * centred, -1, keepdims=True) + EPSILON)
    return (centred * inverse, inverse)


def norm_back(grad_norm, normed, inverse, gain):
    scaled = grad_norm * gain
    return inverse * (
        scaled
        - jnp.mean(scaled, -1, keepdims=True)
        - normed * jnp.mean(scaled * normed, -1, keepdims=True)
    )


def sigmoid_pair(low, high):
    return 1.0 / (1.0 + jnp.exp(high - low))


def three_parts(values):
    high = values.astype(bf16)
    rest = values - high.astype(f32)
    middle = rest.astype(bf16)
    return high, middle, (rest - middle.astype(f32)).astype(bf16)


def aligned(index, size):
    return pl.ds(pl.multiple_of(index * size, size), size)


def run(kernel, name, inputs, specs, outs, out_specs, scratch, grid=()):
    return pl.pallas_call(
        kernel,
        grid=grid,
        in_specs=specs,
        out_specs=out_specs,
        out_shape=[jax.ShapeDtypeStruct(shape, kind) for shape, kind in outs],
        scratch_shapes=scratch,
        compiler_params=pltpu.CompilerParams(
            dimension_semantics=("arbitrary",) * len(grid), vmem_limit_bytes=56 * 1024 * 1024
        ),
        cost_estimate=pl.CostEstimate(flops=1024, bytes_accessed=1024, transcendentals=0),
        name=name,
    )(*inputs)


def start_all(copies):
    for copy in copies:
        copy.start()
    return copies


def wait_all(copies):
    for copy in copies:
        copy.wait()


def unpack_kernel(plan, places, *refs):
    dp, ctx, share, own, experts = plan
    parts, (by_row, by_column, out_ref), (held, sems) = refs[:dp], refs[dp : dp + 3], refs[dp + 3 :]
    size = parts[0].shape[0]
    wait_all(
        start_all(
            [
                pltpu.make_async_copy(part, held.at[aligned(places[i], size)], sems.at[i])
                for i, part in enumerate(parts)
            ]
        )
    )
    small = held[:, 4 * own :]
    by_row[...] = small
    turned = jnp.transpose(small.astype(f32))
    by_column[...] = turned[:SMALL_ROWS]
    for block in range(dp):
        for piece in range(ctx):
            at = block * size + piece * share
            out_ref[block * share : (block + 1) * share, piece * own : (piece + 1) * own] = held[
                at : at + share, 3 * own : 4 * own
            ]


def unpack(places, parts, plan):
    dp, ctx, share, own, experts = plan
    size = parts[0].shape[0]
    width = dp * size
    return run(
        functools.partial(unpack_kernel, plan),
        "unpack",
        [places] + parts,
        [scalar] + [anywhere] * dp,
        [((width, LANES), bf16), ((SMALL_ROWS, width), f32), ((dp * share, ctx * own), bf16)],
        [inside] * 3,
        [pltpu.VMEM((width, 4 * own + LANES), bf16), pltpu.SemaphoreType.DMA((dp,))],
    )


def qkv_kernel(plan, scalars, small_ref, *refs):
    dp, ctx, rows, own, share = plan
    parts, tokens = refs[:dp], refs[dp : dp + ctx]
    qkv_ref, norm_ref, weight_ref, sems = refs[dp + ctx :]
    size = parts[0].shape[0]
    moves = [
        pltpu.make_async_copy(token, norm_ref.at[aligned(scalars[dp + i], rows)], sems.at[i])
        for i, token in enumerate(tokens)
    ] + [
        pltpu.make_async_copy(part, weight_ref.at[aligned(scalars[i], size)], sems.at[ctx + i])
        for i, part in enumerate(parts)
    ]
    start_all(moves)
    width = small_ref.shape[1]
    column = lax.broadcasted_iota(jnp.int32, (width, own), 1) + scalars[dp] * own
    source = lax.broadcasted_iota(jnp.int32, (width, own), 0)
    rank, inner = column // (2 * share), column % (2 * share)
    pair = small_ref[QV : QV + 2, :].astype(bf16)
    biases = []
    for part in range(2):
        picks = [
            (source == (rank + part * (width // (2 * share))) * share + inner - half * share)
            & (inner // share == half)
            for half in range(2)
        ]
        biases.append(
            sum(product(pair[half : half + 1], picks[half].astype(bf16)) for half in range(2))
        )
    bias = jnp.concatenate([biases[0], jnp.zeros_like(biases[0]), biases[1]], 1)
    gain, shift = small_ref[GAIN_ONE : GAIN_ONE + 1, :], small_ref[SHIFT_ONE : SHIFT_ONE + 1, :]
    wait_all(moves)
    tile = min(256, ctx * rows)
    for at in range(0, ctx * rows, tile):
        span = slice(at, at + tile)
        normed, _ = layer_stats(norm_ref[span, :].astype(f32))
        low = (normed * gain + shift).astype(bf16)
        norm_ref[span, :] = low
        qkv_ref[span, :] = (product(low, weight_ref[:, : 3 * own]) + bias).astype(bf16)


def make_qkv(scalars, small, parts, tokens, plan):
    dp, ctx, rows, own, share = plan
    width = tokens[0].shape[1]
    return run(
        functools.partial(qkv_kernel, plan),
        "norm_qkv",
        [scalars, small] + parts + tokens,
        [scalar, inside] + [anywhere] * (dp + ctx),
        [
            ((ctx * rows, 3 * own), bf16),
            ((ctx * rows, width), bf16),
            ((width, parts[0].shape[1]), bf16),
        ],
        [inside] * 3,
        [pltpu.SemaphoreType.DMA((dp + ctx,))],
    )


def score_parts(q_part, k_ref, column, step, block):
    scale = HEAD_DIM ** (-0.5)
    parts = []
    if step:
        parts.append(right_product(q_part, k_ref[0 : step * block, column]) * scale)
    diagonal = right_product(q_part, k_ref[step * block : (step + 1) * block, column]) * scale
    rows = lax.broadcasted_iota(jnp.int32, (block, block), 0)
    keys = lax.broadcasted_iota(jnp.int32, (block, block), 1)
    parts.append(jnp.where(keys <= rows, diagonal, -1e30))
    return parts


def softmax_of(parts):
    row_max = functools.reduce(jnp.maximum, [jnp.max(part, -1, keepdims=True) for part in parts])
    terms = [jnp.exp(part - row_max) for part in parts]
    total = functools.reduce(jnp.add, [jnp.sum(term, -1, keepdims=True) for term in terms])
    inverse = 1.0 / total
    return [term * inverse for term in terms]


def key_spans(step, block):
    spans = [slice(0, step * block)] if step else []
    return spans + [slice(step * block, (step + 1) * block)]


def attention_forward_kernel(heads, block, q_ref, k_ref, v_ref, out_ref):
    for head in range(heads):
        column = slice(head * HEAD_DIM, (head + 1) * HEAD_DIM)
        for step in range(q_ref.shape[0] // block):
            rows = slice(step * block, (step + 1) * block)
            probs = softmax_of(score_parts(q_ref[rows, column], k_ref, column, step, block))
            mixed = functools.reduce(
                jnp.add,
                [
                    product(prob.astype(bf16), v_ref[span, column])
                    for prob, span in zip(probs, key_spans(step, block))
                ],
            )
            out_ref[rows, column] = mixed.astype(bf16)


def attention_backward_kernel(
    heads, block, rows, scalars, q_ref, k_ref, v_ref, *refs
):
    scale = HEAD_DIM ** (-0.5)
    pieces, (dq_ref, dk_ref, dv_ref, held, k_acc, v_acc, sems) = refs[:-7], refs[-7:]
    step_now, lanes = pl.program_id(0), dq_ref.shape[1]

    @pl.when(step_now == 0)
    def _():
        wait_all(
            start_all(
                [
                    pltpu.make_async_copy(piece, held.at[aligned(scalars[i], rows)], sems.at[i])
                    for i, piece in enumerate(pieces)
                ]
            )
        )

    grads = held[...] if held.shape[1] == lanes else held[:, aligned(step_now, lanes)]
    for head in range(heads):
        column = slice(head * HEAD_DIM, (head + 1) * HEAD_DIM)
        for step in reversed(range(q_ref.shape[0] // block)):
            span_rows = slice(step * block, (step + 1) * block)
            spans = key_spans(step, block)
            q_part, o_part = q_ref[span_rows, column], grads[span_rows, column]
            probs = softmax_of(score_parts(q_part, k_ref, column, step, block))
            prob_grads = [right_product(o_part, v_ref[span, column]) for span in spans]
            delta = functools.reduce(
                jnp.add,
                [jnp.sum(p * g, -1, keepdims=True) for p, g in zip(probs, prob_grads)],
            )
            score_grads = [(p * (g - delta)).astype(bf16) for p, g in zip(probs, prob_grads)]
            q_grad = functools.reduce(
                jnp.add,
                [product(s, k_ref[span, column]) for s, span in zip(score_grads, spans)],
            )
            dq_ref[span_rows, column] = (q_grad * scale).astype(bf16)
            first = step == q_ref.shape[0] // block - 1
            for span, score_grad, prob in zip(spans, score_grads, probs):
                key_grad = left_product(score_grad, q_part)
                value_grad = left_product(prob.astype(bf16), o_part)
                k_acc[span, column] = key_grad if first else k_acc[span, column] + key_grad
                v_acc[span, column] = value_grad if first else v_acc[span, column] + value_grad
    dk_ref[...] = (k_acc[...] * scale).astype(bf16)
    dv_ref[...] = v_acc[...].astype(bf16)


def attention_plan(qkv, width):
    length = qkv.shape[0]
    heads = min(2, width // HEAD_DIM)
    block = min(256, length)
    lanes = heads * HEAD_DIM
    steps = width // lanes
    whole = lanes % LANES == 0
    joined = [qkv] * 3 if whole else [qkv[:, i * width : (i + 1) * width] for i in range(3)]

    def spec(part):
        first = part * steps if whole else 0
        return pl.BlockSpec((length, lanes), lambda step: (0, first + step))

    return length, heads, block, lanes, steps, spec, joined


def attention_forward(qkv, width):
    length, heads, block, lanes, steps, spec, joined = attention_plan(qkv, width)
    return run(
        functools.partial(attention_forward_kernel, heads, block),
        "attention_forward",
        joined,
        [spec(0), spec(1), spec(2)],
        [((length, width), bf16)],
        [spec(0)],
        [],
        (steps,),
    )[0]


def attention_backward(scalars, qkv, pieces, width):
    length, heads, block, lanes, steps, spec, joined = attention_plan(qkv, width)
    return run(
        functools.partial(attention_backward_kernel, heads, block, pieces[0].shape[0]),
        "attention_backward",
        [scalars] + joined + pieces,
        [scalar, spec(0), spec(1), spec(2)] + [anywhere] * len(pieces),
        [((length, width), bf16)] * 3,
        [spec(0)] * 3,
        [
            pltpu.VMEM((length, width), bf16),
            pltpu.VMEM((length, lanes), f32),
            pltpu.VMEM((length, lanes), f32),
            pltpu.SemaphoreType.DMA((len(pieces),)),
        ],
        (steps,),
    )


def hidden_kernel(ctx, scalars, small_ref, out_ref, tokens_ref, sort_ref, *refs):
    pieces, (hidden_ref, norm_ref, sorted_ref) = refs[:ctx], refs[ctx:]
    own = pieces[0].shape[1]
    hidden = tokens_ref[...].astype(f32) + (
        sum(
            product(piece[...], out_ref[aligned(scalars[i], own), :])
            for i, piece in enumerate(pieces)
        )
        + small_ref[OUT_BIAS : OUT_BIAS + 1, :]
    )
    hidden_ref[...] = hidden
    normed, _ = layer_stats(hidden)
    low = (
        normed * small_ref[GAIN_TWO : GAIN_TWO + 1, :] + small_ref[SHIFT_TWO : SHIFT_TWO + 1, :]
    ).astype(bf16)
    norm_ref[...] = low
    sorted_ref[...] = product(sort_ref[...], low).astype(bf16)


def make_hidden(scalars, small, full_out, tokens, sort, pieces):
    shape = tokens.shape
    return run(
        functools.partial(hidden_kernel, len(pieces)),
        "hidden",
        [scalars, small, full_out, tokens, sort] + pieces,
        [scalar] + [inside] * (4 + len(pieces)),
        [(shape, f32), (shape, bf16), (shape, bf16)],
        [inside] * 3,
        [],
    )


def mlp_kernel(plan, scalars, small_ref, by_column, *refs):
    dp, ctx, rows, start, count, expert, merged, last = plan
    depth = dp // 2
    refs = list(refs)

    def take(number):
        taken = refs[:number]
        del refs[:number]
        return taken

    x_parts, g_parts = take(ctx), take(ctx)
    parts = take(dp if merged else 2 * dp)
    sums = take(6) if last else []
    if last:
        y_refs, gx_refs = take(ctx), take(ctx)
    else:
        y_ref, gx_ref, dots_out = take(3)
    (gb_ref,) = take(1)
    mine, other = take(1 if merged else 2), take(1 if merged else 2)
    up, down, x_all, g_all, act_all, go_all, gu_all, up_grad, down_grad = take(9)
    held = take(6) if last else []
    in_sems, x_sems, out_sems, held_sems = take(4)
    width, hidden = up.shape
    up_rows, down_rows = width // dp, hidden // dp
    tile = min(256, hidden)
    tiles = [slice(at, at + tile) for at in range(0, hidden, tile)]
    total = ctx * count

    def loads(target, size, which):
        return [
            pltpu.make_async_copy(
                parts[i].at[which] if merged else parts[which * dp + i],
                target.at[aligned(scalars[i], size)],
                in_sems.at[which * dp + i],
            )
            for i in range(dp)
        ]

    def rows_of(block):
        return slice(block * count, (block + 1) * count)

    tokens = [
        pltpu.make_async_copy(
            part.at[start : start + count], x_all.at[rows_of(i)], x_sems.at[i]
        )
        for i, part in enumerate(x_parts)
    ]
    grads = [
        pltpu.make_async_copy(
            part.at[start : start + count], g_all.at[rows_of(i)], x_sems.at[ctx + i]
        )
        for i, part in enumerate(g_parts)
    ]
    ups, downs = loads(up, up_rows, 0), loads(down, down_rows, 1)
    start_all(tokens + ups + grads + downs)
    gathered = [
        pltpu.make_async_copy(ref, held[i], held_sems.at[i]) for i, ref in enumerate(sums)
    ]
    start_all(gathered)
    wait_all(tokens)
    logits = product(x_all[...], small_ref[...])
    route_zero, route_one = logits[:, ROUTER : ROUTER + 1], logits[:, ROUTER + 1 : ROUTER + 2]
    mix_zero, mix_one = logits[:, MIX : MIX + 1], logits[:, MIX + 1 : MIX + 2]
    if expert is None:
        mask = None
        coef = sigmoid_pair(mix_zero, mix_one)
    else:
        place = lax.broadcasted_iota(jnp.int32, (count, 1), 0) + start
        firsts = [place < scalars[dp + block] for block in range(ctx)]
        masks = [(first if expert == 0 else ~first).astype(f32) for first in firsts]
        mask = jnp.concatenate(masks, 0)
        gate = (
            sigmoid_pair(route_zero, route_one)
            if expert == 0
            else sigmoid_pair(route_one, route_zero)
        )
        coef = sigmoid_pair(mix_one, mix_zero) * gate * mask
    wait_all(grads)
    go_all[...] = (g_all[...].astype(f32) * coef).astype(bf16)
    wait_all(ups)

    def forward(cut):
        pre = product(x_all[...], up[:, cut]) + by_column[:, cut]
        square = pre * pre
        bend = jnp.tanh(ROOT * (pre + CUBE * (square * pre)))
        half = 0.5 * (1.0 + bend)
        act_all[:, cut] = (pre * half).astype(bf16)
        return half + (0.5 * ROOT) * pre * (1.0 - bend * bend) * (1.0 + (3.0 * CUBE) * square)

    for number, cut in enumerate(tiles):
        slope = forward(cut)
        if number == 0:
            wait_all(downs)
        grad_act = right_product(go_all[...], down[cut, :])
        grad_up = (grad_act * slope).astype(bf16)
        gu_all[:, cut] = grad_up
        gb_ref[:, cut] = jnp.sum(grad_up.astype(f32), 0, keepdims=True)
        down_grad[cut, :] = left_product(act_all[:, cut], go_all[...]).astype(bf16)
        up_grad[:, cut] = left_product(x_all[...], grad_up).astype(bf16)

    def stores(grad, size, which):
        targets = [
            (mine[0].at[i, which] if merged else mine[which].at[i])
            if i < depth
            else (other[0].at[i - depth, which] if merged else other[which].at[i - depth])
            for i in range(dp)
        ]
        return [
            pltpu.make_async_copy(
                grad.at[aligned(scalars[i], size)], target, out_sems.at[which * dp + i]
            )
            for i, target in enumerate(targets)
        ]

    saved = start_all(stores(up_grad, up_rows, 0) + stores(down_grad, down_rows, 1))
    wait_all(gathered)
    for block in range(ctx):
        span = rows_of(block)
        out = product(act_all[span, :], down[...])
        grad_x = right_product(gu_all[span, :], up[...])
        dot = jnp.sum(g_all[span, :].astype(f32) * out, -1, keepdims=True)
        out = out * coef[span]
        if not last:
            y_ref[span, :], gx_ref[span, :] = out, grad_x
            dots_out[span, :] = dot if mask is None else dot * mask[span]
            continue
        y_dense, gx_dense, dots_dense, y_first, gx_first, dots_first = held
        whole = slice(block * rows, (block + 1) * rows)
        sets = ((y_dense, y_first, out, y_refs), (gx_dense, gx_first, grad_x, gx_refs))
        for dense, first, own, target in sets:
            early = dense[whole, :][:start] + first[span, :][:start]
            middle = dense[whole, :][start:count] + (first[span, :][start:] + own[: count - start])
            late = dense[whole, :][count:] + own[count - start :]
            target[block][0:start, 0:width] = early.astype(bf16)
            target[block][start:count, 0:width] = middle.astype(bf16)
            target[block][count:rows, 0:width] = late.astype(bf16)
        own_dot = dot * mask[span]
        first_dot = dots_first[span, :]
        moe = jnp.concatenate(
            [
                first_dot[:start],
                first_dot[start:] + own_dot[: count - start],
                own_dot[count - start :],
            ],
            0,
        )
        lane = lax.broadcasted_iota(jnp.int32, (rows, LANES), 1)
        both = jnp.where(lane % 2 == 0, dots_dense[whole, :], moe)
        high, middle, low = three_parts(both)
        extra = jnp.where(lane < 2, high.astype(f32), jnp.where(lane < 4, middle.astype(f32), low.astype(f32)))
        gx_refs[block][:, width:] = jnp.where(lane < 6, extra, 0.0).astype(bf16)
    wait_all(saved)


def mlp(scalars, small, bias, x, g, parts, expert, merged, sums):
    ctx = len(x)
    rows, width = x[0].shape
    dp = len(parts) if merged else len(parts) // 2
    depth = dp // 2
    hidden = bias.shape[1]
    count = rows if expert is None else rows * 5 // 8
    start = 0 if expert in (None, 0) else rows - count
    total = ctx * count
    last = expert == 1
    if merged:
        halves = [((depth,) + parts[0].shape, bf16)]
    else:
        halves = [((depth,) + parts[0].shape, bf16), ((depth,) + parts[dp].shape, bf16)]
    if last:
        outs = [((rows, width), bf16)] * ctx + [((rows, width + LANES), bf16)] * ctx
    else:
        outs = [((total, width), f32), ((total, width), f32), ((total, 1), f32)]
    outs = outs + [((1, hidden), f32)] + halves + halves
    small_outs = len(outs) - 2 * len(halves)
    held = [pltpu.VMEM(ref.shape, f32) for ref in sums]
    return run(
        functools.partial(mlp_kernel, (dp, ctx, rows, start, count, expert, merged, last)),
        "mlp",
        [scalars, small, bias] + x + g + parts + sums,
        [scalar, inside, inside] + [anywhere] * (2 * ctx + len(parts) + len(sums)),
        outs,
        [inside] * small_outs + [anywhere] * (2 * len(halves)),
        [
            pltpu.VMEM((width, hidden), bf16),
            pltpu.VMEM((hidden, width), bf16),
            pltpu.VMEM((total, width), bf16),
            pltpu.VMEM((total, width), bf16),
            pltpu.VMEM((total, hidden), bf16),
            pltpu.VMEM((total, width), bf16),
            pltpu.VMEM((total, hidden), bf16),
            pltpu.VMEM((width, hidden), bf16),
            pltpu.VMEM((hidden, width), bf16),
        ]
        + held
        + [
            pltpu.SemaphoreType.DMA((2 * dp,)),
            pltpu.SemaphoreType.DMA((2 * ctx,)),
            pltpu.SemaphoreType.DMA((2 * dp,)),
            pltpu.SemaphoreType.DMA((max(1, len(sums)),)),
        ],
    )


def middle_kernel(
    ctx, scalars, by_row, by_column, out_ref, hidden_ref, norm_ref, g_ref, first_ref, unsort_ref, *refs
):
    gx, pieces = refs[:ctx], refs[ctx : 2 * ctx]
    outs = refs[2 * ctx :]
    base_ref, grad_hidden_ref, out_grad_ref, rows_ref, router_ref = outs[:5]
    grad_pieces = outs[5:]
    rows, width = hidden_ref.shape
    own = pieces[0].shape[1]
    unsort = unsort_ref[...]
    gathered = sum(product(unsort, piece[...]) for piece in gx)
    grad_norm = gathered[:, :width]
    extra = gathered[:, width:]
    dense_dot = extra[:, 0:1] + (extra[:, 2:3] + extra[:, 4:5])
    moe_dot = extra[:, 1:2] + (extra[:, 3:4] + extra[:, 5:6])
    grad_out = g_ref[...].astype(f32)
    first = first_ref[...]
    down_bias = by_column[DOWN_BIAS : DOWN_BIAS + 1, :]
    moe_bias = jnp.where(
        first > 0.5,
        by_column[EXPERT_DOWN : EXPERT_DOWN + 1, :],
        by_column[EXPERT_DOWN + 1 : EXPERT_DOWN + 2, :],
    )
    dense_dot = dense_dot + jnp.sum(grad_out * down_bias, -1, keepdims=True)
    moe_dot = moe_dot + jnp.sum(grad_out * moe_bias, -1, keepdims=True)
    norm = norm_ref[...]
    logits = product(norm, by_row[...])
    route = [
        sigmoid_pair(logits[:, a : a + 1], logits[:, b : b + 1])
        for a, b in ((ROUTER, ROUTER + 1), (ROUTER + 1, ROUTER))
    ]
    mix = [
        sigmoid_pair(logits[:, a : a + 1], logits[:, b : b + 1])
        for a, b in ((MIX, MIX + 1), (MIX + 1, MIX))
    ]
    hot = [first, 1.0 - first]
    gate = route[0] * hot[0] + route[1] * hot[1]
    branch = mix[1] * gate
    hidden = hidden_ref[...]
    base_ref[...] = hidden + (mix[0] * down_bias + branch * moe_bias)
    grad_mix = [dense_dot, moe_dot * gate]
    mean_mix = mix[0] * grad_mix[0] + mix[1] * grad_mix[1]
    grad_gate = moe_dot * mix[1]
    grad_route = [hot[0] * grad_gate, hot[1] * grad_gate]
    mean_route = route[0] * grad_route[0] + route[1] * grad_route[1]
    lane = lax.broadcasted_iota(jnp.int32, (rows, LANES), 1)
    columns = [route[i] * (grad_route[i] - mean_route) for i in range(2)]
    columns += [mix[i] * (grad_mix[i] - mean_mix) for i in range(2)]
    logit_grads = jnp.zeros((rows, LANES), f32)
    for i, column in enumerate(columns):
        logit_grads = jnp.where(lane == i, column, logit_grads)
    split = three_parts(logit_grads)
    weights = by_row[...]
    for part in split:
        grad_norm = grad_norm + right_product(part, weights)
    router_ref[...] = sum(left_product(norm, part) for part in split)
    grad_dense = (grad_out * mix[0]).astype(bf16).astype(f32)
    grad_moe = (grad_out * branch).astype(bf16).astype(f32)
    normed, inverse = layer_stats(hidden)
    gain = by_column[GAIN_TWO : GAIN_TWO + 1, :]
    grad_hidden = grad_out + norm_back(grad_norm, normed, inverse, gain)
    grad_hidden_ref[...] = grad_hidden
    low = grad_hidden.astype(bf16)

    def total(values):
        return jnp.sum(values, 0, keepdims=True)

    sums = [
        total(low.astype(f32)),
        total(grad_norm * normed),
        total(grad_norm),
        total(grad_dense),
        total(grad_moe * hot[0]),
        total(grad_moe * hot[1]),
        jnp.zeros((2, width), f32),
    ]
    rows_ref[...] = jnp.concatenate(sums, 0)
    for i, (piece, target) in enumerate(zip(pieces, grad_pieces)):
        span = aligned(scalars[i], own)
        target[...] = right_product(low, out_ref[span, :]).astype(bf16)
        out_grad_ref[span, :] = left_product(piece[...], low).astype(bf16)


def make_middle(scalars, by_row, by_column, full_out, hidden, norm, g, first, unsort, gx, pieces):
    ctx = len(gx)
    rows, width = hidden.shape
    own = pieces[0].shape[1]
    return run(
        functools.partial(middle_kernel, ctx),
        "middle",
        [scalars, by_row, by_column, full_out, hidden, norm, g, first, unsort] + gx + pieces,
        [scalar] + [inside] * (8 + 2 * ctx),
        [
            ((rows, width), f32),
            ((rows, width), f32),
            ((width, width), bf16),
            ((8, width), f32),
            ((width, LANES), f32),
        ]
        + [((rows, own), bf16)] * ctx,
        [inside] * (5 + ctx),
        [],
    )


def qkv_back_kernel(plan, scalars, norm_ref, dq_ref, dk_ref, dv_ref, weight_ref, *refs):
    dp, ctx, rows, own = plan
    depth = dp // 2
    gn_refs, (mine, other, bias_ref, grad, weight_grad, gn, sems, gn_sems) = refs[:ctx], refs[ctx:]
    width = norm_ref.shape[1]
    size = width // dp
    for part, ref in enumerate((dq_ref, dk_ref, dv_ref)):
        grad[:, part * own : (part + 1) * own] = ref[...]
    tile = min(256, ctx * rows)
    weight = weight_ref[:, : 3 * own]
    for at in range(0, ctx * rows, tile):
        gn[at : at + tile, :] = right_product(grad[at : at + tile, :], weight).astype(bf16)
    sent = start_all(
        [
            pltpu.make_async_copy(gn.at[aligned(scalars[dp + i], rows)], ref, gn_sems.at[i])
            for i, ref in enumerate(gn_refs)
        ]
    )
    step = min(256, width)
    for at in range(0, width, step):
        weight_grad[at : at + step, :] = left_product(norm_ref[:, at : at + step], grad[...]).astype(
            bf16
        )
    saved = start_all(
        [
            pltpu.make_async_copy(
                weight_grad.at[aligned(scalars[i], size)],
                mine.at[i] if i < depth else other.at[i - depth],
                sems.at[i],
            )
            for i in range(dp)
        ]
    )
    bias_ref[...] = jnp.sum(grad[...].astype(f32), 0, keepdims=True)
    wait_all(sent + saved)


def qkv_back(scalars, norm, grads, weight, plan):
    dp, ctx, rows, own = plan
    length, width = norm.shape
    half = ((dp // 2, width // dp, 3 * own), bf16)
    return run(
        functools.partial(qkv_back_kernel, plan),
        "qkv_back",
        [scalars, norm] + list(grads) + [weight],
        [scalar] + [inside] * 5,
        [((rows, width), bf16)] * ctx + [half, half, ((1, 3 * own), f32)],
        [anywhere] * (ctx + 2) + [inside],
        [
            pltpu.VMEM((length, 3 * own), bf16),
            pltpu.VMEM((width, 3 * own), bf16),
            pltpu.VMEM((length, width), bf16),
            pltpu.SemaphoreType.DMA((dp,)),
            pltpu.SemaphoreType.DMA((ctx,)),
        ],
    )


def final_kernel(ctx, by_column, tokens_ref, grad_hidden_ref, *refs):
    pieces, (grad_ref, rows_ref) = refs[:ctx], refs[ctx:]
    grad_norm = sum(piece[...].astype(f32) for piece in pieces)
    normed, inverse = layer_stats(tokens_ref[...].astype(f32))
    gain = by_column[GAIN_ONE : GAIN_ONE + 1, :]
    grad_ref[...] = grad_hidden_ref[...] + norm_back(grad_norm, normed, inverse, gain)
    rows_ref[0:1, :] = jnp.sum(grad_norm * normed, 0, keepdims=True)
    rows_ref[1:2, :] = jnp.sum(grad_norm, 0, keepdims=True)


def make_final(by_column, tokens, grad_hidden, pieces):
    return run(
        functools.partial(final_kernel, len(pieces)),
        "final",
        [by_column, tokens, grad_hidden] + pieces,
        [inside] * (3 + len(pieces)),
        [(tokens.shape, f32), ((2, tokens.shape[1]), f32)],
        [inside] * 2,
        [],
    )


def result_kernel(ctx, base_ref, unsort_ref, *refs):
    pieces, (out_ref,) = refs[:ctx], refs[ctx:]
    unsort = unsort_ref[...]
    out_ref[...] = base_ref[...] + sum(product(unsort, piece[...]) for piece in pieces)


def make_result(base, unsort, pieces):
    return run(
        functools.partial(result_kernel, len(pieces)),
        "result",
        [base, unsort] + pieces,
        [inside] * (2 + len(pieces)),
        [(base.shape, f32)],
        [inside],
        [],
    )[0]


def layer(
    dp,
    ctx,
    tokens,
    cotangent,
    routes,
    ln1_gain,
    ln1_bias,
    qkv_weight,
    qv_bias,
    out_weight,
    out_bias,
    ln2_gain,
    ln2_bias,
    up_weight,
    up_bias,
    down_weight,
    down_bias,
    router_weight,
    mix_weight,
    expert_up,
    expert_up_bias,
    expert_down,
    expert_down_bias,
):
    rows, width = tokens.shape[0] * tokens.shape[1], tokens.shape[2]
    experts, share, hidden = expert_up.shape
    own_hidden = hidden // ctx
    own_width = width // ctx
    unit = hidden // (dp * ctx)
    me = lax.axis_index("ctx")
    place_dp = lax.axis_index("dp")
    core = place_dp % 2
    depth = dp // 2
    shifts = range(1, ctx)
    ring_pairs = [(i, (i + 2) % dp) for i in range(dp)]
    core_pairs = [(i, i ^ 1) for i in range(dp)]
    places = jnp.stack(
        [
            ((place_dp // 2 + depth - t) % depth) * 2 + c
            for c in (core, 1 - core)
            for t in range(depth)
        ]
    ).astype(jnp.int32)
    peers = jnp.stack([me ^ s for s in range(ctx)]).astype(jnp.int32)

    def swap(array, shift):
        return lax.ppermute(array, "ctx", [(i, i ^ shift) for i in range(ctx)])

    def gather_ctx(array):
        return [array] + [swap(array, s) for s in shifts]

    def trade(pieces):
        return [pieces[0]] + [swap(pieces[s], s) for s in shifts]

    def exchange(pieces):
        return trade(
            [lax.dynamic_index_in_dim(pieces, me ^ s, 0, keepdims=False) for s in range(ctx)]
        )

    def natural(pieces):
        whole = jnp.zeros((ctx,) + pieces[0].shape, pieces[0].dtype)
        for s, piece in enumerate(pieces):
            whole = lax.dynamic_update_slice_in_dim(whole, piece[None], me ^ s, 0)
        return whole

    def ring(array):
        return lax.ppermute(array, "dp", ring_pairs)

    def swap_core(array):
        return lax.ppermute(array, "dp", core_pairs)

    def chunks(array):
        size = array.shape[0] // dp
        cut = [
            lax.dynamic_slice_in_dim(array, places[i] * size, size, 0) for i in range(dp)
        ]
        return jnp.stack(cut[:depth]), jnp.stack(cut[depth:])

    def after(array, *others):
        return lax.optimization_barrier((array,) + others)[0]

    tokens = tokens.reshape(rows, width)
    cotangent = cotangent.reshape(rows, width)
    first_hot = routes.reshape(rows) == 0
    first_float = first_hot.astype(f32)
    first_count = jnp.sum(first_float)

    def column(vector):
        return vector.reshape(-1, share).T

    def bias_column(vector):
        return jnp.pad(vector.reshape(unit, 1), ((0, ctx * share - unit), (0, 0)))

    small = jnp.concatenate(
        [
            router_weight,
            mix_weight,
            column(ln1_gain),
            column(ln1_bias),
            column(qv_bias),
            column(out_bias),
            column(ln2_gain),
            column(ln2_bias),
            column(down_bias),
            expert_down_bias.T,
            jnp.broadcast_to(first_count.astype(bf16), (share, 1)),
        ],
        1,
    )
    small = jnp.pad(small, ((0, 0), (0, LANES - small.shape[1])))
    qkv_cut = qkv_weight.reshape(share, 3, ctx, own_width).transpose(2, 0, 1, 3)
    first_cut = jnp.concatenate(
        [
            qkv_cut.reshape(ctx, share, 3 * own_width),
            jnp.broadcast_to(small[None], (ctx, share, LANES)),
        ],
        -1,
    )
    first_rows = natural(exchange(first_cut)).reshape(ctx * share, 3 * own_width + LANES)
    qkv_rows = first_rows[:, : 3 * own_width]
    small_rows = first_rows[:, 3 * own_width :]
    counts = small_rows[::share, COUNT]
    bias_lanes = jnp.concatenate(
        [bias_column(up_bias)] + [bias_column(expert_up_bias[e]) for e in range(experts)], 1
    )
    lane = jnp.arange(LANES)[None, :]
    bias_lanes = jnp.pad(bias_lanes, ((0, 0), (UP_BIAS, LANES - UP_BIAS - bias_lanes.shape[1])))
    small_rows = jnp.where((lane >= UP_BIAS) & (lane < UP_BIAS + experts + 1), bias_lanes, small_rows)
    out_rows = out_weight.reshape(share, ctx, own_width).transpose(1, 0, 2)
    out_rows = out_rows.reshape(ctx * share, own_width)
    first_group = jnp.concatenate([qkv_rows, out_rows, small_rows], 1)

    def gather_dp(streams):
        parts = [[array] for array in streams]
        for _ in range(1, depth):
            for part in parts:
                part.append(ring(part[-1]))
        return parts

    def with_cores(parts):
        return parts + [swap_core(part) for part in parts]

    (first_ring,) = gather_dp([first_group])
    token_parts = gather_ctx(tokens)
    first_parts = with_cores(first_ring)
    plan = (dp, ctx, share, own_width, experts)
    by_row, by_column, out_own = unpack(places, first_parts, plan)
    out_pieces = natural(gather_ctx(out_own))
    full_out = out_pieces.reshape(ctx, dp, share, width).transpose(1, 0, 2, 3).reshape(width, width)

    unit_rows = ctx * share
    ups = jnp.concatenate([up_weight[None], expert_up], 0)
    ups_cut = ups.reshape(experts + 1, share, dp, ctx, unit).transpose(3, 0, 1, 2, 4)
    ups_cut = after(ups_cut.reshape(ctx, experts + 1, share, own_hidden), first_rows)
    ups_rows = natural(exchange(ups_cut)).transpose(1, 0, 2, 3)
    ups_rows = ups_rows.reshape(experts + 1, unit_rows, own_hidden)
    downs = [down_weight] + [expert_down[e] for e in range(experts)]
    merged = downs[0].shape == ups_rows.shape[1:]
    streams = []
    for which in range(experts + 1):
        pair = [ups_rows[which], downs[which]]
        streams += [jnp.stack(pair)] if merged else pair
    streams = list(lax.optimization_barrier(tuple(streams) + (first_ring[-1],)))[:-1]
    rings = [[stream, ring(stream)] for stream in streams]

    order = jnp.arange(rows).astype(f32)
    counted = jnp.cumsum(first_float)
    place = jnp.where(first_hot, counted - 1.0, first_count + order - counted)
    unsort = (place[:, None] == order[None, :]).astype(bf16)
    sort = (place[None, :] == order[:, None]).astype(bf16)
    sorted_grad = product(sort, cotangent).astype(bf16)

    scalars = jnp.concatenate([places, peers])
    qkv, attn_in, own_qkv = make_qkv(
        scalars, by_column, first_parts, token_parts, (dp, ctx, rows, own_width, share)
    )
    attended_heads = attention_forward(qkv, own_width)
    attended = exchange(attended_heads.reshape(ctx, rows, own_width))
    hidden_state, ffn_in, sorted_in = make_hidden(peers, by_column, full_out, tokens, sort, attended)
    ffn_parts = gather_ctx(sorted_in)
    grad_parts = gather_ctx(after(sorted_grad, attended[-1]))

    for _ in range(2, depth):
        stepped = lax.optimization_barrier(tuple(parts[-1] for parts in rings) + (sorted_in,))
        for parts, part in zip(rings, stepped):
            parts.append(ring(part))
    if merged:
        weight_parts = [with_cores(parts) for parts in rings]
    else:
        weight_parts = [
            with_cores(rings[2 * w]) + with_cores(rings[2 * w + 1]) for w in range(experts + 1)
        ]

    row_counts = jnp.stack([counts[me ^ s] for s in range(ctx)]).astype(jnp.int32)
    mlp_scalars = jnp.concatenate([places, row_counts])
    up_biases = by_column[UP_BIAS : UP_BIAS + experts + 1]
    up_biases = up_biases.reshape(experts + 1, dp, -1)[:, :, :unit].reshape(experts + 1, own_hidden)

    class Scatter:
        def __init__(self, mine, other):
            self.mine, self.got, self.step, self.sent = mine, swap_core(other), 0, None

        def move(self, *others):
            if self.step == 0:
                self.got = after(self.got, *others)
            carried = None if self.step == 0 else after(ring(self.sent), *others)
            self.step += 1
            part = self.mine[self.step % depth].astype(f32) + self.got[self.step % depth].astype(f32)
            if carried is not None:
                part = part + carried.astype(f32)
            self.sent = part.astype(bf16) if self.step < depth else part
            return self.sent

        def finish(self, *others):
            while self.step < depth:
                self.move(*others)
            return self.sent

    class Joint:
        def __init__(self, halves):
            half = len(halves) // 2
            self.parts = [Scatter(m, o) for m, o in zip(halves[:half], halves[half:])]

        def move(self, *others):
            return [part.move(*others) for part in self.parts]

        def finish(self, *others):
            done = [part.finish(*others) for part in self.parts]
            return done if len(done) == 2 else [done[0][0], done[0][1]]

    def run_mlp(which, held, sums):
        return mlp(
            held,
            by_row,
            up_biases[which][None],
            ffn_parts,
            grad_parts,
            weight_parts[which],
            which - 1 if which else None,
            merged,
            list(sums),
        )

    dense = run_mlp(0, mlp_scalars, [])
    sum_dense = Joint(dense[4:])
    first = run_mlp(1, after(mlp_scalars, dense[3]), [])
    sum_first = Joint(first[4:])
    sent = sum_dense.move(first[3])
    second = run_mlp(2, after(mlp_scalars, first[3], *sent), dense[:3] + first[:3])
    gb_second = second[2 * ctx]
    grad_pieces = trade(second[ctx : 2 * ctx])
    sum_second = Joint(second[2 * ctx + 1 :])
    sent = sum_first.move(gb_second)
    sent = sum_dense.move(*sent) + sum_second.move(*sent)

    base, grad_hidden, out_grad, middle_rows, router_grad, *att_grads = make_middle(
        after(peers, *sent),
        by_row,
        by_column,
        full_out,
        hidden_state,
        ffn_in,
        cotangent,
        first_float[:, None],
        unsort,
        grad_pieces,
        attended,
    )
    att_grads = trade(att_grads)
    result_pieces = trade([after(piece, att_grads[-1]) for piece in second[:ctx]])
    sent = sum_first.move(middle_rows) + sum_dense.move(middle_rows)

    grad_heads = attention_backward(after(peers, *sent), qkv, att_grads, own_width)
    sent = sum_second.move(grad_heads[0])
    *norm_grads, qkv_mine, qkv_other, grad_b_qkv = qkv_back(
        after(scalars, *sent), attn_in, grad_heads, own_qkv, (dp, ctx, rows, own_width)
    )
    norm_pieces = trade(norm_grads)
    sum_qkv = Scatter(qkv_mine, qkv_other)
    sent = sum_first.move(grad_b_qkv)
    sent = sent + [sum_qkv.move(*sent)]
    dense_sums = sum_dense.finish(*sent)
    grad_inputs, final_rows = make_final(
        after(by_column, *dense_sums, *sent), tokens, grad_hidden, norm_pieces
    )
    sent = sum_second.move(final_rows)
    result = make_result(base, unsort, result_pieces)
    out_grad = out_grad.reshape(dp, ctx, share, width).transpose(1, 0, 2, 3)
    out_grad = after(out_grad.reshape(ctx, dp * share, width), norm_pieces[-1])
    out_part = sum(p.astype(f32) for p in exchange(out_grad))
    out_grad = Scatter(*chunks(out_part.astype(bf16))).finish()
    qkv_part = sum_qkv.finish()
    first_sums, second_sums = sum_first.finish(), sum_second.finish()
    up_sums = [dense_sums[0], first_sums[0], second_sums[0]]
    down_sums = [dense_sums[1], first_sums[1], second_sums[1]]
    upb_grads = [dense[3][0], first[3][0], gb_second[0]]

    def to_owners(part, groups):
        size = part.shape[1] // groups
        pieces = exchange(part.astype(bf16).reshape(ctx, share, part.shape[1]))
        whole = natural(pieces).reshape(ctx, share, groups, size).transpose(1, 2, 0, 3)
        return whole.reshape(share, ctx * part.shape[1]).astype(f32)

    up_grads = [to_owners(part, dp) for part in up_sums]
    qkv_grad = to_owners(qkv_part, 3)

    zero_qv = jnp.zeros((2, width), f32)
    grad_qv = lax.dynamic_update_slice(
        zero_qv,
        jnp.concatenate([grad_b_qkv[:, :own_width], grad_b_qkv[:, 2 * own_width :]], 0),
        (0, me * own_width),
    )

    def own_columns(array):
        whole = jnp.zeros((dp, ctx, array.shape[-1]), f32)
        return lax.dynamic_update_slice_in_dim(whole, array[:, None], me, 1)

    expert_upb = jnp.stack(upb_grads[1:]).reshape(experts, dp, unit).transpose(1, 0, 2)
    small_grads = [
        final_rows[0],
        final_rows[1],
        grad_qv,
        middle_rows[0],
        middle_rows[1],
        middle_rows[2],
        middle_rows[3],
        router_grad[:, :experts],
        router_grad[:, experts : 2 * experts],
        middle_rows[4 : 4 + experts].reshape(experts, dp, ctx, share).transpose(1, 2, 0, 3),
        own_columns(upb_grads[0].reshape(dp, unit)),
        own_columns(expert_upb.reshape(dp, experts * unit)),
    ]
    sizes = [grad.size // (dp * ctx) for grad in small_grads]
    small_sum = jnp.concatenate([g.reshape(dp, ctx, -1) for g in small_grads], -1)
    small_sum = sum(exchange(small_sum.transpose(1, 0, 2)))
    small_sum = small_sum.reshape(dp, 1, -1)[places]
    small_sum = small_sum[:depth] + swap_core(small_sum[depth:])
    pairs = [[(i, (i + dp - 2 * t) % dp) for i in range(dp)] for t in range(depth)]
    small_sum = sum(
        [small_sum[0]] + [lax.ppermute(small_sum[t], "dp", pairs[t]) for t in range(1, depth)]
    )[0]
    outs, at = [], 0
    for size in sizes:
        outs.append(small_sum[at : at + size])
        at += size
    return (
        result[None],
        grad_inputs[None],
        outs[0],
        outs[1],
        qkv_grad,
        outs[2],
        out_grad,
        outs[3],
        outs[4],
        outs[5],
        up_grads[0],
        outs[10],
        down_sums[0],
        outs[6],
        outs[7].reshape(router_weight.shape),
        outs[8].reshape(mix_weight.shape),
        jnp.stack(up_grads[1:]),
        outs[11].reshape(expert_up_bias.shape),
        jnp.stack(down_sums[1:]),
        outs[9].reshape(expert_down_bias.shape),
    )


def solution(mesh):
    both = ("dp", "ctx")
    data = P("dp", "ctx", None)
    vector = P(both)
    matrix = P(both, None)
    expert_matrix = P(None, both, None)
    expert_vector = P(None, both)
    weights = (
        vector,
        vector,
        matrix,
        vector,
        matrix,
        vector,
        vector,
        vector,
        matrix,
        vector,
        matrix,
        vector,
        matrix,
        matrix,
        expert_matrix,
        expert_vector,
        expert_matrix,
        expert_vector,
    )
    return jax.shard_map(
        functools.partial(layer, mesh.shape["dp"], mesh.shape["ctx"]),
        mesh=mesh,
        in_specs=(data, data, data) + weights,
        out_specs=(data, data) + weights,
        check_vma=False,
    )
```

time: 670 us -> 502 us (0.75)
  matrix products: 114 us -> 0.34 us
  Pallas kernels: 25.8 us -> 136 us
  waiting for transfers between devices: 266 us -> 181 us
  local copies, waits for them, and re-layouts: 97.9 us -> 44.6 us
  blocking collectives: 42.7 us -> 0 us
  starting transfers between devices: 67.5 us -> 90.5 us
  between operations: 18 us -> 3.22 us
  other arithmetic: 32.6 us -> 40.8 us
    reduce_scatter x8 -> x0, waiting for transfers between devices: 137 us -> none  [scatter_dp(): lax.psum_scatter(array.astype(bf16), 'dp', scatter_dimension=axis, tiled=...]
    pallas_call x2 -> x12, Pallas kernels: 25.8 us -> 136 us  [run(): pl.pallas_call(kernel, grid=grid, in_specs=specs, out_specs=out_specs, ou...]
    ppermute x7 -> x52, waiting for transfers between devices: 2.26 us -> 99.8 us  [the longest x27 89.6 us: ring(): return lax.ppermute(array, 'dp', ring_pairs)]
    dot_general x19 -> x0, matrix products: 73.4 us -> none  [the longest x8 37 us: left_product(): lax.dot_general(left_op, right_op, (((0,), (0,)), ((), ())), preferred_el...]
    ppermute x48 -> x51, waiting for transfers between devices: 125 us -> 81.1 us  [swap(): return lax.ppermute(array, 'ctx', [(i, i ^ shift) for i in range(ctx)])]
    dot_general x16 -> x1, matrix products: 40.6 us -> 0.34 us  [product(): return jnp.dot(left_op, right_op, preferred_element_type=f32)]
    dynamic_update_slice x32 -> x22, local copies, waits for them, and re-layouts: 39.2 us -> 0.35 us  [natural(): whole = lax.dynamic_update_slice_in_dim(whole, piece[None], me ^ s, 0)]
    all_gather x2 -> x0, blocking collectives: 30.5 us -> none  [the longest x1 16.3 us: gather_dp(): return lax.all_gather(array, 'dp', axis=axis, tiled=True)]
  transfers between devices with their start and end apart: 70 -> 103, of which waited for: 34 -> 46; matrix products, arithmetic and copies ran while one was open for 28% -> 15% of each run, Pallas kernels for 4% -> 22%
where the time goes in v2:
time: 502 us; the launch traced here: 496 us
  waiting for transfers between devices  181 us (36%)
  Pallas kernels  136 us (27%)
  starting transfers between devices  90.5 us (18%)
  local copies, waits for them, and re-layouts  44.6 us (9%)
  other arithmetic  40.8 us (8%)
    pallas_call x12, Pallas kernels, run(): pl.pallas_call(kernel, grid=grid, in_specs=specs, out_specs=out_specs, ou...  136 us
    ppermute x27, waiting for transfers between devices, ring(): return lax.ppermute(array, 'dp', ring_pairs)  89.6 us
    ppermute x51, waiting for transfers between devices, swap(): return lax.ppermute(array, 'ctx', [(i, i ^ shift) for i in range(ctx)])  81.1 us
    ppermute x51, starting transfers between devices, swap(): return lax.ppermute(array, 'ctx', [(i, i ^ shift) for i in range(ctx)])  63.3 us
    ppermute x27, starting transfers between devices, ring(): return lax.ppermute(array, 'dp', ring_pairs)  22.2 us
    convert_element_type x15, other arithmetic, move(): self.sent = part.astype(bf16) if self.step < depth else part  21.2 us
  transfers between devices with their start and end apart: 103, of which 46 were waited for; matrix products, arithmetic and copies ran while one was open for 15% of the time, Pallas kernels for 22%

profile of v2, /device:TPU:0, one launch (start us, length us, event | category | flops | bytes accessed | tf_op | source)
XLA Modules:
  0.0 496.2 jit_solution(5175212826839048209)
XLA Ops:
  6.6 3.0 collective-permute-start
  22.5 4.5 collective-permute-done.3.refs_1_
  30.1 2.8 collective-permute-done.25
  32.9 2.6 collective-permute-done.4.refs_2_
  35.9 2.4 collective-permute-start.27
  38.4 5.0 collective-permute-done.27
  49.3 3.3 unpack.1
  56.5 10.8 %collective-permute-done.14.refs_10_ = bf16[256,1024]{1,0:T(8,128)(2,1)S(1)} collective-permute-done((bf16[256,1024]{1,0:T(8,128)(2,1)S(1)}, bf16[256,1024]{1,0:T(8,128)(2,1)S(1)}, u32[]{:S(2)}, u32[]{:S(2)}) %collective-permute-start.14) | collective-permute-done | bytes 524320 | tf_op jit(solution)/shard_map/ppermute | solution.py:828
  70.2 7.7 %norm_qkv.1 = (bf16[1024,768]{1,0:T(8,128)(2,1)}, bf16[1024,1024]{1,0:T(8,128)(2,1)}, bf16[1024,1152]{1,0:T(8,128)(2,1)}) custom-call(s32[12]{0:T(128)} %concatenate.58.scalars, f32[24,1024]{1,0:T(8,128)} %get-tuple-element.180.small_ref.by_column, bf16[128,1152]{1,0:T(8,128)(2,1)} %copy-done.8, bf16[128,1152]{1,0:T(8,128)(2,1)} %copy-done.21, ...), custom_call_target="tpu_custom_call" | custom-call | flops 1024 | bytes 1024 | tf_op jit(solution)/shard_map/norm_qkv/pallas_call | solution.py:83
  78.0 10.4 %attention_forward.1 = bf16[1024,256]{1,0:T(8,128)(2,1)} custom-call(bf16[1024,768]{1,0:T(8,128)(2,1)} %get-tuple-element.109.q_ref.k_ref.v_ref, bf16[1024,768]{1,0:T(8,128)(2,1)} %get-tuple-element.109.q_ref.k_ref.v_ref, bf16[1024,768]{1,0:T(8,128)(2,1)} %get-tuple-element.109.q_ref.k_ref.v_ref), custom_call_target="tpu_custom_call" | custom-call | flops 1024 | bytes 1024 | tf_op jit(solution)/shard_map/attention_forward/pallas_call | solution.py:83
  92.5 4.0 collective-permute-done.16.refs_1_.refs_5_
  101.5 2.4 collective-permute-done.18.refs_3_.refs_7_
  104.5 3.9 hidden.1
  110.1 2.1 collective-permute-start.32
  115.0 10.3 %collective-permute-done.31.refs_10_ = bf16[2,128,1024]{2,1,0:T(8,128)(2,1)} collective-permute-done((bf16[2,128,1024]{2,1,0:T(8,128)(2,1)S(1)}, bf16[2,128,1024]{2,1,0:T(8,128)(2,1)}, u32[]{:S(2)}, u32[]{:S(2)}) %collective-permute-start.31) | collective-permute-done | bytes 524320 | tf_op jit(solution)/shard_map/ppermute | solution.py:848
  125.8 10.6 %collective-permute-done.32.refs_10_ = bf16[2,128,1024]{2,1,0:T(8,128)(2,1)S(1)} collective-permute-done((bf16[2,128,1024]{2,1,0:T(8,128)(2,1)S(1)}, bf16[2,128,1024]{2,1,0:T(8,128)(2,1)S(1)}, u32[]{:S(2)}, u32[]{:S(2)}) %collective-permute-start.32) | collective-permute-done | bytes 524320 | tf_op jit(solution)/shard_map/ppermute | solution.py:848
  137.6 5.8 %collective-permute-done.33.refs_10_ = bf16[2,128,1024]{2,1,0:T(8,128)(2,1)S(1)} collective-permute-done((bf16[2,128,1024]{2,1,0:T(8,128)(2,1)S(1)}, bf16[2,128,1024]{2,1,0:T(8,128)(2,1)S(1)}, u32[]{:S(2)}, u32[]{:S(2)}) %collective-permute-start.33) | collective-permute-done | bytes 524320 | tf_op jit(solution)/shard_map/ppermute | solution.py:848
  147.8 12.4 %collective-permute-done.34.refs_11_ = bf16[2,128,1024]{2,1,0:T(8,128)(2,1)} collective-permute-done((bf16[2,128,1024]{2,1,0:T(8,128)(2,1)}, bf16[2,128,1024]{2,1,0:T(8,128)(2,1)}, u32[]{:S(2)}, u32[]{:S(2)}) %collective-permute-start.34) | collective-permute-done | bytes 524320 | tf_op jit(solution)/shard_map/ppermute | solution.py:848
  161.6 2.7 maximum_convert_fusion.1
  166.3 4.6 collective-permute-done.20.refs_2_
  171.7 24.6 %mlp.3 = (f32[1024,1024]{1,0:T(8,128)}, f32[1024,1024]{1,0:T(8,128)}, f32[1024,1]{1,0:T(8,128)}, f32[1,1024]{1,0:T(1,128)}, bf16[4,2,128,1024]{3,2,1,0:T(8,128)(2,1)}, /*index=5*/bf16[4,2,128,1024]{3,2,1,0:T(8,128)(2,1)}) custom-call(s32[12]{0:T(128)} %concatenate.55.scalars, bf16[1024,128]{1,0:T(8,128)(2,1)} %get-tuple-element.106.small_ref.by_row, ...), custom_call_target="tpu_custom_call" | custom-call | flops 1024 | bytes 1024 | tf_op jit(solution)/shard_map/mlp/pallas_call | solution.py:83
  197.4 15.0 %collective-permute-done.40.refs_11_ = bf16[2,128,1024]{2,1,0:T(8,128)(2,1)S(1)} collective-permute-done((bf16[2,128,1024]{2,1,0:T(8,128)(2,1)S(1)}, bf16[2,128,1024]{2,1,0:T(8,128)(2,1)S(1)}, u32[]{:S(2)}, u32[]{:S(2)}) %collective-permute-start.40) | collective-permute-done | bytes 524320 | tf_op jit(solution)/shard_map/ppermute | solution.py:848
  215.2 18.6 %mlp.4 = (f32[640,1024]{1,0:T(8,128)}, f32[640,1024]{1,0:T(8,128)}, f32[640,1]{1,0:T(8,128)}, f32[1,1024]{1,0:T(1,128)}, bf16[4,2,128,1024]{3,2,1,0:T(8,128)(2,1)}, /*index=5*/bf16[4,2,128,1024]{3,2,1,0:T(8,128)(2,1)}) custom-call(s32[12]{0:T(128)} %concatenate.55.scalars, bf16[1024,128]{1,0:T(8,128)(2,1)} %get-tuple-element.106.small_ref.by_row, ...), custom_call_target="tpu_custom_call" | custom-call | flops 1024 | bytes 1024 | tf_op jit(solution)/shard_map/mlp/pallas_call | solution.py:83
  241.7 23.0 %mlp.5 = (bf16[256,1024]{1,0:T(8,128)(2,1)}, bf16[256,1024]{1,0:T(8,128)(2,1)}, bf16[256,1024]{1,0:T(8,128)(2,1)}, bf16[256,1024]{1,0:T(8,128)(2,1)}, bf16[256,1...) custom-call(s32[12]{0:T(128)} %concatenate.55.scalars, ...), custom_call_target="tpu_custom_call" | custom-call | flops 1024 | bytes 1024 | tf_op jit(solution)/shard_map/mlp/pallas_call | solution.py:83
  267.7 2.4 collective-permute-start.55
  271.5 9.6 %collective-permute-done.45 = bf16[2,128,1024]{2,1,0:T(8,128)(2,1)} collective-permute-done((bf16[2,128,1024]{2,1,0:T(8,128)(2,1)S(1)}, bf16[2,128,1024]{2,1,0:T(8,128)(2,1)}, u32[]{:S(2)}, u32[]{:S(2)}) %collective-permute-start.45) | collective-permute-done | bytes 524320 | tf_op jit(solution)/shard_map/ppermute | solution.py:848
  281.3 2.4 fusion.8
  286.8 8.7 %collective-permute-done.55.refs_3_ = bf16[256,1152]{1,0:T(8,128)(2,1)S(1)} collective-permute-done((bf16[256,1152]{1,0:T(8,128)(2,1)}, bf16[256,1152]{1,0:T(8,128)(2,1)S(1)}, u32[]{:S(2)}, u32[]{:S(2)}) %collective-permute-start.55) | collective-permute-done | bytes 589856 | tf_op jit(solution)/shard_map/ppermute | solution.py:828
  296.3 10.3 %middle.1 = (f32[256,1024]{1,0:T(8,128)}, f32[256,1024]{1,0:T(8,128)}, bf16[1024,1024]{1,0:T(8,128)(2,1)}, f32[8,1024]{1,0:T(8,128)}, f32[1024,128]{1,0:T(8,128)...) custom-call(s32[4]{0:T(128)} %pad_add_fusion.scalars, ...), custom_call_target="tpu_custom_call" | custom-call | flops 1024 | bytes 1024 | tf_op jit(solution)/shard_map/middle/pallas_call | solution.py:83
  306.6 2.6 collective-permute-done.60
  314.3 2.4 fusion.7
  320.3 18.5 %attention_backward.1 = (bf16[1024,256]{1,0:T(8,128)(2,1)}, bf16[1024,256]{1,0:T(8,128)(2,1)}, bf16[1024,256]{1,0:T(8,128)(2,1)}) custom-call(s32[4]{0:T(128)} %pad_add_fusion.scalars, bf16[1024,768]{1,0:T(8,128)(2,1)} %get-tuple-element.109.q_ref.k_ref.v_ref, bf16[1024,768]{1,0:T(8,128)(2,1)} %get-tuple-element.109.q_ref.k_ref.v_ref, ...), custom_call_target="tpu_custom_call" | custom-call | flops 1024 | bytes 1024 | tf_op jit(solution)/shard_map/attention_backward/pallas_call | solution.py:83
  338.8 2.1 fusion.4
  340.9 8.1 %qkv_back.1 = (bf16[256,1024]{1,0:T(8,128)(2,1)}, bf16[256,1024]{1,0:T(8,128)(2,1)}, bf16[256,1024]{1,0:T(8,128)(2,1)}, bf16[256,1024]{1,0:T(8,128)(2,1)}, bf16[...) custom-call(s32[12]{0:T(128)} %concatenate.58.scalars, ...), custom_call_target="tpu_custom_call" | custom-call | flops 1024 | bytes 1024 | tf_op jit(solution)/shard_map/qkv_back/pallas_call | solution.py:83
  349.0 2.3 fusion.6
  364.1 3.6 result.1
  372.8 10.7 %collective-permute-done.95 = bf16[32,1024]{1,0:T(8,128)(2,1)S(1)} collective-permute-done((bf16[32,1024]{1,0:T(8,128)(2,1)S(1)}, bf16[32,1024]{1,0:T(8,128)(2,1)S(1)}, u32[]{:S(2)}, u32[]{:S(2)}) %collective-permute-start.95) | collective-permute-done | bytes 65568 | tf_op jit(solution)/shard_map/ppermute | solution.py:828
  384.5 3.3 collective-permute-done.96
  389.7 3.3 collective-permute-done.97
  399.5 4.8 collective-permute-done.69.refs_2_
  405.1 4.0 final.1
  422.1 2.4 fusion.3
  437.0 6.9 %collective-permute-done.91 = bf16[32,1024]{1,0:T(8,128)(2,1)S(1)} collective-permute-done((bf16[32,1024]{1,0:T(8,128)(2,1)S(1)}, bf16[32,1024]{1,0:T(8,128)(2,1)S(1)}, u32[]{:S(2)}, u32[]{:S(2)}) %collective-permute-start.91) | collective-permute-done | bytes 65568 | tf_op jit(solution)/shard_map/ppermute | solution.py:828
  444.9 3.3 collective-permute-done.92
  449.2 4.1 collective-permute-done.93
  459.8 10.2 %collective-permute-done.79 = bf16[128,768]{1,0:T(8,128)(2,1)S(1)} collective-permute-done((bf16[128,768]{1,0:T(8,128)(2,1)S(1)}, bf16[128,768]{1,0:T(8,128)(2,1)S(1)}, u32[]{:S(2)}, u32[]{:S(2)}) %collective-permute-start.79) | collective-permute-done | bytes 196640 | tf_op jit(solution)/shard_map/ppermute | solution.py:848
  480.3 2.7 collective-permute-done.88
  492.3 3.0 collective-permute-done.90
  (514 shorter events, 168.9 us)
Async XLA Ops:
  11.1 43.6 %collective-permute-start.13 = (bf16[256,1024]{1,0:T(8,128)(2,1)S(1)}, bf16[256,1024]{1,0:T(8,128)(2,1)S(1)}, u32[]{:S(2)}, u32[]{:S(2)}) collective-permute-start(bf16[256,1024]{1,0:T(8,128)(2,1)S(1)} %bitcast.368), channel_id=1, source_target_pairs={{0,1},{1,0},{2,3},{3,2},{4,5},{5,4},{6,7},{7,6},{8,9},{9,8},{10,11... | collective-permute-start | bytes 1572872 | tf_op jit(solution)/shard_map/ppermute | solution.py:828
  28.6 16.3 %collective-permute-start.6 = (bf16[128,1152]{1,0:T(8,128)(2,1)S(1)}, bf16[128,1152]{1,0:T(8,128)(2,1)S(1)}, u32[]{:S(2)}, u32[]{:S(2)}) collective-permute-start(bf16[128,1152]{1,0:T(8,128)(2,1)S(1)} %pad_maximum_fusion.4.refs_0_), channel_id=1, source_target_pairs={{0,4},{4,0},{8,12},{12,8},{16,20},{20,16},{24,28},{28,24},{1,5},{5... | collective-permute-start | bytes 884744 | tf_op jit(solution)/shard_map/ppermute | solution.py:851
  43.4 23.9 %collective-permute-start.14 = (bf16[256,1024]{1,0:T(8,128)(2,1)S(1)}, bf16[256,1024]{1,0:T(8,128)(2,1)S(1)}, u32[]{:S(2)}, u32[]{:S(2)}) collective-permute-start(bf16[256,1024]{1,0:T(8,128)(2,1)S(1)} %bitcast.369), channel_id=1, source_target_pairs={{0,2},{1,3},{2,0},{3,1},{4,6},{5,7},{6,4},{7,5},{8,10},{9,11},{10,... | collective-permute-start | bytes 1572872 | tf_op jit(solution)/shard_map/ppermute | solution.py:828
  44.9 23.9 %collective-permute-start.15 = (bf16[256,1024]{1,0:T(8,128)(2,1)S(1)}, bf16[256,1024]{1,0:T(8,128)(2,1)S(1)}, u32[]{:S(2)}, u32[]{:S(2)}) collective-permute-start(bf16[256,1024]{1,0:T(8,128)(2,1)S(1)} %bitcast.370), channel_id=1, source_target_pairs={{0,3},{1,2},{2,1},{3,0},{4,7},{5,6},{6,5},{7,4},{8,11},{9,10},{10,... | collective-permute-start | bytes 1572872 | tf_op jit(solution)/shard_map/ppermute | solution.py:828
  52.6 37.5 %collective-permute-start.10 = (bf16[256,1024]{1,0:T(8,128)(2,1)}, bf16[256,1024]{1,0:T(8,128)(2,1)S(1)}, u32[]{:S(2)}, u32[]{:S(2)}) collective-permute-start(bf16[256,1024]{1,0:T(8,128)(2,1)} %get-tuple-element.108), channel_id=1, source_target_pairs={{0,1},{1,0},{2,3},{3,2},{4,5},{5,4},{6,7},{7,6},{8,9},{9,8},{10,11... | collective-permute-start | bytes 1572872 | tf_op jit(solution)/shard_map/ppermute | solution.py:828
  53.4 55.0 %collective-permute-start.28 = (bf16[2,128,1024]{2,1,0:T(8,128)(2,1)S(1)}, bf16[2,128,1024]{2,1,0:T(8,128)(2,1)S(1)}, u32[]{:S(2)}, u32[]{:S(2)}) collective-permute-start(bf16[2,128,1024]{2,1,0:T(8,128)(2,1)S(1)} %pad_maximum_fusion.1.refs_8_), channel_id=1, source_target_pairs={{0,8},{4,12},{8,16},{12,20},{16,24},{20,28},{24,0},{28,4},{1,9},{5... | collective-permute-start | bytes 1572872 | tf_op jit(solution)/shard_map/ppermute | solution.py:848
  54.8 53.7 %collective-permute-start.29 = (bf16[2,128,1024]{2,1,0:T(8,128)(2,1)S(1)}, bf16[2,128,1024]{2,1,0:T(8,128)(2,1)S(1)}, u32[]{:S(2)}, u32[]{:S(2)}) collective-permute-start(bf16[2,128,1024]{2,1,0:T(8,128)(2,1)S(1)} %get-tuple-element.114.refs_8_), channel_id=1, source_target_pairs={{0,8},{4,12},{8,16},{12,20},{16,24},{20,28},{24,0},{28,4},{1,9},{5... | collective-permute-start | bytes 1572872 | tf_op jit(solution)/shard_map/ppermute | solution.py:848
  67.3 24.2 %collective-permute-start.11 = (bf16[256,1024]{1,0:T(8,128)(2,1)S(1)}, bf16[256,1024]{1,0:T(8,128)(2,1)S(1)}, u32[]{:S(2)}, u32[]{:S(2)}) collective-permute-start(bf16[256,1024]{1,0:T(8,128)(2,1)S(1)} %copy-done.63), channel_id=1, source_target_pairs={{0,2},{1,3},{2,0},{3,1},{4,6},{5,7},{6,4},{7,5},{8,10},{9,11},{10,... | collective-permute-start | bytes 1572872 | tf_op jit(solution)/shard_map/ppermute | solution.py:828
  68.8 29.2 %collective-permute-start.12 = (bf16[256,1024]{1,0:T(8,128)(2,1)S(1)}, bf16[256,1024]{1,0:T(8,128)(2,1)S(1)}, u32[]{:S(2)}, u32[]{:S(2)}) collective-permute-start(bf16[256,1024]{1,0:T(8,128)(2,1)S(1)} %copy-done.63), channel_id=1, source_target_pairs={{0,3},{1,2},{2,1},{3,0},{4,7},{5,6},{6,5},{7,4},{8,11},{9,10},{10,... | collective-permute-start | bytes 1572872 | tf_op jit(solution)/shard_map/ppermute | solution.py:828
  90.1 18.4 %collective-permute-start.30 = (bf16[2,128,1024]{2,1,0:T(8,128)(2,1)S(1)}, bf16[2,128,1024]{2,1,0:T(8,128)(2,1)S(1)}, u32[]{:S(2)}, u32[]{:S(2)}) collective-permute-start(bf16[2,128,1024]{2,1,0:T(8,128)(2,1)S(1)} %get-tuple-element.115.refs_8_), channel_id=1, source_target_pairs={{0,8},{4,12},{8,16},{12,20},{16,24},{20,28},{24,0},{28,4},{1,9},{5... | collective-permute-start | bytes 1572872 | tf_op jit(solution)/shard_map/ppermute | solution.py:848
  108.5 16.8 %collective-permute-start.31 = (bf16[2,128,1024]{2,1,0:T(8,128)(2,1)S(1)}, bf16[2,128,1024]{2,1,0:T(8,128)(2,1)}, u32[]{:S(2)}, u32[]{:S(2)}) collective-permute-start(bf16[2,128,1024]{2,1,0:T(8,128)(2,1)S(1)} %collective-permute-done.28.refs_9_), channel_id=1, source_target_pairs={{0,8},{4,12},{8,16},{12,20},{16,24},{20,28},{24,0},{28,4},{1,9},{5... | collective-permute-start | bytes 1572872 | tf_op jit(solution)/shard_map/ppermute | solution.py:848
  110.1 26.3 %collective-permute-start.32 = (bf16[2,128,1024]{2,1,0:T(8,128)(2,1)S(1)}, bf16[2,128,1024]{2,1,0:T(8,128)(2,1)S(1)}, u32[]{:S(2)}, u32[]{:S(2)}) collective-permute-start(bf16[2,128,1024]{2,1,0:T(8,128)(2,1)S(1)} %collective-permute-done.29.refs_9_), channel_id=1, source_target_pairs={{0,8},{4,12},{8,16},{12,20},{16,24},{20,28},{24,0},{28,4},{1,9},{5... | collective-permute-start | bytes 1572872 | tf_op jit(solution)/shard_map/ppermute | solution.py:848
  112.2 31.1 %collective-permute-start.33 = (bf16[2,128,1024]{2,1,0:T(8,128)(2,1)S(1)}, bf16[2,128,1024]{2,1,0:T(8,128)(2,1)S(1)}, u32[]{:S(2)}, u32[]{:S(2)}) collective-permute-start(bf16[2,128,1024]{2,1,0:T(8,128)(2,1)S(1)} %collective-permute-done.30.refs_9_), channel_id=1, source_target_pairs={{0,8},{4,12},{8,16},{12,20},{16,24},{20,28},{24,0},{28,4},{1,9},{5... | collective-permute-start | bytes 1572872 | tf_op jit(solution)/shard_map/ppermute | solution.py:848
  113.1 30.2 %collective-permute-start.35 = (bf16[2,128,1024]{2,1,0:T(8,128)(2,1)S(1)}, bf16[2,128,1024]{2,1,0:T(8,128)(2,1)S(1)}, u32[]{:S(2)}, u32[]{:S(2)}) collective-permute-start(bf16[2,128,1024]{2,1,0:T(8,128)(2,1)S(1)} %pad_maximum_fusion.1.refs_8_), channel_id=1, source_target_pairs={{0,4},{4,0},{8,12},{12,8},{16,20},{20,16},{24,28},{28,24},{1,5},{5... | collective-permute-start | bytes 1572872 | tf_op jit(solution)/shard_map/ppermute | solution.py:851
  113.5 30.4 %collective-permute-start.22 = (bf16[256,1024]{1,0:T(8,128)(2,1)S(1)}, bf16[256,1024]{1,0:T(8,128)(2,1)S(1)}, u32[]{:S(2)}, u32[]{:S(2)}) collective-permute-start(bf16[256,1024]{1,0:T(8,128)(2,1)S(1)} %convolution_convert_fusion.refs_4_), channel_id=1, source_target_pairs={{0,1},{1,0},{2,3},{3,2},{4,5},{5,4},{6,7},{7,6},{8,9},{9,8},{10,11... | collective-permute-start | bytes 1572872 | tf_op jit(solution)/shard_map/ppermute | solution.py:828
  125.3 20.1 %collective-permute-start.23 = (bf16[256,1024]{1,0:T(8,128)(2,1)S(1)}, bf16[256,1024]{1,0:T(8,128)(2,1)S(1)}, u32[]{:S(2)}, u32[]{:S(2)}) collective-permute-start(bf16[256,1024]{1,0:T(8,128)(2,1)S(1)} %convolution_convert_fusion.refs_4_), channel_id=1, source_target_pairs={{0,2},{1,3},{2,0},{3,1},{4,6},{5,7},{6,4},{7,5},{8,10},{9,11},{10,... | collective-permute-start | bytes 1572872 | tf_op jit(solution)/shard_map/ppermute | solution.py:828
  143.4 16.8 %collective-permute-start.34 = (bf16[2,128,1024]{2,1,0:T(8,128)(2,1)}, bf16[2,128,1024]{2,1,0:T(8,128)(2,1)}, u32[]{:S(2)}, u32[]{:S(2)}) collective-permute-start(bf16[2,128,1024]{2,1,0:T(8,128)(2,1)} %collective-permute-done.31.refs_10_), channel_id=1, source_target_pairs={{0,8},{4,12},{8,16},{12,20},{16,24},{20,28},{24,0},{28,4},{1,9},{5... | collective-permute-start | bytes 1572872 | tf_op jit(solution)/shard_map/ppermute | solution.py:848
  143.9 22.4 %collective-permute-start.19 = (bf16[256,1024]{1,0:T(8,128)(2,1)}, bf16[256,1024]{1,0:T(8,128)(2,1)S(1)}, u32[]{:S(2)}, u32[]{:S(2)}) collective-permute-start(bf16[256,1024]{1,0:T(8,128)(2,1)} %get-tuple-element.110.refs_0_), channel_id=1, source_target_pairs={{0,1},{1,0},{2,3},{3,2},{4,5},{5,4},{6,7},{7,6},{8,9},{9,8},{10,11... | collective-permute-start | bytes 1572872 | tf_op jit(solution)/shard_map/ppermute | solution.py:828
  145.4 25.4 %collective-permute-start.20 = (bf16[256,1024]{1,0:T(8,128)(2,1)}, bf16[256,1024]{1,0:T(8,128)(2,1)S(1)}, u32[]{:S(2)}, u32[]{:S(2)}) collective-permute-start(bf16[256,1024]{1,0:T(8,128)(2,1)} %get-tuple-element.110.refs_0_), channel_id=1, source_target_pairs={{0,2},{1,3},{2,0},{3,1},{4,6},{5,7},{6,4},{7,5},{8,10},{9,11},{10,... | collective-permute-start | bytes 1572872 | tf_op jit(solution)/shard_map/ppermute | solution.py:828
  146.5 24.3 %collective-permute-start.21 = (bf16[256,1024]{1,0:T(8,128)(2,1)}, bf16[256,1024]{1,0:T(8,128)(2,1)}, u32[]{:S(2)}, u32[]{:S(2)}) collective-permute-start(bf16[256,1024]{1,0:T(8,128)(2,1)} %get-tuple-element.110.refs_0_), channel_id=1, source_target_pairs={{0,3},{1,2},{2,1},{3,0},{4,7},{5,6},{6,5},{7,4},{8,11},{9,10},{10,... | collective-permute-start | bytes 1572872 | tf_op jit(solution)/shard_map/ppermute | solution.py:828
  147.7 23.2 %collective-permute-start.37 = (bf16[2,128,1024]{2,1,0:T(8,128)(2,1)}, bf16[2,128,1024]{2,1,0:T(8,128)(2,1)}, u32[]{:S(2)}, u32[]{:S(2)}) collective-permute-start(bf16[2,128,1024]{2,1,0:T(8,128)(2,1)} %collective-permute-done.31.refs_10_), channel_id=1, source_target_pairs={{0,4},{4,0},{8,12},{12,8},{16,20},{20,16},{24,28},{28,24},{1,5},{5... | collective-permute-start | bytes 1572872 | tf_op jit(solution)/shard_map/ppermute | solution.py:851
  196.2 38.6 %collective-permute-start.39 = (bf16[4,2,128,1024]{3,2,1,0:T(8,128)(2,1)}, bf16[4,2,128,1024]{3,2,1,0:T(8,128)(2,1)S(1)}, u32[]{:S(2)}, u32[]{:S(2)}) collective-permute-start(bf16[4,2,128,1024]{3,2,1,0:T(8,128)(2,1)} %get-tuple-element.121), channel_id=1, source_target_pairs={{0,4},{4,0},{8,12},{12,8},{16,20},{20,16},{24,28},{28,24},{1,5},{5... | collective-permute-start | bytes 6291464 | tf_op jit(solution)/shard_map/ppermute | solution.py:851
  196.3 16.1 %collective-permute-start.40 = (bf16[2,128,1024]{2,1,0:T(8,128)(2,1)S(1)}, bf16[2,128,1024]{2,1,0:T(8,128)(2,1)S(1)}, u32[]{:S(2)}, u32[]{:S(2)}) collective-permute-start(bf16[2,128,1024]{2,1,0:T(8,128)(2,1)S(1)} %copy-done.46), channel_id=1, source_target_pairs={{0,8},{4,12},{8,16},{12,20},{16,24},{20,28},{24,0},{28,4},{1,9},{5... | collective-permute-start | bytes 1572872 | tf_op jit(solution)/shard_map/ppermute | solution.py:848
  212.5 22.0 %collective-permute-start.47 = (bf16[2,128,1024]{2,1,0:T(8,128)(2,1)S(1)}, bf16[2,128,1024]{2,1,0:T(8,128)(2,1)S(1)}, u32[]{:S(2)}, u32[]{:S(2)}) collective-permute-start(bf16[2,128,1024]{2,1,0:T(8,128)(2,1)S(1)} %copy-done.43), channel_id=1, source_target_pairs={{0,8},{4,12},{8,16},{12,20},{16,24},{20,28},{24,0},{28,4},{1,9},{5... | collective-permute-start | bytes 1572872 | tf_op jit(solution)/shard_map/ppermute | solution.py:848
  233.7 32.8 %collective-permute-start.46 = (bf16[4,2,128,1024]{3,2,1,0:T(8,128)(2,1)}, bf16[4,2,128,1024]{3,2,1,0:T(8,128)(2,1)}, u32[]{:S(2)}, u32[]{:S(2)}) collective-permute-start(bf16[4,2,128,1024]{3,2,1,0:T(8,128)(2,1)} %get-tuple-element.128), channel_id=1, source_target_pairs={{0,4},{4,0},{8,12},{12,8},{16,20},{20,16},{24,28},{28,24},{1,5},{5... | collective-permute-start | bytes 6291464 | tf_op jit(solution)/shard_map/ppermute | solution.py:851
  264.7 19.0 %collective-permute-start.52 = (bf16[4,2,128,1024]{3,2,1,0:T(8,128)(2,1)}, bf16[4,2,128,1024]{3,2,1,0:T(8,128)(2,1)}, u32[]{:S(2)}, u32[]{:S(2)}) collective-permute-start(bf16[4,2,128,1024]{3,2,1,0:T(8,128)(2,1)} %get-tuple-element.141), channel_id=1, source_target_pairs={{0,4},{4,0},{8,12},{12,8},{16,20},{20,16},{24,28},{28,24},{1,5},{5... | collective-permute-start | bytes 6291464 | tf_op jit(solution)/shard_map/ppermute | solution.py:851
  265.0 16.1 %collective-permute-start.45 = (bf16[2,128,1024]{2,1,0:T(8,128)(2,1)S(1)}, bf16[2,128,1024]{2,1,0:T(8,128)(2,1)}, u32[]{:S(2)}, u32[]{:S(2)}) collective-permute-start(bf16[2,128,1024]{2,1,0:T(8,128)(2,1)S(1)} %fusion.9), channel_id=1, source_target_pairs={{0,8},{4,12},{8,16},{12,20},{16,24},{20,28},{24,0},{28,4},{1,9},{5... | collective-permute-start | bytes 1572872 | tf_op jit(solution)/shard_map/ppermute | solution.py:848
  266.5 18.5 %collective-permute-start.53 = (bf16[256,1152]{1,0:T(8,128)(2,1)}, bf16[256,1152]{1,0:T(8,128)(2,1)S(1)}, u32[]{:S(2)}, u32[]{:S(2)}) collective-permute-start(bf16[256,1152]{1,0:T(8,128)(2,1)} %get-tuple-element.147), channel_id=1, source_target_pairs={{0,1},{1,0},{2,3},{3,2},{4,5},{5,4},{6,7},{7,6},{8,9},{9,8},{10,11... | collective-permute-start | bytes 1769480 | tf_op jit(solution)/shard_map/ppermute | solution.py:828
  266.8 20.0 %collective-permute-start.54 = (bf16[256,1152]{1,0:T(8,128)(2,1)}, bf16[256,1152]{1,0:T(8,128)(2,1)S(1)}, u32[]{:S(2)}, u32[]{:S(2)}) collective-permute-start(bf16[256,1152]{1,0:T(8,128)(2,1)} %get-tuple-element.148), channel_id=1, source_target_pairs={{0,2},{1,3},{2,0},{3,1},{4,6},{5,7},{6,4},{7,5},{8,10},{9,11},{10,... | collective-permute-start | bytes 1769480 | tf_op jit(solution)/shard_map/ppermute | solution.py:828
  267.7 27.8 %collective-permute-start.55 = (bf16[256,1152]{1,0:T(8,128)(2,1)}, bf16[256,1152]{1,0:T(8,128)(2,1)S(1)}, u32[]{:S(2)}, u32[]{:S(2)}) collective-permute-start(bf16[256,1152]{1,0:T(8,128)(2,1)} %get-tuple-element.149), channel_id=1, source_target_pairs={{0,3},{1,2},{2,1},{3,0},{4,7},{5,6},{6,5},{7,4},{8,11},{9,10},{10,... | collective-permute-start | bytes 1769480 | tf_op jit(solution)/shard_map/ppermute | solution.py:828
  281.2 25.5 %collective-permute-start.62 = (bf16[2,128,1024]{2,1,0:T(8,128)(2,1)S(1)}, bf16[2,128,1024]{2,1,0:T(8,128)(2,1)}, u32[]{:S(2)}, u32[]{:S(2)}) collective-permute-start(bf16[2,128,1024]{2,1,0:T(8,128)(2,1)S(1)} %fusion.10), channel_id=1, source_target_pairs={{0,8},{4,12},{8,16},{12,20},{16,24},{20,28},{24,0},{28,4},{1,9},{5... | collective-permute-start | bytes 1572872 | tf_op jit(solution)/shard_map/ppermute | solution.py:848
  283.8 25.5 %collective-permute-start.60 = (bf16[2,128,1024]{2,1,0:T(8,128)(2,1)}, bf16[2,128,1024]{2,1,0:T(8,128)(2,1)}, u32[]{:S(2)}, u32[]{:S(2)}) collective-permute-start(bf16[2,128,1024]{2,1,0:T(8,128)(2,1)} %fusion.8), channel_id=1, source_target_pairs={{0,8},{4,12},{8,16},{12,20},{16,24},{20,28},{24,0},{28,4},{1,9},{5... | collective-permute-start | bytes 1572872 | tf_op jit(solution)/shard_map/ppermute | solution.py:848
  285.1 53.7 %collective-permute-start.64 = (bf16[2,128,1024]{2,1,0:T(8,128)(2,1)S(1)}, bf16[2,128,1024]{2,1,0:T(8,128)(2,1)S(1)}, u32[]{:S(2)}, u32[]{:S(2)}) collective-permute-start(bf16[2,128,1024]{2,1,0:T(8,128)(2,1)S(1)} %fusion.11), channel_id=1, source_target_pairs={{0,8},{4,12},{8,16},{12,20},{16,24},{20,28},{24,0},{28,4},{1,9},{5... | collective-permute-start | bytes 1572872 | tf_op jit(solution)/shard_map/ppermute | solution.py:848
  314.3 34.7 %collective-permute-start.63 = (bf16[2,128,1024]{2,1,0:T(8,128)(2,1)S(1)}, bf16[2,128,1024]{2,1,0:T(8,128)(2,1)S(1)}, u32[]{:S(2)}, u32[]{:S(2)}) collective-permute-start(bf16[2,128,1024]{2,1,0:T(8,128)(2,1)S(1)} %fusion.5), channel_id=1, source_target_pairs={{0,8},{4,12},{8,16},{12,20},{16,24},{20,28},{24,0},{28,4},{1,9},{5... | collective-permute-start | bytes 1572872 | tf_op jit(solution)/shard_map/ppermute | solution.py:848
  316.8 43.8 %collective-permute-start.59 = (bf16[256,1024]{1,0:T(8,128)(2,1)}, bf16[256,1024]{1,0:T(8,128)(2,1)}, u32[]{:S(2)}, u32[]{:S(2)}) collective-permute-start(bf16[256,1024]{1,0:T(8,128)(2,1)} %get-tuple-element.159), channel_id=1, source_target_pairs={{0,3},{1,2},{2,1},{3,0},{4,7},{5,6},{6,5},{7,4},{8,11},{9,10},{10,... | collective-permute-start | bytes 1572872 | tf_op jit(solution)/shard_map/ppermute | solution.py:828
  317.3 44.7 %collective-permute-start.58 = (bf16[256,1024]{1,0:T(8,128)(2,1)}, bf16[256,1024]{1,0:T(8,128)(2,1)}, u32[]{:S(2)}, u32[]{:S(2)}) collective-permute-start(bf16[256,1024]{1,0:T(8,128)(2,1)} %get-tuple-element.157), channel_id=1, source_target_pairs={{0,2},{1,3},{2,0},{3,1},{4,6},{5,7},{6,4},{7,5},{8,10},{9,11},{10,... | collective-permute-start | bytes 1572872 | tf_op jit(solution)/shard_map/ppermute | solution.py:828
  318.4 45.7 %collective-permute-start.57 = (bf16[256,1024]{1,0:T(8,128)(2,1)}, bf16[256,1024]{1,0:T(8,128)(2,1)}, u32[]{:S(2)}, u32[]{:S(2)}) collective-permute-start(bf16[256,1024]{1,0:T(8,128)(2,1)} %get-tuple-element.155), channel_id=1, source_target_pairs={{0,1},{1,0},{2,3},{3,2},{4,5},{5,4},{6,7},{7,6},{8,9},{9,8},{10,11... | collective-permute-start | bytes 1572872 | tf_op jit(solution)/shard_map/ppermute | solution.py:828
  351.3 16.5 %collective-permute-start.94 = (bf16[2,128,1024]{2,1,0:T(8,128)(2,1)}, bf16[2,128,1024]{2,1,0:T(8,128)(2,1)}, u32[]{:S(2)}, u32[]{:S(2)}) collective-permute-start(bf16[2,128,1024]{2,1,0:T(8,128)(2,1)} %fusion.6), channel_id=1, source_target_pairs={{0,8},{4,12},{8,16},{12,20},{16,24},{20,28},{24,0},{28,4},{1,9},{5... | collective-permute-start | bytes 1572872 | tf_op jit(solution)/shard_map/ppermute | solution.py:848
  360.5 36.7 %collective-permute-start.61 = (bf16[2,128,1024]{2,1,0:T(8,128)(2,1)}, bf16[2,128,1024]{2,1,0:T(8,128)(2,1)S(1)}, u32[]{:S(2)}, u32[]{:S(2)}) collective-permute-start(bf16[2,128,1024]{2,1,0:T(8,128)(2,1)} %fusion.7), channel_id=1, source_target_pairs={{0,8},{4,12},{8,16},{12,20},{16,24},{20,28},{24,0},{28,4},{1,9},{5... | collective-permute-start | bytes 1572872 | tf_op jit(solution)/shard_map/ppermute | solution.py:848
  362.0 55.5 %collective-permute-start.98 = (bf16[2,128,1024]{2,1,0:T(8,128)(2,1)}, bf16[2,128,1024]{2,1,0:T(8,128)(2,1)}, u32[]{:S(2)}, u32[]{:S(2)}) collective-permute-start(bf16[2,128,1024]{2,1,0:T(8,128)(2,1)} %fusion.4), channel_id=1, source_target_pairs={{0,8},{4,12},{8,16},{12,20},{16,24},{20,28},{24,0},{28,4},{1,9},{5... | collective-permute-start | bytes 1572872 | tf_op jit(solution)/shard_map/ppermute | solution.py:848
  364.1 29.9 %collective-permute-start.67 = (bf16[4,128,768]{2,1,0:T(8,128)(2,1)}, bf16[4,128,768]{2,1,0:T(8,128)(2,1)S(1)}, u32[]{:S(2)}, u32[]{:S(2)}) collective-permute-start(bf16[4,128,768]{2,1,0:T(8,128)(2,1)} %get-tuple-element.177), channel_id=1, source_target_pairs={{0,4},{4,0},{8,12},{12,8},{16,20},{20,16},{24,28},{28,24},{1,5},{5... | collective-permute-start | bytes 2359304 | tf_op jit(solution)/shard_map/ppermute | solution.py:851
  367.7 31.8 %collective-permute-start.68 = (bf16[256,1024]{1,0:T(8,128)(2,1)S(1)}, bf16[256,1024]{1,0:T(8,128)(2,1)S(1)}, u32[]{:S(2)}, u32[]{:S(2)}) collective-permute-start(bf16[256,1024]{1,0:T(8,128)(2,1)S(1)} %copy-done.79), channel_id=1, source_target_pairs={{0,1},{1,0},{2,3},{3,2},{4,5},{5,4},{6,7},{7,6},{8,9},{9,8},{10,11... | collective-permute-start | bytes 1572872 | tf_op jit(solution)/shard_map/ppermute | solution.py:828
  394.1 63.8 %collective-permute-start.84 = (bf16[256,1024]{1,0:T(8,128)(2,1)}, bf16[256,1024]{1,0:T(8,128)(2,1)}, u32[]{:S(2)}, u32[]{:S(2)}) collective-permute-start(bf16[256,1024]{1,0:T(8,128)(2,1)} %get-tuple-element.281), channel_id=1, source_target_pairs={{0,1},{1,0},{2,3},{3,2},{4,5},{5,4},{6,7},{7,6},{8,9},{9,8},{10,11... | collective-permute-start | bytes 1572872 | tf_op jit(solution)/shard_map/ppermute | solution.py:828
  417.5 40.4 %collective-permute-start.85 = (bf16[256,1024]{1,0:T(8,128)(2,1)}, bf16[256,1024]{1,0:T(8,128)(2,1)}, u32[]{:S(2)}, u32[]{:S(2)}) collective-permute-start(bf16[256,1024]{1,0:T(8,128)(2,1)} %get-tuple-element.283), channel_id=1, source_target_pairs={{0,2},{1,3},{2,0},{3,1},{4,6},{5,7},{6,4},{7,5},{8,10},{9,11},{10,... | collective-permute-start | bytes 1572872 | tf_op jit(solution)/shard_map/ppermute | solution.py:828
  428.2 29.7 %collective-permute-start.86 = (bf16[256,1024]{1,0:T(8,128)(2,1)}, bf16[256,1024]{1,0:T(8,128)(2,1)}, u32[]{:S(2)}, u32[]{:S(2)}) collective-permute-start(bf16[256,1024]{1,0:T(8,128)(2,1)} %get-tuple-element.282), channel_id=1, source_target_pairs={{0,3},{1,2},{2,1},{3,0},{4,7},{5,6},{6,5},{7,4},{8,11},{9,10},{10,... | collective-permute-start | bytes 1572872 | tf_op jit(solution)/shard_map/ppermute | solution.py:828
  430.1 25.6 %collective-permute-start.78 = (bf16[128,768]{1,0:T(8,128)(2,1)}, bf16[128,768]{1,0:T(8,128)(2,1)}, u32[]{:S(2)}, u32[]{:S(2)}) collective-permute-start(bf16[128,768]{1,0:T(8,128)(2,1)} %fusion.16), channel_id=1, source_target_pairs={{0,8},{4,12},{8,16},{12,20},{16,24},{20,28},{24,0},{28,4},{1,9},{5... | collective-permute-start | bytes 589832 | tf_op jit(solution)/shard_map/ppermute | solution.py:848
  453.3 17.8 %collective-permute-start.99 = (bf16[2,128,1024]{2,1,0:T(8,128)(2,1)}, bf16[2,128,1024]{2,1,0:T(8,128)(2,1)}, u32[]{:S(2)}, u32[]{:S(2)}) collective-permute-start(bf16[2,128,1024]{2,1,0:T(8,128)(2,1)} %fusion.3), channel_id=1, source_target_pairs={{0,8},{4,12},{8,16},{12,20},{16,24},{20,28},{24,0},{28,4},{1,9},{5... | collective-permute-start | bytes 1572872 | tf_op jit(solution)/shard_map/ppermute | solution.py:848
  459.7 16.8 %collective-permute-start.87 = (bf16[4,32,1024]{2,1,0:T(8,128)(2,1)S(1)}, bf16[4,32,1024]{2,1,0:T(8,128)(2,1)S(1)}, u32[]{:S(2)}, u32[]{:S(2)}) collective-permute-start(bf16[4,32,1024]{2,1,0:T(8,128)(2,1)S(1)} %pad_maximum_fusion.5), channel_id=1, source_target_pairs={{0,4},{4,0},{8,12},{12,8},{16,20},{20,16},{24,28},{28,24},{1,5},{5... | collective-permute-start | bytes 786440 | tf_op jit(solution)/shard_map/ppermute | solution.py:851
  (136 other events, 1380.0 us)

commit v3 on v2

--- a/solution.py
+++ b/solution.py
@@ -79,7 +79,7 @@
     return pl.ds(pl.multiple_of(index * size, size), size)
 
 
-def run(kernel, name, inputs, specs, outs, out_specs, scratch, grid=()):
+def run(kernel, name, micros, inputs, specs, outs, out_specs, scratch, grid=()):
     return pl.pallas_call(
         kernel,
         grid=grid,
@@ -90,9 +90,28 @@
         compiler_params=pltpu.CompilerParams(
             dimension_semantics=("arbitrary",) * len(grid), vmem_limit_bytes=56 * 1024 * 1024
         ),
-        cost_estimate=pl.CostEstimate(flops=1024, bytes_accessed=1024, transcendentals=0),
+        cost_estimate=pl.CostEstimate(
+            flops=int(micros * 10**9), bytes_accessed=1024, transcendentals=0
+        ),
         name=name,
     )(*inputs)
+
+
+def gate_kernel(*refs):
+    in_ref, out_ref = refs[0], refs[-1]
+    for i in range(in_ref.shape[0]):
+        out_ref[i] = in_ref[i]
+
+
+def gate(scalars, *others):
+    return pl.pallas_call(
+        gate_kernel,
+        in_specs=[scalar] + [anywhere] * len(others),
+        out_specs=scalar,
+        out_shape=jax.ShapeDtypeStruct(scalars.shape, scalars.dtype),
+        cost_estimate=pl.CostEstimate(flops=3 * 10**10, bytes_accessed=1024, transcendentals=0),
+        name="gate",
+    )(scalars, *others)
 
 
 def start_all(copies):
@@ -137,6 +156,7 @@
     return run(
         functools.partial(unpack_kernel, plan),
         "unpack",
+        3,
         [places] + parts,
         [scalar] + [anywhere] * dp,
         [((width, LANES), bf16), ((SMALL_ROWS, width), f32), ((dp * share, ctx * own), bf16)],
@@ -191,6 +211,7 @@
     return run(
         functools.partial(qkv_kernel, plan),
         "norm_qkv",
+        8,
         [scalars, small] + parts + tokens,
         [scalar, inside] + [anywhere] * (dp + ctx),
         [
@@ -312,6 +333,7 @@
     return run(
         functools.partial(attention_forward_kernel, heads, block),
         "attention_forward",
+        10,
         joined,
         [spec(0), spec(1), spec(2)],
         [((length, width), bf16)],
@@ -326,6 +348,7 @@
     return run(
         functools.partial(attention_backward_kernel, heads, block, pieces[0].shape[0]),
         "attention_backward",
+        18,
         [scalars] + joined + pieces,
         [scalar, spec(0), spec(1), spec(2)] + [anywhere] * len(pieces),
         [((length, width), bf16)] * 3,
@@ -364,6 +387,7 @@
     return run(
         functools.partial(hidden_kernel, len(pieces)),
         "hidden",
+        4,
         [scalars, small, full_out, tokens, sort] + pieces,
         [scalar] + [inside] * (4 + len(pieces)),
         [(shape, f32), (shape, bf16), (shape, bf16)],
@@ -374,6 +398,7 @@
 
 def mlp_kernel(plan, scalars, small_ref, by_column, *refs):
     dp, ctx, rows, start, count, expert, merged, last = plan
+    base = 2 if expert == 1 else 0
     depth = dp // 2
     refs = list(refs)
 
@@ -391,8 +416,9 @@
         y_ref, gx_ref, dots_out = take(3)
     (gb_ref,) = take(1)
     mine, other = take(1 if merged else 2), take(1 if merged else 2)
-    up, down, x_all, g_all, act_all, go_all, gu_all, up_grad, down_grad = take(9)
-    held = take(6) if last else []
+    up, down, x_all, x_turned, g_all, act_all, go_all, gu_all, up_grad, down_grad = take(10)
+    pre_all, back_all = take(2)
+    held = take(6) if last else take(2)
     in_sems, x_sems, out_sems, held_sems = take(4)
     width, hidden = up.shape
     up_rows, down_rows = width // dp, hidden // dp
@@ -403,7 +429,7 @@
     def loads(target, size, which):
         return [
             pltpu.make_async_copy(
-                parts[i].at[which] if merged else parts[which * dp + i],
+                parts[i].at[base + which] if merged else parts[which * dp + i],
                 target.at[aligned(scalars[i], size)],
                 in_sems.at[which * dp + i],
             )
@@ -449,28 +475,41 @@
             else sigmoid_pair(route_one, route_zero)
         )
         coef = sigmoid_pair(mix_one, mix_zero) * gate * mask
+    x_turned[...] = jnp.transpose(x_all[...])
     wait_all(grads)
     go_all[...] = (g_all[...].astype(f32) * coef).astype(bf16)
     wait_all(ups)
 
-    def forward(cut):
-        pre = product(x_all[...], up[:, cut]) + by_column[:, cut]
-        square = pre * pre
-        bend = jnp.tanh(ROOT * (pre + CUBE * (square * pre)))
-        half = 0.5 * (1.0 + bend)
-        act_all[:, cut] = (pre * half).astype(bf16)
-        return half + (0.5 * ROOT) * pre * (1.0 - bend * bend) * (1.0 + (3.0 * CUBE) * square)
+    piece = 64 if total % 64 == 0 else 16
+
+    def activate(cut):
+        bias = by_column[:, cut]
+        column_sum = jnp.zeros((8, tile), f32)
+        for at in range(0, total, piece):
+            span = slice(at, at + piece)
+            pre = pre_all[span, :] + bias
+            square = pre * pre
+            bend = jnp.tanh((ROOT * pre) * (1.0 + CUBE * square))
+            half = 0.5 + 0.5 * bend
+            act_all[span, cut] = (pre * half).astype(bf16)
+            slope = half + ((0.5 * ROOT) * pre) * (1.0 - bend * bend) * (
+                1.0 + (3.0 * CUBE) * square
+            )
+            grad_up = (back_all[span, :] * slope).astype(bf16)
+            gu_all[span, cut] = grad_up
+            column_sum = column_sum + jnp.sum(
+                grad_up.astype(f32).reshape(piece // 8, 8, tile), 0
+            )
+        gb_ref[:, cut] = jnp.sum(column_sum, 0, keepdims=True)
 
     for number, cut in enumerate(tiles):
-        slope = forward(cut)
+        pre_all[...] = product(x_all[...], up[:, cut])
         if number == 0:
             wait_all(downs)
-        grad_act = right_product(go_all[...], down[cut, :])
-        grad_up = (grad_act * slope).astype(bf16)
-        gu_all[:, cut] = grad_up
-        gb_ref[:, cut] = jnp.sum(grad_up.astype(f32), 0, keepdims=True)
+        back_all[...] = right_product(go_all[...], down[cut, :])
+        activate(cut)
         down_grad[cut, :] = left_product(act_all[:, cut], go_all[...]).astype(bf16)
-        up_grad[:, cut] = left_product(x_all[...], grad_up).astype(bf16)
+        up_grad[:, cut] = product(x_turned[...], gu_all[:, cut]).astype(bf16)
 
     def stores(grad, size, which):
         targets = [
@@ -488,6 +527,7 @@
 
     saved = start_all(stores(up_grad, up_rows, 0) + stores(down_grad, down_rows, 1))
     wait_all(gathered)
+    sums_sent = []
     for block in range(ctx):
         span = rows_of(block)
         out = product(act_all[span, :], down[...])
@@ -495,7 +535,13 @@
         dot = jnp.sum(g_all[span, :].astype(f32) * out, -1, keepdims=True)
         out = out * coef[span]
         if not last:
-            y_ref[span, :], gx_ref[span, :] = out, grad_x
+            held[0][span, :], held[1][span, :] = out, grad_x
+            for number, target in enumerate((y_ref, gx_ref)):
+                copy = pltpu.make_async_copy(
+                    held[number].at[span], target.at[span], held_sems.at[2 * block + number]
+                )
+                copy.start()
+                sums_sent.append(copy)
             dots_out[span, :] = dot if mask is None else dot * mask[span]
             continue
         y_dense, gx_dense, dots_dense, y_first, gx_first, dots_first = held
@@ -523,7 +569,7 @@
         high, middle, low = three_parts(both)
         extra = jnp.where(lane < 2, high.astype(f32), jnp.where(lane < 4, middle.astype(f32), low.astype(f32)))
         gx_refs[block][:, width:] = jnp.where(lane < 6, extra, 0.0).astype(bf16)
-    wait_all(saved)
+    wait_all(saved + sums_sent)
 
 
 def mlp(scalars, small, bias, x, g, parts, expert, merged, sums):
@@ -537,7 +583,7 @@
     total = ctx * count
     last = expert == 1
     if merged:
-        halves = [((depth,) + parts[0].shape, bf16)]
+        halves = [((depth, 2) + parts[0].shape[1:], bf16)]
     else:
         halves = [((depth,) + parts[0].shape, bf16), ((depth,) + parts[dp].shape, bf16)]
     if last:
@@ -546,31 +592,38 @@
         outs = [((total, width), f32), ((total, width), f32), ((total, 1), f32)]
     outs = outs + [((1, hidden), f32)] + halves + halves
     small_outs = len(outs) - 2 * len(halves)
-    held = [pltpu.VMEM(ref.shape, f32) for ref in sums]
+    held = [pltpu.VMEM(ref.shape, f32) for ref in sums] or [pltpu.VMEM((total, width), f32)] * 2
+    tile = min(256, hidden)
     return run(
         functools.partial(mlp_kernel, (dp, ctx, rows, start, count, expert, merged, last)),
         "mlp",
+        20 if total % LANES == 0 and expert is None else 18,
         [scalars, small, bias] + x + g + parts + sums,
         [scalar, inside, inside] + [anywhere] * (2 * ctx + len(parts) + len(sums)),
         outs,
-        [inside] * small_outs + [anywhere] * (2 * len(halves)),
+        ([] if last else [anywhere] * 2)
+        + [inside] * (small_outs if last else small_outs - 2)
+        + [anywhere] * (2 * len(halves)),
         [
             pltpu.VMEM((width, hidden), bf16),
             pltpu.VMEM((hidden, width), bf16),
             pltpu.VMEM((total, width), bf16),
+            pltpu.VMEM((width, total), bf16),
             pltpu.VMEM((total, width), bf16),
             pltpu.VMEM((total, hidden), bf16),
             pltpu.VMEM((total, width), bf16),
             pltpu.VMEM((total, hidden), bf16),
             pltpu.VMEM((width, hidden), bf16),
             pltpu.VMEM((hidden, width), bf16),
+            pltpu.VMEM((total, tile), f32),
+            pltpu.VMEM((total, tile), f32),
         ]
         + held
         + [
             pltpu.SemaphoreType.DMA((2 * dp,)),
             pltpu.SemaphoreType.DMA((2 * ctx,)),
             pltpu.SemaphoreType.DMA((2 * dp,)),
-            pltpu.SemaphoreType.DMA((max(1, len(sums)),)),
+            pltpu.SemaphoreType.DMA((max(2 * ctx, len(sums)),)),
         ],
     )
 
@@ -580,8 +633,9 @@
 ):
     gx, pieces = refs[:ctx], refs[ctx : 2 * ctx]
     outs = refs[2 * ctx :]
-    base_ref, grad_hidden_ref, out_grad_ref, rows_ref, router_ref = outs[:5]
-    grad_pieces = outs[5:]
+    base_ref, grad_hidden_ref, rows_ref, router_ref = outs[:4]
+    out_grads, grad_pieces = outs[4 : 4 + ctx], outs[4 + ctx : 4 + 2 * ctx]
+    out_all, sems = outs[4 + 2 * ctx :]
     rows, width = hidden_ref.shape
     own = pieces[0].shape[1]
     unsort = unsort_ref[...]
@@ -655,35 +709,55 @@
     for i, (piece, target) in enumerate(zip(pieces, grad_pieces)):
         span = aligned(scalars[i], own)
         target[...] = right_product(low, out_ref[span, :]).astype(bf16)
-        out_grad_ref[span, :] = left_product(piece[...], low).astype(bf16)
-
-
-def make_middle(scalars, by_row, by_column, full_out, hidden, norm, g, first, unsort, gx, pieces):
+        part = left_product(piece[...], low).astype(bf16)
+        share = out_all.shape[3]
+        many = own // (ctx * share)
+        for c in range(ctx):
+            columns = part[:, c * own : (c + 1) * own].reshape(many, ctx, share, own)
+            out_all[aligned(scalars[i], many), :, c] = columns
+    wait_all(
+        start_all(
+            [
+                pltpu.make_async_copy(out_all.at[:, scalars[i]], target, sems.at[i])
+                for i, target in enumerate(out_grads)
+            ]
+        )
+    )
+
+
+def make_middle(
+    scalars, by_row, by_column, full_out, hidden, norm, g, first, unsort, gx, pieces, dp
+):
     ctx = len(gx)
     rows, width = hidden.shape
     own = pieces[0].shape[1]
     return run(
         functools.partial(middle_kernel, ctx),
         "middle",
+        11,
         [scalars, by_row, by_column, full_out, hidden, norm, g, first, unsort] + gx + pieces,
         [scalar] + [inside] * (8 + 2 * ctx),
         [
             ((rows, width), f32),
             ((rows, width), f32),
-            ((width, width), bf16),
             ((8, width), f32),
             ((width, LANES), f32),
         ]
+        + [((dp, ctx, width // (dp * ctx), own), bf16)] * ctx
         + [((rows, own), bf16)] * ctx,
-        [inside] * (5 + ctx),
-        [],
+        [inside] * 4 + [anywhere] * ctx + [inside] * ctx,
+        [
+            pltpu.VMEM((dp, ctx, ctx, width // (dp * ctx), own), bf16),
+            pltpu.SemaphoreType.DMA((ctx,)),
+        ],
     )
 
 
 def qkv_back_kernel(plan, scalars, norm_ref, dq_ref, dk_ref, dv_ref, weight_ref, *refs):
     dp, ctx, rows, own = plan
     depth = dp // 2
-    gn_refs, (mine, other, bias_ref, grad, weight_grad, gn, sems, gn_sems) = refs[:ctx], refs[ctx:]
+    out_pieces, gn_refs = refs[:ctx], refs[ctx : 2 * ctx]
+    mine, other, bias_ref, grad, weight_grad, gn, sems, gn_sems = refs[2 * ctx :]
     width = norm_ref.shape[1]
     size = width // dp
     for part, ref in enumerate((dq_ref, dk_ref, dv_ref)):
@@ -700,9 +774,10 @@
     )
     step = min(256, width)
     for at in range(0, width, step):
-        weight_grad[at : at + step, :] = left_product(norm_ref[:, at : at + step], grad[...]).astype(
-            bf16
-        )
+        weight_grad[at : at + step, : 3 * own] = left_product(
+            norm_ref[:, at : at + step], grad[...]
+        ).astype(bf16)
+    weight_grad[:, 3 * own :] = sum(piece[...].astype(f32) for piece in out_pieces).astype(bf16)
     saved = start_all(
         [
             pltpu.make_async_copy(
@@ -717,20 +792,21 @@
     wait_all(sent + saved)
 
 
-def qkv_back(scalars, norm, grads, weight, plan):
+def qkv_back(scalars, norm, grads, weight, out_pieces, plan):
     dp, ctx, rows, own = plan
     length, width = norm.shape
-    half = ((dp // 2, width // dp, 3 * own), bf16)
+    half = ((dp // 2, width // dp, 4 * own), bf16)
     return run(
         functools.partial(qkv_back_kernel, plan),
         "qkv_back",
-        [scalars, norm] + list(grads) + [weight],
-        [scalar] + [inside] * 5,
+        8,
+        [scalars, norm] + list(grads) + [weight] + list(out_pieces),
+        [scalar] + [inside] * (5 + ctx),
         [((rows, width), bf16)] * ctx + [half, half, ((1, 3 * own), f32)],
         [anywhere] * (ctx + 2) + [inside],
         [
             pltpu.VMEM((length, 3 * own), bf16),
-            pltpu.VMEM((width, 3 * own), bf16),
+            pltpu.VMEM((width, 4 * own), bf16),
             pltpu.VMEM((length, width), bf16),
             pltpu.SemaphoreType.DMA((dp,)),
             pltpu.SemaphoreType.DMA((ctx,)),
@@ -738,7 +814,7 @@
     )
 
 
-def final_kernel(ctx, by_column, tokens_ref, grad_hidden_ref, *refs):
+def final_kernel(ctx, order, by_column, tokens_ref, grad_hidden_ref, *refs):
     pieces, (grad_ref, rows_ref) = refs[:ctx], refs[ctx:]
     grad_norm = sum(piece[...].astype(f32) for piece in pieces)
     normed, inverse = layer_stats(tokens_ref[...].astype(f32))
@@ -748,12 +824,13 @@
     rows_ref[1:2, :] = jnp.sum(grad_norm, 0, keepdims=True)
 
 
-def make_final(by_column, tokens, grad_hidden, pieces):
+def make_final(order, by_column, tokens, grad_hidden, pieces):
     return run(
         functools.partial(final_kernel, len(pieces)),
         "final",
-        [by_column, tokens, grad_hidden] + pieces,
-        [inside] * (3 + len(pieces)),
+        4,
+        [order, by_column, tokens, grad_hidden] + pieces,
+        [scalar] + [inside] * (3 + len(pieces)),
         [(tokens.shape, f32), ((2, tokens.shape[1]), f32)],
         [inside] * 2,
         [],
@@ -770,6 +847,7 @@
     return run(
         functools.partial(result_kernel, len(pieces)),
         "result",
+        3.5,
         [base, unsort] + pieces,
         [inside] * (2 + len(pieces)),
         [(base.shape, f32)],
@@ -833,10 +911,8 @@
     def trade(pieces):
         return [pieces[0]] + [swap(pieces[s], s) for s in shifts]
 
-    def exchange(pieces):
-        return trade(
-            [lax.dynamic_index_in_dim(pieces, me ^ s, 0, keepdims=False) for s in range(ctx)]
-        )
+    def by_peer(pieces):
+        return [lax.dynamic_index_in_dim(pieces, me ^ s, 0, keepdims=False) for s in range(ctx)]
 
     def natural(pieces):
         whole = jnp.zeros((ctx,) + pieces[0].shape, pieces[0].dtype)
@@ -850,15 +926,67 @@
     def swap_core(array):
         return lax.ppermute(array, "dp", core_pairs)
 
-    def chunks(array):
-        size = array.shape[0] // dp
-        cut = [
-            lax.dynamic_slice_in_dim(array, places[i] * size, size, 0) for i in range(dp)
-        ]
-        return jnp.stack(cut[:depth]), jnp.stack(cut[depth:])
-
-    def after(array, *others):
-        return lax.optimization_barrier((array,) + others)[0]
+    def sync(*trees):
+        return lax.optimization_barrier(trees)
+
+    class Rings:
+        def __init__(self, arrays):
+            self.parts = [list(arrays)]
+
+        def move(self):
+            self.parts.append([ring(array) for array in self.parts[-1]])
+
+        def rest(self):
+            while len(self.parts) < depth:
+                self.move()
+
+        def pieces(self, others, which):
+            return [part[which] for part in self.parts] + [part[which] for part in others]
+
+    def swap_cores(part):
+        return [swap_core(array) for array in part]
+
+    class Scatter:
+        def __init__(self, *halves):
+            half = len(halves) // 2
+            self.mine, self.step = list(halves[:half]), 0
+            self.got = [swap_core(other) for other in halves[half:]]
+            self.arrived = self.sent = None
+
+        def receive(self, others):
+            if self.sent is None:
+                self.got, others = sync(self.got, others)
+            else:
+                self.arrived, others = sync([ring(part) for part in self.sent], others)
+            return others
+
+        def add(self):
+            self.step += 1
+            at = self.step % depth
+            parts = [m[at].astype(f32) + g[at].astype(f32) for m, g in zip(self.mine, self.got)]
+            if self.arrived is not None:
+                parts = [p + c.astype(f32) for p, c in zip(parts, self.arrived)]
+            self.sent = [part.astype(bf16) if at else part for part in parts]
+
+        def move(self, others):
+            others = self.receive(others)
+            self.add()
+            return others
+
+        def close(self):
+            self.add()
+            while self.step < depth:
+                self.arrived = [ring(part) for part in self.sent]
+                self.add()
+
+    def pin(value, *sums):
+        value, sent = sync(value, [one.sent for one in sums])
+        for one, parts in zip(sums, sent):
+            one.sent = parts
+        return value
+
+    def pair(sums):
+        return sums if len(sums) == 2 else [sums[0][0], sums[0][1]]
 
     tokens = tokens.reshape(rows, width)
     cotangent = cotangent.reshape(rows, width)
@@ -897,7 +1025,11 @@
         ],
         -1,
     )
-    first_rows = natural(exchange(first_cut)).reshape(ctx * share, 3 * own_width + LANES)
+    ups = jnp.concatenate([up_weight[None], expert_up], 0)
+    ups_cut = ups.reshape(experts + 1, share, dp, ctx, unit).transpose(3, 0, 1, 2, 4)
+    ups_sent = by_peer(ups_cut.reshape(ctx, experts + 1, share, own_hidden))
+    first_rows, ups_sent = sync(trade(by_peer(first_cut)), ups_sent)
+    first_rows = natural(first_rows).reshape(ctx * share, 3 * own_width + LANES)
     qkv_rows = first_rows[:, : 3 * own_width]
     small_rows = first_rows[:, 3 * own_width :]
     counts = small_rows[::share, COUNT]
@@ -909,40 +1041,40 @@
     small_rows = jnp.where((lane >= UP_BIAS) & (lane < UP_BIAS + experts + 1), bias_lanes, small_rows)
     out_rows = out_weight.reshape(share, ctx, own_width).transpose(1, 0, 2)
     out_rows = out_rows.reshape(ctx * share, own_width)
-    first_group = jnp.concatenate([qkv_rows, out_rows, small_rows], 1)
-
-    def gather_dp(streams):
-        parts = [[array] for array in streams]
-        for _ in range(1, depth):
-            for part in parts:
-                part.append(ring(part[-1]))
-        return parts
-
-    def with_cores(parts):
-        return parts + [swap_core(part) for part in parts]
-
-    (first_ring,) = gather_dp([first_group])
+    first = Rings([jnp.concatenate([qkv_rows, out_rows, small_rows], 1)])
+
+    first.move()
+    first_others = [swap_cores(first.parts[0])]
     token_parts = gather_ctx(tokens)
-    first_parts = with_cores(first_ring)
+    first.parts[1], first_others[0] = sync(first.parts[1], first_others[0])
+    first.move()
+    first_others.append(swap_cores(first.parts[1]))
+    token_parts, first.parts[2], first_others[1], ups_sent = sync(
+        token_parts, first.parts[2], first_others[1], ups_sent
+    )
+    first.rest()
+    first_others += [swap_cores(part) for part in first.parts[2:-1]]
+    ups_rows, first.parts[-1], first_others = sync(trade(ups_sent), first.parts[-1], first_others)
+    ups_rows = natural(ups_rows).transpose(1, 0, 2, 3)
+    ups_rows = ups_rows.reshape(experts + 1, ctx * share, own_hidden)
+    downs = [down_weight] + [expert_down[e] for e in range(experts)]
+    merged = downs[0].shape == ups_rows.shape[1:]
+    if merged:
+        dense_weights = [jnp.stack([ups_rows[0], downs[0]])]
+        expert_weights = [jnp.stack([ups_rows[1], downs[1], ups_rows[2], downs[2]])]
+    else:
+        dense_weights = [ups_rows[0], downs[0]]
+        expert_weights = [ups_rows[1], downs[1], ups_rows[2], downs[2]]
+    dense_ring = Rings(dense_weights)
+    dense_ring.move()
+    first_others.append(swap_cores(first.parts[-1]))
+    first_parts = first.pieces(first_others, 0)
     plan = (dp, ctx, share, own_width, experts)
     by_row, by_column, out_own = unpack(places, first_parts, plan)
-    out_pieces = natural(gather_ctx(out_own))
-    full_out = out_pieces.reshape(ctx, dp, share, width).transpose(1, 0, 2, 3).reshape(width, width)
-
-    unit_rows = ctx * share
-    ups = jnp.concatenate([up_weight[None], expert_up], 0)
-    ups_cut = ups.reshape(experts + 1, share, dp, ctx, unit).transpose(3, 0, 1, 2, 4)
-    ups_cut = after(ups_cut.reshape(ctx, experts + 1, share, own_hidden), first_rows)
-    ups_rows = natural(exchange(ups_cut)).transpose(1, 0, 2, 3)
-    ups_rows = ups_rows.reshape(experts + 1, unit_rows, own_hidden)
-    downs = [down_weight] + [expert_down[e] for e in range(experts)]
-    merged = downs[0].shape == ups_rows.shape[1:]
-    streams = []
-    for which in range(experts + 1):
-        pair = [ups_rows[which], downs[which]]
-        streams += [jnp.stack(pair)] if merged else pair
-    streams = list(lax.optimization_barrier(tuple(streams) + (first_ring[-1],)))[:-1]
-    rings = [[stream, ring(stream)] for stream in streams]
+    expert_weights, by_row = sync(expert_weights, by_row)
+    expert_ring = Rings(expert_weights)
+    expert_ring.move()
+    out_pieces = gather_ctx(out_own)
 
     order = jnp.arange(rows).astype(f32)
     counted = jnp.cumsum(first_float)
@@ -955,87 +1087,90 @@
     qkv, attn_in, own_qkv = make_qkv(
         scalars, by_column, first_parts, token_parts, (dp, ctx, rows, own_width, share)
     )
+    qkv, dense_ring.parts[1] = sync(qkv, dense_ring.parts[1])
+    dense_ring.move()
     attended_heads = attention_forward(qkv, own_width)
-    attended = exchange(attended_heads.reshape(ctx, rows, own_width))
-    hidden_state, ffn_in, sorted_in = make_hidden(peers, by_column, full_out, tokens, sort, attended)
+    attended_heads, out_pieces = sync(attended_heads, out_pieces)
+    attended = trade(by_peer(attended_heads.reshape(ctx, rows, own_width)))
+    full_out = natural(out_pieces).reshape(ctx, dp, share, width).transpose(1, 0, 2, 3)
+    full_out = full_out.reshape(width, width)
+    hidden_state, ffn_in, sorted_in = make_hidden(
+        peers, by_column, full_out, tokens, sort, attended
+    )
+    sorted_in, expert_ring.parts[1] = sync(sorted_in, expert_ring.parts[1])
+    expert_ring.move()
     ffn_parts = gather_ctx(sorted_in)
-    grad_parts = gather_ctx(after(sorted_grad, attended[-1]))
-
-    for _ in range(2, depth):
-        stepped = lax.optimization_barrier(tuple(parts[-1] for parts in rings) + (sorted_in,))
-        for parts, part in zip(rings, stepped):
-            parts.append(ring(part))
-    if merged:
-        weight_parts = [with_cores(parts) for parts in rings]
-    else:
-        weight_parts = [
-            with_cores(rings[2 * w]) + with_cores(rings[2 * w + 1]) for w in range(experts + 1)
-        ]
-
-    row_counts = jnp.stack([counts[me ^ s] for s in range(ctx)]).astype(jnp.int32)
+    late_columns, late_counts, _ = sync(by_column, counts, sorted_in)
+    row_counts = jnp.stack([late_counts[me ^ s] for s in range(ctx)]).astype(jnp.int32)
     mlp_scalars = jnp.concatenate([places, row_counts])
-    up_biases = by_column[UP_BIAS : UP_BIAS + experts + 1]
+    up_biases = late_columns[UP_BIAS : UP_BIAS + experts + 1]
     up_biases = up_biases.reshape(experts + 1, dp, -1)[:, :, :unit].reshape(experts + 1, own_hidden)
 
-    class Scatter:
-        def __init__(self, mine, other):
-            self.mine, self.got, self.step, self.sent = mine, swap_core(other), 0, None
-
-        def move(self, *others):
-            if self.step == 0:
-                self.got = after(self.got, *others)
-            carried = None if self.step == 0 else after(ring(self.sent), *others)
-            self.step += 1
-            part = self.mine[self.step % depth].astype(f32) + self.got[self.step % depth].astype(f32)
-            if carried is not None:
-                part = part + carried.astype(f32)
-            self.sent = part.astype(bf16) if self.step < depth else part
-            return self.sent
-
-        def finish(self, *others):
-            while self.step < depth:
-                self.move(*others)
-            return self.sent
-
-    class Joint:
-        def __init__(self, halves):
-            half = len(halves) // 2
-            self.parts = [Scatter(m, o) for m, o in zip(halves[:half], halves[half:])]
-
-        def move(self, *others):
-            return [part.move(*others) for part in self.parts]
-
-        def finish(self, *others):
-            done = [part.finish(*others) for part in self.parts]
-            return done if len(done) == 2 else [done[0][0], done[0][1]]
-
-    def run_mlp(which, held, sums):
+    mlp_scalars = gate(mlp_scalars, *dense_ring.parts[2])
+    ffn_parts, dense_ring.parts[2], sorted_grad, up_biases, mlp_scalars = sync(
+        ffn_parts, dense_ring.parts[2], sorted_grad, up_biases, mlp_scalars
+    )
+    dense_ring.rest()
+    grad_parts = [sorted_grad] + [swap(sorted_grad, s) for s in shifts[:2]]
+    expert_ring.parts[2], late_grad = sync(expert_ring.parts[2], sorted_grad)
+    expert_ring.rest()
+    grad_parts += [swap(late_grad, s) for s in shifts[2:]]
+    grad_parts, dense_ring.parts = sync(grad_parts, dense_ring.parts)
+    dense_others = [swap_cores(part) for part in dense_ring.parts]
+    dense_others, early = sync(dense_others, expert_ring.parts[:-1])
+    expert_others = [swap_cores(part) for part in early]
+
+    def run_mlp(which, held, parts, sums):
         return mlp(
             held,
             by_row,
             up_biases[which][None],
             ffn_parts,
             grad_parts,
-            weight_parts[which],
+            parts,
             which - 1 if which else None,
             merged,
             list(sums),
         )
 
-    dense = run_mlp(0, mlp_scalars, [])
-    sum_dense = Joint(dense[4:])
-    first = run_mlp(1, after(mlp_scalars, dense[3]), [])
-    sum_first = Joint(first[4:])
-    sent = sum_dense.move(first[3])
-    second = run_mlp(2, after(mlp_scalars, first[3], *sent), dense[:3] + first[:3])
-    gb_second = second[2 * ctx]
-    grad_pieces = trade(second[ctx : 2 * ctx])
-    sum_second = Joint(second[2 * ctx + 1 :])
-    sent = sum_first.move(gb_second)
-    sent = sum_dense.move(*sent) + sum_second.move(*sent)
-
-    base, grad_hidden, out_grad, middle_rows, router_grad, *att_grads = make_middle(
-        after(peers, *sent),
+    def weights_of(rings, others, first_array):
+        if merged:
+            return rings.pieces(others, 0)
+        return rings.pieces(others, first_array) + rings.pieces(others, first_array + 1)
+
+    dense = run_mlp(0, mlp_scalars, weights_of(dense_ring, dense_others, 0), [])
+    sum_dense = Scatter(*dense[4:])
+    expert_last, expert_others, gb_dense = sync(expert_ring.parts[-1], expert_others, dense[3])
+    expert_ring.parts[-1] = expert_last
+    expert_others = expert_others + [swap_cores(expert_last)]
+    gb_dense = sum_dense.move(gb_dense)
+    first_mlp = run_mlp(
+        1,
+        pin(gate(mlp_scalars), sum_dense),
+        weights_of(expert_ring, expert_others, 0),
+        [],
+    )
+    sum_first = Scatter(*first_mlp[4:])
+    gb_first = sum_dense.move(first_mlp[3])
+    second_mlp = run_mlp(
+        2,
+        pin(mlp_scalars, sum_dense),
+        weights_of(expert_ring, expert_others, 2),
+        dense[:3] + first_mlp[:3],
+    )
+    gb_second = sum_first.move(sum_dense.move(second_mlp[2 * ctx]))
+    grad_sent = list(second_mlp[ctx : 2 * ctx])
+    grad_pieces = trade(grad_sent[:3] + pin(grad_sent[3:], sum_dense, sum_first))
+    grad_pieces, halves, result_sent = sync(
+        grad_pieces, second_mlp[2 * ctx + 1 :], second_mlp[:ctx]
+    )
+    grad_pieces = sum_first.move(sum_dense.receive(grad_pieces))
+    sum_second = Scatter(*halves)
+    result_pieces = [result_sent[0]] + [swap(result_sent[s], s) for s in shifts[:2]]
+
+    middle_peers, sum_dense.arrived = sync(peers, sum_dense.arrived)
+    base, grad_hidden, middle_rows, router_grad, *rest = make_middle(
+        pin(middle_peers, sum_first),
         by_row,
         by_column,
         full_out,
@@ -1046,44 +1181,59 @@
         unsort,
         grad_pieces,
         attended,
-    )
-    att_grads = trade(att_grads)
-    result_pieces = trade([after(piece, att_grads[-1]) for piece in second[:ctx]])
-    sent = sum_first.move(middle_rows) + sum_dense.move(middle_rows)
-
-    grad_heads = attention_backward(after(peers, *sent), qkv, att_grads, own_width)
-    sent = sum_second.move(grad_heads[0])
-    *norm_grads, qkv_mine, qkv_other, grad_b_qkv = qkv_back(
-        after(scalars, *sent), attn_in, grad_heads, own_qkv, (dp, ctx, rows, own_width)
-    )
-    norm_pieces = trade(norm_grads)
-    sum_qkv = Scatter(qkv_mine, qkv_other)
-    sent = sum_first.move(grad_b_qkv)
-    sent = sent + [sum_qkv.move(*sent)]
-    dense_sums = sum_dense.finish(*sent)
+        dp,
+    )
+    out_sent, att_sent = rest[:ctx], rest[ctx:]
+    result_pieces, att_sent = sync(result_pieces, att_sent)
+    att_grads, out_sent = sync(trade(att_sent), out_sent)
+    out_sent = [piece.reshape(width, own_width) for piece in out_sent]
+    out_pieces = trade(out_sent)
+    middle_rows = sum_second.move(sum_first.move(middle_rows))
+
+    grad_heads = attention_backward(pin(peers, sum_first, sum_second), qkv, att_grads, own_width)
+    grad_heads = sum_second.move(sum_first.receive(grad_heads))
+    back_scalars, sum_first.arrived = sync(pin(scalars, sum_second), sum_first.arrived)
+    *norm_grads, last_mine, last_other, grad_b_qkv = qkv_back(
+        back_scalars,
+        attn_in,
+        grad_heads,
+        own_qkv,
+        out_pieces,
+        (dp, ctx, rows, own_width),
+    )
+    sum_last = Scatter(last_mine, last_other)
+    norm_pieces = [norm_grads[0]] + [swap(norm_grads[s], s) for s in shifts[:2]]
+    norm_pieces, late_grads, grad_b_qkv = sync(norm_pieces, list(norm_grads[3:]), grad_b_qkv)
+    norm_pieces += [swap(piece, s) for piece, s in zip(late_grads, shifts[2:])]
+    grad_b_qkv = sum_second.move(sum_last.move(grad_b_qkv))
+    sum_dense.close()
+    sum_first.close()
+    grad_b_qkv = sum_last.move(grad_b_qkv)
+    order_numbers, sum_second.arrived = sync(peers, [ring(part) for part in sum_second.sent])
+    sum_second.close()
+
+    def cut_columns(parts):
+        joined = jnp.concatenate([part.astype(bf16) for part in parts], 1)
+        return by_peer(joined.reshape(ctx, share, joined.shape[1]))
+
+    def from_columns(pieces, at, size, groups):
+        whole = natural([piece[:, at : at + size] for piece in pieces])
+        whole = whole.reshape(ctx, share, groups, size // groups).transpose(1, 2, 0, 3)
+        return whole.reshape(share, ctx * size).astype(f32)
+
+    norm_pieces = pin(norm_pieces, sum_last, sum_second)
+    grad_b_qkv = sum_last.move(grad_b_qkv)
+    sums = [pair(one.sent) for one in (sum_dense, sum_first, sum_second)]
+    early_sent = cut_columns([one[0] for one in sums])
+    norm_pieces, early_sent, result_sent = sync(norm_pieces, early_sent, result_sent)
+    early_pieces = trade(early_sent)
+    result_pieces = result_pieces + [swap(result_sent[s], s) for s in shifts[2:]]
     grad_inputs, final_rows = make_final(
-        after(by_column, *dense_sums, *sent), tokens, grad_hidden, norm_pieces
-    )
-    sent = sum_second.move(final_rows)
-    result = make_result(base, unsort, result_pieces)
-    out_grad = out_grad.reshape(dp, ctx, share, width).transpose(1, 0, 2, 3)
-    out_grad = after(out_grad.reshape(ctx, dp * share, width), norm_pieces[-1])
-    out_part = sum(p.astype(f32) for p in exchange(out_grad))
-    out_grad = Scatter(*chunks(out_part.astype(bf16))).finish()
-    qkv_part = sum_qkv.finish()
-    first_sums, second_sums = sum_first.finish(), sum_second.finish()
-    up_sums = [dense_sums[0], first_sums[0], second_sums[0]]
-    down_sums = [dense_sums[1], first_sums[1], second_sums[1]]
-    upb_grads = [dense[3][0], first[3][0], gb_second[0]]
-
-    def to_owners(part, groups):
-        size = part.shape[1] // groups
-        pieces = exchange(part.astype(bf16).reshape(ctx, share, part.shape[1]))
-        whole = natural(pieces).reshape(ctx, share, groups, size).transpose(1, 2, 0, 3)
-        return whole.reshape(share, ctx * part.shape[1]).astype(f32)
-
-    up_grads = [to_owners(part, dp) for part in up_sums]
-    qkv_grad = to_owners(qkv_part, 3)
+        order_numbers, by_column, tokens, grad_hidden, norm_pieces
+    )
+    final_rows, early_pieces = sum_last.receive((final_rows, early_pieces))
+    sum_last.close()
+    final_rows, result_pieces = pin((final_rows, result_pieces), sum_last)
 
     zero_qv = jnp.zeros((2, width), f32)
     grad_qv = lax.dynamic_update_slice(
@@ -1096,6 +1246,7 @@
         whole = jnp.zeros((dp, ctx, array.shape[-1]), f32)
         return lax.dynamic_update_slice_in_dim(whole, array[:, None], me, 1)
 
+    upb_grads = [gb_dense[0], gb_first[0], gb_second[0]]
     expert_upb = jnp.stack(upb_grads[1:]).reshape(experts, dp, unit).transpose(1, 0, 2)
     small_grads = [
         final_rows[0],
@@ -1113,13 +1264,26 @@
     ]
     sizes = [grad.size // (dp * ctx) for grad in small_grads]
     small_sum = jnp.concatenate([g.reshape(dp, ctx, -1) for g in small_grads], -1)
-    small_sum = sum(exchange(small_sum.transpose(1, 0, 2)))
-    small_sum = small_sum.reshape(dp, 1, -1)[places]
+    small_pieces = trade(by_peer(small_sum.transpose(1, 0, 2)))
+
+    (last_sum,) = sum_last.sent
+    qkv_part, out_sums = last_sum[:, : 3 * own_width], last_sum[:, 3 * own_width :]
+    out_sums = out_sums.reshape(ctx, share, own_width).transpose(1, 0, 2).reshape(share, width)
+    small_sum = sum(small_pieces).reshape(dp, 1, -1)[places]
     small_sum = small_sum[:depth] + swap_core(small_sum[depth:])
     pairs = [[(i, (i + dp - 2 * t) % dp) for i in range(dp)] for t in range(depth)]
     small_sum = sum(
         [small_sum[0]] + [lax.ppermute(small_sum[t], "dp", pairs[t]) for t in range(1, depth)]
     )[0]
+    late_pieces = trade(cut_columns([qkv_part]))
+    result = make_result(base, unsort, result_pieces)
+    up_grads = [
+        from_columns(early_pieces, 0, own_hidden, dp),
+        from_columns(early_pieces, own_hidden, own_hidden, dp),
+        from_columns(early_pieces, 2 * own_hidden, own_hidden, dp),
+    ]
+    qkv_grad = from_columns(late_pieces, 0, 3 * own_width, 3)
+    down_sums = [one[1] for one in sums]
     outs, at = [], 0
     for size in sizes:
         outs.append(small_sum[at : at + size])
@@ -1131,7 +1295,7 @@
         outs[1],
         qkv_grad,
         outs[2],
-        out_grad,
+        out_sums,
         outs[3],
         outs[4],
         outs[5],

time: 502 us -> 426 us (0.85)
  waiting for transfers between devices: 181 us -> 125 us
  starting transfers between devices: 90.5 us -> 76.7 us
  other arithmetic: 40.8 us -> 30.6 us
    ppermute x27 -> x21, waiting for transfers between devices: 89.6 us -> 51.2 us  [ring(): return lax.ppermute(array, 'dp', ring_pairs)]
    ppermute x51 -> x45, waiting for transfers between devices: 81.1 us -> 69.6 us  [swap(): return lax.ppermute(array, 'ctx', [(i, i ^ shift) for i in range(ctx)])]
    convert_element_type x18 -> x13, other arithmetic: 26.6 us -> 17.6 us  [the longest x12 14.9 us: add(): self.sent = [part.astype(bf16) if at else part for part in parts]]
    ppermute x51 -> x45, starting transfers between devices: 63.3 us -> 56 us  [swap(): return lax.ppermute(array, 'ctx', [(i, i ^ shift) for i in range(ctx)])]
    ppermute x27 -> x21, starting transfers between devices: 22.2 us -> 15.9 us  [ring(): return lax.ppermute(array, 'dp', ring_pairs)]
  transfers between devices with their start and end apart: 103 -> 86, of which waited for: 46 -> 33; matrix products, arithmetic and copies ran while one was open for 15% -> 15% of each run, Pallas kernels for 22% -> 31%
where the time goes in v3:
time: 426 us; the launch traced here: 418 us
  Pallas kernels  140 us (33%)
  waiting for transfers between devices  125 us (29%)
  starting transfers between devices  76.7 us (18%)
  local copies, waits for them, and re-layouts  42.5 us (10%)
  other arithmetic  30.6 us (7%)
    pallas_call x12, Pallas kernels, run(): pl.pallas_call(kernel, grid=grid, in_specs=specs, out_specs=out_specs, ou...  138 us
    ppermute x45, waiting for transfers between devices, swap(): return lax.ppermute(array, 'ctx', [(i, i ^ shift) for i in range(ctx)])  69.6 us
    ppermute x45, starting transfers between devices, swap(): return lax.ppermute(array, 'ctx', [(i, i ^ shift) for i in range(ctx)])  56 us
    ppermute x21, waiting for transfers between devices, ring(): return lax.ppermute(array, 'dp', ring_pairs)  51.2 us
    ppermute x21, starting transfers between devices, ring(): return lax.ppermute(array, 'dp', ring_pairs)  15.9 us
    convert_element_type x12, other arithmetic, add(): self.sent = [part.astype(bf16) if at else part for part in parts]  14.9 us
    unnamed x120, local copies, waits for them, and re-layouts  9.13 us
  transfers between devices with their start and end apart: 86, of which 33 were waited for; matrix products, arithmetic and copies ran while one was open for 15% of the time, Pallas kernels for 31%

profile of v3, /device:TPU:0, one launch (start us, length us, event | category | flops | bytes accessed | tf_op | source)
XLA Modules:
  0.0 418.4 jit_solution(15081272907698179018)
XLA Ops:
  0.7 3.0 collective-permute-start.5
  12.2 2.9 collective-permute-start.2
  17.7 2.7 collective-permute-start.7
  23.1 6.5 %collective-permute-done.3.refs_1_ = bf16[128,1152]{1,0:T(8,128)(2,1)S(1)} collective-permute-done((bf16[128,1152]{1,0:T(8,128)(2,1)S(1)}, bf16[128,1152]{1,0:T(8,128)(2,1)S(1)}, u32[]{:S(2)}, u32[]{:S(2)}) %collective-permute-start.3) | collective-permute-done | bytes 294944 | tf_op jit(solution)/shard_map/ppermute | solution.py:924
  31.5 6.8 %collective-permute-done.8.refs_2_ = bf16[128,1152]{1,0:T(8,128)(2,1)} collective-permute-done((bf16[128,1152]{1,0:T(8,128)(2,1)S(1)}, bf16[128,1152]{1,0:T(8,128)(2,1)}, u32[]{:S(2)}, u32[]{:S(2)}) %collective-permute-start.8) | collective-permute-done | bytes 294944 | tf_op jit(solution)/shard_map/ppermute | solution.py:924
  40.5 1.9 collective-permute-start.12
  43.5 3.1 collective-permute-done.10
  46.6 4.6 %collective-permute-done.11 = bf16[3,32,1024]{2,1,0:T(8,128)(2,1)S(1)} collective-permute-done((bf16[3,32,1024]{2,1,0:T(8,128)(2,1)S(1)}, bf16[3,32,1024]{2,1,0:T(8,128)(2,1)S(1)}, u32[]{:S(2)}, u32[]{:S(2)}) %collective-permute-start.11) | collective-permute-done | bytes 196640 | tf_op jit(solution)/shard_map/ppermute | solution.py:906
  53.9 3.3 unpack.1
  60.7 7.7 %norm_qkv.1 = (bf16[1024,768]{1,0:T(8,128)(2,1)}, bf16[1024,1024]{1,0:T(8,128)(2,1)}, bf16[1024,1152]{1,0:T(8,128)(2,1)}) custom-call(s32[12]{0:T(128)} %concatenate.64.scalars, f32[24,1024]{1,0:T(8,128)} %get-tuple-element.304.small_ref.by_column, bf16[128,1152]{1,0:T(8,128)(2,1)} %copy-done.18, bf16[128,1152]{1,0:T(8,128)(2,1)} %copy-done.48, ...), custom_call_target="tpu_custom_call" | custom-call | flops 8000000000 | bytes 1024 | tf_op jit(solution)/shard_map/norm_qkv/pallas_call | solution.py:83
  68.5 4.3 %collective-permute-start.27 = (bf16[2,128,1024]{2,1,0:T(8,128)(2,1)}, bf16[2,128,1024]{2,1,0:T(8,128)(2,1)}, u32[]{:S(2)}, u32[]{:S(2)}) collective-permute-start(bf16[2,128,1024]{2,1,0:T(8,128)(2,1)} %collective-permute-done.16.refs_9_), channel_id=1, source_target_pairs={{0,8},{4,12},{8,16},{12,20},{16,24},{20,28},{24,0},{28,4},{1,9},{5... | collective-permute-start | bytes 1572872 | tf_op jit(solution)/shard_map/ppermute | solution.py:924
  72.8 10.4 %attention_forward.1 = bf16[1024,256]{1,0:T(8,128)(2,1)} custom-call(bf16[1024,768]{1,0:T(8,128)(2,1)} %get-tuple-element.292.q_ref.k_ref.v_ref, bf16[1024,768]{1,0:T(8,128)(2,1)} %get-tuple-element.292.q_ref.k_ref.v_ref, bf16[1024,768]{1,0:T(8,128)(2,1)} %get-tuple-element.292.q_ref.k_ref.v_ref), custom_call_target="tpu_custom_call" | custom-call | flops 10000000000 | bytes 1024 | tf_op jit(solution)/shard_map/attention_forward/pallas_call | solution.py:83
  83.3 1.8 dynamic-slice_bitcast_fusion.8
  91.2 2.4 collective-permute-done.21.refs_2_.refs_6_
  94.3 3.9 hidden.1
  99.9 1.9 collective-permute-start.26
  102.4 2.7 maximum_convert_fusion.1
  108.4 5.0 %collective-permute-done.24.refs_1_ = bf16[256,1024]{1,0:T(8,128)(2,1)S(1)} collective-permute-done((bf16[256,1024]{1,0:T(8,128)(2,1)}, bf16[256,1024]{1,0:T(8,128)(2,1)S(1)}, u32[]{:S(2)}, u32[]{:S(2)}) %collective-permute-start.24) | collective-permute-done | bytes 524320 | tf_op jit(solution)/shard_map/ppermute | solution.py:906
  113.4 9.5 %collective-permute-done.25.refs_2_ = bf16[256,1024]{1,0:T(8,128)(2,1)} collective-permute-done((bf16[256,1024]{1,0:T(8,128)(2,1)}, bf16[256,1024]{1,0:T(8,128)(2,1)}, u32[]{:S(2)}, u32[]{:S(2)}) %collective-permute-start.25) | collective-permute-done | bytes 524320 | tf_op jit(solution)/shard_map/ppermute | solution.py:906
  124.9 8.9 %collective-permute-done.30.refs_10_ = bf16[4,128,1024]{2,1,0:T(8,128)(2,1)} collective-permute-done((bf16[4,128,1024]{2,1,0:T(8,128)(2,1)}, bf16[4,128,1024]{2,1,0:T(8,128)(2,1)}, u32[]{:S(2)}, u32[]{:S(2)}) %collective-permute-start.30) | collective-permute-done | bytes 1048608 | tf_op jit(solution)/shard_map/ppermute | solution.py:924
  134.9 2.2 collective-permute-done.28.refs_5_
  137.2 7.2 %collective-permute-done.29.refs_6_ = bf16[256,1024]{1,0:T(8,128)(2,1)S(1)} collective-permute-done((bf16[256,1024]{1,0:T(8,128)(2,1)S(1)}, bf16[256,1024]{1,0:T(8,128)(2,1)S(1)}, u32[]{:S(2)}, u32[]{:S(2)}) %collective-permute-start.29) | collective-permute-done | bytes 524320 | tf_op jit(solution)/shard_map/ppermute | solution.py:906
  151.0 23.8 %mlp.3 = (f32[1024,1024]{1,0:T(8,128)}, f32[1024,1024]{1,0:T(8,128)}, f32[1024,1]{1,0:T(8,128)}, f32[1,1024]{1,0:T(1,128)}, bf16[4,2,128,1024]{3,2,1,0:T(8,128)(2,1)}, /*index=5*/bf16[4,2,128,1024]{3,2,1,0:T(8,128)(2,1)}) custom-call(s32[12]{0:T(128)} %gate.2.scalars.refs_0_, bf16[1024,128]{1,0:T(8,128)(2,1)} %get-tuple-element.307.small_ref.by_row, ...), custom_call_target="tpu_custom_call" | custom-call | flops 20000000000 | bytes 1024 | tf_op jit(solution)/shard_map/mlp/pallas_call | solution.py:83
  183.1 18.2 %mlp.4 = (f32[640,1024]{1,0:T(8,128)}, f32[640,1024]{1,0:T(8,128)}, f32[640,1]{1,0:T(8,128)}, f32[1,1024]{1,0:T(1,128)}, bf16[4,2,128,1024]{3,2,1,0:T(8,128)(2,1)}, /*index=5*/bf16[4,2,128,1024]{3,2,1,0:T(8,128)(2,1)}) custom-call(s32[12]{0:T(128)} %gate.3.scalars, bf16[1024,128]{1,0:T(8,128)(2,1)} %get-tuple-element.307.small_ref.by_row, ...), custom_call_target="tpu_custom_call" | custom-call | flops 17999998976 | bytes 1024 | tf_op jit(solution)/shard_map/mlp/pallas_call | solution.py:83
  202.7 2.5 collective-permute-start.44
  205.2 22.9 %mlp.5 = (bf16[256,1024]{1,0:T(8,128)(2,1)}, bf16[256,1024]{1,0:T(8,128)(2,1)}, bf16[256,1024]{1,0:T(8,128)(2,1)}, bf16[256,1024]{1,0:T(8,128)(2,1)}, bf16[256,1...) custom-call(s32[12]{0:T(128)} %gate.2.scalars.refs_0_, ...), custom_call_target="tpu_custom_call" | custom-call | flops 17999998976 | bytes 1024 | tf_op jit(solution)/shard_map/mlp/pallas_call | solution.py:83
  237.1 7.7 %collective-permute-done.47.refs_1_ = bf16[256,1152]{1,0:T(8,128)(2,1)} collective-permute-done((bf16[256,1152]{1,0:T(8,128)(2,1)}, bf16[256,1152]{1,0:T(8,128)(2,1)}, u32[]{:S(2)}, u32[]{:S(2)}) %collective-permute-start.47) | collective-permute-done | bytes 589856 | tf_op jit(solution)/shard_map/ppermute | solution.py:906
  244.8 11.6 %collective-permute-done.48.refs_2_ = bf16[256,1152]{1,0:T(8,128)(2,1)} collective-permute-done((bf16[256,1152]{1,0:T(8,128)(2,1)}, bf16[256,1152]{1,0:T(8,128)(2,1)}, u32[]{:S(2)}, u32[]{:S(2)}) %collective-permute-start.48) | collective-permute-done | bytes 589856 | tf_op jit(solution)/shard_map/ppermute | solution.py:906
  258.4 3.8 collective-permute-done.50
  266.0 12.0 %middle.1 = (f32[256,1024]{1,0:T(8,128)}, f32[256,1024]{1,0:T(8,128)}, f32[8,1024]{1,0:T(8,128)}, f32[1024,128]{1,0:T(8,128)}, bf16[8,4,32,256]{3,2,1,0:T(8,128)...) custom-call(s32[4]{0:T(128)} %pad_add_fusion.scalars.order, ...), custom_call_target="tpu_custom_call" | custom-call | flops 11000000512 | bytes 1024 | tf_op jit(solution)/shard_map/middle/pallas_call | solution.py:83
  279.7 1.8 collective-permute-start.59
  281.6 2.1 fusion.1
  284.1 2.2 collective-permute-done.59.refs_3_
  286.8 1.9 collective-permute-start.61
  290.8 18.5 %attention_backward.1 = (bf16[1024,256]{1,0:T(8,128)(2,1)}, bf16[1024,256]{1,0:T(8,128)(2,1)}, bf16[1024,256]{1,0:T(8,128)(2,1)}) custom-call(s32[4]{0:T(128)} %pad_add_fusion.scalars.order, bf16[1024,768]{1,0:T(8,128)(2,1)} %get-tuple-element.292.q_ref.k_ref.v_ref, bf16[1024,768]{1,0:T(8,128)(2,1)} %get-tuple-element.292.q_ref.k_ref.v_ref, ...), custom_call_target="tpu_custom_call" | custom-call | flops 17999998976 | bytes 1024 | tf_op jit(solution)/shard_map/attention_backward/pallas_call | solution.py:83
  309.4 3.3 collective-permute-done.53
  312.6 2.1 fusion.2
  314.7 9.2 %qkv_back.1 = (bf16[256,1024]{1,0:T(8,128)(2,1)}, bf16[256,1024]{1,0:T(8,128)(2,1)}, bf16[256,1024]{1,0:T(8,128)(2,1)}, bf16[256,1024]{1,0:T(8,128)(2,1)}, bf16[...) custom-call(s32[12]{0:T(128)} %concatenate.64.scalars, ...), custom_call_target="tpu_custom_call" | custom-call | flops 8000000000 | bytes 1024 | tf_op jit(solution)/shard_map/qkv_back/pallas_call | solution.py:83
  328.1 1.9 collective-permute-start.68
  341.0 3.1 collective-permute-done.68
  349.7 16.3 %collective-permute-done.67 = bf16[128,1024]{1,0:T(8,128)(2,1)S(1)} collective-permute-done((bf16[128,1024]{1,0:T(8,128)(2,1)S(1)}, bf16[128,1024]{1,0:T(8,128)(2,1)S(1)}, u32[]{:S(2)}, u32[]{:S(2)}) %collective-permute-start.67) | collective-permute-done | bytes 262176 | tf_op jit(solution)/shard_map/ppermute | solution.py:924
  371.1 1.8 collective-permute-start.74
  375.0 4.0 final.1
  379.0 2.0 collective-permute-done.70
  382.4 7.6 %collective-permute-done.73 = bf16[32,3072]{1,0:T(8,128)(2,1)S(1)} collective-permute-done((bf16[32,3072]{1,0:T(8,128)(2,1)S(1)}, bf16[32,3072]{1,0:T(8,128)(2,1)S(1)}, u32[]{:S(2)}, u32[]{:S(2)}) %collective-permute-start.73) | collective-permute-done | bytes 196640 | tf_op jit(solution)/shard_map/ppermute | solution.py:906
  398.2 1.9 collective-permute-done.78
  404.4 1.9 collective-permute-start.82
  406.4 3.6 result.1
  (431 shorter events, 124.7 us)
Async XLA Ops:
  0.7 30.8 %collective-permute-start.5 = (bf16[256,1024]{1,0:T(8,128)(2,1)}, bf16[256,1024]{1,0:T(8,128)(2,1)}, u32[]{:S(2)}, u32[]{:S(2)}) collective-permute-start(bf16[256,1024]{1,0:T(8,128)(2,1)} %bitcast.365), channel_id=1, source_target_pairs={{0,1},{1,0},{2,3},{3,2},{4,5},{5,4},{6,7},{7,6},{8,9},{9,8},{10,11... | collective-permute-start | bytes 1572872 | tf_op jit(solution)/shard_map/ppermute | solution.py:906
  3.7 27.8 %collective-permute-start.6 = (bf16[256,1024]{1,0:T(8,128)(2,1)}, bf16[256,1024]{1,0:T(8,128)(2,1)}, u32[]{:S(2)}, u32[]{:S(2)}) collective-permute-start(bf16[256,1024]{1,0:T(8,128)(2,1)} %bitcast.366), channel_id=1, source_target_pairs={{0,2},{1,3},{2,0},{3,1},{4,6},{5,7},{6,4},{7,5},{8,10},{9,11},{10,... | collective-permute-start | bytes 1572872 | tf_op jit(solution)/shard_map/ppermute | solution.py:906
  17.7 13.8 %collective-permute-start.7 = (bf16[256,1024]{1,0:T(8,128)(2,1)}, bf16[256,1024]{1,0:T(8,128)(2,1)}, u32[]{:S(2)}, u32[]{:S(2)}) collective-permute-start(bf16[256,1024]{1,0:T(8,128)(2,1)} %bitcast.367), channel_id=1, source_target_pairs={{0,3},{1,2},{2,1},{3,0},{4,7},{5,6},{6,5},{7,4},{8,11},{9,10},{10,... | collective-permute-start | bytes 1572872 | tf_op jit(solution)/shard_map/ppermute | solution.py:906
  51.7 16.8 %collective-permute-start.16 = (bf16[2,128,1024]{2,1,0:T(8,128)(2,1)S(1)}, bf16[2,128,1024]{2,1,0:T(8,128)(2,1)}, u32[]{:S(2)}, u32[]{:S(2)}) collective-permute-start(bf16[2,128,1024]{2,1,0:T(8,128)(2,1)S(1)} %pad_maximum_fusion.3.refs_8_), channel_id=1, source_target_pairs={{0,8},{4,12},{8,16},{12,20},{16,24},{20,28},{24,0},{28,4},{1,9},{5... | collective-permute-start | bytes 1572872 | tf_op jit(solution)/shard_map/ppermute | solution.py:924
  57.2 26.0 %collective-permute-start.17 = (bf16[256,1024]{1,0:T(8,128)(2,1)}, bf16[256,1024]{1,0:T(8,128)(2,1)S(1)}, u32[]{:S(2)}, u32[]{:S(2)}) collective-permute-start(bf16[256,1024]{1,0:T(8,128)(2,1)} %get-tuple-element.294), channel_id=1, source_target_pairs={{0,1},{1,0},{2,3},{3,2},{4,5},{5,4},{6,7},{7,6},{8,9},{9,8},{10,11... | collective-permute-start | bytes 1572872 | tf_op jit(solution)/shard_map/ppermute | solution.py:906
  58.1 25.1 %collective-permute-start.18 = (bf16[256,1024]{1,0:T(8,128)(2,1)}, bf16[256,1024]{1,0:T(8,128)(2,1)S(1)}, u32[]{:S(2)}, u32[]{:S(2)}) collective-permute-start(bf16[256,1024]{1,0:T(8,128)(2,1)} %get-tuple-element.294), channel_id=1, source_target_pairs={{0,2},{1,3},{2,0},{3,1},{4,6},{5,7},{6,4},{7,5},{8,10},{9,11},{10,... | collective-permute-start | bytes 1572872 | tf_op jit(solution)/shard_map/ppermute | solution.py:906
  58.9 24.3 %collective-permute-start.19 = (bf16[256,1024]{1,0:T(8,128)(2,1)}, bf16[256,1024]{1,0:T(8,128)(2,1)S(1)}, u32[]{:S(2)}, u32[]{:S(2)}) collective-permute-start(bf16[256,1024]{1,0:T(8,128)(2,1)} %get-tuple-element.294), channel_id=1, source_target_pairs={{0,3},{1,2},{2,1},{3,0},{4,7},{5,6},{6,5},{7,4},{8,11},{9,10},{10,... | collective-permute-start | bytes 1572872 | tf_op jit(solution)/shard_map/ppermute | solution.py:906
  60.7 37.5 %collective-permute-start.23 = (bf16[4,128,1024]{2,1,0:T(8,128)(2,1)S(1)}, bf16[4,128,1024]{2,1,0:T(8,128)(2,1)S(1)}, u32[]{:S(2)}, u32[]{:S(2)}) collective-permute-start(bf16[4,128,1024]{2,1,0:T(8,128)(2,1)S(1)} %pad_maximum_fusion.refs_8_), channel_id=1, source_target_pairs={{0,8},{4,12},{8,16},{12,20},{16,24},{20,28},{24,0},{28,4},{1,9},{5... | collective-permute-start | bytes 3145736 | tf_op jit(solution)/shard_map/ppermute | solution.py:924
  68.5 37.8 %collective-permute-start.27 = (bf16[2,128,1024]{2,1,0:T(8,128)(2,1)}, bf16[2,128,1024]{2,1,0:T(8,128)(2,1)}, u32[]{:S(2)}, u32[]{:S(2)}) collective-permute-start(bf16[2,128,1024]{2,1,0:T(8,128)(2,1)} %collective-permute-done.16.refs_9_), channel_id=1, source_target_pairs={{0,8},{4,12},{8,16},{12,20},{16,24},{20,28},{24,0},{28,4},{1,9},{5... | collective-permute-start | bytes 1572872 | tf_op jit(solution)/shard_map/ppermute | solution.py:924
  98.2 15.1 %collective-permute-start.24 = (bf16[256,1024]{1,0:T(8,128)(2,1)}, bf16[256,1024]{1,0:T(8,128)(2,1)S(1)}, u32[]{:S(2)}, u32[]{:S(2)}) collective-permute-start(bf16[256,1024]{1,0:T(8,128)(2,1)} %get-tuple-element.309.refs_0_), channel_id=1, source_target_pairs={{0,1},{1,0},{2,3},{3,2},{4,5},{5,4},{6,7},{7,6},{8,9},{9,8},{10,11... | collective-permute-start | bytes 1572872 | tf_op jit(solution)/shard_map/ppermute | solution.py:906
  99.3 23.5 %collective-permute-start.25 = (bf16[256,1024]{1,0:T(8,128)(2,1)}, bf16[256,1024]{1,0:T(8,128)(2,1)}, u32[]{:S(2)}, u32[]{:S(2)}) collective-permute-start(bf16[256,1024]{1,0:T(8,128)(2,1)} %get-tuple-element.309.refs_0_), channel_id=1, source_target_pairs={{0,2},{1,3},{2,0},{3,1},{4,6},{5,7},{6,4},{7,5},{8,10},{9,11},{10,... | collective-permute-start | bytes 1572872 | tf_op jit(solution)/shard_map/ppermute | solution.py:906
  99.9 22.9 %collective-permute-start.26 = (bf16[256,1024]{1,0:T(8,128)(2,1)}, bf16[256,1024]{1,0:T(8,128)(2,1)}, u32[]{:S(2)}, u32[]{:S(2)}) collective-permute-start(bf16[256,1024]{1,0:T(8,128)(2,1)} %get-tuple-element.309.refs_0_), channel_id=1, source_target_pairs={{0,3},{1,2},{2,1},{3,0},{4,7},{5,6},{6,5},{7,4},{8,11},{9,10},{10,... | collective-permute-start | bytes 1572872 | tf_op jit(solution)/shard_map/ppermute | solution.py:906
  105.7 28.2 %collective-permute-start.30 = (bf16[4,128,1024]{2,1,0:T(8,128)(2,1)}, bf16[4,128,1024]{2,1,0:T(8,128)(2,1)}, u32[]{:S(2)}, u32[]{:S(2)}) collective-permute-start(bf16[4,128,1024]{2,1,0:T(8,128)(2,1)} %copy-done.32), channel_id=1, source_target_pairs={{0,8},{4,12},{8,16},{12,20},{16,24},{20,28},{24,0},{28,4},{1,9},{5... | collective-permute-start | bytes 3145736 | tf_op jit(solution)/shard_map/ppermute | solution.py:924
  122.8 14.3 %collective-permute-start.28 = (bf16[256,1024]{1,0:T(8,128)(2,1)S(1)}, bf16[256,1024]{1,0:T(8,128)(2,1)S(1)}, u32[]{:S(2)}, u32[]{:S(2)}) collective-permute-start(bf16[256,1024]{1,0:T(8,128)(2,1)S(1)} %convolution_convert_fusion.refs_4_), channel_id=1, source_target_pairs={{0,1},{1,0},{2,3},{3,2},{4,5},{5,4},{6,7},{7,6},{8,9},{9,8},{10,11... | collective-permute-start | bytes 1572872 | tf_op jit(solution)/shard_map/ppermute | solution.py:906
  123.9 20.5 %collective-permute-start.29 = (bf16[256,1024]{1,0:T(8,128)(2,1)S(1)}, bf16[256,1024]{1,0:T(8,128)(2,1)S(1)}, u32[]{:S(2)}, u32[]{:S(2)}) collective-permute-start(bf16[256,1024]{1,0:T(8,128)(2,1)S(1)} %convolution_convert_fusion.refs_4_), channel_id=1, source_target_pairs={{0,2},{1,3},{2,0},{3,1},{4,6},{5,7},{6,4},{7,5},{8,10},{9,11},{10,... | collective-permute-start | bytes 1572872 | tf_op jit(solution)/shard_map/ppermute | solution.py:906
  124.6 19.8 %collective-permute-start.32 = (bf16[2,128,1024]{2,1,0:T(8,128)(2,1)}, bf16[2,128,1024]{2,1,0:T(8,128)(2,1)S(1)}, u32[]{:S(2)}, u32[]{:S(2)}) collective-permute-start(bf16[2,128,1024]{2,1,0:T(8,128)(2,1)} %collective-permute-done.27.refs_1_.refs_10_), channel_id=1, source_target_pairs={{0,8},{4,12},{8,16},{12,20},{16,24},{20,28},{24,0},{28,4},{1,9},{5... | collective-permute-start | bytes 1572872 | tf_op jit(solution)/shard_map/ppermute | solution.py:924
  147.2 27.7 %collective-permute-start.38 = (bf16[4,128,1024]{2,1,0:T(8,128)(2,1)}, bf16[4,128,1024]{2,1,0:T(8,128)(2,1)}, u32[]{:S(2)}, u32[]{:S(2)}) collective-permute-start(bf16[4,128,1024]{2,1,0:T(8,128)(2,1)} %collective-permute-done.30.refs_10_), channel_id=1, source_target_pairs={{0,8},{4,12},{8,16},{12,20},{16,24},{20,28},{24,0},{28,4},{1,9},{5... | collective-permute-start | bytes 3145736 | tf_op jit(solution)/shard_map/ppermute | solution.py:924
  150.0 25.0 %collective-permute-start.39 = (bf16[4,128,1024]{2,1,0:T(8,128)(2,1)S(1)}, bf16[4,128,1024]{2,1,0:T(8,128)(2,1)S(1)}, u32[]{:S(2)}, u32[]{:S(2)}) collective-permute-start(bf16[4,128,1024]{2,1,0:T(8,128)(2,1)S(1)} %pad_maximum_fusion.refs_8_), channel_id=1, source_target_pairs={{0,4},{4,0},{8,12},{12,8},{16,20},{20,16},{24,28},{28,24},{1,5},{5... | collective-permute-start | bytes 3145736 | tf_op jit(solution)/shard_map/ppermute | solution.py:927
  150.2 24.8 %collective-permute-start.40 = (bf16[4,128,1024]{2,1,0:T(8,128)(2,1)}, bf16[4,128,1024]{2,1,0:T(8,128)(2,1)S(1)}, u32[]{:S(2)}, u32[]{:S(2)}) collective-permute-start(bf16[4,128,1024]{2,1,0:T(8,128)(2,1)} %copy-done.32), channel_id=1, source_target_pairs={{0,4},{4,0},{8,12},{12,8},{16,20},{20,16},{24,28},{28,24},{1,5},{5... | collective-permute-start | bytes 3145736 | tf_op jit(solution)/shard_map/ppermute | solution.py:927
  150.6 24.4 %collective-permute-start.41 = (bf16[4,128,1024]{2,1,0:T(8,128)(2,1)}, bf16[4,128,1024]{2,1,0:T(8,128)(2,1)S(1)}, u32[]{:S(2)}, u32[]{:S(2)}) collective-permute-start(bf16[4,128,1024]{2,1,0:T(8,128)(2,1)} %collective-permute-done.30.refs_10_), channel_id=1, source_target_pairs={{0,4},{4,0},{8,12},{12,8},{16,20},{20,16},{24,28},{28,24},{1,5},{5... | collective-permute-start | bytes 3145736 | tf_op jit(solution)/shard_map/ppermute | solution.py:927
  180.6 20.8 %collective-permute-start.42 = (bf16[2,128,1024]{2,1,0:T(8,128)(2,1)S(1)}, bf16[2,128,1024]{2,1,0:T(8,128)(2,1)S(1)}, u32[]{:S(2)}, u32[]{:S(2)}) collective-permute-start(bf16[2,128,1024]{2,1,0:T(8,128)(2,1)S(1)} %fusion.6), channel_id=1, source_target_pairs={{0,8},{4,12},{8,16},{12,20},{16,24},{20,28},{24,0},{28,4},{1,9},{5... | collective-permute-start | bytes 1572872 | tf_op jit(solution)/shard_map/ppermute | solution.py:924
  201.3 30.8 %collective-permute-start.45 = (bf16[4,2,128,1024]{3,2,1,0:T(8,128)(2,1)}, bf16[4,2,128,1024]{3,2,1,0:T(8,128)(2,1)S(1)}, u32[]{:S(2)}, u32[]{:S(2)}) collective-permute-start(bf16[4,2,128,1024]{3,2,1,0:T(8,128)(2,1)} %get-tuple-element.358), channel_id=1, source_target_pairs={{0,4},{4,0},{8,12},{12,8},{16,20},{20,16},{24,28},{28,24},{1,5},{5... | collective-permute-start | bytes 6291464 | tf_op jit(solution)/shard_map/ppermute | solution.py:927
  202.7 28.0 %collective-permute-start.44 = (bf16[2,128,1024]{2,1,0:T(8,128)(2,1)S(1)}, bf16[2,128,1024]{2,1,0:T(8,128)(2,1)S(1)}, u32[]{:S(2)}, u32[]{:S(2)}) collective-permute-start(bf16[2,128,1024]{2,1,0:T(8,128)(2,1)S(1)} %fusion.5), channel_id=1, source_target_pairs={{0,8},{4,12},{8,16},{12,20},{16,24},{20,28},{24,0},{28,4},{1,9},{5... | collective-permute-start | bytes 1572872 | tf_op jit(solution)/shard_map/ppermute | solution.py:924
  228.2 16.6 %collective-permute-start.47 = (bf16[256,1152]{1,0:T(8,128)(2,1)}, bf16[256,1152]{1,0:T(8,128)(2,1)}, u32[]{:S(2)}, u32[]{:S(2)}) collective-permute-start(bf16[256,1152]{1,0:T(8,128)(2,1)} %get-tuple-element.363), channel_id=1, source_target_pairs={{0,1},{1,0},{2,3},{3,2},{4,5},{5,4},{6,7},{7,6},{8,9},{9,8},{10,11... | collective-permute-start | bytes 1769480 | tf_op jit(solution)/shard_map/ppermute | solution.py:906
  229.0 27.3 %collective-permute-start.48 = (bf16[256,1152]{1,0:T(8,128)(2,1)}, bf16[256,1152]{1,0:T(8,128)(2,1)}, u32[]{:S(2)}, u32[]{:S(2)}) collective-permute-start(bf16[256,1152]{1,0:T(8,128)(2,1)} %get-tuple-element.364), channel_id=1, source_target_pairs={{0,2},{1,3},{2,0},{3,1},{4,6},{5,7},{6,4},{7,5},{8,10},{9,11},{10,... | collective-permute-start | bytes 1769480 | tf_op jit(solution)/shard_map/ppermute | solution.py:906
  233.9 23.3 %collective-permute-start.49 = (bf16[256,1152]{1,0:T(8,128)(2,1)}, bf16[256,1152]{1,0:T(8,128)(2,1)}, u32[]{:S(2)}, u32[]{:S(2)}) collective-permute-start(bf16[256,1152]{1,0:T(8,128)(2,1)} %get-tuple-element.365), channel_id=1, source_target_pairs={{0,3},{1,2},{2,1},{3,0},{4,7},{5,6},{6,5},{7,4},{8,11},{9,10},{10,... | collective-permute-start | bytes 1769480 | tf_op jit(solution)/shard_map/ppermute | solution.py:906
  236.0 21.9 %collective-permute-start.46 = (bf16[2,128,1024]{2,1,0:T(8,128)(2,1)S(1)}, bf16[2,128,1024]{2,1,0:T(8,128)(2,1)S(1)}, u32[]{:S(2)}, u32[]{:S(2)}) collective-permute-start(bf16[2,128,1024]{2,1,0:T(8,128)(2,1)S(1)} %fusion.4), channel_id=1, source_target_pairs={{0,8},{4,12},{8,16},{12,20},{16,24},{20,28},{24,0},{28,4},{1,9},{5... | collective-permute-start | bytes 1572872 | tf_op jit(solution)/shard_map/ppermute | solution.py:924
  236.9 25.3 %collective-permute-start.50 = (bf16[2,128,1024]{2,1,0:T(8,128)(2,1)S(1)}, bf16[2,128,1024]{2,1,0:T(8,128)(2,1)S(1)}, u32[]{:S(2)}, u32[]{:S(2)}) collective-permute-start(bf16[2,128,1024]{2,1,0:T(8,128)(2,1)S(1)} %fusion.7), channel_id=1, source_target_pairs={{0,8},{4,12},{8,16},{12,20},{16,24},{20,28},{24,0},{28,4},{1,9},{5... | collective-permute-start | bytes 1572872 | tf_op jit(solution)/shard_map/ppermute | solution.py:924
  257.2 32.5 %collective-permute-start.51 = (bf16[4,2,128,1024]{3,2,1,0:T(8,128)(2,1)}, bf16[4,2,128,1024]{3,2,1,0:T(8,128)(2,1)S(1)}, u32[]{:S(2)}, u32[]{:S(2)}) collective-permute-start(bf16[4,2,128,1024]{3,2,1,0:T(8,128)(2,1)} %get-tuple-element.393), channel_id=1, source_target_pairs={{0,4},{4,0},{8,12},{12,8},{16,20},{20,16},{24,28},{28,24},{1,5},{5... | collective-permute-start | bytes 6291464 | tf_op jit(solution)/shard_map/ppermute | solution.py:927
  263.5 14.5 %collective-permute-start.55 = (bf16[256,1024]{1,0:T(8,128)(2,1)}, bf16[256,1024]{1,0:T(8,128)(2,1)}, u32[]{:S(2)}, u32[]{:S(2)}) collective-permute-start(bf16[256,1024]{1,0:T(8,128)(2,1)} %get-tuple-element.403), channel_id=1, source_target_pairs={{0,1},{1,0},{2,3},{3,2},{4,5},{5,4},{6,7},{7,6},{8,9},{9,8},{10,11... | collective-permute-start | bytes 1572872 | tf_op jit(solution)/shard_map/ppermute | solution.py:906
  266.0 15.6 %collective-permute-start.52 = (bf16[2,128,1024]{2,1,0:T(8,128)(2,1)S(1)}, bf16[2,128,1024]{2,1,0:T(8,128)(2,1)S(1)}, u32[]{:S(2)}, u32[]{:S(2)}) collective-permute-start(bf16[2,128,1024]{2,1,0:T(8,128)(2,1)S(1)} %fusion.3), channel_id=1, source_target_pairs={{0,8},{4,12},{8,16},{12,20},{16,24},{20,28},{24,0},{28,4},{1,9},{5... | collective-permute-start | bytes 1572872 | tf_op jit(solution)/shard_map/ppermute | solution.py:924
  286.2 28.5 %collective-permute-start.60 = (bf16[1024,256]{1,0:T(8,128)(2,1)}, bf16[1024,256]{1,0:T(8,128)(2,1)}, u32[]{:S(2)}, u32[]{:S(2)}) collective-permute-start(bf16[1024,256]{1,0:T(8,128)(2,1)} %bitcast.373), channel_id=1, source_target_pairs={{0,1},{1,0},{2,3},{3,2},{4,5},{5,4},{6,7},{7,6},{8,9},{9,8},{10,11... | collective-permute-start | bytes 1572872 | tf_op jit(solution)/shard_map/ppermute | solution.py:906
  286.8 28.0 %collective-permute-start.61 = (bf16[1024,256]{1,0:T(8,128)(2,1)}, bf16[1024,256]{1,0:T(8,128)(2,1)}, u32[]{:S(2)}, u32[]{:S(2)}) collective-permute-start(bf16[1024,256]{1,0:T(8,128)(2,1)} %bitcast.372), channel_id=1, source_target_pairs={{0,2},{1,3},{2,0},{3,1},{4,6},{5,7},{6,4},{7,5},{8,10},{9,11},{10,... | collective-permute-start | bytes 1572872 | tf_op jit(solution)/shard_map/ppermute | solution.py:906
  288.7 26.1 %collective-permute-start.62 = (bf16[1024,256]{1,0:T(8,128)(2,1)}, bf16[1024,256]{1,0:T(8,128)(2,1)}, u32[]{:S(2)}, u32[]{:S(2)}) collective-permute-start(bf16[1024,256]{1,0:T(8,128)(2,1)} %bitcast.371), channel_id=1, source_target_pairs={{0,3},{1,2},{2,1},{3,0},{4,7},{5,6},{6,5},{7,4},{8,11},{9,10},{10,... | collective-permute-start | bytes 1572872 | tf_op jit(solution)/shard_map/ppermute | solution.py:906
  289.9 19.4 %collective-permute-start.54 = (bf16[2,128,1024]{2,1,0:T(8,128)(2,1)}, bf16[2,128,1024]{2,1,0:T(8,128)(2,1)S(1)}, u32[]{:S(2)}, u32[]{:S(2)}) collective-permute-start(bf16[2,128,1024]{2,1,0:T(8,128)(2,1)} %fusion.1), channel_id=1, source_target_pairs={{0,8},{4,12},{8,16},{12,20},{16,24},{20,28},{24,0},{28,4},{1,9},{5... | collective-permute-start | bytes 1572872 | tf_op jit(solution)/shard_map/ppermute | solution.py:924
  290.0 22.6 %collective-permute-start.53 = (bf16[2,128,1024]{2,1,0:T(8,128)(2,1)S(1)}, bf16[2,128,1024]{2,1,0:T(8,128)(2,1)}, u32[]{:S(2)}, u32[]{:S(2)}) collective-permute-start(bf16[2,128,1024]{2,1,0:T(8,128)(2,1)S(1)} %fusion.8), channel_id=1, source_target_pairs={{0,8},{4,12},{8,16},{12,20},{16,24},{20,28},{24,0},{28,4},{1,9},{5... | collective-permute-start | bytes 1572872 | tf_op jit(solution)/shard_map/ppermute | solution.py:924
  324.0 17.0 %collective-permute-start.63 = (bf16[4,128,1024]{2,1,0:T(8,128)(2,1)}, bf16[4,128,1024]{2,1,0:T(8,128)(2,1)}, u32[]{:S(2)}, u32[]{:S(2)}) collective-permute-start(bf16[4,128,1024]{2,1,0:T(8,128)(2,1)} %get-tuple-element.441), channel_id=1, source_target_pairs={{0,4},{4,0},{8,12},{12,8},{16,20},{20,16},{24,28},{28,24},{1,5},{5... | collective-permute-start | bytes 3145736 | tf_op jit(solution)/shard_map/ppermute | solution.py:927
  325.6 14.8 %collective-permute-start.64 = (bf16[256,1024]{1,0:T(8,128)(2,1)}, bf16[256,1024]{1,0:T(8,128)(2,1)}, u32[]{:S(2)}, u32[]{:S(2)}) collective-permute-start(bf16[256,1024]{1,0:T(8,128)(2,1)} %get-tuple-element.443), channel_id=1, source_target_pairs={{0,1},{1,0},{2,3},{3,2},{4,5},{5,4},{6,7},{7,6},{8,9},{9,8},{10,11... | collective-permute-start | bytes 1572872 | tf_op jit(solution)/shard_map/ppermute | solution.py:906
  326.7 14.3 %collective-permute-start.65 = (bf16[256,1024]{1,0:T(8,128)(2,1)}, bf16[256,1024]{1,0:T(8,128)(2,1)}, u32[]{:S(2)}, u32[]{:S(2)}) collective-permute-start(bf16[256,1024]{1,0:T(8,128)(2,1)} %get-tuple-element.444), channel_id=1, source_target_pairs={{0,2},{1,3},{2,0},{3,1},{4,6},{5,7},{6,4},{7,5},{8,10},{9,11},{10,... | collective-permute-start | bytes 1572872 | tf_op jit(solution)/shard_map/ppermute | solution.py:906
  328.1 16.0 %collective-permute-start.68 = (bf16[2,128,1024]{2,1,0:T(8,128)(2,1)}, bf16[2,128,1024]{2,1,0:T(8,128)(2,1)}, u32[]{:S(2)}, u32[]{:S(2)}) collective-permute-start(bf16[2,128,1024]{2,1,0:T(8,128)(2,1)} %fusion.2), channel_id=1, source_target_pairs={{0,8},{4,12},{8,16},{12,20},{16,24},{20,28},{24,0},{28,4},{1,9},{5... | collective-permute-start | bytes 1572872 | tf_op jit(solution)/shard_map/ppermute | solution.py:924
  345.7 21.4 %collective-permute-start.69 = (bf16[2,128,1024]{2,1,0:T(8,128)(2,1)S(1)}, bf16[2,128,1024]{2,1,0:T(8,128)(2,1)S(1)}, u32[]{:S(2)}, u32[]{:S(2)}) collective-permute-start(bf16[2,128,1024]{2,1,0:T(8,128)(2,1)S(1)} %fusion), channel_id=1, source_target_pairs={{0,8},{4,12},{8,16},{12,20},{16,24},{20,28},{24,0},{28,4},{1,9},{5... | collective-permute-start | bytes 1572872 | tf_op jit(solution)/shard_map/ppermute | solution.py:924
  346.8 19.2 %collective-permute-start.67 = (bf16[128,1024]{1,0:T(8,128)(2,1)S(1)}, bf16[128,1024]{1,0:T(8,128)(2,1)S(1)}, u32[]{:S(2)}, u32[]{:S(2)}) collective-permute-start(bf16[128,1024]{1,0:T(8,128)(2,1)S(1)} %fusion.12), channel_id=1, source_target_pairs={{0,8},{4,12},{8,16},{12,20},{16,24},{20,28},{24,0},{28,4},{1,9},{5... | collective-permute-start | bytes 786440 | tf_op jit(solution)/shard_map/ppermute | solution.py:924
  348.5 20.1 %collective-permute-start.66 = (bf16[256,1024]{1,0:T(8,128)(2,1)S(1)}, bf16[256,1024]{1,0:T(8,128)(2,1)S(1)}, u32[]{:S(2)}, u32[]{:S(2)}) collective-permute-start(bf16[256,1024]{1,0:T(8,128)(2,1)S(1)} %copy-done.41), channel_id=1, source_target_pairs={{0,3},{1,2},{2,1},{3,0},{4,7},{5,6},{6,5},{7,4},{8,11},{9,10},{10,... | collective-permute-start | bytes 1572872 | tf_op jit(solution)/shard_map/ppermute | solution.py:906
  369.8 20.1 %collective-permute-start.73 = (bf16[32,3072]{1,0:T(8,128)(2,1)S(1)}, bf16[32,3072]{1,0:T(8,128)(2,1)S(1)}, u32[]{:S(2)}, u32[]{:S(2)}) collective-permute-start(bf16[32,3072]{1,0:T(8,128)(2,1)S(1)} %get-tuple-element.479), channel_id=1, source_target_pairs={{0,2},{1,3},{2,0},{3,1},{4,6},{5,7},{6,4},{7,5},{8,10},{9,11},{10,... | collective-permute-start | bytes 589832 | tf_op jit(solution)/shard_map/ppermute | solution.py:906
  371.1 18.9 %collective-permute-start.74 = (bf16[32,3072]{1,0:T(8,128)(2,1)S(1)}, bf16[32,3072]{1,0:T(8,128)(2,1)S(1)}, u32[]{:S(2)}, u32[]{:S(2)}) collective-permute-start(bf16[32,3072]{1,0:T(8,128)(2,1)S(1)} %get-tuple-element.480), channel_id=1, source_target_pairs={{0,3},{1,2},{2,1},{3,0},{4,7},{5,6},{6,5},{7,4},{8,11},{9,10},{10,... | collective-permute-start | bytes 589832 | tf_op jit(solution)/shard_map/ppermute | solution.py:906
  372.9 19.9 %collective-permute-start.75 = (bf16[256,1024]{1,0:T(8,128)(2,1)}, bf16[256,1024]{1,0:T(8,128)(2,1)}, u32[]{:S(2)}, u32[]{:S(2)}) collective-permute-start(bf16[256,1024]{1,0:T(8,128)(2,1)} %get-tuple-element.485), channel_id=1, source_target_pairs={{0,3},{1,2},{2,1},{3,0},{4,7},{5,6},{6,5},{7,4},{8,11},{9,10},{10,... | collective-permute-start | bytes 1572872 | tf_op jit(solution)/shard_map/ppermute | solution.py:906
  402.3 14.4 %collective-permute-start.83 = (bf16[32,768]{1,0:T(8,128)(2,1)S(1)}, bf16[32,768]{1,0:T(8,128)(2,1)S(1)}, u32[]{:S(2)}, u32[]{:S(2)}) collective-permute-start(bf16[32,768]{1,0:T(8,128)(2,1)S(1)} %get-tuple-element.629), channel_id=1, source_target_pairs={{0,1},{1,0},{2,3},{3,2},{4,5},{5,4},{6,7},{7,6},{8,9},{9,8},{10,11... | collective-permute-start | bytes 147464 | tf_op jit(solution)/shard_map/ppermute | solution.py:906
  402.8 13.9 %collective-permute-start.84 = (bf16[32,768]{1,0:T(8,128)(2,1)S(1)}, bf16[32,768]{1,0:T(8,128)(2,1)S(1)}, u32[]{:S(2)}, u32[]{:S(2)}) collective-permute-start(bf16[32,768]{1,0:T(8,128)(2,1)S(1)} %get-tuple-element.628), channel_id=1, source_target_pairs={{0,2},{1,3},{2,0},{3,1},{4,6},{5,7},{6,4},{7,5},{8,10},{9,11},{10,... | collective-permute-start | bytes 147464 | tf_op jit(solution)/shard_map/ppermute | solution.py:906
  (96 other events, 953.2 us)

commit v4 on v3

--- a/solution.py
+++ b/solution.py
@@ -15,21 +15,9 @@
 f32 = jnp.float32
 bf16 = jnp.bfloat16
 
-ROUTER, MIX, GAIN_ONE, SHIFT_ONE, QV, OUT_BIAS, GAIN_TWO, SHIFT_TWO, DOWN_BIAS, EXPERT_DOWN, COUNT = (
-    0,
-    2,
-    4,
-    5,
-    6,
-    8,
-    9,
-    10,
-    11,
-    12,
-    14,
-)
-UP_BIAS = 15
-SMALL_ROWS = 24
+ROUTER, MIX, GAIN_ONE, SHIFT_ONE, QV, OUT_BIAS, GAIN_TWO, SHIFT_TWO = 0, 2, 12, 13, 14, 16, 17, 18
+DOWN_BIAS, EXPERT_DOWN, COUNT, UP_BIAS = 19, 20, 22, 23
+SMALL_ROWS = 32
 
 anywhere = pl.BlockSpec(memory_space=pl.ANY)
 inside = pl.BlockSpec(memory_space=pltpu.VMEM)
@@ -633,9 +621,9 @@
 ):
     gx, pieces = refs[:ctx], refs[ctx : 2 * ctx]
     outs = refs[2 * ctx :]
-    base_ref, grad_hidden_ref, rows_ref, router_ref = outs[:4]
-    out_grads, grad_pieces = outs[4 : 4 + ctx], outs[4 + ctx : 4 + 2 * ctx]
-    out_all, sems = outs[4 + 2 * ctx :]
+    base_ref, grad_hidden_ref, rows_ref = outs[:3]
+    out_grads, grad_pieces = outs[3 : 3 + ctx], outs[3 + ctx : 3 + 2 * ctx]
+    out_all, sems = outs[3 + 2 * ctx :]
     rows, width = hidden_ref.shape
     own = pieces[0].shape[1]
     unsort = unsort_ref[...]
@@ -679,12 +667,12 @@
     columns += [mix[i] * (grad_mix[i] - mean_mix) for i in range(2)]
     logit_grads = jnp.zeros((rows, LANES), f32)
     for i, column in enumerate(columns):
-        logit_grads = jnp.where(lane == i, column, logit_grads)
-    split = three_parts(logit_grads)
-    weights = by_row[...]
-    for part in split:
-        grad_norm = grad_norm + right_product(part, weights)
-    router_ref[...] = sum(left_product(norm, part) for part in split)
+        logit_grads = jnp.where((lane % 4 == i) & (lane < 12), column, logit_grads)
+    high, middle, rest = [part.astype(f32) for part in three_parts(logit_grads)]
+    split = jnp.where(lane < 4, high, jnp.where(lane < 8, middle, rest)).astype(bf16)
+    grad_norm = grad_norm + right_product(split, by_row[...])
+    small_grads = left_product(split, norm)
+    small_grads = small_grads[0:4] + (small_grads[4:8] + small_grads[8:12])
     grad_dense = (grad_out * mix[0]).astype(bf16).astype(f32)
     grad_moe = (grad_out * branch).astype(bf16).astype(f32)
     normed, inverse = layer_stats(hidden)
@@ -703,9 +691,8 @@
         total(grad_dense),
         total(grad_moe * hot[0]),
         total(grad_moe * hot[1]),
-        jnp.zeros((2, width), f32),
     ]
-    rows_ref[...] = jnp.concatenate(sums, 0)
+    rows_ref[...] = jnp.concatenate(sums + [small_grads, jnp.zeros((6, width), f32)], 0)
     for i, (piece, target) in enumerate(zip(pieces, grad_pieces)):
         span = aligned(scalars[i], own)
         target[...] = right_product(low, out_ref[span, :]).astype(bf16)
@@ -740,12 +727,11 @@
         [
             ((rows, width), f32),
             ((rows, width), f32),
-            ((8, width), f32),
-            ((width, LANES), f32),
+            ((16, width), f32),
         ]
         + [((dp, ctx, width // (dp * ctx), own), bf16)] * ctx
         + [((rows, own), bf16)] * ctx,
-        [inside] * 4 + [anywhere] * ctx + [inside] * ctx,
+        [inside] * 3 + [anywhere] * ctx + [inside] * ctx,
         [
             pltpu.VMEM((dp, ctx, ctx, width // (dp * ctx), own), bf16),
             pltpu.SemaphoreType.DMA((ctx,)),
@@ -788,7 +774,11 @@
             for i in range(dp)
         ]
     )
-    bias_ref[...] = jnp.sum(grad[...].astype(f32), 0, keepdims=True)
+    bias = jnp.sum(grad[...].astype(f32), 0, keepdims=True)
+    here = lax.broadcasted_iota(jnp.int32, (1, width), 1) // own == scalars[dp]
+    for row, at in enumerate((0, 2 * own)):
+        spread = jnp.concatenate([bias[:, at : at + own]] * ctx, 1)
+        bias_ref[row : row + 1, :] = jnp.where(here, spread, 0.0)
     wait_all(sent + saved)
 
 
@@ -802,7 +792,7 @@
         8,
         [scalars, norm] + list(grads) + [weight] + list(out_pieces),
         [scalar] + [inside] * (5 + ctx),
-        [((rows, width), bf16)] * ctx + [half, half, ((1, 3 * own), f32)],
+        [((rows, width), bf16)] * ctx + [half, half, ((2, width), f32)],
         [anywhere] * (ctx + 2) + [inside],
         [
             pltpu.VMEM((length, 3 * own), bf16),
@@ -1002,8 +992,7 @@
 
     small = jnp.concatenate(
         [
-            router_weight,
-            mix_weight,
+            jnp.concatenate([router_weight, mix_weight] * 3, 1),
             column(ln1_gain),
             column(ln1_bias),
             column(qv_bias),
@@ -1169,7 +1158,7 @@
     result_pieces = [result_sent[0]] + [swap(result_sent[s], s) for s in shifts[:2]]
 
     middle_peers, sum_dense.arrived = sync(peers, sum_dense.arrived)
-    base, grad_hidden, middle_rows, router_grad, *rest = make_middle(
+    base, grad_hidden, middle_rows, *rest = make_middle(
         pin(middle_peers, sum_first),
         by_row,
         by_column,
@@ -1203,14 +1192,17 @@
     )
     sum_last = Scatter(last_mine, last_other)
     norm_pieces = [norm_grads[0]] + [swap(norm_grads[s], s) for s in shifts[:2]]
-    norm_pieces, late_grads, grad_b_qkv = sync(norm_pieces, list(norm_grads[3:]), grad_b_qkv)
-    norm_pieces += [swap(piece, s) for piece, s in zip(late_grads, shifts[2:])]
-    grad_b_qkv = sum_second.move(sum_last.move(grad_b_qkv))
+    late_pieces = [swap(norm_grads[s], s) for s in shifts[2:]]
+    grad_b_qkv = sum_last.move(grad_b_qkv)
+    norm_pieces[1] = sum_last.move(sum_second.move(norm_pieces[1]))
+    small_sources = (grad_b_qkv, middle_rows, gb_dense, gb_first, gb_second)
+    norm_pieces, small_sources, sum_dense.arrived, sum_first.arrived = pin(
+        (norm_pieces, small_sources, sum_dense.arrived, sum_first.arrived), sum_last, sum_second
+    )
+    grad_b_qkv, middle_rows, gb_dense, gb_first, gb_second = small_sources
+    norm_pieces += late_pieces
     sum_dense.close()
     sum_first.close()
-    grad_b_qkv = sum_last.move(grad_b_qkv)
-    order_numbers, sum_second.arrived = sync(peers, [ring(part) for part in sum_second.sent])
-    sum_second.close()
 
     def cut_columns(parts):
         joined = jnp.concatenate([part.astype(bf16) for part in parts], 1)
@@ -1221,94 +1213,67 @@
         whole = whole.reshape(ctx, share, groups, size // groups).transpose(1, 2, 0, 3)
         return whole.reshape(share, ctx * size).astype(f32)
 
-    norm_pieces = pin(norm_pieces, sum_last, sum_second)
-    grad_b_qkv = sum_last.move(grad_b_qkv)
-    sums = [pair(one.sent) for one in (sum_dense, sum_first, sum_second)]
-    early_sent = cut_columns([one[0] for one in sums])
-    norm_pieces, early_sent, result_sent = sync(norm_pieces, early_sent, result_sent)
-    early_pieces = trade(early_sent)
+    norm_pieces, result_sent = sync(norm_pieces, result_sent)
     result_pieces = result_pieces + [swap(result_sent[s], s) for s in shifts[2:]]
-    grad_inputs, final_rows = make_final(
-        order_numbers, by_column, tokens, grad_hidden, norm_pieces
-    )
-    final_rows, early_pieces = sum_last.receive((final_rows, early_pieces))
+    grad_inputs, final_rows = make_final(peers, by_column, tokens, grad_hidden, norm_pieces)
+    final_rows = pin(sum_last.move(final_rows), sum_last)
+
+    small_rows = jnp.concatenate(
+        [middle_rows[:10], final_rows, grad_b_qkv, jnp.zeros((2, width), f32)], 0
+    )
+    small_rows, result_pieces = sync(small_rows, result_pieces)
+    small_pieces = gather_ctx(small_rows)
+
+    small_pieces = sum_last.receive(sum_second.receive(small_pieces))
     sum_last.close()
-    final_rows, result_pieces = pin((final_rows, result_pieces), sum_last)
-
-    zero_qv = jnp.zeros((2, width), f32)
-    grad_qv = lax.dynamic_update_slice(
-        zero_qv,
-        jnp.concatenate([grad_b_qkv[:, :own_width], grad_b_qkv[:, 2 * own_width :]], 0),
-        (0, me * own_width),
-    )
-
-    def own_columns(array):
-        whole = jnp.zeros((dp, ctx, array.shape[-1]), f32)
-        return lax.dynamic_update_slice_in_dim(whole, array[:, None], me, 1)
-
-    upb_grads = [gb_dense[0], gb_first[0], gb_second[0]]
-    expert_upb = jnp.stack(upb_grads[1:]).reshape(experts, dp, unit).transpose(1, 0, 2)
-    small_grads = [
-        final_rows[0],
-        final_rows[1],
-        grad_qv,
-        middle_rows[0],
-        middle_rows[1],
-        middle_rows[2],
-        middle_rows[3],
-        router_grad[:, :experts],
-        router_grad[:, experts : 2 * experts],
-        middle_rows[4 : 4 + experts].reshape(experts, dp, ctx, share).transpose(1, 2, 0, 3),
-        own_columns(upb_grads[0].reshape(dp, unit)),
-        own_columns(expert_upb.reshape(dp, experts * unit)),
-    ]
-    sizes = [grad.size // (dp * ctx) for grad in small_grads]
-    small_sum = jnp.concatenate([g.reshape(dp, ctx, -1) for g in small_grads], -1)
-    small_pieces = trade(by_peer(small_sum.transpose(1, 0, 2)))
-
     (last_sum,) = sum_last.sent
     qkv_part, out_sums = last_sum[:, : 3 * own_width], last_sum[:, 3 * own_width :]
     out_sums = out_sums.reshape(ctx, share, own_width).transpose(1, 0, 2).reshape(share, width)
-    small_sum = sum(small_pieces).reshape(dp, 1, -1)[places]
-    small_sum = small_sum[:depth] + swap_core(small_sum[depth:])
-    pairs = [[(i, (i + dp - 2 * t) % dp) for i in range(dp)] for t in range(depth)]
+    late_pieces = trade(cut_columns([qkv_part]))
+    up_rows = jnp.concatenate([gb_dense, gb_first, gb_second, jnp.zeros((5, own_hidden), f32)], 0)
+    up_rows = jnp.pad(up_rows, ((0, 0), (0, width - own_hidden)))
+    small_sum = jnp.concatenate([sum(small_pieces), up_rows], 0)
+    small_sum, late_pieces = sync(small_sum + swap_core(small_sum), late_pieces)
+    pairs = [[(i, (i + 2 * t) % dp) for i in range(dp)] for t in range(depth)]
     small_sum = sum(
-        [small_sum[0]] + [lax.ppermute(small_sum[t], "dp", pairs[t]) for t in range(1, depth)]
-    )[0]
-    late_pieces = trade(cut_columns([qkv_part]))
+        [small_sum] + [lax.ppermute(small_sum, "dp", pairs[t]) for t in range(1, depth)]
+    )
+    sum_second.close()
+    sums = [pair(one.sent) for one in (sum_dense, sum_first, sum_second)]
+    early_sent, late_pieces = sync(cut_columns([one[0] for one in sums]), late_pieces)
+    early_pieces = trade(early_sent)
     result = make_result(base, unsort, result_pieces)
     up_grads = [
-        from_columns(early_pieces, 0, own_hidden, dp),
-        from_columns(early_pieces, own_hidden, own_hidden, dp),
-        from_columns(early_pieces, 2 * own_hidden, own_hidden, dp),
+        from_columns(early_pieces, which * own_hidden, own_hidden, dp)
+        for which in range(experts + 1)
     ]
     qkv_grad = from_columns(late_pieces, 0, 3 * own_width, 3)
     down_sums = [one[1] for one in sums]
-    outs, at = [], 0
-    for size in sizes:
-        outs.append(small_sum[at : at + size])
-        at += size
+    owner = place_dp * ctx + me
+    own = lax.dynamic_slice(small_sum, (0, owner * share), (12, share))
+    own_qv = lax.dynamic_slice(small_sum[12:14].reshape(-1), (owner * 2 * share,), (2 * share,))
+    own_up = lax.dynamic_slice(small_sum, (16, place_dp * unit), (3, unit))
     return (
         result[None],
         grad_inputs[None],
-        outs[0],
-        outs[1],
+        own[10],
+        own[11],
         qkv_grad,
-        outs[2],
+        own_qv,
         out_sums,
-        outs[3],
-        outs[4],
-        outs[5],
+        own[0],
+        own[1],
+        own[2],
         up_grads[0],
-        outs[10],
+        own_up[0],
         down_sums[0],
-        outs[6],
-        outs[7].reshape(router_weight.shape),
-        outs[8].reshape(mix_weight.shape),
+        own[3],
+        own[6:8].T,
+        own[8:10].T,
         jnp.stack(up_grads[1:]),
-        outs[11].reshape(expert_up_bias.shape),
+        own_up[1:],
         jnp.stack(down_sums[1:]),
-        outs[9].reshape(expert_down_bias.shape),
+        own[4:6],
     )
 
 

time: 426 us -> 419 us (0.984)
  local copies, waits for them, and re-layouts: 42.5 us -> 32.1 us
    slice x11 -> x3, local copies, waits for them, and re-layouts: 6.03 us -> 1.28 us  [the longest x1 0.64 us: layer(): own[4:6]]
    unnamed x120 -> x136, local copies, waits for them, and re-layouts: 9.13 us -> 8.11 us
  transfers between devices with their start and end apart: 86 -> 86, of which waited for: 33 -> 36; matrix products, arithmetic and copies ran while one was open for 15% -> 13% of each run, Pallas kernels for 31% -> 32%
where the time goes in v4:
time: 419 us; the launch traced here: 411 us
  Pallas kernels  139 us (33%)
  waiting for transfers between devices  125 us (30%)
  starting transfers between devices  78.6 us (19%)
  other arithmetic  33 us (8%)
  local copies, waits for them, and re-layouts  32.1 us (8%)
    pallas_call x12, Pallas kernels, run(): pl.pallas_call(kernel, grid=grid, in_specs=specs, out_specs=out_specs, ou...  137 us
    ppermute x45, waiting for transfers between devices, swap(): return lax.ppermute(array, 'ctx', [(i, i ^ shift) for i in range(ctx)])  72.6 us
    ppermute x45, starting transfers between devices, swap(): return lax.ppermute(array, 'ctx', [(i, i ^ shift) for i in range(ctx)])  56.7 us
    ppermute x21, waiting for transfers between devices, ring(): return lax.ppermute(array, 'dp', ring_pairs)  47.4 us
    convert_element_type x12, other arithmetic, add(): self.sent = [part.astype(bf16) if at else part for part in parts]  16.5 us
    ppermute x21, starting transfers between devices, ring(): return lax.ppermute(array, 'dp', ring_pairs)  15.7 us
  transfers between devices with their start and end apart: 86, of which 36 were waited for; matrix products, arithmetic and copies ran while one was open for 13% of the time, Pallas kernels for 32%

profile of v4, /device:TPU:0, one launch (start us, length us, event | category | flops | bytes accessed | tf_op | source)
XLA Modules:
  0.0 411.4 jit_solution(5555509827538348761)
XLA Ops:
  0.7 3.0 collective-permute-start.5
  8.5 2.2 concatenate.40
  12.9 2.9 collective-permute-start.2
  18.1 2.3 collective-permute-start.7
  23.1 6.5 %collective-permute-done.3.refs_1_ = bf16[128,1152]{1,0:T(8,128)(2,1)S(1)} collective-permute-done((bf16[128,1152]{1,0:T(8,128)(2,1)S(1)}, bf16[128,1152]{1,0:T(8,128)(2,1)S(1)}, u32[]{:S(2)}, u32[]{:S(2)}) %collective-permute-start.3) | collective-permute-done | bytes 294944 | tf_op jit(solution)/shard_map/ppermute | solution.py:914
  31.6 6.7 %collective-permute-done.8.refs_2_ = bf16[128,1152]{1,0:T(8,128)(2,1)} collective-permute-done((bf16[128,1152]{1,0:T(8,128)(2,1)S(1)}, bf16[128,1152]{1,0:T(8,128)(2,1)}, u32[]{:S(2)}, u32[]{:S(2)}) %collective-permute-start.8) | collective-permute-done | bytes 294944 | tf_op jit(solution)/shard_map/ppermute | solution.py:914
  40.5 1.9 collective-permute-start.12
  43.5 3.1 collective-permute-done.10
  46.6 4.6 %collective-permute-done.11 = bf16[3,32,1024]{2,1,0:T(8,128)(2,1)S(1)} collective-permute-done((bf16[3,32,1024]{2,1,0:T(8,128)(2,1)S(1)}, bf16[3,32,1024]{2,1,0:T(8,128)(2,1)S(1)}, u32[]{:S(2)}, u32[]{:S(2)}) %collective-permute-start.11) | collective-permute-done | bytes 196640 | tf_op jit(solution)/shard_map/ppermute | solution.py:896
  53.9 3.3 unpack.1
  60.7 7.8 %norm_qkv.1 = (bf16[1024,768]{1,0:T(8,128)(2,1)}, bf16[1024,1024]{1,0:T(8,128)(2,1)}, bf16[1024,1152]{1,0:T(8,128)(2,1)}) custom-call(s32[12]{0:T(128)} %concatenate.47.scalars, f32[32,1024]{1,0:T(8,128)} %get-tuple-element.316.small_ref.by_column, bf16[128,1152]{1,0:T(8,128)(2,1)} %copy-done.18, bf16[128,1152]{1,0:T(8,128)(2,1)} %copy-done.56, ...), custom_call_target="tpu_custom_call" | custom-call | flops 8000000000 | bytes 1024 | tf_op jit(solution)/shard_map/norm_qkv/pallas_call | solution.py:71
  68.5 4.1 %collective-permute-start.27 = (bf16[2,128,1024]{2,1,0:T(8,128)(2,1)}, bf16[2,128,1024]{2,1,0:T(8,128)(2,1)}, u32[]{:S(2)}, u32[]{:S(2)}) collective-permute-start(bf16[2,128,1024]{2,1,0:T(8,128)(2,1)} %collective-permute-done.16.refs_9_), channel_id=1, source_target_pairs={{0,8},{4,12},{8,16},{12,20},{16,24},{20,28},{24,0},{28,4},{1,9},{5... | collective-permute-start | bytes 1572872 | tf_op jit(solution)/shard_map/ppermute | solution.py:914
  72.7 10.4 %attention_forward.1 = bf16[1024,256]{1,0:T(8,128)(2,1)} custom-call(bf16[1024,768]{1,0:T(8,128)(2,1)} %get-tuple-element.304.q_ref.k_ref.v_ref, bf16[1024,768]{1,0:T(8,128)(2,1)} %get-tuple-element.304.q_ref.k_ref.v_ref, bf16[1024,768]{1,0:T(8,128)(2,1)} %get-tuple-element.304.q_ref.k_ref.v_ref), custom_call_target="tpu_custom_call" | custom-call | flops 10000000000 | bytes 1024 | tf_op jit(solution)/shard_map/attention_forward/pallas_call | solution.py:71
  91.2 2.4 collective-permute-done.21.refs_2_.refs_6_
  94.3 4.0 hidden.1
  99.9 1.9 collective-permute-start.26
  102.4 2.7 maximum_convert_fusion.1
  108.3 5.2 %collective-permute-done.24.refs_1_ = bf16[256,1024]{1,0:T(8,128)(2,1)S(1)} collective-permute-done((bf16[256,1024]{1,0:T(8,128)(2,1)}, bf16[256,1024]{1,0:T(8,128)(2,1)S(1)}, u32[]{:S(2)}, u32[]{:S(2)}) %collective-permute-start.24) | collective-permute-done | bytes 524320 | tf_op jit(solution)/shard_map/ppermute | solution.py:896
  113.4 9.4 %collective-permute-done.25.refs_2_ = bf16[256,1024]{1,0:T(8,128)(2,1)} collective-permute-done((bf16[256,1024]{1,0:T(8,128)(2,1)}, bf16[256,1024]{1,0:T(8,128)(2,1)}, u32[]{:S(2)}, u32[]{:S(2)}) %collective-permute-start.25) | collective-permute-done | bytes 524320 | tf_op jit(solution)/shard_map/ppermute | solution.py:896
  124.9 9.1 %collective-permute-done.30.refs_10_ = bf16[4,128,1024]{2,1,0:T(8,128)(2,1)} collective-permute-done((bf16[4,128,1024]{2,1,0:T(8,128)(2,1)}, bf16[4,128,1024]{2,1,0:T(8,128)(2,1)}, u32[]{:S(2)}, u32[]{:S(2)}) %collective-permute-start.30) | collective-permute-done | bytes 1048608 | tf_op jit(solution)/shard_map/ppermute | solution.py:914
  135.0 2.3 collective-permute-done.28.refs_5_
  137.3 7.0 %collective-permute-done.29.refs_6_ = bf16[256,1024]{1,0:T(8,128)(2,1)S(1)} collective-permute-done((bf16[256,1024]{1,0:T(8,128)(2,1)S(1)}, bf16[256,1024]{1,0:T(8,128)(2,1)S(1)}, u32[]{:S(2)}, u32[]{:S(2)}) %collective-permute-start.29) | collective-permute-done | bytes 524320 | tf_op jit(solution)/shard_map/ppermute | solution.py:896
  151.0 23.6 %mlp.3 = (f32[1024,1024]{1,0:T(8,128)}, f32[1024,1024]{1,0:T(8,128)}, f32[1024,1]{1,0:T(8,128)}, f32[1,1024]{1,0:T(1,128)}, bf16[4,2,128,1024]{3,2,1,0:T(8,128)(2,1)}, /*index=5*/bf16[4,2,128,1024]{3,2,1,0:T(8,128)(2,1)}) custom-call(s32[12]{0:T(128)} %gate.2.scalars.refs_0_, bf16[1024,128]{1,0:T(8,128)(2,1)} %get-tuple-element.319.small_ref.by_row, ...), custom_call_target="tpu_custom_call" | custom-call | flops 20000000000 | bytes 1024 | tf_op jit(solution)/shard_map/mlp/pallas_call | solution.py:71
  180.4 1.9 collective-permute-start.42
  183.3 18.1 %mlp.4 = (f32[640,1024]{1,0:T(8,128)}, f32[640,1024]{1,0:T(8,128)}, f32[640,1]{1,0:T(8,128)}, f32[1,1024]{1,0:T(1,128)}, bf16[4,2,128,1024]{3,2,1,0:T(8,128)(2,1)}, /*index=5*/bf16[4,2,128,1024]{3,2,1,0:T(8,128)(2,1)}) custom-call(s32[12]{0:T(128)} %gate.3.scalars, bf16[1024,128]{1,0:T(8,128)(2,1)} %get-tuple-element.319.small_ref.by_row, ...), custom_call_target="tpu_custom_call" | custom-call | flops 17999998976 | bytes 1024 | tf_op jit(solution)/shard_map/mlp/pallas_call | solution.py:71
  202.9 2.2 collective-permute-start.44
  205.1 22.8 %mlp.5 = (bf16[256,1024]{1,0:T(8,128)(2,1)}, bf16[256,1024]{1,0:T(8,128)(2,1)}, bf16[256,1024]{1,0:T(8,128)(2,1)}, bf16[256,1024]{1,0:T(8,128)(2,1)}, bf16[256,1...) custom-call(s32[12]{0:T(128)} %gate.2.scalars.refs_0_, ...), custom_call_target="tpu_custom_call" | custom-call | flops 17999998976 | bytes 1024 | tf_op jit(solution)/shard_map/mlp/pallas_call | solution.py:71
  237.1 7.3 %collective-permute-done.47.refs_1_ = bf16[256,1152]{1,0:T(8,128)(2,1)S(1)} collective-permute-done((bf16[256,1152]{1,0:T(8,128)(2,1)}, bf16[256,1152]{1,0:T(8,128)(2,1)S(1)}, u32[]{:S(2)}, u32[]{:S(2)}) %collective-permute-start.47) | collective-permute-done | bytes 589856 | tf_op jit(solution)/shard_map/ppermute | solution.py:896
  244.4 11.7 %collective-permute-done.48.refs_2_ = bf16[256,1152]{1,0:T(8,128)(2,1)} collective-permute-done((bf16[256,1152]{1,0:T(8,128)(2,1)}, bf16[256,1152]{1,0:T(8,128)(2,1)}, u32[]{:S(2)}, u32[]{:S(2)}) %collective-permute-start.48) | collective-permute-done | bytes 589856 | tf_op jit(solution)/shard_map/ppermute | solution.py:896
  257.8 4.4 %collective-permute-done.50 = bf16[2,128,1024]{2,1,0:T(8,128)(2,1)S(1)} collective-permute-done((bf16[2,128,1024]{2,1,0:T(8,128)(2,1)S(1)}, bf16[2,128,1024]{2,1,0:T(8,128)(2,1)S(1)}, u32[]{:S(2)}, u32[]{:S(2)}) %collective-permute-start.50) | collective-permute-done | bytes 524320 | tf_op jit(solution)/shard_map/ppermute | solution.py:914
  266.1 11.4 %middle.1 = (f32[256,1024]{1,0:T(8,128)}, f32[256,1024]{1,0:T(8,128)}, f32[16,1024]{1,0:T(8,128)}, bf16[8,4,32,256]{3,2,1,0:T(8,128)(2,1)}, bf16[8,4,32,256]{3,2...) custom-call(s32[4]{0:T(128)} %pad_add_fusion.scalars.order, ...), custom_call_target="tpu_custom_call" | custom-call | flops 11000000512 | bytes 1024 | tf_op jit(solution)/shard_map/middle/pallas_call | solution.py:71
  279.3 1.8 collective-permute-start.59
  283.6 2.2 collective-permute-done.59.refs_3_
  292.1 18.5 %attention_backward.1 = (bf16[1024,256]{1,0:T(8,128)(2,1)}, bf16[1024,256]{1,0:T(8,128)(2,1)}, bf16[1024,256]{1,0:T(8,128)(2,1)}) custom-call(s32[4]{0:T(128)} %pad_add_fusion.scalars.order, bf16[1024,768]{1,0:T(8,128)(2,1)} %get-tuple-element.304.q_ref.k_ref.v_ref, bf16[1024,768]{1,0:T(8,128)(2,1)} %get-tuple-element.304.q_ref.k_ref.v_ref, ...), custom_call_target="tpu_custom_call" | custom-call | flops 17999998976 | bytes 1024 | tf_op jit(solution)/shard_map/attention_backward/pallas_call | solution.py:71
  310.7 1.9 collective-permute-done.53
  312.6 2.1 fusion.2
  315.8 9.2 %qkv_back.1 = (bf16[256,1024]{1,0:T(8,128)(2,1)}, bf16[256,1024]{1,0:T(8,128)(2,1)}, bf16[256,1024]{1,0:T(8,128)(2,1)}, bf16[256,1024]{1,0:T(8,128)(2,1)}, bf16[...) custom-call(s32[12]{0:T(128)} %concatenate.47.scalars, ...), custom_call_target="tpu_custom_call" | custom-call | flops 8000000000 | bytes 1024 | tf_op jit(solution)/shard_map/qkv_back/pallas_call | solution.py:71
  327.9 2.0 collective-permute-start.67
  331.0 9.2 %collective-permute-done.66.refs_1_ = bf16[256,1024]{1,0:T(8,128)(2,1)} collective-permute-done((bf16[256,1024]{1,0:T(8,128)(2,1)}, bf16[256,1024]{1,0:T(8,128)(2,1)}, u32[]{:S(2)}, u32[]{:S(2)}) %collective-permute-start.66) | collective-permute-done | bytes 524320 | tf_op jit(solution)/shard_map/ppermute | solution.py:896
  340.2 2.4 collective-permute-done.65
  345.5 7.9 %collective-permute-done.64 = bf16[128,1024]{1,0:T(8,128)(2,1)S(1)} collective-permute-done((bf16[128,1024]{1,0:T(8,128)(2,1)S(1)}, bf16[128,1024]{1,0:T(8,128)(2,1)S(1)}, u32[]{:S(2)}, u32[]{:S(2)}) %collective-permute-start.64) | collective-permute-done | bytes 262176 | tf_op jit(solution)/shard_map/ppermute | solution.py:914
  360.1 4.0 final.1
  364.2 5.8 %collective-permute-done.68 = bf16[128,1024]{1,0:T(8,128)(2,1)S(1)} collective-permute-done((bf16[128,1024]{1,0:T(8,128)(2,1)S(1)}, bf16[128,1024]{1,0:T(8,128)(2,1)S(1)}, u32[]{:S(2)}, u32[]{:S(2)}) %collective-permute-start.68) | collective-permute-done | bytes 262176 | tf_op jit(solution)/shard_map/ppermute | solution.py:914
  375.6 3.6 result.1
  379.2 2.0 collective-permute-done.72
  392.4 1.9 collective-permute-start.81
  394.3 1.9 collective-permute-start.82
  405.3 2.4 collective-permute-done.84
  (412 shorter events, 123.2 us)
Async XLA Ops:
  0.7 30.9 %collective-permute-start.5 = (bf16[256,1024]{1,0:T(8,128)(2,1)}, bf16[256,1024]{1,0:T(8,128)(2,1)}, u32[]{:S(2)}, u32[]{:S(2)}) collective-permute-start(bf16[256,1024]{1,0:T(8,128)(2,1)} %bitcast.333), channel_id=1, source_target_pairs={{0,1},{1,0},{2,3},{3,2},{4,5},{5,4},{6,7},{7,6},{8,9},{9,8},{10,11... | collective-permute-start | bytes 1572872 | tf_op jit(solution)/shard_map/ppermute | solution.py:896
  3.7 27.9 %collective-permute-start.6 = (bf16[256,1024]{1,0:T(8,128)(2,1)}, bf16[256,1024]{1,0:T(8,128)(2,1)}, u32[]{:S(2)}, u32[]{:S(2)}) collective-permute-start(bf16[256,1024]{1,0:T(8,128)(2,1)} %bitcast.334), channel_id=1, source_target_pairs={{0,2},{1,3},{2,0},{3,1},{4,6},{5,7},{6,4},{7,5},{8,10},{9,11},{10,... | collective-permute-start | bytes 1572872 | tf_op jit(solution)/shard_map/ppermute | solution.py:896
  18.1 13.5 %collective-permute-start.7 = (bf16[256,1024]{1,0:T(8,128)(2,1)}, bf16[256,1024]{1,0:T(8,128)(2,1)}, u32[]{:S(2)}, u32[]{:S(2)}) collective-permute-start(bf16[256,1024]{1,0:T(8,128)(2,1)} %bitcast.335), channel_id=1, source_target_pairs={{0,3},{1,2},{2,1},{3,0},{4,7},{5,6},{6,5},{7,4},{8,11},{9,10},{10,... | collective-permute-start | bytes 1572872 | tf_op jit(solution)/shard_map/ppermute | solution.py:896
  38.3 13.0 %collective-permute-start.13 = (bf16[128,1152]{1,0:T(8,128)(2,1)}, bf16[128,1152]{1,0:T(8,128)(2,1)}, u32[]{:S(2)}, u32[]{:S(2)}) collective-permute-start(bf16[128,1152]{1,0:T(8,128)(2,1)} %collective-permute-done.8.refs_2_), channel_id=1, source_target_pairs={{0,8},{4,12},{8,16},{12,20},{16,24},{20,28},{24,0},{28,4},{1,9},{5... | collective-permute-start | bytes 884744 | tf_op jit(solution)/shard_map/ppermute | solution.py:914
  38.3 13.0 %collective-permute-start.14 = (bf16[128,1152]{1,0:T(8,128)(2,1)}, bf16[128,1152]{1,0:T(8,128)(2,1)}, u32[]{:S(2)}, u32[]{:S(2)}) collective-permute-start(bf16[128,1152]{1,0:T(8,128)(2,1)} %collective-permute-done.8.refs_2_), channel_id=1, source_target_pairs={{0,4},{4,0},{8,12},{12,8},{16,20},{20,16},{24,28},{28,24},{1,5},{5... | collective-permute-start | bytes 884744 | tf_op jit(solution)/shard_map/ppermute | solution.py:917
  51.7 16.8 %collective-permute-start.16 = (bf16[2,128,1024]{2,1,0:T(8,128)(2,1)S(1)}, bf16[2,128,1024]{2,1,0:T(8,128)(2,1)}, u32[]{:S(2)}, u32[]{:S(2)}) collective-permute-start(bf16[2,128,1024]{2,1,0:T(8,128)(2,1)S(1)} %pad_maximum_fusion.3.refs_8_), channel_id=1, source_target_pairs={{0,8},{4,12},{8,16},{12,20},{16,24},{20,28},{24,0},{28,4},{1,9},{5... | collective-permute-start | bytes 1572872 | tf_op jit(solution)/shard_map/ppermute | solution.py:914
  57.2 25.9 %collective-permute-start.17 = (bf16[256,1024]{1,0:T(8,128)(2,1)}, bf16[256,1024]{1,0:T(8,128)(2,1)S(1)}, u32[]{:S(2)}, u32[]{:S(2)}) collective-permute-start(bf16[256,1024]{1,0:T(8,128)(2,1)} %get-tuple-element.306), channel_id=1, source_target_pairs={{0,1},{1,0},{2,3},{3,2},{4,5},{5,4},{6,7},{7,6},{8,9},{9,8},{10,11... | collective-permute-start | bytes 1572872 | tf_op jit(solution)/shard_map/ppermute | solution.py:896
  58.2 25.1 %collective-permute-start.18 = (bf16[256,1024]{1,0:T(8,128)(2,1)}, bf16[256,1024]{1,0:T(8,128)(2,1)S(1)}, u32[]{:S(2)}, u32[]{:S(2)}) collective-permute-start(bf16[256,1024]{1,0:T(8,128)(2,1)} %get-tuple-element.306), channel_id=1, source_target_pairs={{0,2},{1,3},{2,0},{3,1},{4,6},{5,7},{6,4},{7,5},{8,10},{9,11},{10,... | collective-permute-start | bytes 1572872 | tf_op jit(solution)/shard_map/ppermute | solution.py:896
  58.9 24.3 %collective-permute-start.19 = (bf16[256,1024]{1,0:T(8,128)(2,1)}, bf16[256,1024]{1,0:T(8,128)(2,1)S(1)}, u32[]{:S(2)}, u32[]{:S(2)}) collective-permute-start(bf16[256,1024]{1,0:T(8,128)(2,1)} %get-tuple-element.306), channel_id=1, source_target_pairs={{0,3},{1,2},{2,1},{3,0},{4,7},{5,6},{6,5},{7,4},{8,11},{9,10},{10,... | collective-permute-start | bytes 1572872 | tf_op jit(solution)/shard_map/ppermute | solution.py:896
  60.7 37.6 %collective-permute-start.23 = (bf16[4,128,1024]{2,1,0:T(8,128)(2,1)S(1)}, bf16[4,128,1024]{2,1,0:T(8,128)(2,1)S(1)}, u32[]{:S(2)}, u32[]{:S(2)}) collective-permute-start(bf16[4,128,1024]{2,1,0:T(8,128)(2,1)S(1)} %pad_maximum_fusion.refs_8_), channel_id=1, source_target_pairs={{0,8},{4,12},{8,16},{12,20},{16,24},{20,28},{24,0},{28,4},{1,9},{5... | collective-permute-start | bytes 3145736 | tf_op jit(solution)/shard_map/ppermute | solution.py:914
  68.5 37.7 %collective-permute-start.27 = (bf16[2,128,1024]{2,1,0:T(8,128)(2,1)}, bf16[2,128,1024]{2,1,0:T(8,128)(2,1)}, u32[]{:S(2)}, u32[]{:S(2)}) collective-permute-start(bf16[2,128,1024]{2,1,0:T(8,128)(2,1)} %collective-permute-done.16.refs_9_), channel_id=1, source_target_pairs={{0,8},{4,12},{8,16},{12,20},{16,24},{20,28},{24,0},{28,4},{1,9},{5... | collective-permute-start | bytes 1572872 | tf_op jit(solution)/shard_map/ppermute | solution.py:914
  98.3 15.1 %collective-permute-start.24 = (bf16[256,1024]{1,0:T(8,128)(2,1)}, bf16[256,1024]{1,0:T(8,128)(2,1)S(1)}, u32[]{:S(2)}, u32[]{:S(2)}) collective-permute-start(bf16[256,1024]{1,0:T(8,128)(2,1)} %get-tuple-element.321.refs_0_), channel_id=1, source_target_pairs={{0,1},{1,0},{2,3},{3,2},{4,5},{5,4},{6,7},{7,6},{8,9},{9,8},{10,11... | collective-permute-start | bytes 1572872 | tf_op jit(solution)/shard_map/ppermute | solution.py:896
  99.4 23.4 %collective-permute-start.25 = (bf16[256,1024]{1,0:T(8,128)(2,1)}, bf16[256,1024]{1,0:T(8,128)(2,1)}, u32[]{:S(2)}, u32[]{:S(2)}) collective-permute-start(bf16[256,1024]{1,0:T(8,128)(2,1)} %get-tuple-element.321.refs_0_), channel_id=1, source_target_pairs={{0,2},{1,3},{2,0},{3,1},{4,6},{5,7},{6,4},{7,5},{8,10},{9,11},{10,... | collective-permute-start | bytes 1572872 | tf_op jit(solution)/shard_map/ppermute | solution.py:896
  99.9 22.9 %collective-permute-start.26 = (bf16[256,1024]{1,0:T(8,128)(2,1)}, bf16[256,1024]{1,0:T(8,128)(2,1)}, u32[]{:S(2)}, u32[]{:S(2)}) collective-permute-start(bf16[256,1024]{1,0:T(8,128)(2,1)} %get-tuple-element.321.refs_0_), channel_id=1, source_target_pairs={{0,3},{1,2},{2,1},{3,0},{4,7},{5,6},{6,5},{7,4},{8,11},{9,10},{10,... | collective-permute-start | bytes 1572872 | tf_op jit(solution)/shard_map/ppermute | solution.py:896
  105.7 28.2 %collective-permute-start.30 = (bf16[4,128,1024]{2,1,0:T(8,128)(2,1)}, bf16[4,128,1024]{2,1,0:T(8,128)(2,1)}, u32[]{:S(2)}, u32[]{:S(2)}) collective-permute-start(bf16[4,128,1024]{2,1,0:T(8,128)(2,1)} %copy-done.31), channel_id=1, source_target_pairs={{0,8},{4,12},{8,16},{12,20},{16,24},{20,28},{24,0},{28,4},{1,9},{5... | collective-permute-start | bytes 3145736 | tf_op jit(solution)/shard_map/ppermute | solution.py:914
  122.8 14.5 %collective-permute-start.28 = (bf16[256,1024]{1,0:T(8,128)(2,1)S(1)}, bf16[256,1024]{1,0:T(8,128)(2,1)S(1)}, u32[]{:S(2)}, u32[]{:S(2)}) collective-permute-start(bf16[256,1024]{1,0:T(8,128)(2,1)S(1)} %convolution_convert_fusion.refs_4_), channel_id=1, source_target_pairs={{0,1},{1,0},{2,3},{3,2},{4,5},{5,4},{6,7},{7,6},{8,9},{9,8},{10,11... | collective-permute-start | bytes 1572872 | tf_op jit(solution)/shard_map/ppermute | solution.py:896
  123.9 20.4 %collective-permute-start.29 = (bf16[256,1024]{1,0:T(8,128)(2,1)S(1)}, bf16[256,1024]{1,0:T(8,128)(2,1)S(1)}, u32[]{:S(2)}, u32[]{:S(2)}) collective-permute-start(bf16[256,1024]{1,0:T(8,128)(2,1)S(1)} %convolution_convert_fusion.refs_4_), channel_id=1, source_target_pairs={{0,2},{1,3},{2,0},{3,1},{4,6},{5,7},{6,4},{7,5},{8,10},{9,11},{10,... | collective-permute-start | bytes 1572872 | tf_op jit(solution)/shard_map/ppermute | solution.py:896
  124.6 19.8 %collective-permute-start.32 = (bf16[2,128,1024]{2,1,0:T(8,128)(2,1)}, bf16[2,128,1024]{2,1,0:T(8,128)(2,1)S(1)}, u32[]{:S(2)}, u32[]{:S(2)}) collective-permute-start(bf16[2,128,1024]{2,1,0:T(8,128)(2,1)} %collective-permute-done.27.refs_1_.refs_10_), channel_id=1, source_target_pairs={{0,8},{4,12},{8,16},{12,20},{16,24},{20,28},{24,0},{28,4},{1,9},{5... | collective-permute-start | bytes 1572872 | tf_op jit(solution)/shard_map/ppermute | solution.py:914
  133.9 11.7 %collective-permute-start.31 = (bf16[256,1024]{1,0:T(8,128)(2,1)S(1)}, bf16[256,1024]{1,0:T(8,128)(2,1)S(1)}, u32[]{:S(2)}, u32[]{:S(2)}) collective-permute-start(bf16[256,1024]{1,0:T(8,128)(2,1)S(1)} %convolution_convert_fusion.refs_4_), channel_id=1, source_target_pairs={{0,3},{1,2},{2,1},{3,0},{4,7},{5,6},{6,5},{7,4},{8,11},{9,10},{10,... | collective-permute-start | bytes 1572872 | tf_op jit(solution)/shard_map/ppermute | solution.py:896
  147.2 27.8 %collective-permute-start.38 = (bf16[4,128,1024]{2,1,0:T(8,128)(2,1)}, bf16[4,128,1024]{2,1,0:T(8,128)(2,1)}, u32[]{:S(2)}, u32[]{:S(2)}) collective-permute-start(bf16[4,128,1024]{2,1,0:T(8,128)(2,1)} %collective-permute-done.30.refs_10_), channel_id=1, source_target_pairs={{0,8},{4,12},{8,16},{12,20},{16,24},{20,28},{24,0},{28,4},{1,9},{5... | collective-permute-start | bytes 3145736 | tf_op jit(solution)/shard_map/ppermute | solution.py:914
  150.0 25.1 %collective-permute-start.39 = (bf16[4,128,1024]{2,1,0:T(8,128)(2,1)S(1)}, bf16[4,128,1024]{2,1,0:T(8,128)(2,1)S(1)}, u32[]{:S(2)}, u32[]{:S(2)}) collective-permute-start(bf16[4,128,1024]{2,1,0:T(8,128)(2,1)S(1)} %pad_maximum_fusion.refs_8_), channel_id=1, source_target_pairs={{0,4},{4,0},{8,12},{12,8},{16,20},{20,16},{24,28},{28,24},{1,5},{5... | collective-permute-start | bytes 3145736 | tf_op jit(solution)/shard_map/ppermute | solution.py:917
  150.2 24.9 %collective-permute-start.40 = (bf16[4,128,1024]{2,1,0:T(8,128)(2,1)}, bf16[4,128,1024]{2,1,0:T(8,128)(2,1)S(1)}, u32[]{:S(2)}, u32[]{:S(2)}) collective-permute-start(bf16[4,128,1024]{2,1,0:T(8,128)(2,1)} %copy-done.31), channel_id=1, source_target_pairs={{0,4},{4,0},{8,12},{12,8},{16,20},{20,16},{24,28},{28,24},{1,5},{5... | collective-permute-start | bytes 3145736 | tf_op jit(solution)/shard_map/ppermute | solution.py:917
  150.6 24.5 %collective-permute-start.41 = (bf16[4,128,1024]{2,1,0:T(8,128)(2,1)}, bf16[4,128,1024]{2,1,0:T(8,128)(2,1)S(1)}, u32[]{:S(2)}, u32[]{:S(2)}) collective-permute-start(bf16[4,128,1024]{2,1,0:T(8,128)(2,1)} %collective-permute-done.30.refs_10_), channel_id=1, source_target_pairs={{0,4},{4,0},{8,12},{12,8},{16,20},{20,16},{24,28},{28,24},{1,5},{5... | collective-permute-start | bytes 3145736 | tf_op jit(solution)/shard_map/ppermute | solution.py:917
  180.4 21.2 %collective-permute-start.42 = (bf16[2,128,1024]{2,1,0:T(8,128)(2,1)S(1)}, bf16[2,128,1024]{2,1,0:T(8,128)(2,1)S(1)}, u32[]{:S(2)}, u32[]{:S(2)}) collective-permute-start(bf16[2,128,1024]{2,1,0:T(8,128)(2,1)S(1)} %fusion.6), channel_id=1, source_target_pairs={{0,8},{4,12},{8,16},{12,20},{16,24},{20,28},{24,0},{28,4},{1,9},{5... | collective-permute-start | bytes 1572872 | tf_op jit(solution)/shard_map/ppermute | solution.py:914
  201.5 30.3 %collective-permute-start.45 = (bf16[4,2,128,1024]{3,2,1,0:T(8,128)(2,1)}, bf16[4,2,128,1024]{3,2,1,0:T(8,128)(2,1)S(1)}, u32[]{:S(2)}, u32[]{:S(2)}) collective-permute-start(bf16[4,2,128,1024]{3,2,1,0:T(8,128)(2,1)} %get-tuple-element.370), channel_id=1, source_target_pairs={{0,4},{4,0},{8,12},{12,8},{16,20},{20,16},{24,28},{28,24},{1,5},{5... | collective-permute-start | bytes 6291464 | tf_op jit(solution)/shard_map/ppermute | solution.py:917
  202.9 27.6 %collective-permute-start.44 = (bf16[2,128,1024]{2,1,0:T(8,128)(2,1)S(1)}, bf16[2,128,1024]{2,1,0:T(8,128)(2,1)S(1)}, u32[]{:S(2)}, u32[]{:S(2)}) collective-permute-start(bf16[2,128,1024]{2,1,0:T(8,128)(2,1)S(1)} %fusion.5), channel_id=1, source_target_pairs={{0,8},{4,12},{8,16},{12,20},{16,24},{20,28},{24,0},{28,4},{1,9},{5... | collective-permute-start | bytes 1572872 | tf_op jit(solution)/shard_map/ppermute | solution.py:914
  228.0 16.4 %collective-permute-start.47 = (bf16[256,1152]{1,0:T(8,128)(2,1)}, bf16[256,1152]{1,0:T(8,128)(2,1)S(1)}, u32[]{:S(2)}, u32[]{:S(2)}) collective-permute-start(bf16[256,1152]{1,0:T(8,128)(2,1)} %get-tuple-element.375), channel_id=1, source_target_pairs={{0,1},{1,0},{2,3},{3,2},{4,5},{5,4},{6,7},{7,6},{8,9},{9,8},{10,11... | collective-permute-start | bytes 1769480 | tf_op jit(solution)/shard_map/ppermute | solution.py:896
  228.8 27.3 %collective-permute-start.48 = (bf16[256,1152]{1,0:T(8,128)(2,1)}, bf16[256,1152]{1,0:T(8,128)(2,1)}, u32[]{:S(2)}, u32[]{:S(2)}) collective-permute-start(bf16[256,1152]{1,0:T(8,128)(2,1)} %get-tuple-element.376), channel_id=1, source_target_pairs={{0,2},{1,3},{2,0},{3,1},{4,6},{5,7},{6,4},{7,5},{8,10},{9,11},{10,... | collective-permute-start | bytes 1769480 | tf_op jit(solution)/shard_map/ppermute | solution.py:896
  234.8 22.2 %collective-permute-start.49 = (bf16[256,1152]{1,0:T(8,128)(2,1)S(1)}, bf16[256,1152]{1,0:T(8,128)(2,1)}, u32[]{:S(2)}, u32[]{:S(2)}) collective-permute-start(bf16[256,1152]{1,0:T(8,128)(2,1)S(1)} %copy-done.37), channel_id=1, source_target_pairs={{0,3},{1,2},{2,1},{3,0},{4,7},{5,6},{6,5},{7,4},{8,11},{9,10},{10,... | collective-permute-start | bytes 1769480 | tf_op jit(solution)/shard_map/ppermute | solution.py:896
  235.9 21.8 %collective-permute-start.46 = (bf16[2,128,1024]{2,1,0:T(8,128)(2,1)S(1)}, bf16[2,128,1024]{2,1,0:T(8,128)(2,1)S(1)}, u32[]{:S(2)}, u32[]{:S(2)}) collective-permute-start(bf16[2,128,1024]{2,1,0:T(8,128)(2,1)S(1)} %fusion.4), channel_id=1, source_target_pairs={{0,8},{4,12},{8,16},{12,20},{16,24},{20,28},{24,0},{28,4},{1,9},{5... | collective-permute-start | bytes 1572872 | tf_op jit(solution)/shard_map/ppermute | solution.py:914
  236.9 25.3 %collective-permute-start.50 = (bf16[2,128,1024]{2,1,0:T(8,128)(2,1)S(1)}, bf16[2,128,1024]{2,1,0:T(8,128)(2,1)S(1)}, u32[]{:S(2)}, u32[]{:S(2)}) collective-permute-start(bf16[2,128,1024]{2,1,0:T(8,128)(2,1)S(1)} %fusion.7), channel_id=1, source_target_pairs={{0,8},{4,12},{8,16},{12,20},{16,24},{20,28},{24,0},{28,4},{1,9},{5... | collective-permute-start | bytes 1572872 | tf_op jit(solution)/shard_map/ppermute | solution.py:914
  257.0 32.3 %collective-permute-start.51 = (bf16[4,2,128,1024]{3,2,1,0:T(8,128)(2,1)}, bf16[4,2,128,1024]{3,2,1,0:T(8,128)(2,1)}, u32[]{:S(2)}, u32[]{:S(2)}) collective-permute-start(bf16[4,2,128,1024]{3,2,1,0:T(8,128)(2,1)} %get-tuple-element.405), channel_id=1, source_target_pairs={{0,4},{4,0},{8,12},{12,8},{16,20},{20,16},{24,28},{28,24},{1,5},{5... | collective-permute-start | bytes 6291464 | tf_op jit(solution)/shard_map/ppermute | solution.py:917
  263.6 13.9 %collective-permute-start.55 = (bf16[256,1024]{1,0:T(8,128)(2,1)}, bf16[256,1024]{1,0:T(8,128)(2,1)S(1)}, u32[]{:S(2)}, u32[]{:S(2)}) collective-permute-start(bf16[256,1024]{1,0:T(8,128)(2,1)} %get-tuple-element.415), channel_id=1, source_target_pairs={{0,1},{1,0},{2,3},{3,2},{4,5},{5,4},{6,7},{7,6},{8,9},{9,8},{10,11... | collective-permute-start | bytes 1572872 | tf_op jit(solution)/shard_map/ppermute | solution.py:896
  264.4 13.1 %collective-permute-start.56 = (bf16[256,1024]{1,0:T(8,128)(2,1)}, bf16[256,1024]{1,0:T(8,128)(2,1)S(1)}, u32[]{:S(2)}, u32[]{:S(2)}) collective-permute-start(bf16[256,1024]{1,0:T(8,128)(2,1)} %get-tuple-element.416), channel_id=1, source_target_pairs={{0,2},{1,3},{2,0},{3,1},{4,6},{5,7},{6,4},{7,5},{8,10},{9,11},{10,... | collective-permute-start | bytes 1572872 | tf_op jit(solution)/shard_map/ppermute | solution.py:896
  266.1 15.0 %collective-permute-start.52 = (bf16[2,128,1024]{2,1,0:T(8,128)(2,1)S(1)}, bf16[2,128,1024]{2,1,0:T(8,128)(2,1)S(1)}, u32[]{:S(2)}, u32[]{:S(2)}) collective-permute-start(bf16[2,128,1024]{2,1,0:T(8,128)(2,1)S(1)} %fusion.3), channel_id=1, source_target_pairs={{0,8},{4,12},{8,16},{12,20},{16,24},{20,28},{24,0},{28,4},{1,9},{5... | collective-permute-start | bytes 1572872 | tf_op jit(solution)/shard_map/ppermute | solution.py:914
  285.8 28.9 %collective-permute-start.60 = (bf16[1024,256]{1,0:T(8,128)(2,1)}, bf16[1024,256]{1,0:T(8,128)(2,1)S(1)}, u32[]{:S(2)}, u32[]{:S(2)}) collective-permute-start(bf16[1024,256]{1,0:T(8,128)(2,1)} %bitcast.341), channel_id=1, source_target_pairs={{0,1},{1,0},{2,3},{3,2},{4,5},{5,4},{6,7},{7,6},{8,9},{9,8},{10,11... | collective-permute-start | bytes 1572872 | tf_op jit(solution)/shard_map/ppermute | solution.py:896
  286.4 28.2 %collective-permute-start.61 = (bf16[1024,256]{1,0:T(8,128)(2,1)}, bf16[1024,256]{1,0:T(8,128)(2,1)S(1)}, u32[]{:S(2)}, u32[]{:S(2)}) collective-permute-start(bf16[1024,256]{1,0:T(8,128)(2,1)} %bitcast.340), channel_id=1, source_target_pairs={{0,2},{1,3},{2,0},{3,1},{4,6},{5,7},{6,4},{7,5},{8,10},{9,11},{10,... | collective-permute-start | bytes 1572872 | tf_op jit(solution)/shard_map/ppermute | solution.py:896
  288.2 26.5 %collective-permute-start.62 = (bf16[1024,256]{1,0:T(8,128)(2,1)}, bf16[1024,256]{1,0:T(8,128)(2,1)S(1)}, u32[]{:S(2)}, u32[]{:S(2)}) collective-permute-start(bf16[1024,256]{1,0:T(8,128)(2,1)} %bitcast.339), channel_id=1, source_target_pairs={{0,3},{1,2},{2,1},{3,0},{4,7},{5,6},{6,5},{7,4},{8,11},{9,10},{10,... | collective-permute-start | bytes 1572872 | tf_op jit(solution)/shard_map/ppermute | solution.py:896
  290.5 20.1 %collective-permute-start.54 = (bf16[2,128,1024]{2,1,0:T(8,128)(2,1)S(1)}, bf16[2,128,1024]{2,1,0:T(8,128)(2,1)S(1)}, u32[]{:S(2)}, u32[]{:S(2)}) collective-permute-start(bf16[2,128,1024]{2,1,0:T(8,128)(2,1)S(1)} %fusion.1), channel_id=1, source_target_pairs={{0,8},{4,12},{8,16},{12,20},{16,24},{20,28},{24,0},{28,4},{1,9},{5... | collective-permute-start | bytes 1572872 | tf_op jit(solution)/shard_map/ppermute | solution.py:914
  290.6 22.0 %collective-permute-start.53 = (bf16[2,128,1024]{2,1,0:T(8,128)(2,1)S(1)}, bf16[2,128,1024]{2,1,0:T(8,128)(2,1)S(1)}, u32[]{:S(2)}, u32[]{:S(2)}) collective-permute-start(bf16[2,128,1024]{2,1,0:T(8,128)(2,1)S(1)} %fusion.8), channel_id=1, source_target_pairs={{0,8},{4,12},{8,16},{12,20},{16,24},{20,28},{24,0},{28,4},{1,9},{5... | collective-permute-start | bytes 1572872 | tf_op jit(solution)/shard_map/ppermute | solution.py:914
  325.1 17.6 %collective-permute-start.63 = (bf16[4,128,1024]{2,1,0:T(8,128)(2,1)}, bf16[4,128,1024]{2,1,0:T(8,128)(2,1)}, u32[]{:S(2)}, u32[]{:S(2)}) collective-permute-start(bf16[4,128,1024]{2,1,0:T(8,128)(2,1)} %get-tuple-element.454), channel_id=1, source_target_pairs={{0,4},{4,0},{8,12},{12,8},{16,20},{20,16},{24,28},{28,24},{1,5},{5... | collective-permute-start | bytes 3145736 | tf_op jit(solution)/shard_map/ppermute | solution.py:917
  325.1 15.1 %collective-permute-start.66 = (bf16[256,1024]{1,0:T(8,128)(2,1)}, bf16[256,1024]{1,0:T(8,128)(2,1)}, u32[]{:S(2)}, u32[]{:S(2)}) collective-permute-start(bf16[256,1024]{1,0:T(8,128)(2,1)} %get-tuple-element.458), channel_id=1, source_target_pairs={{0,1},{1,0},{2,3},{3,2},{4,5},{5,4},{6,7},{7,6},{8,9},{9,8},{10,11... | collective-permute-start | bytes 1572872 | tf_op jit(solution)/shard_map/ppermute | solution.py:896
  326.5 16.1 %collective-permute-start.65 = (bf16[2,128,1024]{2,1,0:T(8,128)(2,1)}, bf16[2,128,1024]{2,1,0:T(8,128)(2,1)}, u32[]{:S(2)}, u32[]{:S(2)}) collective-permute-start(bf16[2,128,1024]{2,1,0:T(8,128)(2,1)} %fusion.2), channel_id=1, source_target_pairs={{0,8},{4,12},{8,16},{12,20},{16,24},{20,28},{24,0},{28,4},{1,9},{5... | collective-permute-start | bytes 1572872 | tf_op jit(solution)/shard_map/ppermute | solution.py:914
  327.9 26.6 %collective-permute-start.67 = (bf16[256,1024]{1,0:T(8,128)(2,1)}, bf16[256,1024]{1,0:T(8,128)(2,1)S(1)}, u32[]{:S(2)}, u32[]{:S(2)}) collective-permute-start(bf16[256,1024]{1,0:T(8,128)(2,1)} %get-tuple-element.461), channel_id=1, source_target_pairs={{0,2},{1,3},{2,0},{3,1},{4,6},{5,7},{6,4},{7,5},{8,10},{9,11},{10,... | collective-permute-start | bytes 1572872 | tf_op jit(solution)/shard_map/ppermute | solution.py:896
  329.9 29.0 %collective-permute-start.69 = (bf16[256,1024]{1,0:T(8,128)(2,1)}, bf16[256,1024]{1,0:T(8,128)(2,1)S(1)}, u32[]{:S(2)}, u32[]{:S(2)}) collective-permute-start(bf16[256,1024]{1,0:T(8,128)(2,1)} %get-tuple-element.477), channel_id=1, source_target_pairs={{0,3},{1,2},{2,1},{3,0},{4,7},{5,6},{6,5},{7,4},{8,11},{9,10},{10,... | collective-permute-start | bytes 1572872 | tf_op jit(solution)/shard_map/ppermute | solution.py:896
  358.9 13.2 %collective-permute-start.70 = (bf16[256,1024]{1,0:T(8,128)(2,1)S(1)}, bf16[256,1024]{1,0:T(8,128)(2,1)S(1)}, u32[]{:S(2)}, u32[]{:S(2)}) collective-permute-start(bf16[256,1024]{1,0:T(8,128)(2,1)S(1)} %copy-done.38), channel_id=1, source_target_pairs={{0,3},{1,2},{2,1},{3,0},{4,7},{5,6},{6,5},{7,4},{8,11},{9,10},{10,... | collective-permute-start | bytes 1572872 | tf_op jit(solution)/shard_map/ppermute | solution.py:896
  360.1 21.1 %collective-permute-start.72 = (bf16[2,128,1024]{2,1,0:T(8,128)(2,1)S(1)}, bf16[2,128,1024]{2,1,0:T(8,128)(2,1)S(1)}, u32[]{:S(2)}, u32[]{:S(2)}) collective-permute-start(bf16[2,128,1024]{2,1,0:T(8,128)(2,1)S(1)} %fusion), channel_id=1, source_target_pairs={{0,8},{4,12},{8,16},{12,20},{16,24},{20,28},{24,0},{28,4},{1,9},{5... | collective-permute-start | bytes 1572872 | tf_op jit(solution)/shard_map/ppermute | solution.py:914
  371.0 13.2 %collective-permute-start.71 = (bf16[128,1024]{1,0:T(8,128)(2,1)S(1)}, bf16[128,1024]{1,0:T(8,128)(2,1)S(1)}, u32[]{:S(2)}, u32[]{:S(2)}) collective-permute-start(bf16[128,1024]{1,0:T(8,128)(2,1)S(1)} %fusion.9), channel_id=1, source_target_pairs={{0,8},{4,12},{8,16},{12,20},{16,24},{20,28},{24,0},{28,4},{1,9},{5... | collective-permute-start | bytes 786440 | tf_op jit(solution)/shard_map/ppermute | solution.py:914
  (105 other events, 990.9 us)

commit v5 on v4

--- a/solution.py
+++ b/solution.py
@@ -237,7 +237,8 @@
     return spans + [slice(step * block, (step + 1) * block)]
 
 
-def attention_forward_kernel(heads, block, q_ref, k_ref, v_ref, out_ref):
+def attention_forward_kernel(heads, block, rows_each, scalars, q_ref, k_ref, v_ref, *refs):
+    out_refs, (held, out_ref, sems) = refs[:-3], refs[-3:]
     for head in range(heads):
         column = slice(head * HEAD_DIM, (head + 1) * HEAD_DIM)
         for step in range(q_ref.shape[0] // block):
@@ -251,6 +252,22 @@
                 ],
             )
             out_ref[rows, column] = mixed.astype(bf16)
+    step_now, lanes = pl.program_id(0), out_ref.shape[1]
+    if held.shape[1] == lanes:
+        held[...] = out_ref[...]
+    else:
+        held[:, aligned(step_now, lanes)] = out_ref[...]
+
+    @pl.when(step_now == pl.num_programs(0) - 1)
+    def _():
+        wait_all(
+            start_all(
+                [
+                    pltpu.make_async_copy(held.at[aligned(scalars[i], rows_each)], ref, sems.at[i])
+                    for i, ref in enumerate(out_refs)
+                ]
+            )
+        )
 
 
 def attention_backward_kernel(
@@ -316,19 +333,24 @@
     return length, heads, block, lanes, steps, spec, joined
 
 
-def attention_forward(qkv, width):
+def attention_forward(scalars, qkv, width, rows):
     length, heads, block, lanes, steps, spec, joined = attention_plan(qkv, width)
+    pieces = length // rows
     return run(
-        functools.partial(attention_forward_kernel, heads, block),
+        functools.partial(attention_forward_kernel, heads, block, rows),
         "attention_forward",
         10,
-        joined,
-        [spec(0), spec(1), spec(2)],
-        [((length, width), bf16)],
-        [spec(0)],
-        [],
+        [scalars] + joined,
+        [scalar, spec(0), spec(1), spec(2)],
+        [((rows, width), bf16)] * pieces,
+        [anywhere] * pieces,
+        [
+            pltpu.VMEM((length, width), bf16),
+            pltpu.VMEM((length, lanes), bf16),
+            pltpu.SemaphoreType.DMA((pieces,)),
+        ],
         (steps,),
-    )[0]
+    )
 
 
 def attention_backward(scalars, qkv, pieces, width):
@@ -1078,9 +1100,9 @@
     )
     qkv, dense_ring.parts[1] = sync(qkv, dense_ring.parts[1])
     dense_ring.move()
-    attended_heads = attention_forward(qkv, own_width)
+    attended_heads = list(attention_forward(peers, qkv, own_width, rows))
     attended_heads, out_pieces = sync(attended_heads, out_pieces)
-    attended = trade(by_peer(attended_heads.reshape(ctx, rows, own_width)))
+    attended = trade(attended_heads)
     full_out = natural(out_pieces).reshape(ctx, dp, share, width).transpose(1, 0, 2, 3)
     full_out = full_out.reshape(width, width)
     hidden_state, ffn_in, sorted_in = make_hidden(
@@ -1201,8 +1223,6 @@
     )
     grad_b_qkv, middle_rows, gb_dense, gb_first, gb_second = small_sources
     norm_pieces += late_pieces
-    sum_dense.close()
-    sum_first.close()
 
     def cut_columns(parts):
         joined = jnp.concatenate([part.astype(bf16) for part in parts], 1)
@@ -1217,6 +1237,11 @@
     result_pieces = result_pieces + [swap(result_sent[s], s) for s in shifts[2:]]
     grad_inputs, final_rows = make_final(peers, by_column, tokens, grad_hidden, norm_pieces)
     final_rows = pin(sum_last.move(final_rows), sum_last)
+    final_rows, sum_dense.arrived, sum_first.arrived = sync(
+        final_rows, sum_dense.arrived, sum_first.arrived
+    )
+    sum_dense.close()
+    sum_first.close()
 
     small_rows = jnp.concatenate(
         [middle_rows[:10], final_rows, grad_b_qkv, jnp.zeros((2, width), f32)], 0

time: 419 us -> 417 us (level)
  waiting for transfers between devices: 125 us -> 120 us
    unnamed x136 -> x138, local copies, waits for them, and re-layouts: 8.11 us -> 9.08 us
  transfers between devices with their start and end apart: 86 -> 86, of which waited for: 36 -> 34; matrix products, arithmetic and copies ran while one was open for 13% -> 13% of each run, Pallas kernels for 32% -> 32%
where the time goes in v5:
time: 417 us; the launch traced here: 410 us
  Pallas kernels  139 us (33%)
  waiting for transfers between devices  120 us (29%)
  starting transfers between devices  80.4 us (19%)
  other arithmetic  33.6 us (8%)
  local copies, waits for them, and re-layouts  33 us (8%)
    pallas_call x12, Pallas kernels, run(): pl.pallas_call(kernel, grid=grid, in_specs=specs, out_specs=out_specs, ou...  137 us
    ppermute x45, waiting for transfers between devices, swap(): return lax.ppermute(array, 'ctx', [(i, i ^ shift) for i in range(ctx)])  71.2 us
    ppermute x45, starting transfers between devices, swap(): return lax.ppermute(array, 'ctx', [(i, i ^ shift) for i in range(ctx)])  55.7 us
    ppermute x21, waiting for transfers between devices, ring(): return lax.ppermute(array, 'dp', ring_pairs)  45.4 us
    ppermute x21, starting transfers between devices, ring(): return lax.ppermute(array, 'dp', ring_pairs)  18 us
    convert_element_type x12, other arithmetic, add(): self.sent = [part.astype(bf16) if at else part for part in parts]  17.4 us
    unnamed x138, local copies, waits for them, and re-layouts  9.08 us
  transfers between devices with their start and end apart: 86, of which 34 were waited for; matrix products, arithmetic and copies ran while one was open for 13% of the time, Pallas kernels for 32%

profile of v5, /device:TPU:0, one launch (start us, length us, event | category | flops | bytes accessed | tf_op | source)
XLA Modules:
  0.0 409.7 jit_solution(8645451078141064216)
XLA Ops:
  0.7 3.0 collective-permute-start.5
  8.5 2.2 concatenate.40
  13.5 2.9 collective-permute-start.2
  18.6 1.8 collective-permute-start.7
  25.6 6.5 %collective-permute-done.3.refs_1_ = bf16[128,1152]{1,0:T(8,128)(2,1)} collective-permute-done((bf16[128,1152]{1,0:T(8,128)(2,1)S(1)}, bf16[128,1152]{1,0:T(8,128)(2,1)}, u32[]{:S(2)}, u32[]{:S(2)}) %collective-permute-start.3) | collective-permute-done | bytes 294944 | tf_op jit(solution)/shard_map/ppermute | solution.py:936
  34.0 7.0 %collective-permute-done.8.refs_2_ = bf16[128,1152]{1,0:T(8,128)(2,1)} collective-permute-done((bf16[128,1152]{1,0:T(8,128)(2,1)}, bf16[128,1152]{1,0:T(8,128)(2,1)}, u32[]{:S(2)}, u32[]{:S(2)}) %collective-permute-start.8) | collective-permute-done | bytes 294944 | tf_op jit(solution)/shard_map/ppermute | solution.py:936
  46.2 3.1 collective-permute-done.10
  49.3 4.7 %collective-permute-done.11 = bf16[3,32,1024]{2,1,0:T(8,128)(2,1)S(1)} collective-permute-done((bf16[3,32,1024]{2,1,0:T(8,128)(2,1)S(1)}, bf16[3,32,1024]{2,1,0:T(8,128)(2,1)S(1)}, u32[]{:S(2)}, u32[]{:S(2)}) %collective-permute-start.11) | collective-permute-done | bytes 196640 | tf_op jit(solution)/shard_map/ppermute | solution.py:918
  56.7 3.3 unpack.1
  61.8 1.8 collective-permute-start.19
  63.7 7.7 %norm_qkv.1 = (bf16[1024,768]{1,0:T(8,128)(2,1)}, bf16[1024,1024]{1,0:T(8,128)(2,1)}, bf16[1024,1152]{1,0:T(8,128)(2,1)}) custom-call(s32[12]{0:T(128)} %concatenate.47.scalars, f32[32,1024]{1,0:T(8,128)} %get-tuple-element.333.small_ref.by_column, bf16[128,1152]{1,0:T(8,128)(2,1)} %copy-done.17, bf16[128,1152]{1,0:T(8,128)(2,1)} %collective-permute-done.3.refs_1_, ...), custom_call_target="tpu_custom_call" | custom-call | flops 8000000000 | bytes 1024 | tf_op jit(solution)/shard_map/norm_qkv/pallas_call | solution.py:71
  71.5 4.2 %collective-permute-start.27 = (bf16[2,128,1024]{2,1,0:T(8,128)(2,1)S(1)}, bf16[2,128,1024]{2,1,0:T(8,128)(2,1)}, u32[]{:S(2)}, u32[]{:S(2)}) collective-permute-start(bf16[2,128,1024]{2,1,0:T(8,128)(2,1)S(1)} %collective-permute-done.16.refs_9_), channel_id=1, source_target_pairs={{0,8},{4,12},{8,16},{12,20},{16,24},{20,28},{24,0},{28,4},{1,9},{5... | collective-permute-start | bytes 1572872 | tf_op jit(solution)/shard_map/ppermute | solution.py:936
  75.7 10.6 %attention_forward.1 = (bf16[256,256]{1,0:T(8,128)(2,1)}, bf16[256,256]{1,0:T(8,128)(2,1)}, bf16[256,256]{1,0:T(8,128)(2,1)}, bf16[256,256]{1,0:T(8,128)(2,1)}) custom-call(s32[4]{0:T(128)} %pad_add_fusion.scalars.order, bf16[1024,768]{1,0:T(8,128)(2,1)} %get-tuple-element.314.q_ref.k_ref.v_ref, bf16[1024,768]{1,0:T(8,128)(2,1)} %get-tuple-element.314.q_ref.k_ref.v_ref, ...), custom_call_target="tpu_custom_call" | custom-call | flops 10000000000 | bytes 1024 | tf_op jit(solution)/shard_map/attention_forward/pallas_call | solution.py:71
  88.2 1.8 collective-permute-start.22
  92.5 2.3 collective-permute-done.21.refs_2_.refs_6_
  95.5 3.9 hidden.1
  101.3 1.7 collective-permute-start.26
  103.6 2.7 maximum_convert_fusion.1
  109.7 5.0 %collective-permute-done.24.refs_1_ = bf16[256,1024]{1,0:T(8,128)(2,1)} collective-permute-done((bf16[256,1024]{1,0:T(8,128)(2,1)}, bf16[256,1024]{1,0:T(8,128)(2,1)}, u32[]{:S(2)}, u32[]{:S(2)}) %collective-permute-start.24) | collective-permute-done | bytes 524320 | tf_op jit(solution)/shard_map/ppermute | solution.py:918
  114.7 9.3 %collective-permute-done.25.refs_2_ = bf16[256,1024]{1,0:T(8,128)(2,1)} collective-permute-done((bf16[256,1024]{1,0:T(8,128)(2,1)}, bf16[256,1024]{1,0:T(8,128)(2,1)}, u32[]{:S(2)}, u32[]{:S(2)}) %collective-permute-start.25) | collective-permute-done | bytes 524320 | tf_op jit(solution)/shard_map/ppermute | solution.py:918
  126.0 9.0 %collective-permute-done.30.refs_10_ = bf16[4,128,1024]{2,1,0:T(8,128)(2,1)} collective-permute-done((bf16[4,128,1024]{2,1,0:T(8,128)(2,1)}, bf16[4,128,1024]{2,1,0:T(8,128)(2,1)}, u32[]{:S(2)}, u32[]{:S(2)}) %collective-permute-start.30) | collective-permute-done | bytes 1048608 | tf_op jit(solution)/shard_map/ppermute | solution.py:936
  137.3 9.1 %collective-permute-done.29.refs_6_ = bf16[256,1024]{1,0:T(8,128)(2,1)S(1)} collective-permute-done((bf16[256,1024]{1,0:T(8,128)(2,1)S(1)}, bf16[256,1024]{1,0:T(8,128)(2,1)S(1)}, u32[]{:S(2)}, u32[]{:S(2)}) %collective-permute-start.29) | collective-permute-done | bytes 524320 | tf_op jit(solution)/shard_map/ppermute | solution.py:918
  151.5 23.4 %mlp.3 = (f32[1024,1024]{1,0:T(8,128)}, f32[1024,1024]{1,0:T(8,128)}, f32[1024,1]{1,0:T(8,128)}, f32[1,1024]{1,0:T(1,128)}, bf16[4,2,128,1024]{3,2,1,0:T(8,128)(2,1)}, /*index=5*/bf16[4,2,128,1024]{3,2,1,0:T(8,128)(2,1)}) custom-call(s32[12]{0:T(128)} %gate.2.scalars.refs_0_, bf16[1024,128]{1,0:T(8,128)(2,1)} %get-tuple-element.336.small_ref.by_row, ...), custom_call_target="tpu_custom_call" | custom-call | flops 20000000000 | bytes 1024 | tf_op jit(solution)/shard_map/mlp/pallas_call | solution.py:71
  180.9 2.0 collective-permute-start.42
  183.9 18.1 %mlp.4 = (f32[640,1024]{1,0:T(8,128)}, f32[640,1024]{1,0:T(8,128)}, f32[640,1]{1,0:T(8,128)}, f32[1,1024]{1,0:T(1,128)}, bf16[4,2,128,1024]{3,2,1,0:T(8,128)(2,1)}, /*index=5*/bf16[4,2,128,1024]{3,2,1,0:T(8,128)(2,1)}) custom-call(s32[12]{0:T(128)} %gate.3.scalars, bf16[1024,128]{1,0:T(8,128)(2,1)} %get-tuple-element.336.small_ref.by_row, ...), custom_call_target="tpu_custom_call" | custom-call | flops 17999998976 | bytes 1024 | tf_op jit(solution)/shard_map/mlp/pallas_call | solution.py:71
  203.4 1.9 collective-permute-start.44
  205.3 22.9 %mlp.5 = (bf16[256,1024]{1,0:T(8,128)(2,1)}, bf16[256,1024]{1,0:T(8,128)(2,1)}, bf16[256,1024]{1,0:T(8,128)(2,1)}, bf16[256,1024]{1,0:T(8,128)(2,1)}, bf16[256,1...) custom-call(s32[12]{0:T(128)} %gate.2.scalars.refs_0_, ...), custom_call_target="tpu_custom_call" | custom-call | flops 17999998976 | bytes 1024 | tf_op jit(solution)/shard_map/mlp/pallas_call | solution.py:71
  230.7 2.1 fusion.4
  238.3 6.4 %collective-permute-done.47.refs_1_ = bf16[256,1152]{1,0:T(8,128)(2,1)} collective-permute-done((bf16[256,1152]{1,0:T(8,128)(2,1)}, bf16[256,1152]{1,0:T(8,128)(2,1)}, u32[]{:S(2)}, u32[]{:S(2)}) %collective-permute-start.47) | collective-permute-done | bytes 589856 | tf_op jit(solution)/shard_map/ppermute | solution.py:918
  244.8 11.6 %collective-permute-done.48.refs_2_ = bf16[256,1152]{1,0:T(8,128)(2,1)} collective-permute-done((bf16[256,1152]{1,0:T(8,128)(2,1)}, bf16[256,1152]{1,0:T(8,128)(2,1)}, u32[]{:S(2)}, u32[]{:S(2)}) %collective-permute-start.48) | collective-permute-done | bytes 589856 | tf_op jit(solution)/shard_map/ppermute | solution.py:918
  258.5 4.8 %collective-permute-done.50 = bf16[2,128,1024]{2,1,0:T(8,128)(2,1)} collective-permute-done((bf16[2,128,1024]{2,1,0:T(8,128)(2,1)S(1)}, bf16[2,128,1024]{2,1,0:T(8,128)(2,1)}, u32[]{:S(2)}, u32[]{:S(2)}) %collective-permute-start.50) | collective-permute-done | bytes 524320 | tf_op jit(solution)/shard_map/ppermute | solution.py:936
  267.5 11.4 %middle.1 = (f32[256,1024]{1,0:T(8,128)}, f32[256,1024]{1,0:T(8,128)}, f32[16,1024]{1,0:T(8,128)}, bf16[8,4,32,256]{3,2,1,0:T(8,128)(2,1)}, bf16[8,4,32,256]{3,2...) custom-call(s32[4]{0:T(128)} %pad_add_fusion.scalars.order, ...), custom_call_target="tpu_custom_call" | custom-call | flops 11000000512 | bytes 1024 | tf_op jit(solution)/shard_map/middle/pallas_call | solution.py:71
  280.6 1.9 collective-permute-start.59
  291.8 1.7 collective-permute-start.53
  293.5 18.5 %attention_backward.1 = (bf16[1024,256]{1,0:T(8,128)(2,1)}, bf16[1024,256]{1,0:T(8,128)(2,1)}, bf16[1024,256]{1,0:T(8,128)(2,1)}) custom-call(s32[4]{0:T(128)} %pad_add_fusion.scalars.order, bf16[1024,768]{1,0:T(8,128)(2,1)} %get-tuple-element.314.q_ref.k_ref.v_ref, bf16[1024,768]{1,0:T(8,128)(2,1)} %get-tuple-element.314.q_ref.k_ref.v_ref, ...), custom_call_target="tpu_custom_call" | custom-call | flops 17999998976 | bytes 1024 | tf_op jit(solution)/shard_map/attention_backward/pallas_call | solution.py:71
  312.0 2.3 collective-permute-done.53
  314.3 2.2 fusion.2
  317.6 9.2 %qkv_back.1 = (bf16[256,1024]{1,0:T(8,128)(2,1)}, bf16[256,1024]{1,0:T(8,128)(2,1)}, bf16[256,1024]{1,0:T(8,128)(2,1)}, bf16[256,1024]{1,0:T(8,128)(2,1)}, bf16[...) custom-call(s32[12]{0:T(128)} %concatenate.47.scalars, ...), custom_call_target="tpu_custom_call" | custom-call | flops 8000000000 | bytes 1024 | tf_op jit(solution)/shard_map/qkv_back/pallas_call | solution.py:71
  329.7 1.8 collective-permute-start.67
  331.8 10.3 %collective-permute-done.66.refs_1_ = bf16[256,1024]{1,0:T(8,128)(2,1)} collective-permute-done((bf16[256,1024]{1,0:T(8,128)(2,1)}, bf16[256,1024]{1,0:T(8,128)(2,1)}, u32[]{:S(2)}, u32[]{:S(2)}) %collective-permute-start.66) | collective-permute-done | bytes 524320 | tf_op jit(solution)/shard_map/ppermute | solution.py:918
  342.1 2.0 collective-permute-done.65
  346.8 7.7 %collective-permute-done.64 = bf16[128,1024]{1,0:T(8,128)(2,1)S(1)} collective-permute-done((bf16[128,1024]{1,0:T(8,128)(2,1)S(1)}, bf16[128,1024]{1,0:T(8,128)(2,1)S(1)}, u32[]{:S(2)}, u32[]{:S(2)}) %collective-permute-start.64) | collective-permute-done | bytes 262176 | tf_op jit(solution)/shard_map/ppermute | solution.py:936
  356.0 1.8 collective-permute-start.70
  357.8 4.1 final.1
  361.9 5.1 %collective-permute-done.68 = bf16[128,1024]{1,0:T(8,128)(2,1)S(1)} collective-permute-done((bf16[128,1024]{1,0:T(8,128)(2,1)S(1)}, bf16[128,1024]{1,0:T(8,128)(2,1)S(1)}, u32[]{:S(2)}, u32[]{:S(2)}) %collective-permute-start.68) | collective-permute-done | bytes 262176 | tf_op jit(solution)/shard_map/ppermute | solution.py:936
  375.9 3.6 result.1
  390.6 4.4 %collective-permute-start.81 = (f32[24,1024]{1,0:T(8,128)S(1)}, f32[24,1024]{1,0:T(8,128)S(1)}, u32[]{:S(2)}, u32[]{:S(2)}) collective-permute-start(f32[24,1024]{1,0:T(8,128)S(1)} %add.359), channel_id=1, source_target_pairs={{0,16},{4,20},{8,24},{12,28},{16,0},{20,4},{24,8},{28,12},{1,17},{... | collective-permute-start | bytes 294920 | tf_op jit(solution)/shard_map/ppermute | solution.py:1264
  404.3 1.7 collective-permute-done.84
  (413 shorter events, 119.8 us)
Async XLA Ops:
  0.7 33.3 %collective-permute-start.5 = (bf16[256,1024]{1,0:T(8,128)(2,1)}, bf16[256,1024]{1,0:T(8,128)(2,1)}, u32[]{:S(2)}, u32[]{:S(2)}) collective-permute-start(bf16[256,1024]{1,0:T(8,128)(2,1)} %bitcast.323), channel_id=1, source_target_pairs={{0,1},{1,0},{2,3},{3,2},{4,5},{5,4},{6,7},{7,6},{8,9},{9,8},{10,11... | collective-permute-start | bytes 1572872 | tf_op jit(solution)/shard_map/ppermute | solution.py:918
  3.7 30.3 %collective-permute-start.6 = (bf16[256,1024]{1,0:T(8,128)(2,1)}, bf16[256,1024]{1,0:T(8,128)(2,1)}, u32[]{:S(2)}, u32[]{:S(2)}) collective-permute-start(bf16[256,1024]{1,0:T(8,128)(2,1)} %bitcast.324), channel_id=1, source_target_pairs={{0,2},{1,3},{2,0},{3,1},{4,6},{5,7},{6,4},{7,5},{8,10},{9,11},{10,... | collective-permute-start | bytes 1572872 | tf_op jit(solution)/shard_map/ppermute | solution.py:918
  18.6 15.4 %collective-permute-start.7 = (bf16[256,1024]{1,0:T(8,128)(2,1)}, bf16[256,1024]{1,0:T(8,128)(2,1)S(1)}, u32[]{:S(2)}, u32[]{:S(2)}) collective-permute-start(bf16[256,1024]{1,0:T(8,128)(2,1)} %bitcast.325), channel_id=1, source_target_pairs={{0,3},{1,2},{2,1},{3,0},{4,7},{5,6},{6,5},{7,4},{8,11},{9,10},{10,... | collective-permute-start | bytes 1572872 | tf_op jit(solution)/shard_map/ppermute | solution.py:918
  41.0 13.1 %collective-permute-start.13 = (bf16[128,1152]{1,0:T(8,128)(2,1)}, bf16[128,1152]{1,0:T(8,128)(2,1)}, u32[]{:S(2)}, u32[]{:S(2)}) collective-permute-start(bf16[128,1152]{1,0:T(8,128)(2,1)} %collective-permute-done.8.refs_2_), channel_id=1, source_target_pairs={{0,8},{4,12},{8,16},{12,20},{16,24},{20,28},{24,0},{28,4},{1,9},{5... | collective-permute-start | bytes 884744 | tf_op jit(solution)/shard_map/ppermute | solution.py:936
  41.0 13.1 %collective-permute-start.14 = (bf16[128,1152]{1,0:T(8,128)(2,1)}, bf16[128,1152]{1,0:T(8,128)(2,1)S(1)}, u32[]{:S(2)}, u32[]{:S(2)}) collective-permute-start(bf16[128,1152]{1,0:T(8,128)(2,1)} %collective-permute-done.8.refs_2_), channel_id=1, source_target_pairs={{0,4},{4,0},{8,12},{12,8},{16,20},{20,16},{24,28},{28,24},{1,5},{5... | collective-permute-start | bytes 884744 | tf_op jit(solution)/shard_map/ppermute | solution.py:939
  54.9 16.6 %collective-permute-start.16 = (bf16[2,128,1024]{2,1,0:T(8,128)(2,1)S(1)}, bf16[2,128,1024]{2,1,0:T(8,128)(2,1)S(1)}, u32[]{:S(2)}, u32[]{:S(2)}) collective-permute-start(bf16[2,128,1024]{2,1,0:T(8,128)(2,1)S(1)} %pad_maximum_fusion.3.refs_8_), channel_id=1, source_target_pairs={{0,8},{4,12},{8,16},{12,20},{16,24},{20,28},{24,0},{28,4},{1,9},{5... | collective-permute-start | bytes 1572872 | tf_op jit(solution)/shard_map/ppermute | solution.py:936
  60.0 26.4 %collective-permute-start.17 = (bf16[256,1024]{1,0:T(8,128)(2,1)}, bf16[256,1024]{1,0:T(8,128)(2,1)S(1)}, u32[]{:S(2)}, u32[]{:S(2)}) collective-permute-start(bf16[256,1024]{1,0:T(8,128)(2,1)} %get-tuple-element.320), channel_id=1, source_target_pairs={{0,1},{1,0},{2,3},{3,2},{4,5},{5,4},{6,7},{7,6},{8,9},{9,8},{10,11... | collective-permute-start | bytes 1572872 | tf_op jit(solution)/shard_map/ppermute | solution.py:918
  60.9 25.6 %collective-permute-start.18 = (bf16[256,1024]{1,0:T(8,128)(2,1)}, bf16[256,1024]{1,0:T(8,128)(2,1)S(1)}, u32[]{:S(2)}, u32[]{:S(2)}) collective-permute-start(bf16[256,1024]{1,0:T(8,128)(2,1)} %get-tuple-element.320), channel_id=1, source_target_pairs={{0,2},{1,3},{2,0},{3,1},{4,6},{5,7},{6,4},{7,5},{8,10},{9,11},{10,... | collective-permute-start | bytes 1572872 | tf_op jit(solution)/shard_map/ppermute | solution.py:918
  61.8 24.7 %collective-permute-start.19 = (bf16[256,1024]{1,0:T(8,128)(2,1)}, bf16[256,1024]{1,0:T(8,128)(2,1)S(1)}, u32[]{:S(2)}, u32[]{:S(2)}) collective-permute-start(bf16[256,1024]{1,0:T(8,128)(2,1)} %get-tuple-element.320), channel_id=1, source_target_pairs={{0,3},{1,2},{2,1},{3,0},{4,7},{5,6},{6,5},{7,4},{8,11},{9,10},{10,... | collective-permute-start | bytes 1572872 | tf_op jit(solution)/shard_map/ppermute | solution.py:918
  63.5 35.9 %collective-permute-start.23 = (bf16[4,128,1024]{2,1,0:T(8,128)(2,1)S(1)}, bf16[4,128,1024]{2,1,0:T(8,128)(2,1)S(1)}, u32[]{:S(2)}, u32[]{:S(2)}) collective-permute-start(bf16[4,128,1024]{2,1,0:T(8,128)(2,1)S(1)} %pad_maximum_fusion.refs_8_), channel_id=1, source_target_pairs={{0,8},{4,12},{8,16},{12,20},{16,24},{20,28},{24,0},{28,4},{1,9},{5... | collective-permute-start | bytes 3145736 | tf_op jit(solution)/shard_map/ppermute | solution.py:936
  71.5 36.1 %collective-permute-start.27 = (bf16[2,128,1024]{2,1,0:T(8,128)(2,1)S(1)}, bf16[2,128,1024]{2,1,0:T(8,128)(2,1)}, u32[]{:S(2)}, u32[]{:S(2)}) collective-permute-start(bf16[2,128,1024]{2,1,0:T(8,128)(2,1)S(1)} %collective-permute-done.16.refs_9_), channel_id=1, source_target_pairs={{0,8},{4,12},{8,16},{12,20},{16,24},{20,28},{24,0},{28,4},{1,9},{5... | collective-permute-start | bytes 1572872 | tf_op jit(solution)/shard_map/ppermute | solution.py:936
  99.4 15.2 %collective-permute-start.24 = (bf16[256,1024]{1,0:T(8,128)(2,1)}, bf16[256,1024]{1,0:T(8,128)(2,1)}, u32[]{:S(2)}, u32[]{:S(2)}) collective-permute-start(bf16[256,1024]{1,0:T(8,128)(2,1)} %get-tuple-element.338.refs_0_), channel_id=1, source_target_pairs={{0,1},{1,0},{2,3},{3,2},{4,5},{5,4},{6,7},{7,6},{8,9},{9,8},{10,11... | collective-permute-start | bytes 1572872 | tf_op jit(solution)/shard_map/ppermute | solution.py:918
  100.7 23.3 %collective-permute-start.25 = (bf16[256,1024]{1,0:T(8,128)(2,1)}, bf16[256,1024]{1,0:T(8,128)(2,1)}, u32[]{:S(2)}, u32[]{:S(2)}) collective-permute-start(bf16[256,1024]{1,0:T(8,128)(2,1)} %get-tuple-element.338.refs_0_), channel_id=1, source_target_pairs={{0,2},{1,3},{2,0},{3,1},{4,6},{5,7},{6,4},{7,5},{8,10},{9,11},{10,... | collective-permute-start | bytes 1572872 | tf_op jit(solution)/shard_map/ppermute | solution.py:918
  101.3 22.7 %collective-permute-start.26 = (bf16[256,1024]{1,0:T(8,128)(2,1)}, bf16[256,1024]{1,0:T(8,128)(2,1)}, u32[]{:S(2)}, u32[]{:S(2)}) collective-permute-start(bf16[256,1024]{1,0:T(8,128)(2,1)} %get-tuple-element.338.refs_0_), channel_id=1, source_target_pairs={{0,3},{1,2},{2,1},{3,0},{4,7},{5,6},{6,5},{7,4},{8,11},{9,10},{10,... | collective-permute-start | bytes 1572872 | tf_op jit(solution)/shard_map/ppermute | solution.py:918
  106.9 28.2 %collective-permute-start.30 = (bf16[4,128,1024]{2,1,0:T(8,128)(2,1)}, bf16[4,128,1024]{2,1,0:T(8,128)(2,1)}, u32[]{:S(2)}, u32[]{:S(2)}) collective-permute-start(bf16[4,128,1024]{2,1,0:T(8,128)(2,1)} %copy-done.30), channel_id=1, source_target_pairs={{0,8},{4,12},{8,16},{12,20},{16,24},{20,28},{24,0},{28,4},{1,9},{5... | collective-permute-start | bytes 3145736 | tf_op jit(solution)/shard_map/ppermute | solution.py:936
  124.0 13.3 %collective-permute-start.28 = (bf16[256,1024]{1,0:T(8,128)(2,1)S(1)}, bf16[256,1024]{1,0:T(8,128)(2,1)S(1)}, u32[]{:S(2)}, u32[]{:S(2)}) collective-permute-start(bf16[256,1024]{1,0:T(8,128)(2,1)S(1)} %convolution_convert_fusion.refs_4_), channel_id=1, source_target_pairs={{0,1},{1,0},{2,3},{3,2},{4,5},{5,4},{6,7},{7,6},{8,9},{9,8},{10,11... | collective-permute-start | bytes 1572872 | tf_op jit(solution)/shard_map/ppermute | solution.py:918
  124.9 21.6 %collective-permute-start.29 = (bf16[256,1024]{1,0:T(8,128)(2,1)S(1)}, bf16[256,1024]{1,0:T(8,128)(2,1)S(1)}, u32[]{:S(2)}, u32[]{:S(2)}) collective-permute-start(bf16[256,1024]{1,0:T(8,128)(2,1)S(1)} %convolution_convert_fusion.refs_4_), channel_id=1, source_target_pairs={{0,2},{1,3},{2,0},{3,1},{4,6},{5,7},{6,4},{7,5},{8,10},{9,11},{10,... | collective-permute-start | bytes 1572872 | tf_op jit(solution)/shard_map/ppermute | solution.py:918
  125.7 20.7 %collective-permute-start.32 = (bf16[2,128,1024]{2,1,0:T(8,128)(2,1)}, bf16[2,128,1024]{2,1,0:T(8,128)(2,1)S(1)}, u32[]{:S(2)}, u32[]{:S(2)}) collective-permute-start(bf16[2,128,1024]{2,1,0:T(8,128)(2,1)} %collective-permute-done.27.refs_1_.refs_10_), channel_id=1, source_target_pairs={{0,8},{4,12},{8,16},{12,20},{16,24},{20,28},{24,0},{28,4},{1,9},{5... | collective-permute-start | bytes 1572872 | tf_op jit(solution)/shard_map/ppermute | solution.py:936
  135.1 11.4 %collective-permute-start.31 = (bf16[256,1024]{1,0:T(8,128)(2,1)S(1)}, bf16[256,1024]{1,0:T(8,128)(2,1)S(1)}, u32[]{:S(2)}, u32[]{:S(2)}) collective-permute-start(bf16[256,1024]{1,0:T(8,128)(2,1)S(1)} %convolution_convert_fusion.refs_4_), channel_id=1, source_target_pairs={{0,3},{1,2},{2,1},{3,0},{4,7},{5,6},{6,5},{7,4},{8,11},{9,10},{10,... | collective-permute-start | bytes 1572872 | tf_op jit(solution)/shard_map/ppermute | solution.py:918
  148.2 27.9 %collective-permute-start.38 = (bf16[4,128,1024]{2,1,0:T(8,128)(2,1)}, bf16[4,128,1024]{2,1,0:T(8,128)(2,1)}, u32[]{:S(2)}, u32[]{:S(2)}) collective-permute-start(bf16[4,128,1024]{2,1,0:T(8,128)(2,1)} %collective-permute-done.30.refs_10_), channel_id=1, source_target_pairs={{0,8},{4,12},{8,16},{12,20},{16,24},{20,28},{24,0},{28,4},{1,9},{5... | collective-permute-start | bytes 3145736 | tf_op jit(solution)/shard_map/ppermute | solution.py:936
  150.7 25.4 %collective-permute-start.39 = (bf16[4,128,1024]{2,1,0:T(8,128)(2,1)S(1)}, bf16[4,128,1024]{2,1,0:T(8,128)(2,1)S(1)}, u32[]{:S(2)}, u32[]{:S(2)}) collective-permute-start(bf16[4,128,1024]{2,1,0:T(8,128)(2,1)S(1)} %pad_maximum_fusion.refs_8_), channel_id=1, source_target_pairs={{0,4},{4,0},{8,12},{12,8},{16,20},{20,16},{24,28},{28,24},{1,5},{5... | collective-permute-start | bytes 3145736 | tf_op jit(solution)/shard_map/ppermute | solution.py:939
  150.9 25.3 %collective-permute-start.40 = (bf16[4,128,1024]{2,1,0:T(8,128)(2,1)}, bf16[4,128,1024]{2,1,0:T(8,128)(2,1)S(1)}, u32[]{:S(2)}, u32[]{:S(2)}) collective-permute-start(bf16[4,128,1024]{2,1,0:T(8,128)(2,1)} %copy-done.30), channel_id=1, source_target_pairs={{0,4},{4,0},{8,12},{12,8},{16,20},{20,16},{24,28},{28,24},{1,5},{5... | collective-permute-start | bytes 3145736 | tf_op jit(solution)/shard_map/ppermute | solution.py:939
  151.2 24.9 %collective-permute-start.41 = (bf16[4,128,1024]{2,1,0:T(8,128)(2,1)}, bf16[4,128,1024]{2,1,0:T(8,128)(2,1)S(1)}, u32[]{:S(2)}, u32[]{:S(2)}) collective-permute-start(bf16[4,128,1024]{2,1,0:T(8,128)(2,1)} %collective-permute-done.30.refs_10_), channel_id=1, source_target_pairs={{0,4},{4,0},{8,12},{12,8},{16,20},{20,16},{24,28},{28,24},{1,5},{5... | collective-permute-start | bytes 3145736 | tf_op jit(solution)/shard_map/ppermute | solution.py:939
  180.9 21.2 %collective-permute-start.42 = (bf16[2,128,1024]{2,1,0:T(8,128)(2,1)S(1)}, bf16[2,128,1024]{2,1,0:T(8,128)(2,1)S(1)}, u32[]{:S(2)}, u32[]{:S(2)}) collective-permute-start(bf16[2,128,1024]{2,1,0:T(8,128)(2,1)S(1)} %fusion.6), channel_id=1, source_target_pairs={{0,8},{4,12},{8,16},{12,20},{16,24},{20,28},{24,0},{28,4},{1,9},{5... | collective-permute-start | bytes 1572872 | tf_op jit(solution)/shard_map/ppermute | solution.py:936
  202.0 30.8 %collective-permute-start.45 = (bf16[4,2,128,1024]{3,2,1,0:T(8,128)(2,1)}, bf16[4,2,128,1024]{3,2,1,0:T(8,128)(2,1)S(1)}, u32[]{:S(2)}, u32[]{:S(2)}) collective-permute-start(bf16[4,2,128,1024]{3,2,1,0:T(8,128)(2,1)} %get-tuple-element.387), channel_id=1, source_target_pairs={{0,4},{4,0},{8,12},{12,8},{16,20},{20,16},{24,28},{28,24},{1,5},{5... | collective-permute-start | bytes 6291464 | tf_op jit(solution)/shard_map/ppermute | solution.py:939
  203.4 27.3 %collective-permute-start.44 = (bf16[2,128,1024]{2,1,0:T(8,128)(2,1)S(1)}, bf16[2,128,1024]{2,1,0:T(8,128)(2,1)S(1)}, u32[]{:S(2)}, u32[]{:S(2)}) collective-permute-start(bf16[2,128,1024]{2,1,0:T(8,128)(2,1)S(1)} %fusion.5), channel_id=1, source_target_pairs={{0,8},{4,12},{8,16},{12,20},{16,24},{20,28},{24,0},{28,4},{1,9},{5... | collective-permute-start | bytes 1572872 | tf_op jit(solution)/shard_map/ppermute | solution.py:936
  228.2 16.5 %collective-permute-start.47 = (bf16[256,1152]{1,0:T(8,128)(2,1)}, bf16[256,1152]{1,0:T(8,128)(2,1)}, u32[]{:S(2)}, u32[]{:S(2)}) collective-permute-start(bf16[256,1152]{1,0:T(8,128)(2,1)} %get-tuple-element.392), channel_id=1, source_target_pairs={{0,1},{1,0},{2,3},{3,2},{4,5},{5,4},{6,7},{7,6},{8,9},{9,8},{10,11... | collective-permute-start | bytes 1769480 | tf_op jit(solution)/shard_map/ppermute | solution.py:918
  229.5 27.0 %collective-permute-start.48 = (bf16[256,1152]{1,0:T(8,128)(2,1)}, bf16[256,1152]{1,0:T(8,128)(2,1)}, u32[]{:S(2)}, u32[]{:S(2)}) collective-permute-start(bf16[256,1152]{1,0:T(8,128)(2,1)} %get-tuple-element.393), channel_id=1, source_target_pairs={{0,2},{1,3},{2,0},{3,1},{4,6},{5,7},{6,4},{7,5},{8,10},{9,11},{10,... | collective-permute-start | bytes 1769480 | tf_op jit(solution)/shard_map/ppermute | solution.py:918
  235.6 22.0 %collective-permute-start.49 = (bf16[256,1152]{1,0:T(8,128)(2,1)S(1)}, bf16[256,1152]{1,0:T(8,128)(2,1)}, u32[]{:S(2)}, u32[]{:S(2)}) collective-permute-start(bf16[256,1152]{1,0:T(8,128)(2,1)S(1)} %copy-done.35), channel_id=1, source_target_pairs={{0,3},{1,2},{2,1},{3,0},{4,7},{5,6},{6,5},{7,4},{8,11},{9,10},{10,... | collective-permute-start | bytes 1769480 | tf_op jit(solution)/shard_map/ppermute | solution.py:918
  236.8 21.7 %collective-permute-start.46 = (bf16[2,128,1024]{2,1,0:T(8,128)(2,1)}, bf16[2,128,1024]{2,1,0:T(8,128)(2,1)S(1)}, u32[]{:S(2)}, u32[]{:S(2)}) collective-permute-start(bf16[2,128,1024]{2,1,0:T(8,128)(2,1)} %fusion.4), channel_id=1, source_target_pairs={{0,8},{4,12},{8,16},{12,20},{16,24},{20,28},{24,0},{28,4},{1,9},{5... | collective-permute-start | bytes 1572872 | tf_op jit(solution)/shard_map/ppermute | solution.py:936
  238.0 25.3 %collective-permute-start.50 = (bf16[2,128,1024]{2,1,0:T(8,128)(2,1)S(1)}, bf16[2,128,1024]{2,1,0:T(8,128)(2,1)}, u32[]{:S(2)}, u32[]{:S(2)}) collective-permute-start(bf16[2,128,1024]{2,1,0:T(8,128)(2,1)S(1)} %fusion.7), channel_id=1, source_target_pairs={{0,8},{4,12},{8,16},{12,20},{16,24},{20,28},{24,0},{28,4},{1,9},{5... | collective-permute-start | bytes 1572872 | tf_op jit(solution)/shard_map/ppermute | solution.py:936
  257.7 32.5 %collective-permute-start.51 = (bf16[4,2,128,1024]{3,2,1,0:T(8,128)(2,1)}, bf16[4,2,128,1024]{3,2,1,0:T(8,128)(2,1)}, u32[]{:S(2)}, u32[]{:S(2)}) collective-permute-start(bf16[4,2,128,1024]{3,2,1,0:T(8,128)(2,1)} %get-tuple-element.422), channel_id=1, source_target_pairs={{0,4},{4,0},{8,12},{12,8},{16,20},{20,16},{24,28},{28,24},{1,5},{5... | collective-permute-start | bytes 6291464 | tf_op jit(solution)/shard_map/ppermute | solution.py:939
  264.9 14.0 %collective-permute-start.55 = (bf16[256,1024]{1,0:T(8,128)(2,1)S(1)}, bf16[256,1024]{1,0:T(8,128)(2,1)S(1)}, u32[]{:S(2)}, u32[]{:S(2)}) collective-permute-start(bf16[256,1024]{1,0:T(8,128)(2,1)S(1)} %copy-done.45), channel_id=1, source_target_pairs={{0,1},{1,0},{2,3},{3,2},{4,5},{5,4},{6,7},{7,6},{8,9},{9,8},{10,11... | collective-permute-start | bytes 1572872 | tf_op jit(solution)/shard_map/ppermute | solution.py:918
  266.2 12.7 %collective-permute-start.56 = (bf16[256,1024]{1,0:T(8,128)(2,1)S(1)}, bf16[256,1024]{1,0:T(8,128)(2,1)S(1)}, u32[]{:S(2)}, u32[]{:S(2)}) collective-permute-start(bf16[256,1024]{1,0:T(8,128)(2,1)S(1)} %copy-done.44), channel_id=1, source_target_pairs={{0,2},{1,3},{2,0},{3,1},{4,6},{5,7},{6,4},{7,5},{8,10},{9,11},{10,... | collective-permute-start | bytes 1572872 | tf_op jit(solution)/shard_map/ppermute | solution.py:918
  267.5 15.0 %collective-permute-start.52 = (bf16[2,128,1024]{2,1,0:T(8,128)(2,1)S(1)}, bf16[2,128,1024]{2,1,0:T(8,128)(2,1)S(1)}, u32[]{:S(2)}, u32[]{:S(2)}) collective-permute-start(bf16[2,128,1024]{2,1,0:T(8,128)(2,1)S(1)} %fusion.3), channel_id=1, source_target_pairs={{0,8},{4,12},{8,16},{12,20},{16,24},{20,28},{24,0},{28,4},{1,9},{5... | collective-permute-start | bytes 1572872 | tf_op jit(solution)/shard_map/ppermute | solution.py:936
  286.7 29.8 %collective-permute-start.60 = (bf16[1024,256]{1,0:T(8,128)(2,1)}, bf16[1024,256]{1,0:T(8,128)(2,1)S(1)}, u32[]{:S(2)}, u32[]{:S(2)}) collective-permute-start(bf16[1024,256]{1,0:T(8,128)(2,1)} %bitcast.331), channel_id=1, source_target_pairs={{0,1},{1,0},{2,3},{3,2},{4,5},{5,4},{6,7},{7,6},{8,9},{9,8},{10,11... | collective-permute-start | bytes 1572872 | tf_op jit(solution)/shard_map/ppermute | solution.py:918
  288.0 28.5 %collective-permute-start.61 = (bf16[1024,256]{1,0:T(8,128)(2,1)}, bf16[1024,256]{1,0:T(8,128)(2,1)S(1)}, u32[]{:S(2)}, u32[]{:S(2)}) collective-permute-start(bf16[1024,256]{1,0:T(8,128)(2,1)} %bitcast.330), channel_id=1, source_target_pairs={{0,2},{1,3},{2,0},{3,1},{4,6},{5,7},{6,4},{7,5},{8,10},{9,11},{10,... | collective-permute-start | bytes 1572872 | tf_op jit(solution)/shard_map/ppermute | solution.py:918
  289.6 26.9 %collective-permute-start.62 = (bf16[1024,256]{1,0:T(8,128)(2,1)}, bf16[1024,256]{1,0:T(8,128)(2,1)S(1)}, u32[]{:S(2)}, u32[]{:S(2)}) collective-permute-start(bf16[1024,256]{1,0:T(8,128)(2,1)} %bitcast.329), channel_id=1, source_target_pairs={{0,3},{1,2},{2,1},{3,0},{4,7},{5,6},{6,5},{7,4},{8,11},{9,10},{10,... | collective-permute-start | bytes 1572872 | tf_op jit(solution)/shard_map/ppermute | solution.py:918
  291.5 20.5 %collective-permute-start.54 = (bf16[2,128,1024]{2,1,0:T(8,128)(2,1)S(1)}, bf16[2,128,1024]{2,1,0:T(8,128)(2,1)S(1)}, u32[]{:S(2)}, u32[]{:S(2)}) collective-permute-start(bf16[2,128,1024]{2,1,0:T(8,128)(2,1)S(1)} %fusion.1), channel_id=1, source_target_pairs={{0,8},{4,12},{8,16},{12,20},{16,24},{20,28},{24,0},{28,4},{1,9},{5... | collective-permute-start | bytes 1572872 | tf_op jit(solution)/shard_map/ppermute | solution.py:936
  291.8 22.5 %collective-permute-start.53 = (bf16[2,128,1024]{2,1,0:T(8,128)(2,1)S(1)}, bf16[2,128,1024]{2,1,0:T(8,128)(2,1)S(1)}, u32[]{:S(2)}, u32[]{:S(2)}) collective-permute-start(bf16[2,128,1024]{2,1,0:T(8,128)(2,1)S(1)} %fusion.8), channel_id=1, source_target_pairs={{0,8},{4,12},{8,16},{12,20},{16,24},{20,28},{24,0},{28,4},{1,9},{5... | collective-permute-start | bytes 1572872 | tf_op jit(solution)/shard_map/ppermute | solution.py:936
  326.9 17.2 %collective-permute-start.63 = (bf16[4,128,1024]{2,1,0:T(8,128)(2,1)}, bf16[4,128,1024]{2,1,0:T(8,128)(2,1)}, u32[]{:S(2)}, u32[]{:S(2)}) collective-permute-start(bf16[4,128,1024]{2,1,0:T(8,128)(2,1)} %get-tuple-element.471), channel_id=1, source_target_pairs={{0,4},{4,0},{8,12},{12,8},{16,20},{20,16},{24,28},{28,24},{1,5},{5... | collective-permute-start | bytes 3145736 | tf_op jit(solution)/shard_map/ppermute | solution.py:939
  327.0 15.1 %collective-permute-start.66 = (bf16[256,1024]{1,0:T(8,128)(2,1)}, bf16[256,1024]{1,0:T(8,128)(2,1)}, u32[]{:S(2)}, u32[]{:S(2)}) collective-permute-start(bf16[256,1024]{1,0:T(8,128)(2,1)} %get-tuple-element.475), channel_id=1, source_target_pairs={{0,1},{1,0},{2,3},{3,2},{4,5},{5,4},{6,7},{7,6},{8,9},{9,8},{10,11... | collective-permute-start | bytes 1572872 | tf_op jit(solution)/shard_map/ppermute | solution.py:918
  327.9 16.1 %collective-permute-start.65 = (bf16[2,128,1024]{2,1,0:T(8,128)(2,1)}, bf16[2,128,1024]{2,1,0:T(8,128)(2,1)}, u32[]{:S(2)}, u32[]{:S(2)}) collective-permute-start(bf16[2,128,1024]{2,1,0:T(8,128)(2,1)} %fusion.2), channel_id=1, source_target_pairs={{0,8},{4,12},{8,16},{12,20},{16,24},{20,28},{24,0},{28,4},{1,9},{5... | collective-permute-start | bytes 1572872 | tf_op jit(solution)/shard_map/ppermute | solution.py:936
  329.7 25.9 %collective-permute-start.67 = (bf16[256,1024]{1,0:T(8,128)(2,1)}, bf16[256,1024]{1,0:T(8,128)(2,1)S(1)}, u32[]{:S(2)}, u32[]{:S(2)}) collective-permute-start(bf16[256,1024]{1,0:T(8,128)(2,1)} %get-tuple-element.478), channel_id=1, source_target_pairs={{0,2},{1,3},{2,0},{3,1},{4,6},{5,7},{6,4},{7,5},{8,10},{9,11},{10,... | collective-permute-start | bytes 1572872 | tf_op jit(solution)/shard_map/ppermute | solution.py:918
  331.5 24.1 %collective-permute-start.69 = (bf16[256,1024]{1,0:T(8,128)(2,1)}, bf16[256,1024]{1,0:T(8,128)(2,1)S(1)}, u32[]{:S(2)}, u32[]{:S(2)}) collective-permute-start(bf16[256,1024]{1,0:T(8,128)(2,1)} %get-tuple-element.494), channel_id=1, source_target_pairs={{0,3},{1,2},{2,1},{3,0},{4,7},{5,6},{6,5},{7,4},{8,11},{9,10},{10,... | collective-permute-start | bytes 1572872 | tf_op jit(solution)/shard_map/ppermute | solution.py:918
  355.7 11.3 %collective-permute-start.68 = (bf16[128,1024]{1,0:T(8,128)(2,1)S(1)}, bf16[128,1024]{1,0:T(8,128)(2,1)S(1)}, u32[]{:S(2)}, u32[]{:S(2)}) collective-permute-start(bf16[128,1024]{1,0:T(8,128)(2,1)S(1)} %fusion.10), channel_id=1, source_target_pairs={{0,8},{4,12},{8,16},{12,20},{16,24},{20,28},{24,0},{28,4},{1,9},{5... | collective-permute-start | bytes 786440 | tf_op jit(solution)/shard_map/ppermute | solution.py:936
  356.0 16.4 %collective-permute-start.70 = (bf16[256,1024]{1,0:T(8,128)(2,1)S(1)}, bf16[256,1024]{1,0:T(8,128)(2,1)S(1)}, u32[]{:S(2)}, u32[]{:S(2)}) collective-permute-start(bf16[256,1024]{1,0:T(8,128)(2,1)S(1)} %copy-done.36), channel_id=1, source_target_pairs={{0,3},{1,2},{2,1},{3,0},{4,7},{5,6},{6,5},{7,4},{8,11},{9,10},{10,... | collective-permute-start | bytes 1572872 | tf_op jit(solution)/shard_map/ppermute | solution.py:918
  357.8 21.7 %collective-permute-start.72 = (bf16[2,128,1024]{2,1,0:T(8,128)(2,1)S(1)}, bf16[2,128,1024]{2,1,0:T(8,128)(2,1)S(1)}, u32[]{:S(2)}, u32[]{:S(2)}) collective-permute-start(bf16[2,128,1024]{2,1,0:T(8,128)(2,1)S(1)} %fusion), channel_id=1, source_target_pairs={{0,8},{4,12},{8,16},{12,20},{16,24},{20,28},{24,0},{28,4},{1,9},{5... | collective-permute-start | bytes 1572872 | tf_op jit(solution)/shard_map/ppermute | solution.py:936
  (106 other events, 1025.4 us)

commit v6 on v5

--- a/solution.py
+++ b/solution.py
@@ -1175,7 +1175,7 @@
     grad_pieces, halves, result_sent = sync(
         grad_pieces, second_mlp[2 * ctx + 1 :], second_mlp[:ctx]
     )
-    grad_pieces = sum_first.move(sum_dense.receive(grad_pieces))
+    grad_pieces = sum_dense.receive(sum_first.move(grad_pieces))
     sum_second = Scatter(*halves)
     result_pieces = [result_sent[0]] + [swap(result_sent[s], s) for s in shifts[:2]]
 

time: 417 us -> 417 us (level)
  no operation moved by 1% of the time
where the time goes in v6:
time: 417 us; the launch traced here: 410 us
  Pallas kernels  139 us (33%)
  waiting for transfers between devices  120 us (29%)
  starting transfers between devices  80.5 us (19%)
  other arithmetic  33.8 us (8%)
  local copies, waits for them, and re-layouts  33 us (8%)
    pallas_call x12, Pallas kernels, run(): pl.pallas_call(kernel, grid=grid, in_specs=specs, out_specs=out_specs, ou...  137 us
    ppermute x45, waiting for transfers between devices, swap(): return lax.ppermute(array, 'ctx', [(i, i ^ shift) for i in range(ctx)])  71.3 us
    ppermute x45, starting transfers between devices, swap(): return lax.ppermute(array, 'ctx', [(i, i ^ shift) for i in range(ctx)])  55.7 us
    ppermute x21, waiting for transfers between devices, ring(): return lax.ppermute(array, 'dp', ring_pairs)  45 us
    ppermute x21, starting transfers between devices, ring(): return lax.ppermute(array, 'dp', ring_pairs)  18 us
    convert_element_type x12, other arithmetic, add(): self.sent = [part.astype(bf16) if at else part for part in parts]  17.6 us
    unnamed x138, local copies, waits for them, and re-layouts  9.08 us
  transfers between devices with their start and end apart: 86, of which 34 were waited for; matrix products, arithmetic and copies ran while one was open for 13% of the time, Pallas kernels for 32%

profile of v6, /device:TPU:0, one launch (start us, length us, event | category | flops | bytes accessed | tf_op | source)
XLA Modules:
  0.0 409.6 jit_solution(9247632208414680989)
XLA Ops:
  0.7 3.0 collective-permute-start.5
  8.5 2.2 concatenate.40
  13.5 2.9 collective-permute-start.2
  18.6 1.8 collective-permute-start.7
  25.6 6.5 %collective-permute-done.3.refs_1_ = bf16[128,1152]{1,0:T(8,128)(2,1)} collective-permute-done((bf16[128,1152]{1,0:T(8,128)(2,1)S(1)}, bf16[128,1152]{1,0:T(8,128)(2,1)}, u32[]{:S(2)}, u32[]{:S(2)}) %collective-permute-start.3) | collective-permute-done | bytes 294944 | tf_op jit(solution)/shard_map/ppermute | solution.py:936
  34.0 7.0 %collective-permute-done.8.refs_2_ = bf16[128,1152]{1,0:T(8,128)(2,1)} collective-permute-done((bf16[128,1152]{1,0:T(8,128)(2,1)}, bf16[128,1152]{1,0:T(8,128)(2,1)}, u32[]{:S(2)}, u32[]{:S(2)}) %collective-permute-start.8) | collective-permute-done | bytes 294944 | tf_op jit(solution)/shard_map/ppermute | solution.py:936
  46.2 3.1 collective-permute-done.10
  49.3 4.7 %collective-permute-done.11 = bf16[3,32,1024]{2,1,0:T(8,128)(2,1)S(1)} collective-permute-done((bf16[3,32,1024]{2,1,0:T(8,128)(2,1)S(1)}, bf16[3,32,1024]{2,1,0:T(8,128)(2,1)S(1)}, u32[]{:S(2)}, u32[]{:S(2)}) %collective-permute-start.11) | collective-permute-done | bytes 196640 | tf_op jit(solution)/shard_map/ppermute | solution.py:918
  56.7 3.3 unpack.1
  61.8 1.8 collective-permute-start.19
  63.7 7.7 %norm_qkv.1 = (bf16[1024,768]{1,0:T(8,128)(2,1)}, bf16[1024,1024]{1,0:T(8,128)(2,1)}, bf16[1024,1152]{1,0:T(8,128)(2,1)}) custom-call(s32[12]{0:T(128)} %concatenate.47.scalars, f32[32,1024]{1,0:T(8,128)} %get-tuple-element.333.small_ref.by_column, bf16[128,1152]{1,0:T(8,128)(2,1)} %copy-done.17, bf16[128,1152]{1,0:T(8,128)(2,1)} %collective-permute-done.3.refs_1_, ...), custom_call_target="tpu_custom_call" | custom-call | flops 8000000000 | bytes 1024 | tf_op jit(solution)/shard_map/norm_qkv/pallas_call | solution.py:71
  71.5 4.2 %collective-permute-start.27 = (bf16[2,128,1024]{2,1,0:T(8,128)(2,1)S(1)}, bf16[2,128,1024]{2,1,0:T(8,128)(2,1)}, u32[]{:S(2)}, u32[]{:S(2)}) collective-permute-start(bf16[2,128,1024]{2,1,0:T(8,128)(2,1)S(1)} %collective-permute-done.16.refs_9_), channel_id=1, source_target_pairs={{0,8},{4,12},{8,16},{12,20},{16,24},{20,28},{24,0},{28,4},{1,9},{5... | collective-permute-start | bytes 1572872 | tf_op jit(solution)/shard_map/ppermute | solution.py:936
  75.7 10.6 %attention_forward.1 = (bf16[256,256]{1,0:T(8,128)(2,1)}, bf16[256,256]{1,0:T(8,128)(2,1)}, bf16[256,256]{1,0:T(8,128)(2,1)}, bf16[256,256]{1,0:T(8,128)(2,1)}) custom-call(s32[4]{0:T(128)} %pad_add_fusion.scalars.order, bf16[1024,768]{1,0:T(8,128)(2,1)} %get-tuple-element.314.q_ref.k_ref.v_ref, bf16[1024,768]{1,0:T(8,128)(2,1)} %get-tuple-element.314.q_ref.k_ref.v_ref, ...), custom_call_target="tpu_custom_call" | custom-call | flops 10000000000 | bytes 1024 | tf_op jit(solution)/shard_map/attention_forward/pallas_call | solution.py:71
  88.2 1.8 collective-permute-start.22
  92.5 2.3 collective-permute-done.21.refs_2_.refs_6_
  95.5 3.9 hidden.1
  103.6 2.7 maximum_convert_fusion.1
  109.7 5.0 %collective-permute-done.24.refs_1_ = bf16[256,1024]{1,0:T(8,128)(2,1)} collective-permute-done((bf16[256,1024]{1,0:T(8,128)(2,1)}, bf16[256,1024]{1,0:T(8,128)(2,1)}, u32[]{:S(2)}, u32[]{:S(2)}) %collective-permute-start.24) | collective-permute-done | bytes 524320 | tf_op jit(solution)/shard_map/ppermute | solution.py:918
  114.7 9.3 %collective-permute-done.25.refs_2_ = bf16[256,1024]{1,0:T(8,128)(2,1)} collective-permute-done((bf16[256,1024]{1,0:T(8,128)(2,1)}, bf16[256,1024]{1,0:T(8,128)(2,1)}, u32[]{:S(2)}, u32[]{:S(2)}) %collective-permute-start.25) | collective-permute-done | bytes 524320 | tf_op jit(solution)/shard_map/ppermute | solution.py:918
  126.0 9.0 %collective-permute-done.30.refs_10_ = bf16[4,128,1024]{2,1,0:T(8,128)(2,1)} collective-permute-done((bf16[4,128,1024]{2,1,0:T(8,128)(2,1)}, bf16[4,128,1024]{2,1,0:T(8,128)(2,1)}, u32[]{:S(2)}, u32[]{:S(2)}) %collective-permute-start.30) | collective-permute-done | bytes 1048608 | tf_op jit(solution)/shard_map/ppermute | solution.py:936
  137.3 9.1 %collective-permute-done.29.refs_6_ = bf16[256,1024]{1,0:T(8,128)(2,1)S(1)} collective-permute-done((bf16[256,1024]{1,0:T(8,128)(2,1)S(1)}, bf16[256,1024]{1,0:T(8,128)(2,1)S(1)}, u32[]{:S(2)}, u32[]{:S(2)}) %collective-permute-start.29) | collective-permute-done | bytes 524320 | tf_op jit(solution)/shard_map/ppermute | solution.py:918
  151.5 23.4 %mlp.3 = (f32[1024,1024]{1,0:T(8,128)}, f32[1024,1024]{1,0:T(8,128)}, f32[1024,1]{1,0:T(8,128)}, f32[1,1024]{1,0:T(1,128)}, bf16[4,2,128,1024]{3,2,1,0:T(8,128)(2,1)}, /*index=5*/bf16[4,2,128,1024]{3,2,1,0:T(8,128)(2,1)}) custom-call(s32[12]{0:T(128)} %gate.2.scalars.refs_0_, bf16[1024,128]{1,0:T(8,128)(2,1)} %get-tuple-element.336.small_ref.by_row, ...), custom_call_target="tpu_custom_call" | custom-call | flops 20000000000 | bytes 1024 | tf_op jit(solution)/shard_map/mlp/pallas_call | solution.py:71
  180.9 2.0 collective-permute-start.42
  183.9 18.1 %mlp.4 = (f32[640,1024]{1,0:T(8,128)}, f32[640,1024]{1,0:T(8,128)}, f32[640,1]{1,0:T(8,128)}, f32[1,1024]{1,0:T(1,128)}, bf16[4,2,128,1024]{3,2,1,0:T(8,128)(2,1)}, /*index=5*/bf16[4,2,128,1024]{3,2,1,0:T(8,128)(2,1)}) custom-call(s32[12]{0:T(128)} %gate.3.scalars, bf16[1024,128]{1,0:T(8,128)(2,1)} %get-tuple-element.336.small_ref.by_row, ...), custom_call_target="tpu_custom_call" | custom-call | flops 17999998976 | bytes 1024 | tf_op jit(solution)/shard_map/mlp/pallas_call | solution.py:71
  203.4 1.9 collective-permute-start.44
  205.3 22.9 %mlp.5 = (bf16[256,1024]{1,0:T(8,128)(2,1)}, bf16[256,1024]{1,0:T(8,128)(2,1)}, bf16[256,1024]{1,0:T(8,128)(2,1)}, bf16[256,1024]{1,0:T(8,128)(2,1)}, bf16[256,1...) custom-call(s32[12]{0:T(128)} %gate.2.scalars.refs_0_, ...), custom_call_target="tpu_custom_call" | custom-call | flops 17999998976 | bytes 1024 | tf_op jit(solution)/shard_map/mlp/pallas_call | solution.py:71
  230.7 2.1 fusion.4
  238.3 6.4 %collective-permute-done.48.refs_1_ = bf16[256,1152]{1,0:T(8,128)(2,1)} collective-permute-done((bf16[256,1152]{1,0:T(8,128)(2,1)}, bf16[256,1152]{1,0:T(8,128)(2,1)}, u32[]{:S(2)}, u32[]{:S(2)}) %collective-permute-start.48) | collective-permute-done | bytes 589856 | tf_op jit(solution)/shard_map/ppermute | solution.py:918
  244.8 11.6 %collective-permute-done.49.refs_2_ = bf16[256,1152]{1,0:T(8,128)(2,1)} collective-permute-done((bf16[256,1152]{1,0:T(8,128)(2,1)}, bf16[256,1152]{1,0:T(8,128)(2,1)}, u32[]{:S(2)}, u32[]{:S(2)}) %collective-permute-start.49) | collective-permute-done | bytes 589856 | tf_op jit(solution)/shard_map/ppermute | solution.py:918
  258.5 4.5 %collective-permute-done.46 = bf16[2,128,1024]{2,1,0:T(8,128)(2,1)S(1)} collective-permute-done((bf16[2,128,1024]{2,1,0:T(8,128)(2,1)}, bf16[2,128,1024]{2,1,0:T(8,128)(2,1)S(1)}, u32[]{:S(2)}, u32[]{:S(2)}) %collective-permute-start.46) | collective-permute-done | bytes 524320 | tf_op jit(solution)/shard_map/ppermute | solution.py:936
  263.0 1.8 fusion.3
  267.3 11.4 %middle.1 = (f32[256,1024]{1,0:T(8,128)}, f32[256,1024]{1,0:T(8,128)}, f32[16,1024]{1,0:T(8,128)}, bf16[8,4,32,256]{3,2,1,0:T(8,128)(2,1)}, bf16[8,4,32,256]{3,2...) custom-call(s32[4]{0:T(128)} %pad_add_fusion.scalars.order, ...), custom_call_target="tpu_custom_call" | custom-call | flops 11000000512 | bytes 1024 | tf_op jit(solution)/shard_map/middle/pallas_call | solution.py:71
  280.5 1.9 collective-permute-start.59
  291.7 1.7 collective-permute-start.53
  293.4 18.5 %attention_backward.1 = (bf16[1024,256]{1,0:T(8,128)(2,1)}, bf16[1024,256]{1,0:T(8,128)(2,1)}, bf16[1024,256]{1,0:T(8,128)(2,1)}) custom-call(s32[4]{0:T(128)} %pad_add_fusion.scalars.order, bf16[1024,768]{1,0:T(8,128)(2,1)} %get-tuple-element.314.q_ref.k_ref.v_ref, bf16[1024,768]{1,0:T(8,128)(2,1)} %get-tuple-element.314.q_ref.k_ref.v_ref, ...), custom_call_target="tpu_custom_call" | custom-call | flops 17999998976 | bytes 1024 | tf_op jit(solution)/shard_map/attention_backward/pallas_call | solution.py:71
  311.9 2.3 collective-permute-done.53
  314.2 2.2 fusion.2
  317.5 9.2 %qkv_back.1 = (bf16[256,1024]{1,0:T(8,128)(2,1)}, bf16[256,1024]{1,0:T(8,128)(2,1)}, bf16[256,1024]{1,0:T(8,128)(2,1)}, bf16[256,1024]{1,0:T(8,128)(2,1)}, bf16[...) custom-call(s32[12]{0:T(128)} %concatenate.47.scalars, ...), custom_call_target="tpu_custom_call" | custom-call | flops 8000000000 | bytes 1024 | tf_op jit(solution)/shard_map/qkv_back/pallas_call | solution.py:71
  329.6 1.8 collective-permute-start.67
  331.7 10.3 %collective-permute-done.66.refs_1_ = bf16[256,1024]{1,0:T(8,128)(2,1)} collective-permute-done((bf16[256,1024]{1,0:T(8,128)(2,1)}, bf16[256,1024]{1,0:T(8,128)(2,1)}, u32[]{:S(2)}, u32[]{:S(2)}) %collective-permute-start.66) | collective-permute-done | bytes 524320 | tf_op jit(solution)/shard_map/ppermute | solution.py:918
  342.0 1.9 collective-permute-done.65
  346.7 7.7 %collective-permute-done.64 = bf16[128,1024]{1,0:T(8,128)(2,1)S(1)} collective-permute-done((bf16[128,1024]{1,0:T(8,128)(2,1)S(1)}, bf16[128,1024]{1,0:T(8,128)(2,1)S(1)}, u32[]{:S(2)}, u32[]{:S(2)}) %collective-permute-start.64) | collective-permute-done | bytes 262176 | tf_op jit(solution)/shard_map/ppermute | solution.py:936
  355.8 1.9 collective-permute-start.70
  357.7 4.1 final.1
  361.8 5.1 %collective-permute-done.68 = bf16[128,1024]{1,0:T(8,128)(2,1)S(1)} collective-permute-done((bf16[128,1024]{1,0:T(8,128)(2,1)S(1)}, bf16[128,1024]{1,0:T(8,128)(2,1)S(1)}, u32[]{:S(2)}, u32[]{:S(2)}) %collective-permute-start.68) | collective-permute-done | bytes 262176 | tf_op jit(solution)/shard_map/ppermute | solution.py:936
  375.8 3.6 result.1
  390.5 4.4 %collective-permute-start.81 = (f32[24,1024]{1,0:T(8,128)S(1)}, f32[24,1024]{1,0:T(8,128)S(1)}, u32[]{:S(2)}, u32[]{:S(2)}) collective-permute-start(f32[24,1024]{1,0:T(8,128)S(1)} %add.359), channel_id=1, source_target_pairs={{0,16},{4,20},{8,24},{12,28},{16,0},{20,4},{24,8},{28,12},{1,17},{... | collective-permute-start | bytes 294920 | tf_op jit(solution)/shard_map/ppermute | solution.py:1264
  404.1 1.7 collective-permute-done.84
  (413 shorter events, 119.9 us)
Async XLA Ops:
  0.7 33.3 %collective-permute-start.5 = (bf16[256,1024]{1,0:T(8,128)(2,1)}, bf16[256,1024]{1,0:T(8,128)(2,1)}, u32[]{:S(2)}, u32[]{:S(2)}) collective-permute-start(bf16[256,1024]{1,0:T(8,128)(2,1)} %bitcast.323), channel_id=1, source_target_pairs={{0,1},{1,0},{2,3},{3,2},{4,5},{5,4},{6,7},{7,6},{8,9},{9,8},{10,11... | collective-permute-start | bytes 1572872 | tf_op jit(solution)/shard_map/ppermute | solution.py:918
  3.7 30.3 %collective-permute-start.6 = (bf16[256,1024]{1,0:T(8,128)(2,1)}, bf16[256,1024]{1,0:T(8,128)(2,1)}, u32[]{:S(2)}, u32[]{:S(2)}) collective-permute-start(bf16[256,1024]{1,0:T(8,128)(2,1)} %bitcast.324), channel_id=1, source_target_pairs={{0,2},{1,3},{2,0},{3,1},{4,6},{5,7},{6,4},{7,5},{8,10},{9,11},{10,... | collective-permute-start | bytes 1572872 | tf_op jit(solution)/shard_map/ppermute | solution.py:918
  18.6 15.4 %collective-permute-start.7 = (bf16[256,1024]{1,0:T(8,128)(2,1)}, bf16[256,1024]{1,0:T(8,128)(2,1)S(1)}, u32[]{:S(2)}, u32[]{:S(2)}) collective-permute-start(bf16[256,1024]{1,0:T(8,128)(2,1)} %bitcast.325), channel_id=1, source_target_pairs={{0,3},{1,2},{2,1},{3,0},{4,7},{5,6},{6,5},{7,4},{8,11},{9,10},{10,... | collective-permute-start | bytes 1572872 | tf_op jit(solution)/shard_map/ppermute | solution.py:918
  41.0 13.1 %collective-permute-start.13 = (bf16[128,1152]{1,0:T(8,128)(2,1)}, bf16[128,1152]{1,0:T(8,128)(2,1)}, u32[]{:S(2)}, u32[]{:S(2)}) collective-permute-start(bf16[128,1152]{1,0:T(8,128)(2,1)} %collective-permute-done.8.refs_2_), channel_id=1, source_target_pairs={{0,8},{4,12},{8,16},{12,20},{16,24},{20,28},{24,0},{28,4},{1,9},{5... | collective-permute-start | bytes 884744 | tf_op jit(solution)/shard_map/ppermute | solution.py:936
  41.0 13.1 %collective-permute-start.14 = (bf16[128,1152]{1,0:T(8,128)(2,1)}, bf16[128,1152]{1,0:T(8,128)(2,1)S(1)}, u32[]{:S(2)}, u32[]{:S(2)}) collective-permute-start(bf16[128,1152]{1,0:T(8,128)(2,1)} %collective-permute-done.8.refs_2_), channel_id=1, source_target_pairs={{0,4},{4,0},{8,12},{12,8},{16,20},{20,16},{24,28},{28,24},{1,5},{5... | collective-permute-start | bytes 884744 | tf_op jit(solution)/shard_map/ppermute | solution.py:939
  54.9 16.6 %collective-permute-start.16 = (bf16[2,128,1024]{2,1,0:T(8,128)(2,1)S(1)}, bf16[2,128,1024]{2,1,0:T(8,128)(2,1)S(1)}, u32[]{:S(2)}, u32[]{:S(2)}) collective-permute-start(bf16[2,128,1024]{2,1,0:T(8,128)(2,1)S(1)} %pad_maximum_fusion.3.refs_8_), channel_id=1, source_target_pairs={{0,8},{4,12},{8,16},{12,20},{16,24},{20,28},{24,0},{28,4},{1,9},{5... | collective-permute-start | bytes 1572872 | tf_op jit(solution)/shard_map/ppermute | solution.py:936
  60.0 26.4 %collective-permute-start.17 = (bf16[256,1024]{1,0:T(8,128)(2,1)}, bf16[256,1024]{1,0:T(8,128)(2,1)S(1)}, u32[]{:S(2)}, u32[]{:S(2)}) collective-permute-start(bf16[256,1024]{1,0:T(8,128)(2,1)} %get-tuple-element.320), channel_id=1, source_target_pairs={{0,1},{1,0},{2,3},{3,2},{4,5},{5,4},{6,7},{7,6},{8,9},{9,8},{10,11... | collective-permute-start | bytes 1572872 | tf_op jit(solution)/shard_map/ppermute | solution.py:918
  60.9 25.6 %collective-permute-start.18 = (bf16[256,1024]{1,0:T(8,128)(2,1)}, bf16[256,1024]{1,0:T(8,128)(2,1)S(1)}, u32[]{:S(2)}, u32[]{:S(2)}) collective-permute-start(bf16[256,1024]{1,0:T(8,128)(2,1)} %get-tuple-element.320), channel_id=1, source_target_pairs={{0,2},{1,3},{2,0},{3,1},{4,6},{5,7},{6,4},{7,5},{8,10},{9,11},{10,... | collective-permute-start | bytes 1572872 | tf_op jit(solution)/shard_map/ppermute | solution.py:918
  61.8 24.7 %collective-permute-start.19 = (bf16[256,1024]{1,0:T(8,128)(2,1)}, bf16[256,1024]{1,0:T(8,128)(2,1)S(1)}, u32[]{:S(2)}, u32[]{:S(2)}) collective-permute-start(bf16[256,1024]{1,0:T(8,128)(2,1)} %get-tuple-element.320), channel_id=1, source_target_pairs={{0,3},{1,2},{2,1},{3,0},{4,7},{5,6},{6,5},{7,4},{8,11},{9,10},{10,... | collective-permute-start | bytes 1572872 | tf_op jit(solution)/shard_map/ppermute | solution.py:918
  63.5 35.9 %collective-permute-start.23 = (bf16[4,128,1024]{2,1,0:T(8,128)(2,1)S(1)}, bf16[4,128,1024]{2,1,0:T(8,128)(2,1)S(1)}, u32[]{:S(2)}, u32[]{:S(2)}) collective-permute-start(bf16[4,128,1024]{2,1,0:T(8,128)(2,1)S(1)} %pad_maximum_fusion.refs_8_), channel_id=1, source_target_pairs={{0,8},{4,12},{8,16},{12,20},{16,24},{20,28},{24,0},{28,4},{1,9},{5... | collective-permute-start | bytes 3145736 | tf_op jit(solution)/shard_map/ppermute | solution.py:936
  71.5 36.1 %collective-permute-start.27 = (bf16[2,128,1024]{2,1,0:T(8,128)(2,1)S(1)}, bf16[2,128,1024]{2,1,0:T(8,128)(2,1)}, u32[]{:S(2)}, u32[]{:S(2)}) collective-permute-start(bf16[2,128,1024]{2,1,0:T(8,128)(2,1)S(1)} %collective-permute-done.16.refs_9_), channel_id=1, source_target_pairs={{0,8},{4,12},{8,16},{12,20},{16,24},{20,28},{24,0},{28,4},{1,9},{5... | collective-permute-start | bytes 1572872 | tf_op jit(solution)/shard_map/ppermute | solution.py:936
  99.4 15.2 %collective-permute-start.24 = (bf16[256,1024]{1,0:T(8,128)(2,1)}, bf16[256,1024]{1,0:T(8,128)(2,1)}, u32[]{:S(2)}, u32[]{:S(2)}) collective-permute-start(bf16[256,1024]{1,0:T(8,128)(2,1)} %get-tuple-element.338.refs_0_), channel_id=1, source_target_pairs={{0,1},{1,0},{2,3},{3,2},{4,5},{5,4},{6,7},{7,6},{8,9},{9,8},{10,11... | collective-permute-start | bytes 1572872 | tf_op jit(solution)/shard_map/ppermute | solution.py:918
  100.7 23.3 %collective-permute-start.25 = (bf16[256,1024]{1,0:T(8,128)(2,1)}, bf16[256,1024]{1,0:T(8,128)(2,1)}, u32[]{:S(2)}, u32[]{:S(2)}) collective-permute-start(bf16[256,1024]{1,0:T(8,128)(2,1)} %get-tuple-element.338.refs_0_), channel_id=1, source_target_pairs={{0,2},{1,3},{2,0},{3,1},{4,6},{5,7},{6,4},{7,5},{8,10},{9,11},{10,... | collective-permute-start | bytes 1572872 | tf_op jit(solution)/shard_map/ppermute | solution.py:918
  101.3 22.7 %collective-permute-start.26 = (bf16[256,1024]{1,0:T(8,128)(2,1)}, bf16[256,1024]{1,0:T(8,128)(2,1)}, u32[]{:S(2)}, u32[]{:S(2)}) collective-permute-start(bf16[256,1024]{1,0:T(8,128)(2,1)} %get-tuple-element.338.refs_0_), channel_id=1, source_target_pairs={{0,3},{1,2},{2,1},{3,0},{4,7},{5,6},{6,5},{7,4},{8,11},{9,10},{10,... | collective-permute-start | bytes 1572872 | tf_op jit(solution)/shard_map/ppermute | solution.py:918
  106.9 28.2 %collective-permute-start.30 = (bf16[4,128,1024]{2,1,0:T(8,128)(2,1)}, bf16[4,128,1024]{2,1,0:T(8,128)(2,1)}, u32[]{:S(2)}, u32[]{:S(2)}) collective-permute-start(bf16[4,128,1024]{2,1,0:T(8,128)(2,1)} %copy-done.30), channel_id=1, source_target_pairs={{0,8},{4,12},{8,16},{12,20},{16,24},{20,28},{24,0},{28,4},{1,9},{5... | collective-permute-start | bytes 3145736 | tf_op jit(solution)/shard_map/ppermute | solution.py:936
  124.0 13.3 %collective-permute-start.28 = (bf16[256,1024]{1,0:T(8,128)(2,1)S(1)}, bf16[256,1024]{1,0:T(8,128)(2,1)S(1)}, u32[]{:S(2)}, u32[]{:S(2)}) collective-permute-start(bf16[256,1024]{1,0:T(8,128)(2,1)S(1)} %convolution_convert_fusion.refs_4_), channel_id=1, source_target_pairs={{0,1},{1,0},{2,3},{3,2},{4,5},{5,4},{6,7},{7,6},{8,9},{9,8},{10,11... | collective-permute-start | bytes 1572872 | tf_op jit(solution)/shard_map/ppermute | solution.py:918
  124.9 21.6 %collective-permute-start.29 = (bf16[256,1024]{1,0:T(8,128)(2,1)S(1)}, bf16[256,1024]{1,0:T(8,128)(2,1)S(1)}, u32[]{:S(2)}, u32[]{:S(2)}) collective-permute-start(bf16[256,1024]{1,0:T(8,128)(2,1)S(1)} %convolution_convert_fusion.refs_4_), channel_id=1, source_target_pairs={{0,2},{1,3},{2,0},{3,1},{4,6},{5,7},{6,4},{7,5},{8,10},{9,11},{10,... | collective-permute-start | bytes 1572872 | tf_op jit(solution)/shard_map/ppermute | solution.py:918
  125.7 20.7 %collective-permute-start.32 = (bf16[2,128,1024]{2,1,0:T(8,128)(2,1)}, bf16[2,128,1024]{2,1,0:T(8,128)(2,1)S(1)}, u32[]{:S(2)}, u32[]{:S(2)}) collective-permute-start(bf16[2,128,1024]{2,1,0:T(8,128)(2,1)} %collective-permute-done.27.refs_1_.refs_10_), channel_id=1, source_target_pairs={{0,8},{4,12},{8,16},{12,20},{16,24},{20,28},{24,0},{28,4},{1,9},{5... | collective-permute-start | bytes 1572872 | tf_op jit(solution)/shard_map/ppermute | solution.py:936
  135.1 11.4 %collective-permute-start.31 = (bf16[256,1024]{1,0:T(8,128)(2,1)S(1)}, bf16[256,1024]{1,0:T(8,128)(2,1)S(1)}, u32[]{:S(2)}, u32[]{:S(2)}) collective-permute-start(bf16[256,1024]{1,0:T(8,128)(2,1)S(1)} %convolution_convert_fusion.refs_4_), channel_id=1, source_target_pairs={{0,3},{1,2},{2,1},{3,0},{4,7},{5,6},{6,5},{7,4},{8,11},{9,10},{10,... | collective-permute-start | bytes 1572872 | tf_op jit(solution)/shard_map/ppermute | solution.py:918
  148.2 27.9 %collective-permute-start.38 = (bf16[4,128,1024]{2,1,0:T(8,128)(2,1)}, bf16[4,128,1024]{2,1,0:T(8,128)(2,1)}, u32[]{:S(2)}, u32[]{:S(2)}) collective-permute-start(bf16[4,128,1024]{2,1,0:T(8,128)(2,1)} %collective-permute-done.30.refs_10_), channel_id=1, source_target_pairs={{0,8},{4,12},{8,16},{12,20},{16,24},{20,28},{24,0},{28,4},{1,9},{5... | collective-permute-start | bytes 3145736 | tf_op jit(solution)/shard_map/ppermute | solution.py:936
  150.7 25.4 %collective-permute-start.39 = (bf16[4,128,1024]{2,1,0:T(8,128)(2,1)S(1)}, bf16[4,128,1024]{2,1,0:T(8,128)(2,1)S(1)}, u32[]{:S(2)}, u32[]{:S(2)}) collective-permute-start(bf16[4,128,1024]{2,1,0:T(8,128)(2,1)S(1)} %pad_maximum_fusion.refs_8_), channel_id=1, source_target_pairs={{0,4},{4,0},{8,12},{12,8},{16,20},{20,16},{24,28},{28,24},{1,5},{5... | collective-permute-start | bytes 3145736 | tf_op jit(solution)/shard_map/ppermute | solution.py:939
  150.9 25.3 %collective-permute-start.40 = (bf16[4,128,1024]{2,1,0:T(8,128)(2,1)}, bf16[4,128,1024]{2,1,0:T(8,128)(2,1)S(1)}, u32[]{:S(2)}, u32[]{:S(2)}) collective-permute-start(bf16[4,128,1024]{2,1,0:T(8,128)(2,1)} %copy-done.30), channel_id=1, source_target_pairs={{0,4},{4,0},{8,12},{12,8},{16,20},{20,16},{24,28},{28,24},{1,5},{5... | collective-permute-start | bytes 3145736 | tf_op jit(solution)/shard_map/ppermute | solution.py:939
  151.2 24.9 %collective-permute-start.41 = (bf16[4,128,1024]{2,1,0:T(8,128)(2,1)}, bf16[4,128,1024]{2,1,0:T(8,128)(2,1)S(1)}, u32[]{:S(2)}, u32[]{:S(2)}) collective-permute-start(bf16[4,128,1024]{2,1,0:T(8,128)(2,1)} %collective-permute-done.30.refs_10_), channel_id=1, source_target_pairs={{0,4},{4,0},{8,12},{12,8},{16,20},{20,16},{24,28},{28,24},{1,5},{5... | collective-permute-start | bytes 3145736 | tf_op jit(solution)/shard_map/ppermute | solution.py:939
  180.9 21.2 %collective-permute-start.42 = (bf16[2,128,1024]{2,1,0:T(8,128)(2,1)S(1)}, bf16[2,128,1024]{2,1,0:T(8,128)(2,1)S(1)}, u32[]{:S(2)}, u32[]{:S(2)}) collective-permute-start(bf16[2,128,1024]{2,1,0:T(8,128)(2,1)S(1)} %fusion.6), channel_id=1, source_target_pairs={{0,8},{4,12},{8,16},{12,20},{16,24},{20,28},{24,0},{28,4},{1,9},{5... | collective-permute-start | bytes 1572872 | tf_op jit(solution)/shard_map/ppermute | solution.py:936
  202.0 30.8 %collective-permute-start.45 = (bf16[4,2,128,1024]{3,2,1,0:T(8,128)(2,1)}, bf16[4,2,128,1024]{3,2,1,0:T(8,128)(2,1)S(1)}, u32[]{:S(2)}, u32[]{:S(2)}) collective-permute-start(bf16[4,2,128,1024]{3,2,1,0:T(8,128)(2,1)} %get-tuple-element.387), channel_id=1, source_target_pairs={{0,4},{4,0},{8,12},{12,8},{16,20},{20,16},{24,28},{28,24},{1,5},{5... | collective-permute-start | bytes 6291464 | tf_op jit(solution)/shard_map/ppermute | solution.py:939
  203.4 27.3 %collective-permute-start.44 = (bf16[2,128,1024]{2,1,0:T(8,128)(2,1)S(1)}, bf16[2,128,1024]{2,1,0:T(8,128)(2,1)S(1)}, u32[]{:S(2)}, u32[]{:S(2)}) collective-permute-start(bf16[2,128,1024]{2,1,0:T(8,128)(2,1)S(1)} %fusion.5), channel_id=1, source_target_pairs={{0,8},{4,12},{8,16},{12,20},{16,24},{20,28},{24,0},{28,4},{1,9},{5... | collective-permute-start | bytes 1572872 | tf_op jit(solution)/shard_map/ppermute | solution.py:936
  228.2 16.5 %collective-permute-start.48 = (bf16[256,1152]{1,0:T(8,128)(2,1)}, bf16[256,1152]{1,0:T(8,128)(2,1)}, u32[]{:S(2)}, u32[]{:S(2)}) collective-permute-start(bf16[256,1152]{1,0:T(8,128)(2,1)} %get-tuple-element.393), channel_id=1, source_target_pairs={{0,1},{1,0},{2,3},{3,2},{4,5},{5,4},{6,7},{7,6},{8,9},{9,8},{10,11... | collective-permute-start | bytes 1769480 | tf_op jit(solution)/shard_map/ppermute | solution.py:918
  229.5 27.0 %collective-permute-start.49 = (bf16[256,1152]{1,0:T(8,128)(2,1)}, bf16[256,1152]{1,0:T(8,128)(2,1)}, u32[]{:S(2)}, u32[]{:S(2)}) collective-permute-start(bf16[256,1152]{1,0:T(8,128)(2,1)} %get-tuple-element.394), channel_id=1, source_target_pairs={{0,2},{1,3},{2,0},{3,1},{4,6},{5,7},{6,4},{7,5},{8,10},{9,11},{10,... | collective-permute-start | bytes 1769480 | tf_op jit(solution)/shard_map/ppermute | solution.py:918
  235.6 22.0 %collective-permute-start.50 = (bf16[256,1152]{1,0:T(8,128)(2,1)S(1)}, bf16[256,1152]{1,0:T(8,128)(2,1)}, u32[]{:S(2)}, u32[]{:S(2)}) collective-permute-start(bf16[256,1152]{1,0:T(8,128)(2,1)S(1)} %copy-done.35), channel_id=1, source_target_pairs={{0,3},{1,2},{2,1},{3,0},{4,7},{5,6},{6,5},{7,4},{8,11},{9,10},{10,... | collective-permute-start | bytes 1769480 | tf_op jit(solution)/shard_map/ppermute | solution.py:918
  236.8 21.7 %collective-permute-start.47 = (bf16[2,128,1024]{2,1,0:T(8,128)(2,1)S(1)}, bf16[2,128,1024]{2,1,0:T(8,128)(2,1)}, u32[]{:S(2)}, u32[]{:S(2)}) collective-permute-start(bf16[2,128,1024]{2,1,0:T(8,128)(2,1)S(1)} %fusion.7), channel_id=1, source_target_pairs={{0,8},{4,12},{8,16},{12,20},{16,24},{20,28},{24,0},{28,4},{1,9},{5... | collective-permute-start | bytes 1572872 | tf_op jit(solution)/shard_map/ppermute | solution.py:936
  238.0 24.9 %collective-permute-start.46 = (bf16[2,128,1024]{2,1,0:T(8,128)(2,1)}, bf16[2,128,1024]{2,1,0:T(8,128)(2,1)S(1)}, u32[]{:S(2)}, u32[]{:S(2)}) collective-permute-start(bf16[2,128,1024]{2,1,0:T(8,128)(2,1)} %fusion.4), channel_id=1, source_target_pairs={{0,8},{4,12},{8,16},{12,20},{16,24},{20,28},{24,0},{28,4},{1,9},{5... | collective-permute-start | bytes 1572872 | tf_op jit(solution)/shard_map/ppermute | solution.py:936
  257.7 32.4 %collective-permute-start.51 = (bf16[4,2,128,1024]{3,2,1,0:T(8,128)(2,1)}, bf16[4,2,128,1024]{3,2,1,0:T(8,128)(2,1)}, u32[]{:S(2)}, u32[]{:S(2)}) collective-permute-start(bf16[4,2,128,1024]{3,2,1,0:T(8,128)(2,1)} %get-tuple-element.422), channel_id=1, source_target_pairs={{0,4},{4,0},{8,12},{12,8},{16,20},{20,16},{24,28},{28,24},{1,5},{5... | collective-permute-start | bytes 6291464 | tf_op jit(solution)/shard_map/ppermute | solution.py:939
  264.8 14.0 %collective-permute-start.55 = (bf16[256,1024]{1,0:T(8,128)(2,1)S(1)}, bf16[256,1024]{1,0:T(8,128)(2,1)S(1)}, u32[]{:S(2)}, u32[]{:S(2)}) collective-permute-start(bf16[256,1024]{1,0:T(8,128)(2,1)S(1)} %copy-done.45), channel_id=1, source_target_pairs={{0,1},{1,0},{2,3},{3,2},{4,5},{5,4},{6,7},{7,6},{8,9},{9,8},{10,11... | collective-permute-start | bytes 1572872 | tf_op jit(solution)/shard_map/ppermute | solution.py:918
  266.1 12.7 %collective-permute-start.56 = (bf16[256,1024]{1,0:T(8,128)(2,1)S(1)}, bf16[256,1024]{1,0:T(8,128)(2,1)S(1)}, u32[]{:S(2)}, u32[]{:S(2)}) collective-permute-start(bf16[256,1024]{1,0:T(8,128)(2,1)S(1)} %copy-done.44), channel_id=1, source_target_pairs={{0,2},{1,3},{2,0},{3,1},{4,6},{5,7},{6,4},{7,5},{8,10},{9,11},{10,... | collective-permute-start | bytes 1572872 | tf_op jit(solution)/shard_map/ppermute | solution.py:918
  267.3 15.0 %collective-permute-start.52 = (bf16[2,128,1024]{2,1,0:T(8,128)(2,1)S(1)}, bf16[2,128,1024]{2,1,0:T(8,128)(2,1)S(1)}, u32[]{:S(2)}, u32[]{:S(2)}) collective-permute-start(bf16[2,128,1024]{2,1,0:T(8,128)(2,1)S(1)} %fusion.3), channel_id=1, source_target_pairs={{0,8},{4,12},{8,16},{12,20},{16,24},{20,28},{24,0},{28,4},{1,9},{5... | collective-permute-start | bytes 1572872 | tf_op jit(solution)/shard_map/ppermute | solution.py:936
  286.6 29.8 %collective-permute-start.60 = (bf16[1024,256]{1,0:T(8,128)(2,1)}, bf16[1024,256]{1,0:T(8,128)(2,1)S(1)}, u32[]{:S(2)}, u32[]{:S(2)}) collective-permute-start(bf16[1024,256]{1,0:T(8,128)(2,1)} %bitcast.331), channel_id=1, source_target_pairs={{0,1},{1,0},{2,3},{3,2},{4,5},{5,4},{6,7},{7,6},{8,9},{9,8},{10,11... | collective-permute-start | bytes 1572872 | tf_op jit(solution)/shard_map/ppermute | solution.py:918
  287.9 28.5 %collective-permute-start.61 = (bf16[1024,256]{1,0:T(8,128)(2,1)}, bf16[1024,256]{1,0:T(8,128)(2,1)S(1)}, u32[]{:S(2)}, u32[]{:S(2)}) collective-permute-start(bf16[1024,256]{1,0:T(8,128)(2,1)} %bitcast.330), channel_id=1, source_target_pairs={{0,2},{1,3},{2,0},{3,1},{4,6},{5,7},{6,4},{7,5},{8,10},{9,11},{10,... | collective-permute-start | bytes 1572872 | tf_op jit(solution)/shard_map/ppermute | solution.py:918
  289.5 26.9 %collective-permute-start.62 = (bf16[1024,256]{1,0:T(8,128)(2,1)}, bf16[1024,256]{1,0:T(8,128)(2,1)S(1)}, u32[]{:S(2)}, u32[]{:S(2)}) collective-permute-start(bf16[1024,256]{1,0:T(8,128)(2,1)} %bitcast.329), channel_id=1, source_target_pairs={{0,3},{1,2},{2,1},{3,0},{4,7},{5,6},{6,5},{7,4},{8,11},{9,10},{10,... | collective-permute-start | bytes 1572872 | tf_op jit(solution)/shard_map/ppermute | solution.py:918
  291.3 20.5 %collective-permute-start.54 = (bf16[2,128,1024]{2,1,0:T(8,128)(2,1)S(1)}, bf16[2,128,1024]{2,1,0:T(8,128)(2,1)S(1)}, u32[]{:S(2)}, u32[]{:S(2)}) collective-permute-start(bf16[2,128,1024]{2,1,0:T(8,128)(2,1)S(1)} %fusion.1), channel_id=1, source_target_pairs={{0,8},{4,12},{8,16},{12,20},{16,24},{20,28},{24,0},{28,4},{1,9},{5... | collective-permute-start | bytes 1572872 | tf_op jit(solution)/shard_map/ppermute | solution.py:936
  291.7 22.5 %collective-permute-start.53 = (bf16[2,128,1024]{2,1,0:T(8,128)(2,1)S(1)}, bf16[2,128,1024]{2,1,0:T(8,128)(2,1)S(1)}, u32[]{:S(2)}, u32[]{:S(2)}) collective-permute-start(bf16[2,128,1024]{2,1,0:T(8,128)(2,1)S(1)} %fusion.8), channel_id=1, source_target_pairs={{0,8},{4,12},{8,16},{12,20},{16,24},{20,28},{24,0},{28,4},{1,9},{5... | collective-permute-start | bytes 1572872 | tf_op jit(solution)/shard_map/ppermute | solution.py:936
  326.8 17.1 %collective-permute-start.63 = (bf16[4,128,1024]{2,1,0:T(8,128)(2,1)}, bf16[4,128,1024]{2,1,0:T(8,128)(2,1)}, u32[]{:S(2)}, u32[]{:S(2)}) collective-permute-start(bf16[4,128,1024]{2,1,0:T(8,128)(2,1)} %get-tuple-element.471), channel_id=1, source_target_pairs={{0,4},{4,0},{8,12},{12,8},{16,20},{20,16},{24,28},{28,24},{1,5},{5... | collective-permute-start | bytes 3145736 | tf_op jit(solution)/shard_map/ppermute | solution.py:939
  326.9 15.1 %collective-permute-start.66 = (bf16[256,1024]{1,0:T(8,128)(2,1)}, bf16[256,1024]{1,0:T(8,128)(2,1)}, u32[]{:S(2)}, u32[]{:S(2)}) collective-permute-start(bf16[256,1024]{1,0:T(8,128)(2,1)} %get-tuple-element.475), channel_id=1, source_target_pairs={{0,1},{1,0},{2,3},{3,2},{4,5},{5,4},{6,7},{7,6},{8,9},{9,8},{10,11... | collective-permute-start | bytes 1572872 | tf_op jit(solution)/shard_map/ppermute | solution.py:918
  327.8 16.1 %collective-permute-start.65 = (bf16[2,128,1024]{2,1,0:T(8,128)(2,1)}, bf16[2,128,1024]{2,1,0:T(8,128)(2,1)}, u32[]{:S(2)}, u32[]{:S(2)}) collective-permute-start(bf16[2,128,1024]{2,1,0:T(8,128)(2,1)} %fusion.2), channel_id=1, source_target_pairs={{0,8},{4,12},{8,16},{12,20},{16,24},{20,28},{24,0},{28,4},{1,9},{5... | collective-permute-start | bytes 1572872 | tf_op jit(solution)/shard_map/ppermute | solution.py:936
  329.6 25.9 %collective-permute-start.67 = (bf16[256,1024]{1,0:T(8,128)(2,1)}, bf16[256,1024]{1,0:T(8,128)(2,1)S(1)}, u32[]{:S(2)}, u32[]{:S(2)}) collective-permute-start(bf16[256,1024]{1,0:T(8,128)(2,1)} %get-tuple-element.478), channel_id=1, source_target_pairs={{0,2},{1,3},{2,0},{3,1},{4,6},{5,7},{6,4},{7,5},{8,10},{9,11},{10,... | collective-permute-start | bytes 1572872 | tf_op jit(solution)/shard_map/ppermute | solution.py:918
  331.4 24.1 %collective-permute-start.69 = (bf16[256,1024]{1,0:T(8,128)(2,1)}, bf16[256,1024]{1,0:T(8,128)(2,1)S(1)}, u32[]{:S(2)}, u32[]{:S(2)}) collective-permute-start(bf16[256,1024]{1,0:T(8,128)(2,1)} %get-tuple-element.494), channel_id=1, source_target_pairs={{0,3},{1,2},{2,1},{3,0},{4,7},{5,6},{6,5},{7,4},{8,11},{9,10},{10,... | collective-permute-start | bytes 1572872 | tf_op jit(solution)/shard_map/ppermute | solution.py:918
  355.5 11.3 %collective-permute-start.68 = (bf16[128,1024]{1,0:T(8,128)(2,1)S(1)}, bf16[128,1024]{1,0:T(8,128)(2,1)S(1)}, u32[]{:S(2)}, u32[]{:S(2)}) collective-permute-start(bf16[128,1024]{1,0:T(8,128)(2,1)S(1)} %fusion.10), channel_id=1, source_target_pairs={{0,8},{4,12},{8,16},{12,20},{16,24},{20,28},{24,0},{28,4},{1,9},{5... | collective-permute-start | bytes 786440 | tf_op jit(solution)/shard_map/ppermute | solution.py:936
  355.8 16.4 %collective-permute-start.70 = (bf16[256,1024]{1,0:T(8,128)(2,1)S(1)}, bf16[256,1024]{1,0:T(8,128)(2,1)S(1)}, u32[]{:S(2)}, u32[]{:S(2)}) collective-permute-start(bf16[256,1024]{1,0:T(8,128)(2,1)S(1)} %copy-done.36), channel_id=1, source_target_pairs={{0,3},{1,2},{2,1},{3,0},{4,7},{5,6},{6,5},{7,4},{8,11},{9,10},{10,... | collective-permute-start | bytes 1572872 | tf_op jit(solution)/shard_map/ppermute | solution.py:918
  357.7 21.7 %collective-permute-start.72 = (bf16[2,128,1024]{2,1,0:T(8,128)(2,1)S(1)}, bf16[2,128,1024]{2,1,0:T(8,128)(2,1)S(1)}, u32[]{:S(2)}, u32[]{:S(2)}) collective-permute-start(bf16[2,128,1024]{2,1,0:T(8,128)(2,1)S(1)} %fusion), channel_id=1, source_target_pairs={{0,8},{4,12},{8,16},{12,20},{16,24},{20,28},{24,0},{28,4},{1,9},{5... | collective-permute-start | bytes 1572872 | tf_op jit(solution)/shard_map/ppermute | solution.py:936
  (106 other events, 1020.6 us)
